TPU v7x, 256 devices: a whole 4x4x8 slice. The times are simulated.
256 devices in a mesh: user: 32 (over y, z), hist: 8 (over x, core).
Axes of the slice: x: 4, y: 4, z: 8, core: 2. Of those that a mesh axis runs over, the one named last changes fastest.
Arguments:
- quot_ids: int32 [64, 2048], P('user', 'hist'), may hold values from 0 to 2047
- rem_ids: int32 [64, 2048], P('user', 'hist'), may hold values from 0 to 65535, as said below
- lengths: int32 [64], P('user'), may hold values from 426 to 2048, as said below
- log_decay: float32 [64, 4, 2048], P('user', None, 'hist'), may hold values from -1.1 to 0
- quot_table: bfloat16 [2048, 256], replicated, may hold values from -6 to 6
- rem_table: bfloat16 [65536, 256], P('user'), may hold values from -6 to 6
- w_query: bfloat16 [256, 256], replicated, may hold values from -0.375 to 0.375
- w_key: bfloat16 [256, 256], replicated, may hold values from -0.375 to 0.375
- w_value: bfloat16 [256, 256], replicated, may hold values from -0.375 to 0.375
- w_out: bfloat16 [256, 256], replicated, may hold values from -0.375 to 0.375
- cotangent: bfloat16 [64, 2048, 256], P('user', 'hist'), may hold values from -0.59765625 to 0.59765625
Outputs:
- output: bfloat16 [64, 2048, 256], P('user', 'hist')
- quot_grad: float32 [2048, 256], replicated
- rem_grad: float32 [65536, 256], P('user')
Inputs may be any that keep to these rules, and one draw needn't show every extreme that they name: rem_ids[u, t] // 2048 names a shard of the remainder table. In each aligned block of 256 events of one user (events b * 256 to (b + 1) * 256 - 1), no shard is named by more than 16 events, and one shard, the same for all blocks, is named by exactly 16. The valid events of user u are its first lengths[u] ones.
All inputs are finite; a program needn't handle non-finite values.
Results may differ from a plain program's by a relative error of at most 0.0073.
Values may be sent and summed in bfloat16 or wider, within the bound.
No kernel may reach another device: no remote copies, remote signals or barrier semaphores. Data moves between devices by JAX's collectives and lax.ppermute only.
A program may use at most 192 MiB of HBM per device.

v0:
```python
import math

import jax
import jax.numpy as jnp
from jax import lax
from jax.sharding import PartitionSpec as P

largest_value = lax.Precision.HIGHEST


def carried_in(part, axis, combine, identity):
    place = lax.axis_index(axis)
    gathered = jax.tree.map(lambda a: lax.all_gather(a, axis), part)
    state = jax.tree.map(lambda a, e: jnp.zeros_like(a) + jnp.asarray(e, a.dtype), part, identity)

    def one(step, state):
        return combine(
            state, jax.tree.map(lambda a: lax.dynamic_index_in_dim(a, step, 0, False), gathered)
        )

    return lax.fori_loop(0, place, one, state)


def carried_in_2(shard, axis, combine, identity):
    peers, place = (lax.axis_size(axis), lax.axis_index(axis))
    everything = jax.tree.map(
        lambda part, kind: lax.all_gather(part.astype(kind), axis),
        shard,
        (jnp.bfloat16, jnp.bfloat16),
    )
    start = jax.tree.map(
        lambda part, zero: jnp.broadcast_to(jnp.asarray(zero, part.dtype), part.shape),
        shard,
        identity,
    )

    def step(k, before):
        at = peers - 1 - k
        reached = at > place
        new = combine(
            before, jax.tree.map(lambda part, own: part[at].astype(own.dtype), everything, shard)
        )
        return jax.tree.map(lambda a, b: jnp.where(reached, a, b), new, before)

    return lax.fori_loop(0, peers, step, start)


def decay_mask(cumulative):
    length = cumulative.shape[-1]
    gap = cumulative[..., :, None] - cumulative[..., None, :]
    lower_tri = jnp.arange(length)[:, None] >= jnp.arange(length)[None, :]
    return jnp.where(lower_tri, jnp.exp(jnp.minimum(gap, 0.0)), 0.0)


def link_states(earlier, following):
    return (earlier[0] * following[0], following[0][..., None, None] * earlier[1] + following[1])


def body(
    quot_ids,
    rem_ids,
    lengths,
    log_decay,
    quot_table,
    rem_table,
    w_query,
    w_key,
    w_value,
    w_out,
    cotangent,
):
    user_count, block_len = quot_ids.shape
    feature_width = quot_table.shape[1]
    head_count = log_decay.shape[1]
    head_size = feature_width // head_count
    shards = lax.axis_size("user")
    hist_dev = lax.axis_size("hist")
    rows_own = rem_table.shape[0]
    capacity = 2 * block_len // shards
    history = block_len * hist_dev
    score_scale = 1.0 / math.sqrt(head_size * history)
    slot_total = float(user_count * shards * history)
    own_events = jnp.sum(lengths.astype(jnp.float32))
    all_events = lax.psum(own_events, "user")
    grad_ratio = slot_total / all_events
    flat_ids = rem_ids.reshape(-1)
    owners = flat_ids // rows_own
    matches = (
        owners.reshape(user_count, block_len)[..., None] == jnp.arange(shards, dtype=jnp.int32)
    ).astype(jnp.int32)
    before = jnp.cumsum(matches, axis=1) - matches
    ranking = jnp.sum(before * matches, axis=-1).reshape(-1)
    user_of = jnp.repeat(jnp.arange(user_count, dtype=jnp.int32), block_len)
    slot_index = (owners * user_count + user_of) * capacity + ranking
    requests = (
        jnp.full((shards * user_count * capacity,), -1, jnp.int32).at[slot_index].set(flat_ids)
    )
    requests = requests.reshape(shards, user_count * capacity)
    base_row = lax.axis_index("user") * rows_own
    wanted = lax.all_to_all(requests, "user", split_axis=0, concat_axis=0, tiled=True)
    present = wanted >= 0
    local_row = jnp.where(present, wanted - base_row, 0)
    found_rows = jnp.where(present[..., None], rem_table[local_row], jnp.zeros((), jnp.bfloat16))
    answered = lax.all_to_all(found_rows, "user", split_axis=0, concat_axis=0, tiled=True)
    rem_emb = answered.reshape(-1, feature_width)[slot_index]
    quot_emb = quot_table[quot_ids.reshape(-1)]
    embedded = (quot_emb.astype(jnp.float32) * rem_emb.astype(jnp.float32)).astype(jnp.bfloat16)

    def project(matrix):
        result = jnp.dot(embedded, matrix, preferred_element_type=jnp.float32).astype(jnp.bfloat16)
        return result.reshape(user_count, block_len, head_count, head_size)

    query_rows = project(w_query)
    key_rows = project(w_key)
    value_rows = project(w_value)
    cumulative = jnp.cumsum(log_decay, axis=-1)
    block_end = cumulative[..., -1]
    decay_all = jnp.exp(block_end)
    growth = jnp.exp(cumulative).transpose(0, 2, 1)[..., None]
    falloff = jnp.exp(block_end[..., None] - cumulative).transpose(0, 2, 1)[..., None]
    local_state = jnp.einsum(
        "ulhd,ulhe->uhde",
        key_rows.astype(jnp.float32) * falloff,
        value_rows.astype(jnp.float32),
        precision=largest_value,
    )
    entering = carried_in(
        (decay_all, local_state),
        "hist",
        link_states,
        (jnp.ones_like(decay_all), jnp.zeros_like(local_state)),
    )[1]

    def forward_user(inputs):
        single_query, single_key, single_value, cum_one, grow_one, state_one = inputs
        score_matrix = jnp.einsum(
            "tbc,xbc->btx", single_query, single_key, preferred_element_type=jnp.float32
        )
        weight_matrix = (score_scale * score_matrix * decay_mask(cum_one)).astype(jnp.bfloat16)
        within_bounds = jnp.einsum(
            "tov,vtp->otp", weight_matrix, single_value, preferred_element_type=jnp.float32
        )
        carried = score_scale * jnp.einsum(
            "lhd,hde->lhe",
            single_query.astype(jnp.float32) * grow_one,
            state_one,
            precision=largest_value,
        )
        return ((within_bounds + carried).astype(jnp.bfloat16), weight_matrix)

    mixed, weight_matrix = lax.map(
        forward_user, (query_rows, key_rows, value_rows, cumulative, growth, entering)
    )
    output = jnp.dot(
        mixed.reshape(-1, feature_width), w_out, preferred_element_type=jnp.float32
    ).astype(jnp.bfloat16)
    output = output.reshape(user_count, block_len, feature_width)
    position = lax.axis_index("hist") * block_len + jnp.arange(block_len, dtype=jnp.int32)
    in_history = position[None, :] < lengths[:, None]
    masked_cot = jnp.where(in_history[..., None], cotangent.astype(jnp.float32), 0.0).astype(
        jnp.bfloat16
    )
    dmixed = jnp.dot(
        masked_cot.reshape(-1, feature_width), w_out.T, preferred_element_type=jnp.float32
    ).astype(jnp.bfloat16)
    dmixed = dmixed.reshape(user_count, block_len, head_count, head_size)
    local_grad = jnp.einsum(
        "ulhd,ulhe->uhde",
        query_rows.astype(jnp.float32) * growth,
        dmixed.astype(jnp.float32),
        precision=largest_value,
    )
    leaving = carried_in_2(
        (decay_all, local_grad),
        "hist",
        link_states,
        (jnp.ones_like(decay_all), jnp.zeros_like(local_grad)),
    )[1]

    def backward_user(inputs):
        (
            single_query,
            single_key,
            single_value,
            dmixed_one,
            cum_one,
            grow_one,
            fall_one,
            weight_one,
            state_one,
            leaving_single,
        ) = inputs
        dscores = jnp.einsum(
            "lhe,mhe->hlm", dmixed_one, single_value, preferred_element_type=jnp.float32
        )
        weight_gradient = (score_scale * dscores * decay_mask(cum_one)).astype(jnp.bfloat16)
        dquery = jnp.einsum(
            "tov,vtp->otp", weight_gradient, single_key, preferred_element_type=jnp.float32
        ) + score_scale * grow_one * jnp.einsum(
            "hde,lhe->lhd", state_one, dmixed_one.astype(jnp.float32), precision=largest_value
        )
        dkeys = jnp.einsum(
            "euq,uex->qex", weight_gradient, single_query, preferred_element_type=jnp.float32
        ) + score_scale * fall_one * jnp.einsum(
            "kcg,wkg->wkc",
            leaving_single,
            single_value.astype(jnp.float32),
            precision=largest_value,
        )
        dvalue = jnp.einsum(
            "hlm,lhe->mhe", weight_one, dmixed_one, preferred_element_type=jnp.float32
        ) + score_scale * fall_one * jnp.einsum(
            "zxr,czx->czr", leaving_single, single_key.astype(jnp.float32), precision=largest_value
        )
        return (
            dquery.astype(jnp.bfloat16),
            dkeys.astype(jnp.bfloat16),
            dvalue.astype(jnp.bfloat16),
        )

    dquery, dkeys, dvalue = lax.map(
        backward_user,
        (
            query_rows,
            key_rows,
            value_rows,
            dmixed,
            cumulative,
            growth,
            falloff,
            weight_matrix,
            entering,
            leaving,
        ),
    )
    dembedded = jnp.dot(
        dquery.reshape(-1, feature_width), w_query.T, preferred_element_type=jnp.float32
    )
    dembedded = dembedded + jnp.dot(
        dkeys.reshape(-1, feature_width), w_key.T, preferred_element_type=jnp.float32
    )
    dembedded = dembedded + jnp.dot(
        dvalue.reshape(-1, feature_width), w_value.T, preferred_element_type=jnp.float32
    )
    quot_part = jax.ops.segment_sum(
        dembedded * rem_emb.astype(jnp.float32),
        quot_ids.reshape(-1),
        num_segments=quot_table.shape[0],
    )
    event_terms = dembedded * quot_emb.astype(jnp.float32)
    rem_send = (
        jnp.zeros((shards * user_count * capacity, feature_width), jnp.float32)
        .at[slot_index]
        .set(event_terms)
    )
    rem_send = rem_send.reshape(shards, user_count * capacity, feature_width)
    rem_back = lax.all_to_all(rem_send, "user", split_axis=0, concat_axis=0, tiled=True)
    present_ids = wanted >= 0
    local_rows = jnp.where(present_ids, wanted - base_row, 0).reshape(-1)
    rem_part = jax.ops.segment_sum(
        rem_back.reshape(-1, feature_width), local_rows, num_segments=rows_own
    )
    quot_part = grad_ratio * quot_part
    rem_part = grad_ratio * rem_part
    quot_grad = lax.psum(quot_part, ("user", "hist"))
    rem_grad = lax.psum(rem_part, "hist")
    return (output, quot_grad, rem_grad)


def solution(mesh):
    return jax.shard_map(
        body,
        mesh=mesh,
        in_specs=(
            P("user", "hist"),
            P("user", "hist"),
            P("user"),
            P("user", None, "hist"),
            P(),
            P("user", None),
            P(),
            P(),
            P(),
            P(),
            P("user", "hist", None),
        ),
        out_specs=(P("user", "hist", None), P(), P("user", None)),
        check_vma=False,
    )
```

profile of v0, /device:TPU:1, one launch (start us, length us, event | category | flops | bytes accessed | tf_op | source)
XLA Modules:
  0.0 588.0 jit_solution(10004334027409384725)
XLA Ops:
  7.2 0.8 and_select_fusion.1
  8.7 0.7 copy.121
  9.4 1.2 reduce-window.14
  11.0 2.4 scatter_custom_fusion
  13.4 0.7 all_to_all.12
  14.1 12.0 %all-to-all-start = ((s32[32,1,32]{2,1,0:T(1,128)}), s32[32,1,32]{2,1,0:T(1,128)S(1)}, u32[]{:S(2)}, u32[]{:S(2)}) async-start(s32[32,1,32]{2,1,0:T(1,128)} %all_to_all.12), calls=%async_computation | async-start | bytes 32768 | tf_op jit(solution)/shard_map/all_to_all | solution.py:100
  26.2 0.7 reshape.410
  26.9 2.4 reduce-window.16
  29.9 0.7 fusion.87
  30.6 4.1 all-to-all-done
  35.4 3.9 gather_fusion.1
  39.4 1.0 broadcast_select_fusion
  40.4 5.1 all-to-all-start.1
  45.7 11.9 %all-gather.3 = bf16[16,4,1]{1,2,0:T(2,128)(2,1)S(1)} all-gather(bf16[2,4,1]{1,2,0:T(2,128)(2,1)S(1)} %get-tuple-element.494), channel_id=5, replica_groups=mesh['user'=32,'hist'=8] {'hist'}, dimensions={0}, use_global_device_ids=true | all-gather | bytes 144 | tf_op jit(solution)/shard_map/all_gather | solution.py:27
  60.3 3.0 gather_fusion
  63.3 8.9 %all-gather = f32[16,4,1]{1,2,0:T(1,128)} all-gather(f32[2,4,1]{1,2,0:T(1,128)S(1)} %get-tuple-element.495), channel_id=2, replica_groups=mesh['user'=32,'hist'=8] {'hist'}, dimensions={0}, use_global_device_ids=true | all-gather | bytes 288 | tf_op jit(solution)/shard_map/all_gather | solution.py:13
  72.2 2.0 gather_fusion.2
  74.7 0.9 convert_multiply_fusion.5
  75.6 1.1 convolution_convert_fusion.2
  76.7 0.8 copy.88
  77.5 1.0 reshape.409
  78.6 1.7 convert_multiply_fusion.6
  80.3 1.1 convolution_convert_fusion.4
  81.4 1.0 reshape.489
  82.4 1.2 copy.95
  83.7 2.1 fusion.79
  86.2 14.8 %all-gather.2 = bf16[16,4,64,64]{3,2,1,0:T(8,128)(2,1)} all-gather(bf16[2,4,64,64]{3,2,1,0:T(8,128)(2,1)S(1)} %convolution_convert_fusion.5), channel_id=4, replica_groups=mesh['user'=32,'hist'=8] {'hist'}, dimensions={0}, use_global_device_ids=true | all-gather | bytes 589824 | tf_op jit(solution)/shard_map/all_gather | solution.py:27
  101.0 13.4 %while.57 = (s32[]{:T(128)}, f32[2,4,64,64]{3,2,1,0:T(8,128)S(1)}, s32[]{:T(128)}, bf16[8,2,4]{2,1,0:T(2,128)(2,1)}, bf16[8,2,4,64,64]{4,3,2,1,0:T(8,128)(2,1)},...) while((s32[]{:T(128)}, f32[2,4,64,64]{3,2,1,0:T(8,128)S(1)}, s32[]{:T(128)}, ...), condition=%wide.region_13.14_spmd.clone, body=%wide.region_12.13_spmd.clone.sunk | while | flops 163856 | bytes 327935 | solution.py:45
  101.7 1.0 fusion.168
  103.4 1.0 fusion.168
  105.1 1.0 fusion.168
  106.8 1.0 fusion.168
  107.9 0.7 bitcast_convert_fusion.2
  108.5 1.0 fusion.168
  110.2 1.0 fusion.168
  111.9 1.0 fusion.168
  113.5 1.0 fusion.168
  114.6 1.9 while.54
  115.2 1.1 bitcast_add_fusion.2
  116.5 4.2 while.55
  116.5 1.3 bitcast_dynamic-update-slice_fusion.2
  118.6 1.3 bitcast_dynamic-update-slice_fusion.2
  120.7 0.7 copy-done.7
  121.4 0.7 broadcast.273
  122.1 9.1 %while.56 = (s32[]{:T(128)}, bf16[2,256,4,64]{1,3,2,0:T(8,128)(2,1)}, bf16[2,256,4,64]{1,3,2,0:T(8,128)(2,1)S(1)}, bf16[2,256,4,64]{1,3,2,0:T(8,128)(2,1)S(1)}, ...) while((s32[]{:T(128)}, ...), condition=%wide.region_15.16_spmd, body=%wide.region_14.15_spmd.sunk | while | flops 287442944 | bytes 7786197 | solution.py:221
  123.5 1.3 fusion.167
  126.0 0.7 copy-done.6
  126.7 0.7 multiply_bitcast_fusion.3
  128.0 1.3 fusion.167
  130.6 0.7 copy-done.6
  131.6 1.2 copy.108
  134.1 3.5 scatter_custom_fusion.2
  137.6 9.6 %all-to-all-start.2 = ((f32[32,32,256]{2,1,0:T(8,128)}), f32[32,32,256]{2,1,0:T(8,128)}, u32[]{:S(2)}, u32[]{:S(2)}) async-start(f32[32,32,256]{2,1,0:T(8,128)} %bitcast.331), calls=%async_computation.2 | async-start | bytes 2097152 | tf_op jit(solution)/shard_map/all_to_all | solution.py:257
  147.9 76.5 %psum.21 = f32[]{:T(128)} all-reduce(f32[]{:T(128)} %convert_reduce_fusion), channel_id=1, replica_groups=mesh['user'=32,'hist'=8] {'user'}, use_global_device_ids=true, to_apply=%region_11.12 | all-reduce | flops 1 | bytes 8 | tf_op jit(solution)/shard_map/psum | solution.py:84
  225.0 4.3 scatter_custom_fusion.1
  229.4 1.5 broadcast_multiply_fusion.1
  231.6 7.0 %scatter_custom_fusion.3 = f32[2048,256]{1,0:T(8,128)S(1)} fusion(s32[1024]{0:T(1024)S(1)} %reshape.473, f32[1024,256]{1,0:T(8,128)} %bitcast.52, f32[]{:T(128)} %constant.162.clone.1), kind=kCustom, calls=%fused_computation.108 | custom fusion | flops 262144 | bytes 2097664 | tf_op jit(solution)/shard_map/scatter-add | solution.py:260
  238.7 1.5 broadcast_multiply_fusion
  240.2 0.9 copy-done.8
  241.4 1.0 convolution_convert_fusion.1
  242.4 262.5 %all-reduce.3.cloned.1.call-done = f32[2048,256]{1,0:T(8,128)} async-done(((f32[2048,256]{1,0:T(8,128)}), f32[2048,256]{1,0:T(8,128)}) %all-reduce.3.cloned.1.call-update) | async-done | bytes 2097168 | tf_op jit(solution)/shard_map/psum | solution.py:265
  504.9 72.1 %all-reduce.5.cloned.1.call-done = f32[2048,256]{1,0:T(8,128)} async-done(((f32[2048,256]{1,0:T(8,128)}), f32[2048,256]{1,0:T(8,128)}) %all-reduce.5.cloned.1.call-update) | async-done | bytes 2097168 | tf_op jit(solution)/shard_map/psum | solution.py:266
  577.0 3.2 copy.177
  580.2 1.3 copy.178
  (149 shorter events, 20.5 us)
Async XLA Ops:
  7.2 28.2 %copy-start = (bf16[2048,256]{1,0:T(8,128)(2,1)S(1)}, bf16[2048,256]{1,0:T(8,128)(2,1)}, u32[]{:S(2)}) copy-start(bf16[2048,256]{1,0:T(8,128)(2,1)} %param.24) | copy-start | bytes 3145732
  11.0 61.2 %copy-start.18 = (s32[512,1]{0,1:T(1,128)}, s32[512,1]{0,1:T(1,128)S(1)}, u32[]{:S(2)}) copy-start(s32[512,1]{0,1:T(1,128)S(1)} %compare_select_fusion.1) | copy-start | bytes 6148
  14.1 20.6 %all-to-all-start = ((s32[32,1,32]{2,1,0:T(1,128)}), s32[32,1,32]{2,1,0:T(1,128)S(1)}, u32[]{:S(2)}, u32[]{:S(2)}) async-start(s32[32,1,32]{2,1,0:T(1,128)} %all_to_all.12), calls=%async_computation | async-start | bytes 32768 | tf_op jit(solution)/shard_map/all_to_all | solution.py:100
  39.4 6.2 %copy-start.19 = (s32[2]{0:T(128)S(1)}, s32[2]{0:T(128)}, u32[]{:S(2)}) copy-start(s32[2]{0:T(128)} %param.21) | copy-start | bytes 28
  39.4 6.3 %copy-start.16 = (s32[2,256]{1,0:T(2,128)S(1)}, s32[2,256]{1,0:T(2,128)}, u32[]{:S(2)}) copy-start(s32[2,256]{1,0:T(2,128)} %param.19) | copy-start | bytes 6148
  39.4 20.0 %copy-start.14 = (bf16[2,256,256]{2,1,0:T(8,128)(2,1)S(1)}, bf16[2,256,256]{2,1,0:T(8,128)(2,1)}, u32[]{:S(2)}) copy-start(bf16[2,256,256]{2,1,0:T(8,128)(2,1)} %param.29) | copy-start | bytes 786436
  39.4 20.1 %copy-start.10 = (bf16[256,256]{1,0:T(8,128)(2,1)S(1)}, bf16[256,256]{1,0:T(8,128)(2,1)}, u32[]{:S(2)}) copy-start(bf16[256,256]{1,0:T(8,128)(2,1)} %param.28) | copy-start | bytes 393220
  40.4 31.8 %all-to-all-start.1 = ((bf16[32,32,256]{2,1,0:T(8,128)(2,1)}), bf16[32,32,256]{2,1,0:T(8,128)(2,1)S(1)}, u32[]{:S(2)}, u32[]{:S(2)}) async-start(bf16[32,32,256]{2,1,0:T(8,128)(2,1)} %broadcast_select_fusion), calls=%async_computation.1 | async-start | bytes 1048576 | tf_op jit(solution)/shard_map/all_to_all | solution.py:104
  45.5 69.0 %all-gather.6.cloned.1.call-start = ((), (), s32[]{:S(2)}) async-start(), calls=%async_computation.5 | async-start | bytes 2359296 | tf_op jit(solution)/shard_map/all_gather | solution.py:13
  60.3 13.8 %copy-start.9 = (bf16[256,256]{1,0:T(8,128)(2,1)S(1)}, bf16[256,256]{1,0:T(8,128)(2,1)}, u32[]{:S(2)}) copy-start(bf16[256,256]{1,0:T(8,128)(2,1)} %param.25) | copy-start | bytes 393220
  74.2 6.1 %copy-start.1 = (bf16[512,256]{1,0:T(8,128)(2,1)}, bf16[512,256]{1,0:T(8,128)(2,1)S(1)}, u32[]{:S(2)}) copy-start(bf16[512,256]{1,0:T(8,128)(2,1)S(1)} %gather_fusion.2) | copy-start | bytes 786436
  120.7 0.7 copy-start.7
  124.7 1.0 copy-start.5
  126.0 0.7 copy-start.6
  129.3 1.0 copy-start.5
  130.6 0.7 copy-start.6
  131.3 2.2 copy-start.12
  132.8 0.9 copy-start.13
  134.0 91.0 %copy-start.3 = (f32[512,256]{1,0:T(8,128)}, f32[512,256]{1,0:T(8,128)S(1)}, u32[]{:S(2)}) copy-start(f32[512,256]{1,0:T(8,128)S(1)} %convolution_add_fusion) | copy-start | bytes 1572868
  134.1 13.3 %copy-start.20 = (s32[2]{0:T(128)S(1)}, s32[2]{0:T(128)}, u32[]{:S(2)}) copy-start(s32[2]{0:T(128)} %param.21) | copy-start | bytes 28
  134.1 90.3 %copy-start.17 = (s32[2,256]{1,0:T(2,128)S(1)}, s32[2,256]{1,0:T(2,128)}, u32[]{:S(2)}) copy-start(s32[2,256]{1,0:T(2,128)} %param.19) | copy-start | bytes 6148
  134.1 90.9 %copy-start.2 = (bf16[512,256]{1,0:T(8,128)(2,1)S(1)}, bf16[512,256]{1,0:T(8,128)(2,1)}, u32[]{:S(2)}) copy-start(bf16[512,256]{1,0:T(8,128)(2,1)} %copy-done.1) | copy-start | bytes 786436
  137.6 94.0 %all-to-all-start.2 = ((f32[32,32,256]{2,1,0:T(8,128)}), f32[32,32,256]{2,1,0:T(8,128)}, u32[]{:S(2)}, u32[]{:S(2)}) async-start(f32[32,32,256]{2,1,0:T(8,128)} %bitcast.331), calls=%async_computation.2 | async-start | bytes 2097152 | tf_op jit(solution)/shard_map/all_to_all | solution.py:257
  147.3 357.6 %all-reduce.3.cloned.1.call-start = ((), (), s32[]{:S(2)}) async-start(), calls=%async_computation.3 | async-start | bytes 4194304 | tf_op jit(solution)/shard_map/psum | solution.py:265
  230.8 0.7 copy-start.15
  230.9 346.1 %all-reduce.5.cloned.1.call-start = ((), (), s32[]{:S(2)}) async-start(), calls=%async_computation.4 | async-start | bytes 4194304 | tf_op jit(solution)/shard_map/psum | solution.py:266
  240.1 0.9 copy-start.8
  240.1 1.3 copy-start.11
  577.0 3.2 copy-start.4
Sparse Core Ops, SparseCore 0:
  86.0 27.4 all-gather.5
  231.0 273.8 all-reduce.2
  507.8 69.1 all-reduce.4
where the time goes:
time: 591 us; the launch traced here: 588 us
  waiting for transfers between devices  339 us (57%)
  blocking collectives  112 us (19%)
  other arithmetic  43.9 us (7%)
  local copies, waits for them, and re-layouts  33.3 us (6%)
  starting transfers between devices  27.1 us (5%)
  matrix products  17.2 us (3%)
  between operations  14.9 us (3%)
    psum x1, waiting for transfers between devices, body(): quot_grad = lax.psum(quot_part, ('user', 'hist'))  262 us
    psum x1, blocking collectives, body(): all_events = lax.psum(own_events, 'user')  76.5 us
    psum x1, waiting for transfers between devices, body(): rem_grad = lax.psum(rem_part, 'hist')  72.1 us
    all_gather x2, blocking collectives, carried_in_2(): lax.all_gather(part.astype(kind), axis)  26.7 us
    all_to_all x1, starting transfers between devices, body(): lax.all_to_all(requests, 'user', split_axis=0, concat_axis=0, tiled=True)  12 us
  transfers between devices with their start and end apart: 6, of which 3 were waited for; matrix products, arithmetic and copies ran while one was open for 7% of the time, Pallas kernels for 0%

commit v1 on v0

v1 whole, which is shorter than its diff:
```python
import math

import jax
import jax.numpy as jnp
from jax import lax
from jax.experimental import pallas as pl
from jax.experimental.pallas import tpu as pltpu
from jax.sharding import PartitionSpec as P

f32 = jnp.float32
bf16 = jnp.bfloat16
i32 = jnp.int32
EXACT = lax.Precision.HIGHEST
VM = pl.BlockSpec(memory_space=pltpu.VMEM)
SM = pl.BlockSpec(memory_space=pltpu.SMEM)

NN = (((1,), (0,)), ((), ()))
NT = (((1,), (1,)), ((), ()))
TN = (((0,), (0,)), ((), ()))


def dot(a, b, dims=NN, precision=None):
    return lax.dot_general(a, b, dims, preferred_element_type=f32, precision=precision)


def iota(shape, dim):
    return lax.broadcasted_iota(i32, shape, dim)


def where_bf16(mask, a):
    return jnp.where(mask, a, 0.0).astype(bf16)


def halves(whole):
    return (whole >> 4).astype(f32), (whole & 15).astype(f32)


def spread_column(row):
    n = row.shape[1]
    diagonal = iota((n, n), 0) == iota((n, n), 1)
    high, low = halves(row)
    ones = jnp.ones((n, 128), bf16)
    column = 16.0 * dot(where_bf16(diagonal, high), ones) + dot(where_bf16(diagonal, low), ones)
    return column.astype(i32)


def tiled_match(column, width):
    n = column.shape[0]
    lanes = iota((n, 128), 1)
    parts = [where_bf16(column == lanes + j * 128, 1.0) for j in range(width // 128)]
    return jnp.concatenate(parts, axis=1)


def call(kernel, outs, args, specs=None, scratch=(), limit=40):
    return pl.pallas_call(
        kernel,
        out_shape=tuple(jax.ShapeDtypeStruct(s, d) for s, d in outs),
        in_specs=specs if specs is not None else [VM] * len(args),
        out_specs=tuple(VM for _ in outs),
        scratch_shapes=list(scratch),
        compiler_params=pltpu.CompilerParams(vmem_limit_bytes=limit * 1024 * 1024),
    )(*args)


def request_kernel(len_ref, ids_ref, out_ref, slot_ref, *, rows_own, cap):
    users, block = ids_ref.shape
    shards, _, lanes = out_ref.shape
    shift = rows_own.bit_length() - 1
    earlier = where_bf16(iota((block, block), 0) < iota((block, block), 1), 1.0)
    place = iota((lanes, block), 0)
    total = jnp.zeros((shards, lanes), f32)
    count = jnp.int32(0)
    slot_ref[...] = jnp.zeros_like(slot_ref)
    for u in range(users):
        ids = ids_ref[u : u + 1, :]
        owner = ids >> shift
        named = iota((shards, block), 0) == owner
        named_16 = where_bf16(named, 1.0)
        before = dot(named_16, earlier)
        rank = jnp.sum(jnp.where(named, before, 0.0), axis=0, keepdims=True).astype(i32)
        high, low = halves((ids & (rows_own - 1)) + 1)
        chosen = place == rank + u * cap
        total = total + 16.0 * dot(named_16, where_bf16(chosen, high), NT)
        total = total + dot(named_16, where_bf16(chosen, low), NT)
        slot_ref[u : u + 1, :] = (owner * users + u) * cap + rank
        count = count + len_ref[u]
    wanted = jnp.where(iota((shards, lanes), 1) == users * cap, count, total.astype(i32))
    out_ref[:, 0, :] = wanted


def spread_wanted(wanted, per):
    return halves(wanted)


def answer_kernel(wanted_ref, table_ref, out_ref, hot_ref, *, per):
    shards, _, lanes = wanted_ref.shape
    slots = shards * per
    rows = table_ref.shape[0]
    wanted = jnp.where(iota((shards, lanes), 1) < per, wanted_ref[:, 0, :], 0)
    high, low = halves(wanted)
    repeat = where_bf16(iota((slots, shards), 0) // per == iota((slots, shards), 1), 1.0)
    own = iota((slots, lanes), 0) % per == iota((slots, lanes), 1)
    ones = jnp.ones((lanes, 128), bf16)
    high = dot(where_bf16(own, dot(repeat, high.astype(bf16))), ones)
    low = dot(where_bf16(own, dot(repeat, low.astype(bf16))), ones)
    column = (16.0 * high + low).astype(i32) - 1
    spot = iota((slots, 128), 1)
    for j in range(rows // 128):
        hot_ref[:, j * 128 : (j + 1) * 128] = where_bf16(column == spot + j * 128, 1.0)
    out_ref[...] = dot(hot_ref[...], table_ref[...]).astype(bf16)


def quotient_kernel(
    len_ref, at_ref, ids_ref, table_ref, cot_ref, w_out_ref, quot_ref, dmixed_ref
):
    users, block = ids_ref.shape
    rows, width = table_ref.shape
    for u in range(users):
        hot = tiled_match(spread_column(ids_ref[u : u + 1, :]), rows)
        quot_ref[u * block : (u + 1) * block, :] = dot(hot, table_ref[...]).astype(bf16)
        valid = at_ref[0] * block + iota((block, width), 0) < len_ref[u]
        masked = jnp.where(valid, cot_ref[u].astype(f32), 0.0).astype(bf16)
        dmixed_ref[u * block : (u + 1) * block, :] = dot(masked, w_out_ref[...], NT).astype(bf16)


def decays(log_decay, width):
    heads, block = log_decay.shape
    upper = jnp.where(iota((block, block), 0) <= iota((block, block), 1), 1.0, 0.0)
    lower = jnp.where(iota((block, block), 0) >= iota((block, block), 1), 1.0, 0.0)
    padded = jnp.concatenate([log_decay, jnp.zeros((8 - heads, block), f32)], axis=0)
    rows = dot(padded, upper, precision=EXACT)
    columns = dot(lower, padded, NT, precision=EXACT)
    return rows, columns


def over_heads(columns, heads, width):
    n = columns.shape[0]
    head_of = iota((n, width), 1) // (width // heads)
    wide = jnp.broadcast_to(columns[:, 0:1], (n, width))
    for h in range(1, heads):
        wide = jnp.where(head_of == h, jnp.broadcast_to(columns[:, h : h + 1], (n, width)), wide)
    return wide


def diagonal_heads(square, heads):
    width = square.shape[1]
    size = width // heads
    head_of = iota((size, width), 1) // size
    out = square[0:size, :]
    for h in range(1, heads):
        out = jnp.where(head_of == h, square[h * size : (h + 1) * size, :], out)
    return out


def block_diagonal(state, heads):
    size, width = state.shape
    head_of = iota((size, width), 1) // (width // heads)
    return jnp.concatenate([where_bf16(head_of == h, state) for h in range(heads)], axis=0)


def project_kernel(
    at_ref,
    answered_ref,
    slot_ref,
    quot_ref,
    dmixed_ref,
    decay_ref,
    wq_ref,
    wk_ref,
    wv_ref,
    rem_ref,
    q_ref,
    k_ref,
    v_ref,
    payload_ref,
):
    users, heads, block = decay_ref.shape
    slots, width = answered_ref.shape
    peers = payload_ref.shape[0]
    size = width // heads
    me = at_ref[0]
    ends = []
    for u in range(users):
        at = slice(u * block, (u + 1) * block)
        hot = tiled_match(spread_column(slot_ref[u : u + 1, :]), slots)
        rem = dot(hot, answered_ref[...]).astype(bf16)
        rem_ref[at, :] = rem
        embedded = (quot_ref[at, :].astype(f32) * rem.astype(f32)).astype(bf16)
        q = dot(embedded, wq_ref[...]).astype(bf16)
        k = dot(embedded, wk_ref[...]).astype(bf16)
        v = dot(embedded, wv_ref[...]).astype(bf16)
        q_ref[at, :] = q
        k_ref[at, :] = k
        v_ref[at, :] = v
        _, columns = decays(decay_ref[u], width)
        wide = over_heads(columns, heads, width)
        end = wide[block - 1 : block, :]
        ends.append(end)
        falling = (k.astype(f32) * jnp.exp(end - wide)).astype(bf16)
        growing = (q.astype(f32) * jnp.exp(wide)).astype(bf16)
        state = diagonal_heads(dot(falling, v, TN), heads).astype(bf16)
        grad = diagonal_heads(dot(growing, dmixed_ref[at, :], TN), heads).astype(bf16)
        for peer in range(peers):
            payload_ref[peer, u * size : (u + 1) * size, :] = jnp.where(peer > me, state, grad)
    rows = iota((16, width), 0)
    tail = jnp.zeros((16, width), f32)
    for u in range(users):
        left = ends[u]
        for part in range(3):
            piece = left.astype(bf16).astype(f32)
            left = left - piece
            tail = jnp.where(rows == part * users + u, piece, tail)
    tail = tail.astype(bf16)
    for peer in range(peers):
        payload_ref[peer, users * size :, :] = tail


def within_kernel(
    q_ref, k_ref, v_ref, dmixed_ref, decay_ref, mixed_ref, dq_ref, dk_ref, dv_ref, *, scale
):
    users, heads, block = decay_ref.shape
    width = q_ref.shape[1]
    head_of = iota((block, width), 1) // (width // heads)
    lower_tri = iota((block, block), 0) >= iota((block, block), 1)
    for u in range(users):
        at = slice(u * block, (u + 1) * block)
        q, k, v, dmixed = q_ref[at, :], k_ref[at, :], v_ref[at, :], dmixed_ref[at, :]
        rows, columns = decays(decay_ref[u], width)
        mixed = jnp.zeros((block, width), f32)
        dq = jnp.zeros((block, width), f32)
        dk = jnp.zeros((block, width), f32)
        dv = jnp.zeros((block, width), f32)
        zero = jnp.zeros((), bf16)
        for h in range(heads):
            own = head_of == h
            q_h = jnp.where(own, q, zero)
            k_h = jnp.where(own, k, zero)
            v_h = jnp.where(own, v, zero)
            d_h = jnp.where(own, dmixed, zero)
            gap = columns[:, h : h + 1] - rows[h : h + 1, :]
            mask = jnp.where(lower_tri, scale * jnp.exp(jnp.minimum(gap, 0.0)), 0.0)
            weights = (dot(q_h, k, NT) * mask).astype(bf16)
            dweights = (dot(d_h, v, NT) * mask).astype(bf16)
            mixed = mixed + dot(weights, v_h)
            dq = dq + dot(dweights, k_h)
            dk = dk + dot(dweights, q_h, TN)
            dv = dv + dot(weights, d_h, TN)
        mixed_ref[at, :] = mixed
        dq_ref[at, :] = dq
        dk_ref[at, :] = dk
        dv_ref[at, :] = dv


def gradient_kernel(
    at_ref,
    payload_ref,
    mixed_ref,
    dq_ref,
    dk_ref,
    dv_ref,
    q_ref,
    k_ref,
    v_ref,
    dmixed_ref,
    decay_ref,
    wq_ref,
    wk_ref,
    wv_ref,
    w_out_ref,
    rem_ref,
    quot_ref,
    slot_ref,
    ids_ref,
    out_ref,
    rem_send_ref,
    quot_part_ref,
    *,
    scale,
):
    users, heads, block = decay_ref.shape
    width = q_ref.shape[1]
    peers = payload_ref.shape[0]
    size = width // heads
    slots = rem_send_ref.shape[0]
    rows_all = quot_part_ref.shape[0]
    me = at_ref[0]
    rem_terms, quot_terms = [], []
    for u in range(users):
        at = slice(u * block, (u + 1) * block)
        ends = []
        for peer in range(peers):
            tail = payload_ref[peer, users * size :, :].astype(f32)
            ends.append(
                tail[u : u + 1, :]
                + tail[users + u : users + u + 1, :]
                + tail[2 * users + u : 2 * users + u + 1, :]
            )
        entering = jnp.zeros((size, width), f32)
        for peer in range(peers):
            part = payload_ref[peer, u * size : (u + 1) * size, :].astype(f32)
            linked = jnp.exp(ends[peer]) * entering + part
            entering = jnp.where(peer < me, linked, entering)
        leaving = jnp.zeros((size, width), f32)
        for peer in reversed(range(peers)):
            part = payload_ref[peer, u * size : (u + 1) * size, :].astype(f32)
            linked = jnp.exp(ends[peer]) * leaving + part
            leaving = jnp.where(peer > me, linked, leaving)
        entering = block_diagonal(entering, heads)
        leaving = block_diagonal(leaving, heads)
        q, k, v, dmixed = q_ref[at, :], k_ref[at, :], v_ref[at, :], dmixed_ref[at, :]
        _, columns = decays(decay_ref[u], width)
        wide = over_heads(columns, heads, width)
        growth = scale * jnp.exp(wide)
        falloff = scale * jnp.exp(wide[block - 1 : block, :] - wide)
        mixed = (mixed_ref[at, :] + growth * dot(q, entering)).astype(bf16)
        out_ref[u] = dot(mixed, w_out_ref[...]).astype(bf16)
        dq = (dq_ref[at, :] + growth * dot(dmixed, entering, NT)).astype(bf16)
        dk = (dk_ref[at, :] + falloff * dot(v, leaving, NT)).astype(bf16)
        dv = (dv_ref[at, :] + falloff * dot(k, leaving)).astype(bf16)
        dembedded = dot(dq, wq_ref[...], NT) + dot(dk, wk_ref[...], NT) + dot(dv, wv_ref[...], NT)
        rem_terms.append((dembedded * quot_ref[at, :].astype(f32)).astype(bf16))
        quot_terms.append((dembedded * rem_ref[at, :].astype(f32)).astype(bf16))
    rem_terms = jnp.concatenate(rem_terms, axis=0)
    quot_terms = jnp.concatenate(quot_terms, axis=0)
    slot = jnp.concatenate([slot_ref[u : u + 1, :] for u in range(users)], axis=1)
    ids = jnp.concatenate([ids_ref[u : u + 1, :] for u in range(users)], axis=1)
    spot = iota((block, users * block), 0)
    for j in range(slots // block):
        hot = where_bf16(spot + j * block == slot, 1.0)
        rem_send_ref[j * block : (j + 1) * block, :] = dot(hot, rem_terms).astype(bf16)
    for j in range(rows_all // block):
        hot = where_bf16(spot + j * block == ids, 1.0)
        quot_part_ref[j * block : (j + 1) * block, :] = dot(hot, quot_terms).astype(bf16)


def collect_kernel(wanted_ref, back_ref, out_ref, *, per):
    shards, _, lanes = wanted_ref.shape
    slots = shards * per
    rows, width = out_ref.shape
    chunk = 256
    wanted = jnp.where(iota((shards, lanes), 1) < per, wanted_ref[:, 0, :], 0)
    high, low = halves(wanted)
    tile = where_bf16(iota((lanes, slots), 1) % per == iota((lanes, slots), 0), 1.0)
    own = iota((shards, slots), 1) // per == iota((shards, slots), 0)
    high = jnp.sum(jnp.where(own, dot(high.astype(bf16), tile), 0.0), axis=0, keepdims=True)
    low = jnp.sum(jnp.where(own, dot(low.astype(bf16), tile), 0.0), axis=0, keepdims=True)
    row = (16.0 * high + low).astype(i32) - 1
    spot = iota((chunk, slots), 0)
    back = back_ref[...]
    for j in range(rows // chunk):
        hot = where_bf16(spot + j * chunk == row, 1.0)
        out_ref[j * chunk : (j + 1) * chunk, :] = dot(hot, back).astype(bf16)


def exchange(array, axis):
    return lax.all_to_all(array, axis, split_axis=0, concat_axis=0, tiled=True)


def added(parts):
    return jnp.sum(parts.astype(f32), axis=0).astype(bf16)


def body(
    quot_ids,
    rem_ids,
    lengths,
    log_decay,
    quot_table,
    rem_table,
    w_query,
    w_key,
    w_value,
    w_out,
    cotangent,
):
    users, block = quot_ids.shape
    rows_all, width = quot_table.shape
    heads = log_decay.shape[1]
    size = width // heads
    shards = lax.axis_size("user")
    peers = lax.axis_size("hist")
    rows_own = rem_table.shape[0]
    cap = 2 * block // shards
    per = users * cap
    slots = shards * per
    scale = 1.0 / math.sqrt(size * block * peers)
    at = lax.axis_index("hist").astype(i32).reshape(1)
    lanes = (per // 128 + 1) * 128

    def bound(kernel, **fixed):
        def run(*refs):
            kernel(*refs, **fixed)

        run.__name__ = kernel.__name__
        return run

    requests, slot = call(
        bound(request_kernel, rows_own=rows_own, cap=cap),
        [((shards, 1, lanes), i32), ((8, block), i32)],
        (lengths, rem_ids),
        [SM, VM],
    )
    wanted = exchange(requests, "user")
    quot_emb, dmixed = call(
        quotient_kernel,
        [((users * block, width), bf16)] * 2,
        (lengths, at, quot_ids, quot_table, cotangent, w_out),
        [SM, SM, VM, VM, VM, VM],
    )
    (found,) = call(
        bound(answer_kernel, per=per),
        [((slots, width), bf16)],
        (wanted, rem_table),
        scratch=[pltpu.VMEM((slots, rows_own), bf16)],
    )
    answered = exchange(found.reshape(shards, per, width), "user").reshape(slots, width)
    rem_emb, q, k, v, payload = call(
        project_kernel,
        [((users * block, width), bf16)] * 4 + [((peers, users * size + 16, width), bf16)],
        (at, answered, slot, quot_emb, dmixed, log_decay, w_query, w_key, w_value),
        [SM] + [VM] * 8,
    )
    states = exchange(payload, "hist")
    mixed, dq, dk, dv = call(
        bound(within_kernel, scale=scale),
        [((users * block, width), f32)] * 4,
        (q, k, v, dmixed, log_decay),
    )
    output, rem_send, quot_part = call(
        bound(gradient_kernel, scale=scale),
        [((users, block, width), bf16), ((slots, width), bf16), ((rows_all, width), bf16)],
        (
            at,
            states,
            mixed,
            dq,
            dk,
            dv,
            q,
            k,
            v,
            dmixed,
            log_decay,
            w_query,
            w_key,
            w_value,
            w_out,
            rem_emb,
            quot_emb,
            slot,
            quot_ids,
        ),
        [SM] + [VM] * 18,
    )
    rem_back = exchange(rem_send.reshape(shards, per, width), "user").reshape(slots, width)
    quot_back = exchange(quot_part.reshape(peers, rows_all // peers, width), "hist")
    quot_sum = added(quot_back)
    quot_back = exchange(quot_sum.reshape(shards, -1, width), "user")
    (rem_part,) = call(
        bound(collect_kernel, per=per), [((rows_own, width), bf16)], (wanted, rem_back)
    )
    rem_back = exchange(rem_part.reshape(peers, rows_own // peers, width), "hist")
    rem_sum = added(rem_back)
    quot_sum = added(quot_back)
    quot_sum = exchange(jnp.broadcast_to(quot_sum, (shards,) + quot_sum.shape), "user")
    both = jnp.concatenate([rem_sum, quot_sum.reshape(-1, width)], axis=0)
    both = exchange(jnp.broadcast_to(both, (peers,) + both.shape), "hist")
    all_events = jnp.sum(wanted[:, 0, per].astype(f32))
    grad_ratio = float(users * shards * block * peers) / all_events
    rem_rows = rows_own // peers
    rem_grad = grad_ratio * both[:, :rem_rows].astype(f32).reshape(rows_own, width)
    quot_grad = grad_ratio * both[:, rem_rows:].astype(f32).reshape(rows_all, width)
    return (output, quot_grad, rem_grad)


def solution(mesh):
    return jax.shard_map(
        body,
        mesh=mesh,
        in_specs=(
            P("user", "hist"),
            P("user", "hist"),
            P("user"),
            P("user", None, "hist"),
            P(),
            P("user", None),
            P(),
            P(),
            P(),
            P(),
            P("user", "hist", None),
        ),
        out_specs=(P("user", "hist", None), P(), P("user", None)),
        check_vma=False,
    )
```

time: 591 us -> 202 us (0.34)
  waiting for transfers between devices: 339 us -> 85 us
  blocking collectives: 112 us -> 38.8 us
  other arithmetic: 43.9 us -> 4.19 us
  local copies, waits for them, and re-layouts: 33.3 us -> 11 us
  Pallas kernels: 0 us -> 18.3 us
  matrix products: 17.2 us -> 0 us
  starting transfers between devices: 27.1 us -> 41.8 us
  between operations: 14.9 us -> 1.52 us
    psum x2 -> x0, waiting for transfers between devices: 335 us -> none  [the longest x1 262 us: body(): quot_grad = lax.psum(quot_part, ('user', 'hist'))]
    all_to_all x3 -> x7, waiting for transfers between devices: 4.12 us -> 85 us  [exchange(): return lax.all_to_all(array, axis, split_axis=0, concat_axis=0, tiled=True)]
    psum x1 -> x0, blocking collectives: 76.5 us -> none  [body(): all_events = lax.psum(own_events, 'user')]
    all_to_all x0 -> x2, blocking collectives: none -> 38.8 us  [exchange(): return lax.all_to_all(array, axis, split_axis=0, concat_axis=0, tiled=True)]
    all_gather x3 -> x0, blocking collectives: 35.6 us -> none  [the longest x2 26.7 us: carried_in_2(): lax.all_gather(part.astype(kind), axis)]
    pallas_call x0 -> x7, Pallas kernels: none -> 18.3 us  [call(): pl.pallas_call(kernel, out_shape=tuple((jax.ShapeDtypeStruct(s, d) for s,...]
    dot_general x30 -> x0, matrix products: 17.2 us -> none  [the longest x2 2.6 us: forward_user(): jnp.einsum('tbc,xbc->btx', single_query, single_key, preferred_element_ty...]
    all_to_all x3 -> x7, starting transfers between devices: 26.8 us -> 41.8 us  [exchange(): return lax.all_to_all(array, axis, split_axis=0, concat_axis=0, tiled=True)]
  transfers between devices with their start and end apart: 6 -> 7, of which waited for: 3 -> 7; matrix products, arithmetic and copies ran while one was open for 7% -> 1% of each run, Pallas kernels for 0% -> 3%
where the time goes in v1:
time: 202 us; the launch traced here: 201 us
  waiting for transfers between devices  85 us (42%)
  starting transfers between devices  41.8 us (21%)
  blocking collectives  38.8 us (19%)
  Pallas kernels  18.3 us (9%)
  local copies, waits for them, and re-layouts  11 us (5%)
  other arithmetic  4.19 us (2%)
    all_to_all x7, waiting for transfers between devices, exchange(): return lax.all_to_all(array, axis, split_axis=0, concat_axis=0, tiled=True)  85 us
    all_to_all x7, starting transfers between devices, exchange(): return lax.all_to_all(array, axis, split_axis=0, concat_axis=0, tiled=True)  41.8 us
    all_to_all x2, blocking collectives, exchange(): return lax.all_to_all(array, axis, split_axis=0, concat_axis=0, tiled=True)  38.8 us
    pallas_call x7, Pallas kernels, call(): pl.pallas_call(kernel, out_shape=tuple((jax.ShapeDtypeStruct(s, d) for s,...  18.3 us
    unnamed x38, local copies, waits for them, and re-layouts  8.89 us
  transfers between devices with their start and end apart: 7, of which 7 were waited for; matrix products, arithmetic and copies ran while one was open for 1% of the time, Pallas kernels for 3%

profile of v1, /device:TPU:1, one launch (start us, length us, event | category | flops | bytes accessed | tf_op | source)
XLA Modules:
  0.0 200.7 jit_solution(8216368175810940474)
XLA Ops:
  0.6 0.0 copy-start.15
  0.6 0.0 copy-start.14
  0.7 0.0 copy-start.16
  0.7 0.7 copy-done.16
  1.3 0.0 copy-start.18
  1.3 0.7 copy-done.18
  2.0 0.0 copy-start.17
  2.0 1.1 shard_map.130
  3.1 20.5 %all_to_all.45.refs_0_ = s32[32,1,128]{2,1,0:T(1,128)S(1)} all-to-all(s32[32,1,128]{2,1,0:T(1,128)S(1)} %get-tuple-element.19), channel_id=1, replica_groups=mesh['user'=32,'hist'=8] {'user'}, dimensions={0} | all-to-all | bytes 32768 | tf_op jit(solution)/shard_map/all_to_all | solution.py:356
  23.6 0.0 copy-start
  23.6 1.2 copy-done
  24.8 0.0 copy-start.1
  24.8 0.0 copy-start.6
  24.8 0.0 copy-start.8
  24.8 0.0 copy-start.9
  24.8 0.0 copy-start.10
  24.8 3.1 %shard_map.131 = bf16[1024,256]{1,0:T(8,128)(2,1)} custom-call(s32[32,1,128]{2,1,0:T(1,128)S(1)} %all_to_all.45.refs_0_, bf16[2048,256]{1,0:T(8,128)(2,1)S(1)} %copy-done), custom_call_target="tpu_custom_call" | custom-call | tf_op jit(solution)/shard_map/pallas_call | solution.py:55
  27.9 3.9 %all-to-all-start.1 = ((bf16[32,32,256]{2,1,0:T(8,128)(2,1)}), bf16[32,32,256]{2,1,0:T(8,128)(2,1)S(1)}, u32[]{:S(2)}, u32[]{:S(2)}) async-start(bf16[32,32,256]{2,1,0:T(8,128)(2,1)} %bitcast.1), calls=%async_computation.1 | async-start | bytes 1048576 | tf_op jit(solution)/shard_map/all_to_all | solution.py:356
  31.9 0.0 copy-done.15
  31.9 0.0 copy-done.17
  31.9 0.0 copy-done.1
  31.9 0.0 copy-done.6
  31.9 0.0 copy-start.11
  31.9 0.9 copy-done.11
  32.8 1.5 shard_map.132
  34.3 10.5 %all-to-all-done.1 = bf16[32,32,256]{2,1,0:T(8,128)(2,1)S(1)} async-done(((bf16[32,32,256]{2,1,0:T(8,128)(2,1)}), bf16[32,32,256]{2,1,0:T(8,128)(2,1)S(1)}, u32[]{:S(2)}, u32[]{:S(2)}) %all-to-all-start.1) | async-done | bytes 524320 | tf_op jit(solution)/shard_map/all_to_all | solution.py:356
  44.8 0.0 copy-done.14
  44.8 0.0 copy-done.8
  44.8 0.0 copy-done.9
  44.8 0.0 copy-done.10
  44.8 4.0 %shard_map.133 = (bf16[512,256]{1,0:T(8,128)(2,1)S(1)}, bf16[512,256]{1,0:T(8,128)(2,1)S(1)}, bf16[512,256]{1,0:T(8,128)(2,1)S(1)}, bf16[512,256]{1,0:T(8,128)(2,1)S(1)}, bf16[8,144,256]{2,1,0:T(8,128)(2,1)}) custom-call(s32[1]{0:T(128)} %bitcast.at_ref.refs_0_, bf16[1024,256]{1,0:T(8,128)(2,1)S(1)} %bitcast.12, ...), custom_call_target="tpu_custom_call" | custom-call | tf_op jit(solution)/shard_map/pallas_call | solution.py:55
  48.8 0.0 copy-start.12
  48.9 0.7 copy-done.12
  49.6 9.5 %all-to-all-start.2 = ((bf16[8,144,256]{2,1,0:T(8,128)(2,1)}), bf16[8,144,256]{2,1,0:T(8,128)(2,1)S(1)}, u32[]{:S(2)}, u32[]{:S(2)}) async-start(bf16[8,144,256]{2,1,0:T(8,128)(2,1)} %get-tuple-element.23), calls=%async_computation.2 | async-start | bytes 1179648 | tf_op jit(solution)/shard_map/all_to_all | solution.py:356
  59.0 3.1 %shard_map.134 = (f32[512,256]{1,0:T(8,128)S(1)}, f32[512,256]{1,0:T(8,128)S(1)}, f32[512,256]{1,0:T(8,128)S(1)}, f32[512,256]{1,0:T(8,128)S(1)}) custom-call(bf16[512,256]{1,0:T(8,128)(2,1)S(1)} %get-tuple-element.24.refs_0_.refs_6_, bf16[512,256]{1,0:T(8,128)(2,1)S(1)} %get-tuple-element.25.refs_1_.refs_7_, ...), custom_call_target="tpu_custom_call" | custom-call | tf_op jit(solution)/shard_map/pallas_call | solution.py:55
  62.2 0.0 copy-start.2
  62.2 0.8 copy-done.2
  63.0 0.0 copy-start.4
  63.0 0.8 copy-done.4
  63.8 5.4 %all-to-all-done.2.refs_1_ = bf16[8,144,256]{2,1,0:T(8,128)(2,1)S(1)} async-done(((bf16[8,144,256]{2,1,0:T(8,128)(2,1)}), bf16[8,144,256]{2,1,0:T(8,128)(2,1)S(1)}, u32[]{:S(2)}, u32[]{:S(2)}) %all-to-all-start.2) | async-done | bytes 589856 | tf_op jit(solution)/shard_map/all_to_all | solution.py:356
  69.2 1.0 copy-done.3
  70.2 1.0 copy-done.5
  71.3 0.9 copy-done.13
  72.2 3.1 %shard_map.135 = (bf16[2,256,256]{2,1,0:T(8,128)(2,1)}, bf16[1024,256]{1,0:T(8,128)(2,1)S(1)}, bf16[2048,256]{1,0:T(8,128)(2,1)S(1)}) custom-call(s32[1]{0:T(128)} %bitcast.at_ref.refs_0_, bf16[8,144,256]{2,1,0:T(8,128)(2,1)S(1)} %all-to-all-done.2.refs_1_, f32[512,256]{1,0:T(8,128)S(1)} %get-tuple-element.27.refs_2_, ...), custom_call_target="tpu_custom_call" | custom-call | tf_op jit(solution)/shard_map/pallas_call | solution.py:55
  75.3 0.0 copy-start.7
  75.3 18.4 %all_to_all.46 = bf16[8,256,256]{2,1,0:T(8,128)(2,1)S(1)} all-to-all(bf16[8,256,256]{2,1,0:T(8,128)(2,1)S(1)} %bitcast.13), channel_id=1, replica_groups=mesh['user'=32,'hist'=8] {'hist'}, dimensions={0} | all-to-all | bytes 2097152 | tf_op jit(solution)/shard_map/all_to_all | solution.py:356
  93.7 0.0 copy-done.7
  93.7 5.0 %all-to-all-start.3 = ((bf16[32,32,256]{2,1,0:T(8,128)(2,1)}), bf16[32,32,256]{2,1,0:T(8,128)(2,1)S(1)}, u32[]{:S(2)}, u32[]{:S(2)}) async-start(bf16[32,32,256]{2,1,0:T(8,128)(2,1)} %bitcast.14), calls=%async_computation.3 | async-start | bytes 1048576 | tf_op jit(solution)/shard_map/all_to_all | solution.py:356
  98.7 0.8 reduce_sum.47
  99.6 13.2 %all-to-all-done.3 = bf16[32,32,256]{2,1,0:T(8,128)(2,1)S(1)} async-done(((bf16[32,32,256]{2,1,0:T(8,128)(2,1)}), bf16[32,32,256]{2,1,0:T(8,128)(2,1)S(1)}, u32[]{:S(2)}, u32[]{:S(2)}) %all-to-all-start.3) | async-done | bytes 524320 | tf_op jit(solution)/shard_map/all_to_all | solution.py:356
  112.7 8.0 %all-to-all-start.6 = ((bf16[32,8,256]{2,1,0:T(8,128)(2,1)}), bf16[32,8,256]{2,1,0:T(8,128)(2,1)S(1)}, u32[]{:S(2)}, u32[]{:S(2)}) async-start(bf16[32,8,256]{2,1,0:T(8,128)(2,1)} %bitcast.7), calls=%async_computation.6 | async-start | bytes 262144 | tf_op jit(solution)/shard_map/all_to_all | solution.py:356
  120.7 2.4 %shard_map.136 = bf16[2048,256]{1,0:T(8,128)(2,1)} custom-call(s32[32,1,128]{2,1,0:T(1,128)S(1)} %all_to_all.45.refs_0_, bf16[1024,256]{1,0:T(8,128)(2,1)S(1)} %bitcast.11), custom_call_target="tpu_custom_call" | custom-call | tf_op jit(solution)/shard_map/pallas_call | solution.py:55
  123.1 6.8 %all-to-all-done.6 = bf16[32,8,256]{2,1,0:T(8,128)(2,1)S(1)} async-done(((bf16[32,8,256]{2,1,0:T(8,128)(2,1)}), bf16[32,8,256]{2,1,0:T(8,128)(2,1)S(1)}, u32[]{:S(2)}, u32[]{:S(2)}) %all-to-all-start.6) | async-done | bytes 131104 | tf_op jit(solution)/shard_map/all_to_all | solution.py:356
  129.9 6.2 %all-to-all-start.4 = ((bf16[8,256,256]{2,1,0:T(8,128)(2,1)}), bf16[8,256,256]{2,1,0:T(8,128)(2,1)S(1)}, u32[]{:S(2)}, u32[]{:S(2)}) async-start(bf16[8,256,256]{2,1,0:T(8,128)(2,1)} %bitcast.5), calls=%async_computation.4 | async-start | bytes 2097152 | tf_op jit(solution)/shard_map/all_to_all | solution.py:356
  136.1 15.1 %all-to-all-done.4 = bf16[8,256,256]{2,1,0:T(8,128)(2,1)S(1)} async-done(((bf16[8,256,256]{2,1,0:T(8,128)(2,1)}), bf16[8,256,256]{2,1,0:T(8,128)(2,1)S(1)}, u32[]{:S(2)}, u32[]{:S(2)}) %all-to-all-start.4) | async-done | bytes 1048608 | tf_op jit(solution)/shard_map/all_to_all | solution.py:356
  151.2 0.7 broadcast_in_dim.6
  151.8 3.9 %all-to-all-start.7 = ((bf16[32,8,256]{2,1,0:T(8,128)(2,1)}), bf16[32,8,256]{2,1,0:T(8,128)(2,1)S(1)}, u32[]{:S(2)}, u32[]{:S(2)}) async-start(bf16[32,8,256]{2,1,0:T(8,128)(2,1)} %broadcast_in_dim.6), calls=%async_computation.7 | async-start | bytes 262144 | tf_op jit(solution)/shard_map/all_to_all | solution.py:356
  155.7 0.1 reduce_sum.46
  155.9 9.1 %all-to-all-done.7 = bf16[32,8,256]{2,1,0:T(8,128)(2,1)S(1)} async-done(((bf16[32,8,256]{2,1,0:T(8,128)(2,1)}), bf16[32,8,256]{2,1,0:T(8,128)(2,1)S(1)}, u32[]{:S(2)}, u32[]{:S(2)}) %all-to-all-start.7) | async-done | bytes 131104 | tf_op jit(solution)/shard_map/all_to_all | solution.py:356
  165.0 1.5 broadcast_in_dim.7
  166.4 5.4 %all-to-all-start.8 = ((bf16[8,512,256]{2,1,0:T(8,128)(2,1)}), bf16[8,512,256]{2,1,0:T(8,128)(2,1)S(1)}, u32[]{:S(2)}, u32[]{:S(2)}) async-start(bf16[8,512,256]{2,1,0:T(8,128)(2,1)} %broadcast_in_dim.7), calls=%async_computation.8 | async-start | bytes 4194304 | tf_op jit(solution)/shard_map/all_to_all | solution.py:356
  171.8 0.7 fusion
  173.2 25.0 %all-to-all-done.8 = bf16[8,512,256]{2,1,0:T(8,128)(2,1)S(1)} async-done(((bf16[8,512,256]{2,1,0:T(8,128)(2,1)}), bf16[8,512,256]{2,1,0:T(8,128)(2,1)S(1)}, u32[]{:S(2)}, u32[]{:S(2)}) %all-to-all-start.8) | async-done | bytes 2097184 | tf_op jit(solution)/shard_map/all_to_all | solution.py:356
  198.2 2.5 %convert_multiply_fusion = (f32[8,256,256]{2,1,0:T(8,128)}, f32[8,256,256]{2,1,0:T(8,128)}) fusion(bf16[8,512,256]{2,1,0:T(8,128)(2,1)S(1)} %all-to-all-done.8, f32[]{:T(128)S(6)} %div.3), kind=kLoop, calls=%fused_computation | loop fusion | flops 2097152 | bytes 6291460 | tf_op jit(solution)/shard_map/mul | solution.py:471
  (5 shorter events, 0.1 us)
Async XLA Ops:
  0.6 31.2 %copy-start.15 = (s32[2,256]{1,0:T(2,128)S(1)}, s32[2,256]{1,0:T(2,128)}, u32[]{:S(2)}) copy-start(s32[2,256]{1,0:T(2,128)} %refs_18_.1) | copy-start | bytes 6148
  0.6 44.2 %copy-start.14 = (f32[2,4,256]{2,1,0:T(4,128)S(1)}, f32[2,4,256]{2,1,0:T(4,128)}, u32[]{:S(2)}) copy-start(f32[2,4,256]{2,1,0:T(4,128)} %refs_10_.1) | copy-start | bytes 24580
  0.7 0.7 copy-start.16
  1.3 0.7 copy-start.18
  2.0 29.9 %copy-start.17 = (s32[2]{0:T(128)S(1)}, s32[2]{0:T(128)}, u32[]{:S(2)}) copy-start(s32[2]{0:T(128)} %len_ref.1) | copy-start | bytes 28
  23.6 1.2 copy-start
  24.8 7.1 %copy-start.1 = (bf16[2048,256]{1,0:T(8,128)(2,1)S(1)}, bf16[2048,256]{1,0:T(8,128)(2,1)}, u32[]{:S(2)}) copy-start(bf16[2048,256]{1,0:T(8,128)(2,1)} %table_ref.1) | copy-start | bytes 3145732
  24.8 7.1 %copy-start.6 = (bf16[256,256]{1,0:T(8,128)(2,1)S(1)}, bf16[256,256]{1,0:T(8,128)(2,1)}, u32[]{:S(2)}) copy-start(bf16[256,256]{1,0:T(8,128)(2,1)} %refs_14_.1) | copy-start | bytes 393220
  24.8 20.0 %copy-start.8 = (bf16[256,256]{1,0:T(8,128)(2,1)S(1)}, bf16[256,256]{1,0:T(8,128)(2,1)}, u32[]{:S(2)}) copy-start(bf16[256,256]{1,0:T(8,128)(2,1)} %refs_11_.1) | copy-start | bytes 393220
  24.8 20.0 %copy-start.9 = (bf16[256,256]{1,0:T(8,128)(2,1)S(1)}, bf16[256,256]{1,0:T(8,128)(2,1)}, u32[]{:S(2)}) copy-start(bf16[256,256]{1,0:T(8,128)(2,1)} %refs_12_.1) | copy-start | bytes 393220
  24.8 20.0 %copy-start.10 = (bf16[256,256]{1,0:T(8,128)(2,1)S(1)}, bf16[256,256]{1,0:T(8,128)(2,1)}, u32[]{:S(2)}) copy-start(bf16[256,256]{1,0:T(8,128)(2,1)} %refs_13_.1) | copy-start | bytes 393220
  27.9 16.9 %all-to-all-start.1 = ((bf16[32,32,256]{2,1,0:T(8,128)(2,1)}), bf16[32,32,256]{2,1,0:T(8,128)(2,1)S(1)}, u32[]{:S(2)}, u32[]{:S(2)}) async-start(bf16[32,32,256]{2,1,0:T(8,128)(2,1)} %bitcast.1), calls=%async_computation.1 | async-start | bytes 1048576 | tf_op jit(solution)/shard_map/all_to_all | solution.py:356
  31.9 1.0 copy-start.11
  48.8 0.7 copy-start.12
  49.6 19.6 %all-to-all-start.2 = ((bf16[8,144,256]{2,1,0:T(8,128)(2,1)}), bf16[8,144,256]{2,1,0:T(8,128)(2,1)S(1)}, u32[]{:S(2)}, u32[]{:S(2)}) async-start(bf16[8,144,256]{2,1,0:T(8,128)(2,1)} %get-tuple-element.23), calls=%async_computation.2 | async-start | bytes 1179648 | tf_op jit(solution)/shard_map/all_to_all | solution.py:356
  62.2 0.8 copy-start.2
  63.0 0.8 copy-start.4
  69.2 1.0 copy-start.3
  70.2 1.0 copy-start.5
  71.3 0.9 copy-start.13
  75.3 18.4 %copy-start.7 = (bf16[1024,256]{1,0:T(8,128)(2,1)}, bf16[1024,256]{1,0:T(8,128)(2,1)S(1)}, u32[]{:S(2)}) copy-start(bf16[1024,256]{1,0:T(8,128)(2,1)S(1)} %get-tuple-element.33) | copy-start | bytes 1572868
  93.7 19.0 %all-to-all-start.3 = ((bf16[32,32,256]{2,1,0:T(8,128)(2,1)}), bf16[32,32,256]{2,1,0:T(8,128)(2,1)S(1)}, u32[]{:S(2)}, u32[]{:S(2)}) async-start(bf16[32,32,256]{2,1,0:T(8,128)(2,1)} %bitcast.14), calls=%async_computation.3 | async-start | bytes 1048576 | tf_op jit(solution)/shard_map/all_to_all | solution.py:356
  112.7 17.1 %all-to-all-start.6 = ((bf16[32,8,256]{2,1,0:T(8,128)(2,1)}), bf16[32,8,256]{2,1,0:T(8,128)(2,1)S(1)}, u32[]{:S(2)}, u32[]{:S(2)}) async-start(bf16[32,8,256]{2,1,0:T(8,128)(2,1)} %bitcast.7), calls=%async_computation.6 | async-start | bytes 262144 | tf_op jit(solution)/shard_map/all_to_all | solution.py:356
  129.9 21.3 %all-to-all-start.4 = ((bf16[8,256,256]{2,1,0:T(8,128)(2,1)}), bf16[8,256,256]{2,1,0:T(8,128)(2,1)S(1)}, u32[]{:S(2)}, u32[]{:S(2)}) async-start(bf16[8,256,256]{2,1,0:T(8,128)(2,1)} %bitcast.5), calls=%async_computation.4 | async-start | bytes 2097152 | tf_op jit(solution)/shard_map/all_to_all | solution.py:356
  151.8 13.1 %all-to-all-start.7 = ((bf16[32,8,256]{2,1,0:T(8,128)(2,1)}), bf16[32,8,256]{2,1,0:T(8,128)(2,1)S(1)}, u32[]{:S(2)}, u32[]{:S(2)}) async-start(bf16[32,8,256]{2,1,0:T(8,128)(2,1)} %broadcast_in_dim.6), calls=%async_computation.7 | async-start | bytes 262144 | tf_op jit(solution)/shard_map/all_to_all | solution.py:356
  166.4 31.8 %all-to-all-start.8 = ((bf16[8,512,256]{2,1,0:T(8,128)(2,1)}), bf16[8,512,256]{2,1,0:T(8,128)(2,1)S(1)}, u32[]{:S(2)}, u32[]{:S(2)}) async-start(bf16[8,512,256]{2,1,0:T(8,128)(2,1)} %broadcast_in_dim.7), calls=%async_computation.8 | async-start | bytes 4194304 | tf_op jit(solution)/shard_map/all_to_all | solution.py:356

commit v2 on v1

--- a/solution.py
+++ b/solution.py
@@ -1,3 +1,4 @@
+import functools
 import math
 
 import jax
@@ -51,7 +52,7 @@
     return jnp.concatenate(parts, axis=1)
 
 
-def call(kernel, outs, args, specs=None, scratch=(), limit=40):
+def call(kernel, outs, args, specs=None, scratch=(), limit=20):
     return pl.pallas_call(
         kernel,
         out_shape=tuple(jax.ShapeDtypeStruct(s, d) for s, d in outs),
@@ -86,10 +87,6 @@
         count = count + len_ref[u]
     wanted = jnp.where(iota((shards, lanes), 1) == users * cap, count, total.astype(i32))
     out_ref[:, 0, :] = wanted
-
-
-def spread_wanted(wanted, per):
-    return halves(wanted)
 
 
 def answer_kernel(wanted_ref, table_ref, out_ref, hot_ref, *, per):
@@ -251,6 +248,17 @@
         dv_ref[at, :] = dv
 
 
+def sum_halves(ids, terms, core, keep_ref, give_ref):
+    half = keep_ref.shape[0]
+    chunk = min(256, half)
+    spot = iota((chunk, ids.shape[1]), 0)
+    for ref, owner in ((give_ref, 1 - core), (keep_ref, core)):
+        near = ids - owner * half
+        for j in range(half // chunk):
+            hot = where_bf16(spot + j * chunk == near, 1.0)
+            ref[j * chunk : (j + 1) * chunk, :] = dot(hot, terms).astype(ref.dtype)
+
+
 def gradient_kernel(
     at_ref,
     payload_ref,
@@ -273,7 +281,8 @@
     ids_ref,
     out_ref,
     rem_send_ref,
-    quot_part_ref,
+    keep_ref,
+    give_ref,
     *,
     scale,
 ):
@@ -282,7 +291,6 @@
     peers = payload_ref.shape[0]
     size = width // heads
     slots = rem_send_ref.shape[0]
-    rows_all = quot_part_ref.shape[0]
     me = at_ref[0]
     rem_terms, quot_terms = [], []
     for u in range(users):
@@ -328,16 +336,12 @@
     for j in range(slots // block):
         hot = where_bf16(spot + j * block == slot, 1.0)
         rem_send_ref[j * block : (j + 1) * block, :] = dot(hot, rem_terms).astype(bf16)
-    for j in range(rows_all // block):
-        hot = where_bf16(spot + j * block == ids, 1.0)
-        quot_part_ref[j * block : (j + 1) * block, :] = dot(hot, quot_terms).astype(bf16)
-
-
-def collect_kernel(wanted_ref, back_ref, out_ref, *, per):
+    sum_halves(ids, quot_terms, me % 2, keep_ref, give_ref)
+
+
+def collect_kernel(at_ref, wanted_ref, back_ref, keep_ref, give_ref, *, per):
     shards, _, lanes = wanted_ref.shape
     slots = shards * per
-    rows, width = out_ref.shape
-    chunk = 256
     wanted = jnp.where(iota((shards, lanes), 1) < per, wanted_ref[:, 0, :], 0)
     high, low = halves(wanted)
     tile = where_bf16(iota((lanes, slots), 1) % per == iota((lanes, slots), 0), 1.0)
@@ -345,11 +349,33 @@
     high = jnp.sum(jnp.where(own, dot(high.astype(bf16), tile), 0.0), axis=0, keepdims=True)
     low = jnp.sum(jnp.where(own, dot(low.astype(bf16), tile), 0.0), axis=0, keepdims=True)
     row = (16.0 * high + low).astype(i32) - 1
-    spot = iota((chunk, slots), 0)
-    back = back_ref[...]
-    for j in range(rows // chunk):
-        hot = where_bf16(spot + j * chunk == row, 1.0)
-        out_ref[j * chunk : (j + 1) * chunk, :] = dot(hot, back).astype(bf16)
+    sum_halves(row, back_ref[...], at_ref[0] % 2, keep_ref, give_ref)
+
+
+def split_kernel(at_ref, keep_ref, got_ref, *out_refs):
+    chips = len(out_refs)
+    rows = out_refs[0].shape[0]
+    for d, out_ref in enumerate(out_refs):
+        base = pl.multiple_of(lax.rem(at_ref[0] // 2 + d, chips) * rows, rows)
+        both = keep_ref[pl.ds(base, rows), :] + got_ref[pl.ds(base, rows), :].astype(f32)
+        out_ref[...] = both.astype(bf16)
+
+
+def place_kernel(at_ref, wanted_ref, *refs, per, total):
+    out_ref = refs[-1]
+    chunks = refs[:-1]
+    chips = len(chunks) // 2
+    rows = chunks[0].shape[0]
+    shards, _, lanes = wanted_ref.shape
+    counted = jnp.where(iota((shards, lanes), 1) == per, wanted_ref[:, 0, :], 0)
+    ratio = total / jnp.sum(counted.astype(f32), axis=(0, 1), keepdims=True)
+    chip, core = at_ref[0] // 2, at_ref[0] % 2
+    for other in range(2):
+        half = core + other - 2 * core * other
+        for d in range(chips):
+            spot = half * chips + lax.rem(chip + chips - d, chips)
+            base = pl.multiple_of(spot * rows, rows)
+            out_ref[pl.ds(base, rows), :] = ratio * chunks[other * chips + d][...].astype(f32)
 
 
 def exchange(array, axis):
@@ -358,6 +384,43 @@
 
 def added(parts):
     return jnp.sum(parts.astype(f32), axis=0).astype(bf16)
+
+
+def to_core(array):
+    peers = lax.axis_size("hist")
+    return lax.ppermute(array, "hist", [(i, i ^ 1) for i in range(peers)])
+
+
+def to_chip(array, steps):
+    peers = lax.axis_size("hist")
+    return lax.ppermute(array, "hist", [(i, (i + 2 * steps) % peers) for i in range(peers)])
+
+
+def reduced(at, keep, give):
+    chips = lax.axis_size("hist") // 2
+    rows = keep.shape[0] // chips
+    chunks = call(
+        split_kernel,
+        [((rows, keep.shape[1]), bf16)] * chips,
+        (at, keep, to_core(give)),
+        [SM, VM, VM],
+    )
+    got = [to_chip(chunks[d], d) for d in range(1, chips)]
+    return sum((c.astype(f32) for c in got), chunks[0].astype(f32)).astype(bf16)
+
+
+def gathered(at, wanted, chunk, per, total):
+    chips = lax.axis_size("hist") // 2
+    mine = [chunk] + [to_chip(chunk, d) for d in range(1, chips)]
+    theirs = [to_core(c) for c in mine]
+    kernel = functools.partial(place_kernel, per=per, total=total)
+    (out,) = call(
+        kernel,
+        [((2 * chips * chunk.shape[0], chunk.shape[1]), f32)],
+        (at, wanted, *mine, *theirs),
+        [SM] + [VM] * (1 + 2 * chips),
+    )
+    return out
 
 
 def body(
@@ -387,15 +450,8 @@
     at = lax.axis_index("hist").astype(i32).reshape(1)
     lanes = (per // 128 + 1) * 128
 
-    def bound(kernel, **fixed):
-        def run(*refs):
-            kernel(*refs, **fixed)
-
-        run.__name__ = kernel.__name__
-        return run
-
     requests, slot = call(
-        bound(request_kernel, rows_own=rows_own, cap=cap),
+        functools.partial(request_kernel, rows_own=rows_own, cap=cap),
         [((shards, 1, lanes), i32), ((8, block), i32)],
         (lengths, rem_ids),
         [SM, VM],
@@ -408,7 +464,7 @@
         [SM, SM, VM, VM, VM, VM],
     )
     (found,) = call(
-        bound(answer_kernel, per=per),
+        functools.partial(answer_kernel, per=per),
         [((slots, width), bf16)],
         (wanted, rem_table),
         scratch=[pltpu.VMEM((slots, rows_own), bf16)],
@@ -422,13 +478,18 @@
     )
     states = exchange(payload, "hist")
     mixed, dq, dk, dv = call(
-        bound(within_kernel, scale=scale),
+        functools.partial(within_kernel, scale=scale),
         [((users * block, width), f32)] * 4,
         (q, k, v, dmixed, log_decay),
     )
-    output, rem_send, quot_part = call(
-        bound(gradient_kernel, scale=scale),
-        [((users, block, width), bf16), ((slots, width), bf16), ((rows_all, width), bf16)],
+    output, rem_send, keep, give = call(
+        functools.partial(gradient_kernel, scale=scale),
+        [
+            ((users, block, width), bf16),
+            ((slots, width), bf16),
+            ((rows_all // 2, width), f32),
+            ((rows_all // 2, width), bf16),
+        ],
         (
             at,
             states,
@@ -453,23 +514,20 @@
         [SM] + [VM] * 18,
     )
     rem_back = exchange(rem_send.reshape(shards, per, width), "user").reshape(slots, width)
-    quot_back = exchange(quot_part.reshape(peers, rows_all // peers, width), "hist")
-    quot_sum = added(quot_back)
+    quot_sum = reduced(at, keep, give)
     quot_back = exchange(quot_sum.reshape(shards, -1, width), "user")
-    (rem_part,) = call(
-        bound(collect_kernel, per=per), [((rows_own, width), bf16)], (wanted, rem_back)
-    )
-    rem_back = exchange(rem_part.reshape(peers, rows_own // peers, width), "hist")
-    rem_sum = added(rem_back)
+    keep, give = call(
+        functools.partial(collect_kernel, per=per),
+        [((rows_own // 2, width), f32), ((rows_own // 2, width), bf16)],
+        (at, wanted, rem_back),
+        [SM, VM, VM],
+    )
+    rem_sum = reduced(at, keep, give)
     quot_sum = added(quot_back)
     quot_sum = exchange(jnp.broadcast_to(quot_sum, (shards,) + quot_sum.shape), "user")
-    both = jnp.concatenate([rem_sum, quot_sum.reshape(-1, width)], axis=0)
-    both = exchange(jnp.broadcast_to(both, (peers,) + both.shape), "hist")
-    all_events = jnp.sum(wanted[:, 0, per].astype(f32))
-    grad_ratio = float(users * shards * block * peers) / all_events
-    rem_rows = rows_own // peers
-    rem_grad = grad_ratio * both[:, :rem_rows].astype(f32).reshape(rows_own, width)
-    quot_grad = grad_ratio * both[:, rem_rows:].astype(f32).reshape(rows_all, width)
+    total = float(users * shards * block * peers)
+    rem_grad = gathered(at, wanted, rem_sum, per, total)
+    quot_grad = gathered(at, wanted, quot_sum.reshape(-1, width), per, total)
     return (output, quot_grad, rem_grad)
 
 

time: 202 us -> 164 us (0.81)
  waiting for transfers between devices: 85 us -> 26.5 us
  blocking collectives: 38.8 us -> 48 us
  starting transfers between devices: 41.8 us -> 50.9 us
  local copies, waits for them, and re-layouts: 11 us -> 15.9 us
  other arithmetic: 4.19 us -> 0.18 us
  Pallas kernels: 18.3 us -> 20.6 us
    all_to_all x7 -> x3, waiting for transfers between devices: 85 us -> 23.2 us  [exchange(): return lax.all_to_all(array, axis, split_axis=0, concat_axis=0, tiled=True)]
    ppermute x0 -> x22, starting transfers between devices: none -> 32.5 us  [the longest x10 19.9 us: to_core(): return lax.ppermute(array, 'hist', [(i, i ^ 1) for i in range(peers)])]
    all_to_all x7 -> x3, starting transfers between devices: 41.8 us -> 18.4 us  [exchange(): return lax.all_to_all(array, axis, split_axis=0, concat_axis=0, tiled=True)]
    all_to_all x2 -> x3, blocking collectives: 38.8 us -> 48 us  [exchange(): return lax.all_to_all(array, axis, split_axis=0, concat_axis=0, tiled=True)]
    unnamed x38 -> x52, local copies, waits for them, and re-layouts: 8.89 us -> 15.9 us
    ppermute x0 -> x22, waiting for transfers between devices: none -> 3.25 us  [the longest x10 1.77 us: to_core(): return lax.ppermute(array, 'hist', [(i, i ^ 1) for i in range(peers)])]
    mul x1 -> x0, other arithmetic: 2.46 us -> none  [body(): grad_ratio * both[:, :rem_rows].astype(f32).reshape(rows_own, width)]
    pallas_call x7 -> x11, Pallas kernels: 18.3 us -> 20.6 us  [call(): pl.pallas_call(kernel, out_shape=tuple((jax.ShapeDtypeStruct(s, d) for s,...]
  transfers between devices with their start and end apart: 7 -> 25, of which waited for: 7 -> 5; matrix products, arithmetic and copies ran while one was open for 1% -> 0% of each run, Pallas kernels for 3% -> 5%
where the time goes in v2:
time: 164 us; the launch traced here: 163 us
  starting transfers between devices  50.9 us (31%)
  blocking collectives  48 us (29%)
  waiting for transfers between devices  26.5 us (16%)
  Pallas kernels  20.6 us (13%)
  local copies, waits for them, and re-layouts  15.9 us (10%)
    all_to_all x3, blocking collectives, exchange(): return lax.all_to_all(array, axis, split_axis=0, concat_axis=0, tiled=True)  48 us
    all_to_all x3, waiting for transfers between devices, exchange(): return lax.all_to_all(array, axis, split_axis=0, concat_axis=0, tiled=True)  23.2 us
    pallas_call x11, Pallas kernels, call(): pl.pallas_call(kernel, out_shape=tuple((jax.ShapeDtypeStruct(s, d) for s,...  20.6 us
    ppermute x10, starting transfers between devices, to_core(): return lax.ppermute(array, 'hist', [(i, i ^ 1) for i in range(peers)])  19.9 us
    all_to_all x3, starting transfers between devices, exchange(): return lax.all_to_all(array, axis, split_axis=0, concat_axis=0, tiled=True)  18.4 us
    unnamed x52, local copies, waits for them, and re-layouts  15.9 us
    ppermute x12, starting transfers between devices, to_chip(): lax.ppermute(array, 'hist', [(i, (i + 2 * steps) % peers) for i in range(...  12.5 us
  transfers between devices with their start and end apart: 25, of which 5 were waited for; matrix products, arithmetic and copies ran while one was open for 0% of the time, Pallas kernels for 5%

profile of v2, /device:TPU:1, one launch (start us, length us, event | category | flops | bytes accessed | tf_op | source)
XLA Modules:
  0.0 162.9 jit_solution(11138680184964464407)
XLA Ops:
  0.7 0.7 copy-done.22
  1.3 0.7 copy-done.24
  2.0 1.1 shard_map.130
  3.1 20.5 %all_to_all.30.wanted_ref = s32[32,1,128]{2,1,0:T(1,128)S(1)} all-to-all(s32[32,1,128]{2,1,0:T(1,128)S(1)} %get-tuple-element.30), channel_id=1, replica_groups=mesh['user'=32,'hist'=8] {'user'}, dimensions={0} | all-to-all | bytes 32768 | tf_op jit(solution)/shard_map/all_to_all | solution.py:382
  23.6 1.2 copy-done
  24.8 3.1 %shard_map.131 = bf16[1024,256]{1,0:T(8,128)(2,1)} custom-call(s32[32,1,128]{2,1,0:T(1,128)S(1)} %all_to_all.30.wanted_ref, bf16[2048,256]{1,0:T(8,128)(2,1)S(1)} %copy-done), custom_call_target="tpu_custom_call" | custom-call | tf_op jit(solution)/shard_map/pallas_call | solution.py:56
  27.9 3.9 %all-to-all-start.1 = ((bf16[32,32,256]{2,1,0:T(8,128)(2,1)}), bf16[32,32,256]{2,1,0:T(8,128)(2,1)S(1)}, u32[]{:S(2)}, u32[]{:S(2)}) async-start(bf16[32,32,256]{2,1,0:T(8,128)(2,1)} %bitcast.1), calls=%async_computation.1 | async-start | bytes 1048576 | tf_op jit(solution)/shard_map/all_to_all | solution.py:382
  31.9 0.0 copy-start.17
  31.9 0.9 copy-done.17
  32.8 1.5 shard_map.132
  34.3 10.5 %all-to-all-done.1 = bf16[32,32,256]{2,1,0:T(8,128)(2,1)S(1)} async-done(((bf16[32,32,256]{2,1,0:T(8,128)(2,1)}), bf16[32,32,256]{2,1,0:T(8,128)(2,1)S(1)}, u32[]{:S(2)}, u32[]{:S(2)}) %all-to-all-start.1) | async-done | bytes 524320 | tf_op jit(solution)/shard_map/all_to_all | solution.py:382
  44.8 4.0 %shard_map.133 = (bf16[512,256]{1,0:T(8,128)(2,1)S(1)}, bf16[512,256]{1,0:T(8,128)(2,1)S(1)}, bf16[512,256]{1,0:T(8,128)(2,1)S(1)}, bf16[512,256]{1,0:T(8,128)(2,1)S(1)}, bf16[8,144,256]{2,1,0:T(8,128)(2,1)}) custom-call(s32[1]{0:T(128)} %bitcast.at_ref, bf16[1024,256]{1,0:T(8,128)(2,1)S(1)} %bitcast.9, s32[8,256]{1,0:T(8,128)S(1)} %get-tuple-element.31.slot_ref, ...), custom_call_target="tpu_custom_call" | custom-call | tf_op jit(solution)/shard_map/pallas_call | solution.py:56
  48.8 0.7 copy-done.18
  49.5 9.5 %all-to-all-start.2 = ((bf16[8,144,256]{2,1,0:T(8,128)(2,1)}), bf16[8,144,256]{2,1,0:T(8,128)(2,1)S(1)}, u32[]{:S(2)}, u32[]{:S(2)}) async-start(bf16[8,144,256]{2,1,0:T(8,128)(2,1)} %get-tuple-element.34), calls=%async_computation.2 | async-start | bytes 1179648 | tf_op jit(solution)/shard_map/all_to_all | solution.py:382
  59.0 3.1 %shard_map.134 = (f32[512,256]{1,0:T(8,128)S(1)}, f32[512,256]{1,0:T(8,128)S(1)}, f32[512,256]{1,0:T(8,128)S(1)}, f32[512,256]{1,0:T(8,128)S(1)}) custom-call(bf16[512,256]{1,0:T(8,128)(2,1)S(1)} %get-tuple-element.35.q_ref, bf16[512,256]{1,0:T(8,128)(2,1)S(1)} %get-tuple-element.36.k_ref, bf16[512,256]{1,0:T(8,128)(2,1)S(1)} %get-tuple-element.37.v_ref, ...), custom_call_target="tpu_custom_call" | custom-call | tf_op jit(solution)/shard_map/pallas_call | solution.py:56
  62.1 0.8 copy-done.2
  62.9 0.8 copy-done.4
  63.7 0.8 copy-done.6
  64.5 4.7 %all-to-all-done.2.payload_ref = bf16[8,144,256]{2,1,0:T(8,128)(2,1)S(1)} async-done(((bf16[8,144,256]{2,1,0:T(8,128)(2,1)}), bf16[8,144,256]{2,1,0:T(8,128)(2,1)S(1)}, u32[]{:S(2)}, u32[]{:S(2)}) %all-to-all-start.2) | async-done | bytes 589856 | tf_op jit(solution)/shard_map/all_to_all | solution.py:382
  69.2 1.0 copy-done.3
  70.2 1.0 copy-done.5
  71.2 1.0 copy-done.7
  72.3 0.9 copy-done.9
  73.2 0.9 copy-done.12
  74.1 0.9 copy-done.14
  75.0 0.9 copy-done.16
  75.9 0.9 copy-done.19
  76.9 3.0 %shard_map.135 = (bf16[2,256,256]{2,1,0:T(8,128)(2,1)}, bf16[1024,256]{1,0:T(8,128)(2,1)S(1)}, f32[1024,256]{1,0:T(8,128)S(1)}, bf16[1024,256]{1,0:T(8,128)(2,1)S(1)}) custom-call(s32[1]{0:T(128)} %bitcast.at_ref, bf16[8,144,256]{2,1,0:T(8,128)(2,1)S(1)} %all-to-all-done.2.payload_ref, f32[512,256]{1,0:T(8,128)S(1)} %get-tuple-element.38.mixed_ref, ...), custom_call_target="tpu_custom_call" | custom-call | tf_op jit(solution)/shard_map/pallas_call | solution.py:56
  79.9 0.8 copy-done.10
  80.7 0.8 copy-done.25
  81.5 5.0 %all-to-all-start.5 = ((bf16[32,32,256]{2,1,0:T(8,128)(2,1)}), bf16[32,32,256]{2,1,0:T(8,128)(2,1)S(1)}, u32[]{:S(2)}, u32[]{:S(2)}) async-start(bf16[32,32,256]{2,1,0:T(8,128)(2,1)} %bitcast.10), calls=%async_computation.5 | async-start | bytes 1048576 | tf_op jit(solution)/shard_map/all_to_all | solution.py:382
  86.5 1.2 collective-permute-start
  87.7 1.7 %collective-permute-done.got_ref = bf16[1024,256]{1,0:T(8,128)(2,1)S(1)} collective-permute-done((bf16[1024,256]{1,0:T(8,128)(2,1)}, bf16[1024,256]{1,0:T(8,128)(2,1)S(1)}, u32[]{:S(2)}, u32[]{:S(2)}) %collective-permute-start) | collective-permute-done | bytes 524320 | tf_op jit(solution)/shard_map/ppermute | solution.py:391
  89.5 0.1 shard_map.136
  89.6 0.4 collective-permute-start.1
  89.9 1.8 %collective-permute-start.2 = (bf16[256,256]{1,0:T(8,128)(2,1)S(1)}, bf16[256,256]{1,0:T(8,128)(2,1)S(1)}, u32[]{:S(2)}, u32[]{:S(2)}) collective-permute-start(bf16[256,256]{1,0:T(8,128)(2,1)S(1)} %get-tuple-element.48), channel_id=1, source_target_pairs={{0,4},{1,5},{2,6},{3,7},{4,0},{5,1},{6,2},{7,3},{8,12},{9,13},{10,... | collective-permute-start | bytes 393224 | tf_op jit(solution)/shard_map/ppermute | solution.py:396
  91.7 0.7 collective-permute-start.3
  92.4 8.1 %all-to-all-done.5 = bf16[32,32,256]{2,1,0:T(8,128)(2,1)S(1)} async-done(((bf16[32,32,256]{2,1,0:T(8,128)(2,1)}), bf16[32,32,256]{2,1,0:T(8,128)(2,1)S(1)}, u32[]{:S(2)}, u32[]{:S(2)}) %all-to-all-start.5) | async-done | bytes 524320 | tf_op jit(solution)/shard_map/all_to_all | solution.py:382
  100.5 1.4 shard_map.138
  101.9 4.1 %collective-permute-start.11 = (bf16[1024,256]{1,0:T(8,128)(2,1)S(1)}, bf16[1024,256]{1,0:T(8,128)(2,1)S(1)}, u32[]{:S(2)}, u32[]{:S(2)}) collective-permute-start(bf16[1024,256]{1,0:T(8,128)(2,1)S(1)} %get-tuple-element.52), channel_id=1, source_target_pairs={{0,1},{1,0},{2,3},{3,2},{4,5},{5,4},{6,7},{7,6},{8,9},{9,8},{10,11... | collective-permute-start | bytes 1572872 | tf_op jit(solution)/shard_map/ppermute | solution.py:391
  106.0 0.1 fusion
  106.1 14.1 %all_to_all.31 = bf16[32,8,256]{2,1,0:T(8,128)(2,1)S(1)} all-to-all(bf16[32,8,256]{2,1,0:T(8,128)(2,1)S(1)} %fusion), channel_id=1, replica_groups=mesh['user'=32,'hist'=8] {'user'}, dimensions={0} | all-to-all | bytes 262144 | tf_op jit(solution)/shard_map/all_to_all | solution.py:382
  120.2 13.5 %all_to_all.32 = bf16[32,8,256]{2,1,0:T(8,128)(2,1)S(1)} all-to-all(bf16[32,8,256]{2,1,0:T(8,128)(2,1)S(1)} %broadcast_in_dim.3), channel_id=1, replica_groups=mesh['user'=32,'hist'=8] {'user'}, dimensions={0} | all-to-all | bytes 262144 | tf_op jit(solution)/shard_map/all_to_all | solution.py:382
  133.7 0.9 collective-permute-start.6
  134.6 1.2 collective-permute-start.5
  135.8 0.1 shard_map.139
  135.9 0.1 collective-permute-start.12
  136.0 3.0 %collective-permute-start.13 = (bf16[256,256]{1,0:T(8,128)(2,1)S(1)}, bf16[256,256]{1,0:T(8,128)(2,1)S(1)}, u32[]{:S(2)}, u32[]{:S(2)}) collective-permute-start(bf16[256,256]{1,0:T(8,128)(2,1)S(1)} %get-tuple-element.55), channel_id=1, source_target_pairs={{0,4},{1,5},{2,6},{3,7},{4,0},{5,1},{6,2},{7,3},{8,12},{9,13},{10,... | collective-permute-start | bytes 393224 | tf_op jit(solution)/shard_map/ppermute | solution.py:396
  138.9 0.9 collective-permute-start.14
  139.8 3.9 %collective-permute-start.7 = (bf16[256,256]{1,0:T(8,128)(2,1)S(1)}, bf16[256,256]{1,0:T(8,128)(2,1)S(1)}, u32[]{:S(2)}, u32[]{:S(2)}) collective-permute-start(bf16[256,256]{1,0:T(8,128)(2,1)S(1)} %bitcast.13), channel_id=1, source_target_pairs={{0,1},{1,0},{2,3},{3,2},{4,5},{5,4},{6,7},{7,6},{8,9},{9,8},{10,11... | collective-permute-start | bytes 393224 | tf_op jit(solution)/shard_map/ppermute | solution.py:391
  143.8 1.8 %collective-permute-start.4 = (bf16[256,256]{1,0:T(8,128)(2,1)S(1)}, bf16[256,256]{1,0:T(8,128)(2,1)S(1)}, u32[]{:S(2)}, u32[]{:S(2)}) collective-permute-start(bf16[256,256]{1,0:T(8,128)(2,1)S(1)} %bitcast.14), channel_id=1, source_target_pairs={{0,2},{1,3},{2,4},{3,5},{4,6},{5,7},{6,0},{7,1},{8,10},{9,11},{10,... | collective-permute-start | bytes 393224 | tf_op jit(solution)/shard_map/ppermute | solution.py:396
  145.6 0.7 collective-permute-start.10
  146.3 2.4 %collective-permute-start.9 = (bf16[256,256]{1,0:T(8,128)(2,1)S(1)}, bf16[256,256]{1,0:T(8,128)(2,1)S(1)}, u32[]{:S(2)}, u32[]{:S(2)}) collective-permute-start(bf16[256,256]{1,0:T(8,128)(2,1)S(1)} %collective-permute-done.5.refs_2_), channel_id=1, source_target_pairs={{0,1},{1,0},{2,3},{3,2},{4,5},{5,4},{6,7},{7,6},{8,9},{9,8},{10,11... | collective-permute-start | bytes 393224 | tf_op jit(solution)/shard_map/ppermute | solution.py:391
  148.7 0.1 add_convert_fusion.refs_0_
  148.7 0.7 collective-permute-start.17
  149.5 1.1 collective-permute-start.16
  150.6 1.7 %collective-permute-start.8 = (bf16[256,256]{1,0:T(8,128)(2,1)S(1)}, bf16[256,256]{1,0:T(8,128)(2,1)S(1)}, u32[]{:S(2)}, u32[]{:S(2)}) collective-permute-start(bf16[256,256]{1,0:T(8,128)(2,1)S(1)} %collective-permute-done.4.refs_1_), channel_id=1, source_target_pairs={{0,1},{1,0},{2,3},{3,2},{4,5},{5,4},{6,7},{7,6},{8,9},{9,8},{10,11... | collective-permute-start | bytes 393224 | tf_op jit(solution)/shard_map/ppermute | solution.py:391
  152.4 0.1 collective-permute-start.18
  152.5 1.4 collective-permute-done.17.refs_3_
  153.9 1.2 collective-permute-start.21
  155.1 3.3 %collective-permute-start.20 = (bf16[256,256]{1,0:T(8,128)(2,1)S(1)}, bf16[256,256]{1,0:T(8,128)(2,1)S(1)}, u32[]{:S(2)}, u32[]{:S(2)}) collective-permute-start(bf16[256,256]{1,0:T(8,128)(2,1)S(1)} %collective-permute-done.16.refs_2_), channel_id=1, source_target_pairs={{0,1},{1,0},{2,3},{3,2},{4,5},{5,4},{6,7},{7,6},{8,9},{9,8},{10,11... | collective-permute-start | bytes 393224 | tf_op jit(solution)/shard_map/ppermute | solution.py:391
  158.4 1.3 collective-permute-start.19
  159.7 1.6 shard_map.137
  161.3 1.6 shard_map.140
  (56 shorter events, 0.2 us)
Async XLA Ops:
  0.6 31.2 %copy-start.21 = (s32[2,256]{1,0:T(2,128)S(1)}, s32[2,256]{1,0:T(2,128)}, u32[]{:S(2)}) copy-start(s32[2,256]{1,0:T(2,128)} %ids_ref.5) | copy-start | bytes 6148
  0.6 44.1 %copy-start.20 = (f32[2,4,256]{2,1,0:T(4,128)S(1)}, f32[2,4,256]{2,1,0:T(4,128)}, u32[]{:S(2)}) copy-start(f32[2,4,256]{2,1,0:T(4,128)} %decay_ref.5) | copy-start | bytes 24580
  0.7 0.7 copy-start.22
  1.3 0.7 copy-start.24
  2.0 29.8 %copy-start.23 = (s32[2]{0:T(128)S(1)}, s32[2]{0:T(128)}, u32[]{:S(2)}) copy-start(s32[2]{0:T(128)} %len_ref.3) | copy-start | bytes 28
  23.6 1.2 copy-start
  24.8 7.0 %copy-start.1 = (bf16[2048,256]{1,0:T(8,128)(2,1)S(1)}, bf16[2048,256]{1,0:T(8,128)(2,1)}, u32[]{:S(2)}) copy-start(bf16[2048,256]{1,0:T(8,128)(2,1)} %table_ref.3) | copy-start | bytes 3145732
  24.8 7.0 %copy-start.8 = (bf16[256,256]{1,0:T(8,128)(2,1)S(1)}, bf16[256,256]{1,0:T(8,128)(2,1)}, u32[]{:S(2)}) copy-start(bf16[256,256]{1,0:T(8,128)(2,1)} %w_out_ref.3) | copy-start | bytes 393220
  24.8 20.0 %copy-start.11 = (bf16[256,256]{1,0:T(8,128)(2,1)S(1)}, bf16[256,256]{1,0:T(8,128)(2,1)}, u32[]{:S(2)}) copy-start(bf16[256,256]{1,0:T(8,128)(2,1)} %wq_ref.3) | copy-start | bytes 393220
  24.8 20.0 %copy-start.13 = (bf16[256,256]{1,0:T(8,128)(2,1)S(1)}, bf16[256,256]{1,0:T(8,128)(2,1)}, u32[]{:S(2)}) copy-start(bf16[256,256]{1,0:T(8,128)(2,1)} %wk_ref.3) | copy-start | bytes 393220
  24.8 20.0 %copy-start.15 = (bf16[256,256]{1,0:T(8,128)(2,1)S(1)}, bf16[256,256]{1,0:T(8,128)(2,1)}, u32[]{:S(2)}) copy-start(bf16[256,256]{1,0:T(8,128)(2,1)} %wv_ref.3) | copy-start | bytes 393220
  27.9 16.9 %all-to-all-start.1 = ((bf16[32,32,256]{2,1,0:T(8,128)(2,1)}), bf16[32,32,256]{2,1,0:T(8,128)(2,1)S(1)}, u32[]{:S(2)}, u32[]{:S(2)}) async-start(bf16[32,32,256]{2,1,0:T(8,128)(2,1)} %bitcast.1), calls=%async_computation.1 | async-start | bytes 1048576 | tf_op jit(solution)/shard_map/all_to_all | solution.py:382
  31.9 1.0 copy-start.17
  48.8 0.7 copy-start.18
  49.5 19.6 %all-to-all-start.2 = ((bf16[8,144,256]{2,1,0:T(8,128)(2,1)}), bf16[8,144,256]{2,1,0:T(8,128)(2,1)S(1)}, u32[]{:S(2)}, u32[]{:S(2)}) async-start(bf16[8,144,256]{2,1,0:T(8,128)(2,1)} %get-tuple-element.34), calls=%async_computation.2 | async-start | bytes 1179648 | tf_op jit(solution)/shard_map/all_to_all | solution.py:382
  62.1 0.8 copy-start.2
  62.9 0.8 copy-start.4
  63.7 0.8 copy-start.6
  69.2 1.0 copy-start.3
  70.2 1.0 copy-start.5
  71.2 1.0 copy-start.7
  72.3 0.9 copy-start.9
  73.2 0.9 copy-start.12
  74.1 0.9 copy-start.14
  75.0 0.9 copy-start.16
  75.9 0.9 copy-start.19
  79.9 0.8 copy-start.10
  80.7 0.8 copy-start.25
  81.5 19.1 %all-to-all-start.5 = ((bf16[32,32,256]{2,1,0:T(8,128)(2,1)}), bf16[32,32,256]{2,1,0:T(8,128)(2,1)S(1)}, u32[]{:S(2)}, u32[]{:S(2)}) async-start(bf16[32,32,256]{2,1,0:T(8,128)(2,1)} %bitcast.10), calls=%async_computation.5 | async-start | bytes 1048576 | tf_op jit(solution)/shard_map/all_to_all | solution.py:382
  86.5 3.0 %collective-permute-start = (bf16[1024,256]{1,0:T(8,128)(2,1)}, bf16[1024,256]{1,0:T(8,128)(2,1)S(1)}, u32[]{:S(2)}, u32[]{:S(2)}) collective-permute-start(bf16[1024,256]{1,0:T(8,128)(2,1)} %copy-done.25), channel_id=1, source_target_pairs={{0,1},{1,0},{2,3},{3,2},{4,5},{5,4},{6,7},{7,6},{8,9},{9,8},{10,11... | collective-permute-start | bytes 1572872 | tf_op jit(solution)/shard_map/ppermute | solution.py:391
  89.6 16.4 %collective-permute-start.1 = (bf16[256,256]{1,0:T(8,128)(2,1)S(1)}, bf16[256,256]{1,0:T(8,128)(2,1)S(1)}, u32[]{:S(2)}, u32[]{:S(2)}) collective-permute-start(bf16[256,256]{1,0:T(8,128)(2,1)S(1)} %get-tuple-element.47), channel_id=1, source_target_pairs={{0,2},{1,3},{2,4},{3,5},{4,6},{5,7},{6,0},{7,1},{8,10},{9,11},{10,... | collective-permute-start | bytes 393224 | tf_op jit(solution)/shard_map/ppermute | solution.py:396
  89.9 16.1 %collective-permute-start.2 = (bf16[256,256]{1,0:T(8,128)(2,1)S(1)}, bf16[256,256]{1,0:T(8,128)(2,1)S(1)}, u32[]{:S(2)}, u32[]{:S(2)}) collective-permute-start(bf16[256,256]{1,0:T(8,128)(2,1)S(1)} %get-tuple-element.48), channel_id=1, source_target_pairs={{0,4},{1,5},{2,6},{3,7},{4,0},{5,1},{6,2},{7,3},{8,12},{9,13},{10,... | collective-permute-start | bytes 393224 | tf_op jit(solution)/shard_map/ppermute | solution.py:396
  91.7 14.3 %collective-permute-start.3 = (bf16[256,256]{1,0:T(8,128)(2,1)S(1)}, bf16[256,256]{1,0:T(8,128)(2,1)S(1)}, u32[]{:S(2)}, u32[]{:S(2)}) collective-permute-start(bf16[256,256]{1,0:T(8,128)(2,1)S(1)} %get-tuple-element.49), channel_id=1, source_target_pairs={{0,6},{1,7},{2,0},{3,1},{4,2},{5,3},{6,4},{7,5},{8,14},{9,15},{10,... | collective-permute-start | bytes 393224 | tf_op jit(solution)/shard_map/ppermute | solution.py:396
  101.9 33.9 %collective-permute-start.11 = (bf16[1024,256]{1,0:T(8,128)(2,1)S(1)}, bf16[1024,256]{1,0:T(8,128)(2,1)S(1)}, u32[]{:S(2)}, u32[]{:S(2)}) collective-permute-start(bf16[1024,256]{1,0:T(8,128)(2,1)S(1)} %get-tuple-element.52), channel_id=1, source_target_pairs={{0,1},{1,0},{2,3},{3,2},{4,5},{5,4},{6,7},{7,6},{8,9},{9,8},{10,11... | collective-permute-start | bytes 1572872 | tf_op jit(solution)/shard_map/ppermute | solution.py:391
  133.7 6.1 %collective-permute-start.6 = (bf16[256,256]{1,0:T(8,128)(2,1)S(1)}, bf16[256,256]{1,0:T(8,128)(2,1)S(1)}, u32[]{:S(2)}, u32[]{:S(2)}) collective-permute-start(bf16[256,256]{1,0:T(8,128)(2,1)S(1)} %bitcast.11), channel_id=1, source_target_pairs={{0,6},{1,7},{2,0},{3,1},{4,2},{5,3},{6,4},{7,5},{8,14},{9,15},{10,... | collective-permute-start | bytes 393224 | tf_op jit(solution)/shard_map/ppermute | solution.py:396
  134.6 9.1 %collective-permute-start.5 = (bf16[256,256]{1,0:T(8,128)(2,1)S(1)}, bf16[256,256]{1,0:T(8,128)(2,1)S(1)}, u32[]{:S(2)}, u32[]{:S(2)}) collective-permute-start(bf16[256,256]{1,0:T(8,128)(2,1)S(1)} %bitcast.12), channel_id=1, source_target_pairs={{0,4},{1,5},{2,6},{3,7},{4,0},{5,1},{6,2},{7,3},{8,12},{9,13},{10,... | collective-permute-start | bytes 393224 | tf_op jit(solution)/shard_map/ppermute | solution.py:396
  135.9 9.7 %collective-permute-start.12 = (bf16[256,256]{1,0:T(8,128)(2,1)S(1)}, bf16[256,256]{1,0:T(8,128)(2,1)S(1)}, u32[]{:S(2)}, u32[]{:S(2)}) collective-permute-start(bf16[256,256]{1,0:T(8,128)(2,1)S(1)} %get-tuple-element.54), channel_id=1, source_target_pairs={{0,2},{1,3},{2,4},{3,5},{4,6},{5,7},{6,0},{7,1},{8,10},{9,11},{10,... | collective-permute-start | bytes 393224 | tf_op jit(solution)/shard_map/ppermute | solution.py:396
  136.0 10.3 %collective-permute-start.13 = (bf16[256,256]{1,0:T(8,128)(2,1)S(1)}, bf16[256,256]{1,0:T(8,128)(2,1)S(1)}, u32[]{:S(2)}, u32[]{:S(2)}) collective-permute-start(bf16[256,256]{1,0:T(8,128)(2,1)S(1)} %get-tuple-element.55), channel_id=1, source_target_pairs={{0,4},{1,5},{2,6},{3,7},{4,0},{5,1},{6,2},{7,3},{8,12},{9,13},{10,... | collective-permute-start | bytes 393224 | tf_op jit(solution)/shard_map/ppermute | solution.py:396
  138.9 9.7 %collective-permute-start.14 = (bf16[256,256]{1,0:T(8,128)(2,1)S(1)}, bf16[256,256]{1,0:T(8,128)(2,1)S(1)}, u32[]{:S(2)}, u32[]{:S(2)}) collective-permute-start(bf16[256,256]{1,0:T(8,128)(2,1)S(1)} %get-tuple-element.56), channel_id=1, source_target_pairs={{0,6},{1,7},{2,0},{3,1},{4,2},{5,3},{6,4},{7,5},{8,14},{9,15},{10,... | collective-permute-start | bytes 393224 | tf_op jit(solution)/shard_map/ppermute | solution.py:396
  139.8 9.6 %collective-permute-start.7 = (bf16[256,256]{1,0:T(8,128)(2,1)S(1)}, bf16[256,256]{1,0:T(8,128)(2,1)S(1)}, u32[]{:S(2)}, u32[]{:S(2)}) collective-permute-start(bf16[256,256]{1,0:T(8,128)(2,1)S(1)} %bitcast.13), channel_id=1, source_target_pairs={{0,1},{1,0},{2,3},{3,2},{4,5},{5,4},{6,7},{7,6},{8,9},{9,8},{10,11... | collective-permute-start | bytes 393224 | tf_op jit(solution)/shard_map/ppermute | solution.py:391
  143.8 6.9 %collective-permute-start.4 = (bf16[256,256]{1,0:T(8,128)(2,1)S(1)}, bf16[256,256]{1,0:T(8,128)(2,1)S(1)}, u32[]{:S(2)}, u32[]{:S(2)}) collective-permute-start(bf16[256,256]{1,0:T(8,128)(2,1)S(1)} %bitcast.14), channel_id=1, source_target_pairs={{0,2},{1,3},{2,4},{3,5},{4,6},{5,7},{6,0},{7,1},{8,10},{9,11},{10,... | collective-permute-start | bytes 393224 | tf_op jit(solution)/shard_map/ppermute | solution.py:396
  145.6 5.1 %collective-permute-start.10 = (bf16[256,256]{1,0:T(8,128)(2,1)S(1)}, bf16[256,256]{1,0:T(8,128)(2,1)S(1)}, u32[]{:S(2)}, u32[]{:S(2)}) collective-permute-start(bf16[256,256]{1,0:T(8,128)(2,1)S(1)} %collective-permute-done.6.refs_3_), channel_id=1, source_target_pairs={{0,1},{1,0},{2,3},{3,2},{4,5},{5,4},{6,7},{7,6},{8,9},{9,8},{10,11... | collective-permute-start | bytes 393224 | tf_op jit(solution)/shard_map/ppermute | solution.py:391
  146.3 6.1 %collective-permute-start.9 = (bf16[256,256]{1,0:T(8,128)(2,1)S(1)}, bf16[256,256]{1,0:T(8,128)(2,1)S(1)}, u32[]{:S(2)}, u32[]{:S(2)}) collective-permute-start(bf16[256,256]{1,0:T(8,128)(2,1)S(1)} %collective-permute-done.5.refs_2_), channel_id=1, source_target_pairs={{0,1},{1,0},{2,3},{3,2},{4,5},{5,4},{6,7},{7,6},{8,9},{9,8},{10,11... | collective-permute-start | bytes 393224 | tf_op jit(solution)/shard_map/ppermute | solution.py:391
  148.7 5.2 %collective-permute-start.17 = (bf16[256,256]{1,0:T(8,128)(2,1)S(1)}, bf16[256,256]{1,0:T(8,128)(2,1)S(1)}, u32[]{:S(2)}, u32[]{:S(2)}) collective-permute-start(bf16[256,256]{1,0:T(8,128)(2,1)S(1)} %add_convert_fusion.refs_0_), channel_id=1, source_target_pairs={{0,6},{1,7},{2,0},{3,1},{4,2},{5,3},{6,4},{7,5},{8,14},{9,15},{10,... | collective-permute-start | bytes 393224 | tf_op jit(solution)/shard_map/ppermute | solution.py:396
  149.5 5.6 %collective-permute-start.16 = (bf16[256,256]{1,0:T(8,128)(2,1)S(1)}, bf16[256,256]{1,0:T(8,128)(2,1)S(1)}, u32[]{:S(2)}, u32[]{:S(2)}) collective-permute-start(bf16[256,256]{1,0:T(8,128)(2,1)S(1)} %add_convert_fusion.refs_0_), channel_id=1, source_target_pairs={{0,4},{1,5},{2,6},{3,7},{4,0},{5,1},{6,2},{7,3},{8,12},{9,13},{10,... | collective-permute-start | bytes 393224 | tf_op jit(solution)/shard_map/ppermute | solution.py:396
  150.6 7.7 %collective-permute-start.15 = (bf16[256,256]{1,0:T(8,128)(2,1)S(1)}, bf16[256,256]{1,0:T(8,128)(2,1)S(1)}, u32[]{:S(2)}, u32[]{:S(2)}) collective-permute-start(bf16[256,256]{1,0:T(8,128)(2,1)S(1)} %add_convert_fusion.refs_0_), channel_id=1, source_target_pairs={{0,2},{1,3},{2,4},{3,5},{4,6},{5,7},{6,0},{7,1},{8,10},{9,11},{10,... | collective-permute-start | bytes 393224 | tf_op jit(solution)/shard_map/ppermute | solution.py:396
  150.6 9.1 %collective-permute-start.8 = (bf16[256,256]{1,0:T(8,128)(2,1)S(1)}, bf16[256,256]{1,0:T(8,128)(2,1)S(1)}, u32[]{:S(2)}, u32[]{:S(2)}) collective-permute-start(bf16[256,256]{1,0:T(8,128)(2,1)S(1)} %collective-permute-done.4.refs_1_), channel_id=1, source_target_pairs={{0,1},{1,0},{2,3},{3,2},{4,5},{5,4},{6,7},{7,6},{8,9},{9,8},{10,11... | collective-permute-start | bytes 393224 | tf_op jit(solution)/shard_map/ppermute | solution.py:391
  152.4 8.9 %collective-permute-start.18 = (bf16[256,256]{1,0:T(8,128)(2,1)S(1)}, bf16[256,256]{1,0:T(8,128)(2,1)S(1)}, u32[]{:S(2)}, u32[]{:S(2)}) collective-permute-start(bf16[256,256]{1,0:T(8,128)(2,1)S(1)} %add_convert_fusion.refs_0_), channel_id=1, source_target_pairs={{0,1},{1,0},{2,3},{3,2},{4,5},{5,4},{6,7},{7,6},{8,9},{9,8},{10,11... | collective-permute-start | bytes 393224 | tf_op jit(solution)/shard_map/ppermute | solution.py:391
  153.9 7.4 %collective-permute-start.21 = (bf16[256,256]{1,0:T(8,128)(2,1)S(1)}, bf16[256,256]{1,0:T(8,128)(2,1)S(1)}, u32[]{:S(2)}, u32[]{:S(2)}) collective-permute-start(bf16[256,256]{1,0:T(8,128)(2,1)S(1)} %collective-permute-done.17.refs_3_), channel_id=1, source_target_pairs={{0,1},{1,0},{2,3},{3,2},{4,5},{5,4},{6,7},{7,6},{8,9},{9,8},{10,11... | collective-permute-start | bytes 393224 | tf_op jit(solution)/shard_map/ppermute | solution.py:391
  155.1 6.2 %collective-permute-start.20 = (bf16[256,256]{1,0:T(8,128)(2,1)S(1)}, bf16[256,256]{1,0:T(8,128)(2,1)S(1)}, u32[]{:S(2)}, u32[]{:S(2)}) collective-permute-start(bf16[256,256]{1,0:T(8,128)(2,1)S(1)} %collective-permute-done.16.refs_2_), channel_id=1, source_target_pairs={{0,1},{1,0},{2,3},{3,2},{4,5},{5,4},{6,7},{7,6},{8,9},{9,8},{10,11... | collective-permute-start | bytes 393224 | tf_op jit(solution)/shard_map/ppermute | solution.py:391
  158.4 3.0 %collective-permute-start.19 = (bf16[256,256]{1,0:T(8,128)(2,1)S(1)}, bf16[256,256]{1,0:T(8,128)(2,1)S(1)}, u32[]{:S(2)}, u32[]{:S(2)}) collective-permute-start(bf16[256,256]{1,0:T(8,128)(2,1)S(1)} %collective-permute-done.15.refs_1_), channel_id=1, source_target_pairs={{0,1},{1,0},{2,3},{3,2},{4,5},{5,4},{6,7},{7,6},{8,9},{9,8},{10,11... | collective-permute-start | bytes 393224 | tf_op jit(solution)/shard_map/ppermute | solution.py:391

commit v3 on v2

--- a/solution.py
+++ b/solution.py
@@ -11,9 +11,12 @@
 f32 = jnp.float32
 bf16 = jnp.bfloat16
 i32 = jnp.int32
+FULL = 62
+MOST = 60
 EXACT = lax.Precision.HIGHEST
 VM = pl.BlockSpec(memory_space=pltpu.VMEM)
 SM = pl.BlockSpec(memory_space=pltpu.SMEM)
+HB = pl.BlockSpec(memory_space=pltpu.HBM)
 
 NN = (((1,), (0,)), ((), ()))
 NT = (((1,), (1,)), ((), ()))
@@ -52,23 +55,46 @@
     return jnp.concatenate(parts, axis=1)
 
 
-def call(kernel, outs, args, specs=None, scratch=(), limit=20):
+def begin(pairs, arrived, at=0):
+    copies = [
+        pltpu.make_async_copy(source, target, arrived.at[at + i])
+        for i, (source, target) in enumerate(pairs)
+    ]
+    for copy in copies:
+        copy.start()
+    return copies
+
+
+def finish(copies):
+    for copy in copies:
+        copy.wait()
+
+
+def dma(n):
+    return pltpu.SemaphoreType.DMA((n,))
+
+
+def call(kernel, outs, args, specs=None, scratch=(), out_specs=None, limit=16):
     return pl.pallas_call(
         kernel,
         out_shape=tuple(jax.ShapeDtypeStruct(s, d) for s, d in outs),
         in_specs=specs if specs is not None else [VM] * len(args),
-        out_specs=tuple(VM for _ in outs),
+        out_specs=tuple(out_specs if out_specs is not None else (VM for _ in outs)),
         scratch_shapes=list(scratch),
         compiler_params=pltpu.CompilerParams(vmem_limit_bytes=limit * 1024 * 1024),
     )(*args)
 
 
-def request_kernel(len_ref, ids_ref, out_ref, slot_ref, *, rows_own, cap):
+def request_kernel(
+    len_ref, ids_hbm, out_ref, slot_ref, ids_ref, arrived, *, rows_own, cap
+):
+    copies = begin([(ids_hbm, ids_ref)], arrived)
     users, block = ids_ref.shape
     shards, _, lanes = out_ref.shape
     shift = rows_own.bit_length() - 1
     earlier = where_bf16(iota((block, block), 0) < iota((block, block), 1), 1.0)
     place = iota((lanes, block), 0)
+    finish(copies)
     total = jnp.zeros((shards, lanes), f32)
     count = jnp.int32(0)
     slot_ref[...] = jnp.zeros_like(slot_ref)
@@ -89,7 +115,10 @@
     out_ref[:, 0, :] = wanted
 
 
-def answer_kernel(wanted_ref, table_ref, out_ref, hot_ref, *, per):
+def answer_kernel(
+    wanted_ref, table_hbm, out_hbm, hot_ref, table_ref, out_ref, arrived, *, per
+):
+    copies = begin([(table_hbm, table_ref)], arrived)
     shards, _, lanes = wanted_ref.shape
     slots = shards * per
     rows = table_ref.shape[0]
@@ -104,20 +133,40 @@
     spot = iota((slots, 128), 1)
     for j in range(rows // 128):
         hot_ref[:, j * 128 : (j + 1) * 128] = where_bf16(column == spot + j * 128, 1.0)
-    out_ref[...] = dot(hot_ref[...], table_ref[...]).astype(bf16)
+    finish(copies)
+    copies = []
+    part = slots // 4
+    for j in range(4):
+        at = slice(j * part, (j + 1) * part)
+        out_ref[at, :] = dot(hot_ref[at, :], table_ref[...]).astype(bf16)
+        copies += begin([(out_ref.at[at, :], out_hbm.at[at, :])], arrived, 1 + j)
+    finish(copies)
 
 
 def quotient_kernel(
-    len_ref, at_ref, ids_ref, table_ref, cot_ref, w_out_ref, quot_ref, dmixed_ref
+    len_ref,
+    at_ref,
+    ids_ref,
+    table_ref,
+    cot_ref,
+    decay_ref,
+    w_out_ref,
+    quot_ref,
+    dmixed_ref,
+    wide_ref,
 ):
     users, block = ids_ref.shape
+    heads = decay_ref.shape[1]
     rows, width = table_ref.shape
     for u in range(users):
+        at = slice(u * block, (u + 1) * block)
         hot = tiled_match(spread_column(ids_ref[u : u + 1, :]), rows)
-        quot_ref[u * block : (u + 1) * block, :] = dot(hot, table_ref[...]).astype(bf16)
+        quot_ref[at, :] = dot(hot, table_ref[...]).astype(bf16)
         valid = at_ref[0] * block + iota((block, width), 0) < len_ref[u]
         masked = jnp.where(valid, cot_ref[u].astype(f32), 0.0).astype(bf16)
-        dmixed_ref[u * block : (u + 1) * block, :] = dot(masked, w_out_ref[...], NT).astype(bf16)
+        dmixed_ref[at, :] = dot(masked, w_out_ref[...], NT).astype(bf16)
+        _, columns = decays(decay_ref[u], width)
+        wide_ref[at, :] = over_heads(columns, heads, width)
 
 
 def decays(log_decay, width):
@@ -157,48 +206,69 @@
 
 def project_kernel(
     at_ref,
+    slot_hbm,
     answered_ref,
+    quot_hbm,
+    wq_hbm,
+    wk_hbm,
+    wv_hbm,
+    wide_hbm,
+    dmixed_hbm,
+    rem_hbm,
+    payload_hbm,
     slot_ref,
     quot_ref,
-    dmixed_ref,
-    decay_ref,
     wq_ref,
     wk_ref,
     wv_ref,
+    wide_ref,
+    dmixed_ref,
     rem_ref,
-    q_ref,
-    k_ref,
-    v_ref,
-    payload_ref,
+    states_ref,
+    arrived,
+    *,
+    users,
+    heads,
 ):
-    users, heads, block = decay_ref.shape
     slots, width = answered_ref.shape
-    peers = payload_ref.shape[0]
+    block = quot_ref.shape[0] // users
+    peers = payload_hbm.shape[0]
     size = width // heads
     me = at_ref[0]
     ends = []
+    copies = begin(
+        (
+            (slot_hbm, slot_ref),
+            (quot_hbm, quot_ref),
+            (wq_hbm, wq_ref),
+            (wk_hbm, wk_ref),
+            (wv_hbm, wv_ref),
+            (wide_hbm, wide_ref),
+            (dmixed_hbm, dmixed_ref),
+        ),
+        arrived,
+    )
+    finish(copies[:1])
+    hot = [tiled_match(spread_column(slot_ref[u : u + 1, :]), slots) for u in range(users)]
+    finish(copies[1:])
+    copies = []
     for u in range(users):
         at = slice(u * block, (u + 1) * block)
-        hot = tiled_match(spread_column(slot_ref[u : u + 1, :]), slots)
-        rem = dot(hot, answered_ref[...]).astype(bf16)
-        rem_ref[at, :] = rem
-        embedded = (quot_ref[at, :].astype(f32) * rem.astype(f32)).astype(bf16)
+        rem_ref[at, :] = dot(hot[u], answered_ref[...]).astype(bf16)
+        copies += begin([(rem_ref.at[at, :], rem_hbm.at[at, :])], arrived, u)
+        embedded = (quot_ref[at, :].astype(f32) * rem_ref[at, :].astype(f32)).astype(bf16)
         q = dot(embedded, wq_ref[...]).astype(bf16)
         k = dot(embedded, wk_ref[...]).astype(bf16)
         v = dot(embedded, wv_ref[...]).astype(bf16)
-        q_ref[at, :] = q
-        k_ref[at, :] = k
-        v_ref[at, :] = v
-        _, columns = decays(decay_ref[u], width)
-        wide = over_heads(columns, heads, width)
+        wide = wide_ref[at, :]
         end = wide[block - 1 : block, :]
         ends.append(end)
         falling = (k.astype(f32) * jnp.exp(end - wide)).astype(bf16)
         growing = (q.astype(f32) * jnp.exp(wide)).astype(bf16)
         state = diagonal_heads(dot(falling, v, TN), heads).astype(bf16)
         grad = diagonal_heads(dot(growing, dmixed_ref[at, :], TN), heads).astype(bf16)
-        for peer in range(peers):
-            payload_ref[peer, u * size : (u + 1) * size, :] = jnp.where(peer > me, state, grad)
+        states_ref[0, u * size : (u + 1) * size, :] = state
+        states_ref[1, u * size : (u + 1) * size, :] = grad
     rows = iota((16, width), 0)
     tail = jnp.zeros((16, width), f32)
     for u in range(users):
@@ -208,20 +278,39 @@
             left = left - piece
             tail = jnp.where(rows == part * users + u, piece, tail)
     tail = tail.astype(bf16)
-    for peer in range(peers):
-        payload_ref[peer, users * size :, :] = tail
+    states_ref[0, users * size :, :] = tail
+    states_ref[1, users * size :, :] = tail
+    which = [jnp.where(peer > me, 0, 1) for peer in range(peers)]
+    pairs = [(states_ref.at[which[peer]], payload_hbm.at[peer]) for peer in range(peers)]
+    finish(copies + begin(pairs, arrived, users))
 
 
 def within_kernel(
-    q_ref, k_ref, v_ref, dmixed_ref, decay_ref, mixed_ref, dq_ref, dk_ref, dv_ref, *, scale
+    quot_ref,
+    rem_ref,
+    dmixed_ref,
+    decay_ref,
+    wq_ref,
+    wk_ref,
+    wv_ref,
+    out_hbm,
+    out_ref,
+    arrived,
+    *,
+    scale,
 ):
     users, heads, block = decay_ref.shape
-    width = q_ref.shape[1]
+    width = quot_ref.shape[1]
+    copies = []
     head_of = iota((block, width), 1) // (width // heads)
     lower_tri = iota((block, block), 0) >= iota((block, block), 1)
     for u in range(users):
         at = slice(u * block, (u + 1) * block)
-        q, k, v, dmixed = q_ref[at, :], k_ref[at, :], v_ref[at, :], dmixed_ref[at, :]
+        embedded = (quot_ref[at, :].astype(f32) * rem_ref[at, :].astype(f32)).astype(bf16)
+        q = dot(embedded, wq_ref[...]).astype(bf16)
+        k = dot(embedded, wk_ref[...]).astype(bf16)
+        v = dot(embedded, wv_ref[...]).astype(bf16)
+        dmixed = dmixed_ref[at, :]
         rows, columns = decays(decay_ref[u], width)
         mixed = jnp.zeros((block, width), f32)
         dq = jnp.zeros((block, width), f32)
@@ -242,59 +331,84 @@
             dq = dq + dot(dweights, k_h)
             dk = dk + dot(dweights, q_h, TN)
             dv = dv + dot(weights, d_h, TN)
-        mixed_ref[at, :] = mixed
-        dq_ref[at, :] = dq
-        dk_ref[at, :] = dk
-        dv_ref[at, :] = dv
-
-
-def sum_halves(ids, terms, core, keep_ref, give_ref):
-    half = keep_ref.shape[0]
+        for i, part in enumerate((mixed, dq, dk, dv)):
+            out_ref[i, at, :] = part
+        copies += begin([(out_ref.at[:, at, :], out_hbm.at[:, at, :])], arrived, u)
+    finish(copies)
+
+
+def sum_half(ids, terms, owner, out_ref):
+    half = out_ref.shape[0]
     chunk = min(256, half)
     spot = iota((chunk, ids.shape[1]), 0)
-    for ref, owner in ((give_ref, 1 - core), (keep_ref, core)):
-        near = ids - owner * half
-        for j in range(half // chunk):
-            hot = where_bf16(spot + j * chunk == near, 1.0)
-            ref[j * chunk : (j + 1) * chunk, :] = dot(hot, terms).astype(ref.dtype)
+    near = ids - owner * half
+    for j in range(half // chunk):
+        hot = where_bf16(spot + j * chunk == near, 1.0)
+        out_ref[j * chunk : (j + 1) * chunk, :] = dot(hot, terms).astype(out_ref.dtype)
 
 
 def gradient_kernel(
     at_ref,
     payload_ref,
-    mixed_ref,
-    dq_ref,
-    dk_ref,
-    dv_ref,
-    q_ref,
-    k_ref,
-    v_ref,
+    within_hbm,
+    dmixed_hbm,
+    wide_hbm,
+    rem_hbm,
+    quot_hbm,
+    slot_hbm,
+    ids_hbm,
+    wq_hbm,
+    wk_hbm,
+    wv_hbm,
+    w_out_hbm,
+    out_hbm,
+    rem_send_hbm,
+    keep_hbm,
+    give_hbm,
+    within_ref,
     dmixed_ref,
-    decay_ref,
+    wide_ref,
+    rem_ref,
+    quot_ref,
+    slot_ref,
+    ids_ref,
     wq_ref,
     wk_ref,
     wv_ref,
     w_out_ref,
-    rem_ref,
-    quot_ref,
-    slot_ref,
-    ids_ref,
     out_ref,
     rem_send_ref,
     keep_ref,
     give_ref,
+    arrived,
     *,
     scale,
+    heads,
 ):
-    users, heads, block = decay_ref.shape
-    width = q_ref.shape[1]
+    users, block = ids_ref.shape
+    width = quot_ref.shape[1]
+    copies = begin(
+        (
+            (quot_hbm, quot_ref),
+            (rem_hbm, rem_ref),
+            (wq_hbm, wq_ref),
+            (wk_hbm, wk_ref),
+            (wv_hbm, wv_ref),
+            (wide_hbm, wide_ref),
+            (dmixed_hbm, dmixed_ref),
+            (w_out_hbm, w_out_ref),
+            (within_hbm, within_ref),
+            (slot_hbm, slot_ref),
+            (ids_hbm, ids_ref),
+        ),
+        arrived,
+    )
     peers = payload_ref.shape[0]
     size = width // heads
     slots = rem_send_ref.shape[0]
     me = at_ref[0]
-    rem_terms, quot_terms = [], []
+    carried = []
     for u in range(users):
-        at = slice(u * block, (u + 1) * block)
         ends = []
         for peer in range(peers):
             tail = payload_ref[peer, users * size :, :].astype(f32)
@@ -313,18 +427,27 @@
             part = payload_ref[peer, u * size : (u + 1) * size, :].astype(f32)
             linked = jnp.exp(ends[peer]) * leaving + part
             leaving = jnp.where(peer > me, linked, leaving)
-        entering = block_diagonal(entering, heads)
-        leaving = block_diagonal(leaving, heads)
-        q, k, v, dmixed = q_ref[at, :], k_ref[at, :], v_ref[at, :], dmixed_ref[at, :]
-        _, columns = decays(decay_ref[u], width)
-        wide = over_heads(columns, heads, width)
+        carried.append((block_diagonal(entering, heads), block_diagonal(leaving, heads)))
+    finish(copies)
+    copies = []
+    rem_terms, quot_terms = [], []
+    for u in range(users):
+        at = slice(u * block, (u + 1) * block)
+        entering, leaving = carried[u]
+        embedded = (quot_ref[at, :].astype(f32) * rem_ref[at, :].astype(f32)).astype(bf16)
+        q = dot(embedded, wq_ref[...]).astype(bf16)
+        k = dot(embedded, wk_ref[...]).astype(bf16)
+        v = dot(embedded, wv_ref[...]).astype(bf16)
+        dmixed = dmixed_ref[at, :]
+        wide = wide_ref[at, :]
         growth = scale * jnp.exp(wide)
         falloff = scale * jnp.exp(wide[block - 1 : block, :] - wide)
-        mixed = (mixed_ref[at, :] + growth * dot(q, entering)).astype(bf16)
+        mixed = (within_ref[0, at, :] + growth * dot(q, entering)).astype(bf16)
         out_ref[u] = dot(mixed, w_out_ref[...]).astype(bf16)
-        dq = (dq_ref[at, :] + growth * dot(dmixed, entering, NT)).astype(bf16)
-        dk = (dk_ref[at, :] + falloff * dot(v, leaving, NT)).astype(bf16)
-        dv = (dv_ref[at, :] + falloff * dot(k, leaving)).astype(bf16)
+        copies += begin([(out_ref.at[u], out_hbm.at[u])], arrived, u)
+        dq = (within_ref[1, at, :] + growth * dot(dmixed, entering, NT)).astype(bf16)
+        dk = (within_ref[2, at, :] + falloff * dot(v, leaving, NT)).astype(bf16)
+        dv = (within_ref[3, at, :] + falloff * dot(k, leaving)).astype(bf16)
         dembedded = dot(dq, wq_ref[...], NT) + dot(dk, wk_ref[...], NT) + dot(dv, wv_ref[...], NT)
         rem_terms.append((dembedded * quot_ref[at, :].astype(f32)).astype(bf16))
         quot_terms.append((dembedded * rem_ref[at, :].astype(f32)).astype(bf16))
@@ -336,7 +459,12 @@
     for j in range(slots // block):
         hot = where_bf16(spot + j * block == slot, 1.0)
         rem_send_ref[j * block : (j + 1) * block, :] = dot(hot, rem_terms).astype(bf16)
-    sum_halves(ids, quot_terms, me % 2, keep_ref, give_ref)
+    copies += begin([(rem_send_ref, rem_send_hbm)], arrived, users)
+    sum_half(ids, quot_terms, 1 - me % 2, give_ref)
+    copies += begin([(give_ref, give_hbm)], arrived, users + 1)
+    sum_half(ids, quot_terms, me % 2, keep_ref)
+    copies += begin([(keep_ref, keep_hbm)], arrived, users + 2)
+    finish(copies)
 
 
 def collect_kernel(at_ref, wanted_ref, back_ref, keep_ref, give_ref, *, per):
@@ -349,7 +477,8 @@
     high = jnp.sum(jnp.where(own, dot(high.astype(bf16), tile), 0.0), axis=0, keepdims=True)
     low = jnp.sum(jnp.where(own, dot(low.astype(bf16), tile), 0.0), axis=0, keepdims=True)
     row = (16.0 * high + low).astype(i32) - 1
-    sum_halves(row, back_ref[...], at_ref[0] % 2, keep_ref, give_ref)
+    sum_half(row, back_ref[...], 1 - at_ref[0] % 2, give_ref)
+    sum_half(row, back_ref[...], at_ref[0] % 2, keep_ref)
 
 
 def split_kernel(at_ref, keep_ref, got_ref, *out_refs):
@@ -361,11 +490,34 @@
         out_ref[...] = both.astype(bf16)
 
 
+def cut(chunk, shards):
+    rows, width = chunk.shape
+    lanes = width // 128
+    part = rows * lanes // shards
+    return [
+        chunk[i // lanes * part : (i // lanes + 1) * part, i % lanes * 128 : (i % lanes + 1) * 128]
+        for i in range(shards)
+    ]
+
+
+def total_kernel(*refs):
+    total = sum((ref[...].astype(f32) for ref in refs[1:-1]), refs[0][...].astype(f32))
+    for i, tile in enumerate(cut(total, refs[-1].shape[0])):
+        refs[-1][i] = tile.astype(bf16)
+
+
+def repeat_kernel(tiles_ref, out_ref):
+    total = jnp.sum(tiles_ref[...].astype(f32), axis=0).astype(bf16)
+    for i in range(out_ref.shape[0]):
+        out_ref[i] = total
+
+
 def place_kernel(at_ref, wanted_ref, *refs, per, total):
-    out_ref = refs[-1]
-    chunks = refs[:-1]
+    out_hbm, out_ref, arrived = refs[-3:]
+    chunks = refs[:-3]
+    copies = []
     chips = len(chunks) // 2
-    rows = chunks[0].shape[0]
+    _, rows, width = out_ref.shape
     shards, _, lanes = wanted_ref.shape
     counted = jnp.where(iota((shards, lanes), 1) == per, wanted_ref[:, 0, :], 0)
     ratio = total / jnp.sum(counted.astype(f32), axis=(0, 1), keepdims=True)
@@ -375,15 +527,23 @@
         for d in range(chips):
             spot = half * chips + lax.rem(chip + chips - d, chips)
             base = pl.multiple_of(spot * rows, rows)
-            out_ref[pl.ds(base, rows), :] = ratio * chunks[other * chips + d][...].astype(f32)
+            chunk = chunks[other * chips + d]
+            n = other * chips + d
+            if len(chunk.shape) == 2:
+                out_ref[n] = ratio * chunk[...].astype(f32)
+            else:
+                part = chunk.shape[1]
+                for i in range(shards):
+                    across = i % (width // 128) * 128
+                    down = i // (width // 128) * part
+                    tile = ratio * chunk[i].astype(f32)
+                    out_ref[n, down : down + part, across : across + 128] = tile
+            copies += begin([(out_ref.at[n], out_hbm.at[pl.ds(base, rows), :])], arrived, n)
+    finish(copies)
 
 
 def exchange(array, axis):
     return lax.all_to_all(array, axis, split_axis=0, concat_axis=0, tiled=True)
-
-
-def added(parts):
-    return jnp.sum(parts.astype(f32), axis=0).astype(bf16)
 
 
 def to_core(array):
@@ -405,21 +565,22 @@
         (at, keep, to_core(give)),
         [SM, VM, VM],
     )
-    got = [to_chip(chunks[d], d) for d in range(1, chips)]
-    return sum((c.astype(f32) for c in got), chunks[0].astype(f32)).astype(bf16)
-
-
-def gathered(at, wanted, chunk, per, total):
+    return [chunks[0]] + [to_chip(chunks[d], d) for d in range(1, chips)]
+
+
+def everywhere(chunk):
     chips = lax.axis_size("hist") // 2
     mine = [chunk] + [to_chip(chunk, d) for d in range(1, chips)]
-    theirs = [to_core(c) for c in mine]
+    return mine + [to_core(c) for c in mine]
+
+
+def placed(at, wanted, chunks, rows, width, per, total):
     kernel = functools.partial(place_kernel, per=per, total=total)
-    (out,) = call(
-        kernel,
-        [((2 * chips * chunk.shape[0], chunk.shape[1]), f32)],
-        (at, wanted, *mine, *theirs),
-        [SM] + [VM] * (1 + 2 * chips),
-    )
+    specs = [SM] + [VM] * (1 + len(chunks))
+    n = len(chunks)
+    scratch = [pltpu.VMEM((n, rows // n, width), f32), dma(n)]
+    args = (at, wanted, *chunks)
+    (out,) = call(kernel, [((rows, width), f32)], args, specs, scratch, [HB])
     return out
 
 
@@ -454,80 +615,102 @@
         functools.partial(request_kernel, rows_own=rows_own, cap=cap),
         [((shards, 1, lanes), i32), ((8, block), i32)],
         (lengths, rem_ids),
-        [SM, VM],
+        [SM, HB],
+        [pltpu.VMEM((users, block), i32), dma(1)],
+        limit=FULL,
     )
     wanted = exchange(requests, "user")
-    quot_emb, dmixed = call(
+    quot_emb, dmixed, wide = call(
         quotient_kernel,
-        [((users * block, width), bf16)] * 2,
-        (lengths, at, quot_ids, quot_table, cotangent, w_out),
-        [SM, SM, VM, VM, VM, VM],
+        [
+            ((users * block, width), bf16),
+            ((users * block, width), bf16),
+            ((users * block, width), f32),
+        ],
+        (lengths, at, quot_ids, quot_table, cotangent, log_decay, w_out),
+        [SM, SM] + [VM] * 5,
+        limit=FULL,
     )
     (found,) = call(
         functools.partial(answer_kernel, per=per),
         [((slots, width), bf16)],
         (wanted, rem_table),
-        scratch=[pltpu.VMEM((slots, rows_own), bf16)],
+        [VM, HB],
+        [
+            pltpu.VMEM((slots, rows_own), bf16),
+            pltpu.VMEM((rows_own, width), bf16),
+            pltpu.VMEM((slots, width), bf16),
+            dma(5),
+        ],
+        [HB],
+        FULL,
     )
     answered = exchange(found.reshape(shards, per, width), "user").reshape(slots, width)
-    rem_emb, q, k, v, payload = call(
-        project_kernel,
-        [((users * block, width), bf16)] * 4 + [((peers, users * size + 16, width), bf16)],
-        (at, answered, slot, quot_emb, dmixed, log_decay, w_query, w_key, w_value),
-        [SM] + [VM] * 8,
+    events = pltpu.VMEM((users * block, width), bf16)
+    square = pltpu.VMEM((width, width), bf16)
+    rem_emb, payload = call(
+        functools.partial(project_kernel, users=users, heads=heads),
+        [((users * block, width), bf16), ((peers, users * size + 16, width), bf16)],
+        (at, slot, answered, quot_emb, w_query, w_key, w_value, wide, dmixed),
+        [SM, HB, VM] + [HB] * 6,
+        [pltpu.VMEM((8, block), i32), events]
+        + [square] * 3
+        + [pltpu.VMEM((users * block, width), f32), events, events]
+        + [pltpu.VMEM((2, users * size + 16, width), bf16), dma(8 + users + peers)],
+        [HB, HB],
+        MOST,
     )
     states = exchange(payload, "hist")
-    mixed, dq, dk, dv = call(
+    parts = (4, users * block, width)
+    (within,) = call(
         functools.partial(within_kernel, scale=scale),
-        [((users * block, width), f32)] * 4,
-        (q, k, v, dmixed, log_decay),
+        [(parts, f32)],
+        (quot_emb, rem_emb, dmixed, log_decay, w_query, w_key, w_value),
+        scratch=[pltpu.VMEM(parts, f32), dma(users)],
+        out_specs=[HB],
+        limit=FULL,
     )
     output, rem_send, keep, give = call(
-        functools.partial(gradient_kernel, scale=scale),
+        functools.partial(gradient_kernel, scale=scale, heads=heads),
         [
             ((users, block, width), bf16),
             ((slots, width), bf16),
             ((rows_all // 2, width), f32),
             ((rows_all // 2, width), bf16),
         ],
-        (
-            at,
-            states,
-            mixed,
-            dq,
-            dk,
-            dv,
-            q,
-            k,
-            v,
-            dmixed,
-            log_decay,
-            w_query,
-            w_key,
-            w_value,
-            w_out,
-            rem_emb,
-            quot_emb,
-            slot,
-            quot_ids,
-        ),
-        [SM] + [VM] * 18,
+        (at, states, within, dmixed, wide, rem_emb, quot_emb, slot, quot_ids)
+        + (w_query, w_key, w_value, w_out),
+        [SM, VM] + [HB] * 11,
+        [pltpu.VMEM(parts, f32), events]
+        + [pltpu.VMEM((users * block, width), f32), events, events]
+        + [pltpu.VMEM((8, block), i32), pltpu.VMEM((users, block), i32)]
+        + [square] * 4
+        + [pltpu.VMEM((users, block, width), bf16), pltpu.VMEM((slots, width), bf16)]
+        + [pltpu.VMEM((rows_all // 2, width), f32), pltpu.VMEM((rows_all // 2, width), bf16)]
+        + [dma(12)],
+        [HB] * 4,
+        MOST,
     )
     rem_back = exchange(rem_send.reshape(shards, per, width), "user").reshape(slots, width)
-    quot_sum = reduced(at, keep, give)
-    quot_back = exchange(quot_sum.reshape(shards, -1, width), "user")
+    tiles = (shards, rows_all // peers * width // shards // 128, 128)
+    (quot_tiles,) = call(total_kernel, [(tiles, bf16)], reduced(at, keep, give))
+    rem_back, quot_tiles = lax.optimization_barrier((rem_back, quot_tiles))
+    quot_back = exchange(quot_tiles, "user")
     keep, give = call(
         functools.partial(collect_kernel, per=per),
         [((rows_own // 2, width), f32), ((rows_own // 2, width), bf16)],
         (at, wanted, rem_back),
         [SM, VM, VM],
     )
-    rem_sum = reduced(at, keep, give)
-    quot_sum = added(quot_back)
-    quot_sum = exchange(jnp.broadcast_to(quot_sum, (shards,) + quot_sum.shape), "user")
+    rem_sum = sum(c.astype(f32) for c in reduced(at, keep, give)).astype(bf16)
+    (quot_tiles,) = call(repeat_kernel, [(tiles, bf16)], (quot_back,))
+    quot_tiles, rem_sum = lax.optimization_barrier((quot_tiles, rem_sum))
+    quot_tiles = exchange(quot_tiles, "user")
+    rem_chunks = everywhere(rem_sum)
+    quot_tiles, *rem_chunks = lax.optimization_barrier((quot_tiles, *rem_chunks))
     total = float(users * shards * block * peers)
-    rem_grad = gathered(at, wanted, rem_sum, per, total)
-    quot_grad = gathered(at, wanted, quot_sum.reshape(-1, width), per, total)
+    rem_grad = placed(at, wanted, rem_chunks, rows_own, width, per, total)
+    quot_grad = placed(at, wanted, everywhere(quot_tiles), rows_all, width, per, total)
     return (output, quot_grad, rem_grad)
 
 

time: 164 us -> 159 us (0.970)
  blocking collectives: 48 us -> 20.7 us
  starting transfers between devices: 50.9 us -> 65.2 us
  Pallas kernels: 20.6 us -> 34 us
  local copies, waits for them, and re-layouts: 15.9 us -> 2.85 us
  waiting for transfers between devices: 26.5 us -> 34.5 us
    all_to_all x3 -> x1, blocking collectives: 48 us -> 20.7 us  [exchange(): return lax.all_to_all(array, axis, split_axis=0, concat_axis=0, tiled=True)]
    all_to_all x3 -> x5, starting transfers between devices: 18.4 us -> 34.8 us  [exchange(): return lax.all_to_all(array, axis, split_axis=0, concat_axis=0, tiled=True)]
    pallas_call x11 -> x13, Pallas kernels: 20.6 us -> 34 us  [call(): pl.pallas_call(kernel, out_shape=tuple((jax.ShapeDtypeStruct(s, d) for s,...]
    unnamed x52 -> x8, local copies, waits for them, and re-layouts: 15.9 us -> 2.85 us
    ppermute x12, waiting for transfers between devices: 1.48 us -> 6.32 us  [to_chip(): lax.ppermute(array, 'hist', [(i, (i + 2 * steps) % peers) for i in range(...]
    ppermute x10, starting transfers between devices: 19.9 us -> 16.8 us  [to_core(): return lax.ppermute(array, 'hist', [(i, i ^ 1) for i in range(peers)])]
    all_to_all x3 -> x5, waiting for transfers between devices: 23.2 us -> 26.1 us  [exchange(): return lax.all_to_all(array, axis, split_axis=0, concat_axis=0, tiled=True)]
  transfers between devices with their start and end apart: 25 -> 27, of which waited for: 5 -> 9; matrix products, arithmetic and copies ran while one was open for 0% -> 0% of each run, Pallas kernels for 5% -> 8%
where the time goes in v3:
time: 159 us; the launch traced here: 158 us
  starting transfers between devices  65.2 us (41%)
  waiting for transfers between devices  34.5 us (22%)
  Pallas kernels  34 us (21%)
  blocking collectives  20.7 us (13%)
  local copies, waits for them, and re-layouts  2.85 us (2%)
    all_to_all x5, starting transfers between devices, exchange(): return lax.all_to_all(array, axis, split_axis=0, concat_axis=0, tiled=True)  34.8 us
    pallas_call x13, Pallas kernels, call(): pl.pallas_call(kernel, out_shape=tuple((jax.ShapeDtypeStruct(s, d) for s,...  34 us
    all_to_all x5, waiting for transfers between devices, exchange(): return lax.all_to_all(array, axis, split_axis=0, concat_axis=0, tiled=True)  26.1 us
    all_to_all x1, blocking collectives, exchange(): return lax.all_to_all(array, axis, split_axis=0, concat_axis=0, tiled=True)  20.7 us
    ppermute x10, starting transfers between devices, to_core(): return lax.ppermute(array, 'hist', [(i, i ^ 1) for i in range(peers)])  16.8 us
    ppermute x12, starting transfers between devices, to_chip(): lax.ppermute(array, 'hist', [(i, (i + 2 * steps) % peers) for i in range(...  13.6 us
    ppermute x12, waiting for transfers between devices, to_chip(): lax.ppermute(array, 'hist', [(i, (i + 2 * steps) % peers) for i in range(...  6.32 us
  transfers between devices with their start and end apart: 27, of which 9 were waited for; matrix products, arithmetic and copies ran while one was open for 0% of the time, Pallas kernels for 8%

profile of v3, /device:TPU:1, one launch (start us, length us, event | category | flops | bytes accessed | tf_op | source)
XLA Modules:
  0.0 158.4 jit_solution(16642202544993720746)
XLA Ops:
  0.6 2.5 %shard_map.130 = (s32[32,1,128]{2,1,0:T(1,128)}, s32[8,256]{1,0:T(8,128)}) custom-call(s32[2]{0:T(128)} %len_ref.3, s32[2,256]{1,0:T(2,128)} %ids_hbm.2), custom_call_target="tpu_custom_call" | custom-call | tf_op jit(solution)/shard_map/pallas_call | solution.py:78
  3.2 20.7 %all_to_all.30.wanted_ref = s32[32,1,128]{2,1,0:T(1,128)} all-to-all(s32[32,1,128]{2,1,0:T(1,128)} %get-tuple-element.38), channel_id=1, replica_groups=mesh['user'=32,'hist'=8] {'user'}, dimensions={0} | all-to-all | bytes 32768 | tf_op jit(solution)/shard_map/all_to_all | solution.py:546
  23.9 4.3 %shard_map.131 = bf16[1024,256]{1,0:T(8,128)(2,1)} custom-call(s32[32,1,128]{2,1,0:T(1,128)} %all_to_all.30.wanted_ref, bf16[2048,256]{1,0:T(8,128)(2,1)} %table_hbm.1), custom_call_target="tpu_custom_call" | custom-call | tf_op jit(solution)/shard_map/pallas_call | solution.py:78
  28.2 3.9 %all-to-all-start.1 = ((bf16[32,32,256]{2,1,0:T(8,128)(2,1)}), bf16[32,32,256]{2,1,0:T(8,128)(2,1)S(1)}, u32[]{:S(2)}, u32[]{:S(2)}) async-start(bf16[32,32,256]{2,1,0:T(8,128)(2,1)} %bitcast.7), calls=%async_computation.1 | async-start | bytes 1048576 | tf_op jit(solution)/shard_map/all_to_all | solution.py:546
  32.1 3.8 %shard_map.132 = (bf16[512,256]{1,0:T(8,128)(2,1)}, bf16[512,256]{1,0:T(8,128)(2,1)}, f32[512,256]{1,0:T(8,128)}) custom-call(s32[2]{0:T(128)} %len_ref.3, s32[1]{0:T(128)} %bitcast.at_ref, s32[2,256]{1,0:T(2,128)} %ids_hbm.3, bf16[2048,256]{1,0:T(8,128)(2,1)} %table_ref.1, bf16[2,256,256]{2,1,0:T(8,128)(2,1)} %cot_ref.1, f32[2,4,256]{2,1,0:T(4,128)} %decay_ref.3, ...), custom_call_target="tpu_custom_call" | custom-call | tf_op jit(solution)/shard_map/pallas_call | solution.py:78
  35.8 9.2 %all-to-all-done.1 = bf16[32,32,256]{2,1,0:T(8,128)(2,1)S(1)} async-done(((bf16[32,32,256]{2,1,0:T(8,128)(2,1)}), bf16[32,32,256]{2,1,0:T(8,128)(2,1)S(1)}, u32[]{:S(2)}, u32[]{:S(2)}) %all-to-all-start.1) | async-done | bytes 524320 | tf_op jit(solution)/shard_map/all_to_all | solution.py:546
  45.1 0.8 copy-done.3
  45.9 4.9 %shard_map.133 = (bf16[512,256]{1,0:T(8,128)(2,1)}, bf16[8,144,256]{2,1,0:T(8,128)(2,1)}) custom-call(s32[1]{0:T(128)} %bitcast.at_ref, s32[8,256]{1,0:T(8,128)} %get-tuple-element.37.slot_hbm, bf16[1024,256]{1,0:T(8,128)(2,1)} %bitcast.6, bf16[512,256]{1,0:T(8,128)(2,1)} %get-tuple-element.39.quot_hbm.quot_ref, bf16[256,256]{1,0:T(8,128)(2,1)} %wq_hbm.3, ...), custom_call_target="tpu_custom_call" | custom-call | tf_op jit(solution)/shard_map/pallas_call | solution.py:78
  50.8 9.5 %all-to-all-start.2 = ((bf16[8,144,256]{2,1,0:T(8,128)(2,1)}), bf16[8,144,256]{2,1,0:T(8,128)(2,1)S(1)}, u32[]{:S(2)}, u32[]{:S(2)}) async-start(bf16[8,144,256]{2,1,0:T(8,128)(2,1)} %get-tuple-element.42), calls=%async_computation.2 | async-start | bytes 1179648 | tf_op jit(solution)/shard_map/all_to_all | solution.py:546
  60.3 5.7 %shard_map.134.within_hbm = f32[4,512,256]{2,1,0:T(8,128)} custom-call(bf16[512,256]{1,0:T(8,128)(2,1)} %get-tuple-element.39.quot_hbm.quot_ref, bf16[512,256]{1,0:T(8,128)(2,1)} %get-tuple-element.43.rem_ref.rem_hbm, bf16[512,256]{1,0:T(8,128)(2,1)} %get-tuple-element.41.dmixed_hbm.dmixed_ref, f32[2,4,256]{2,1,0:T(4,128)} %decay_ref.3, ...), custom_call_target="tpu_custom_call" | custom-call | tf_op jit(solution)/shard_map/pallas_call | solution.py:78
  66.0 4.5 %all-to-all-done.2.payload_ref = bf16[8,144,256]{2,1,0:T(8,128)(2,1)S(1)} async-done(((bf16[8,144,256]{2,1,0:T(8,128)(2,1)}), bf16[8,144,256]{2,1,0:T(8,128)(2,1)S(1)}, u32[]{:S(2)}, u32[]{:S(2)}) %all-to-all-start.2) | async-done | bytes 589856 | tf_op jit(solution)/shard_map/all_to_all | solution.py:546
  70.5 0.8 copy-done.2
  71.3 6.8 %shard_map.135 = (bf16[2,256,256]{2,1,0:T(8,128)(2,1)}, bf16[1024,256]{1,0:T(8,128)(2,1)}, f32[1024,256]{1,0:T(8,128)}, bf16[1024,256]{1,0:T(8,128)(2,1)}) custom-call(s32[1]{0:T(128)} %bitcast.at_ref, bf16[8,144,256]{2,1,0:T(8,128)(2,1)} %copy-done.2, f32[4,512,256]{2,1,0:T(8,128)} %shard_map.134.within_hbm, ...), custom_call_target="tpu_custom_call" | custom-call | tf_op jit(solution)/shard_map/pallas_call | solution.py:78
  78.1 5.0 %all-to-all-start.3 = ((bf16[32,32,256]{2,1,0:T(8,128)(2,1)}), bf16[32,32,256]{2,1,0:T(8,128)(2,1)S(1)}, u32[]{:S(2)}, u32[]{:S(2)}) async-start(bf16[32,32,256]{2,1,0:T(8,128)(2,1)} %bitcast.8), calls=%async_computation.3 | async-start | bytes 1048576 | tf_op jit(solution)/shard_map/all_to_all | solution.py:546
  83.1 1.2 collective-permute-start
  84.4 1.7 %collective-permute-done.got_ref = bf16[1024,256]{1,0:T(8,128)(2,1)S(1)} collective-permute-done((bf16[1024,256]{1,0:T(8,128)(2,1)}, bf16[1024,256]{1,0:T(8,128)(2,1)S(1)}, u32[]{:S(2)}, u32[]{:S(2)}) %collective-permute-start) | collective-permute-done | bytes 524320 | tf_op jit(solution)/shard_map/ppermute | solution.py:551
  86.1 1.2 copy-done
  87.3 0.1 shard_map.136
  87.4 0.4 collective-permute-start.1
  87.8 1.8 %collective-permute-start.2 = (bf16[256,256]{1,0:T(8,128)(2,1)S(1)}, bf16[256,256]{1,0:T(8,128)(2,1)S(1)}, u32[]{:S(2)}, u32[]{:S(2)}) collective-permute-start(bf16[256,256]{1,0:T(8,128)(2,1)S(1)} %get-tuple-element.50), channel_id=1, source_target_pairs={{0,4},{1,5},{2,6},{3,7},{4,0},{5,1},{6,2},{7,3},{8,12},{9,13},{10,... | collective-permute-start | bytes 393224 | tf_op jit(solution)/shard_map/ppermute | solution.py:556
  89.6 0.7 collective-permute-start.3
  90.3 3.7 %collective-permute-done.1.refs_1_ = bf16[256,256]{1,0:T(8,128)(2,1)S(1)} collective-permute-done((bf16[256,256]{1,0:T(8,128)(2,1)S(1)}, bf16[256,256]{1,0:T(8,128)(2,1)S(1)}, u32[]{:S(2)}, u32[]{:S(2)}) %collective-permute-start.1) | collective-permute-done | bytes 131104 | tf_op jit(solution)/shard_map/ppermute | solution.py:556
  94.0 1.6 %collective-permute-done.2.refs_2_ = bf16[256,256]{1,0:T(8,128)(2,1)S(1)} collective-permute-done((bf16[256,256]{1,0:T(8,128)(2,1)S(1)}, bf16[256,256]{1,0:T(8,128)(2,1)S(1)}, u32[]{:S(2)}, u32[]{:S(2)}) %collective-permute-start.2) | collective-permute-done | bytes 131104 | tf_op jit(solution)/shard_map/ppermute | solution.py:556
  95.7 0.9 collective-permute-done.3.refs_3_
  96.6 0.7 shard_map.137
  97.3 0.0 all-to-all-done.3
  97.3 1.4 shard_map.139
  98.7 3.9 %collective-permute-start.4 = (bf16[1024,256]{1,0:T(8,128)(2,1)S(1)}, bf16[1024,256]{1,0:T(8,128)(2,1)S(1)}, u32[]{:S(2)}, u32[]{:S(2)}) collective-permute-start(bf16[1024,256]{1,0:T(8,128)(2,1)S(1)} %get-tuple-element.55), channel_id=1, source_target_pairs={{0,1},{1,0},{2,3},{3,2},{4,5},{5,4},{6,7},{7,6},{8,9},{9,8},{10,11... | collective-permute-start | bytes 1572872 | tf_op jit(solution)/shard_map/ppermute | solution.py:551
  102.6 7.1 %all-to-all-start.4 = ((bf16[32,16,128]{2,1,0:T(8,128)(2,1)}), bf16[32,16,128]{2,1,0:T(8,128)(2,1)S(1)}, u32[]{:S(2)}, u32[]{:S(2)}) async-start(bf16[32,16,128]{2,1,0:T(8,128)(2,1)} %shard_map.137), calls=%async_computation.4 | async-start | bytes 262144 | tf_op jit(solution)/shard_map/all_to_all | solution.py:546
  109.8 0.0 collective-permute-done.4.got_ref
  109.8 0.1 shard_map.140
  109.9 0.1 collective-permute-start.5
  110.1 3.3 %collective-permute-start.6 = (bf16[256,256]{1,0:T(8,128)(2,1)S(1)}, bf16[256,256]{1,0:T(8,128)(2,1)S(1)}, u32[]{:S(2)}, u32[]{:S(2)}) collective-permute-start(bf16[256,256]{1,0:T(8,128)(2,1)S(1)} %get-tuple-element.58), channel_id=1, source_target_pairs={{0,4},{1,5},{2,6},{3,7},{4,0},{5,1},{6,2},{7,3},{8,12},{9,13},{10,... | collective-permute-start | bytes 393224 | tf_op jit(solution)/shard_map/ppermute | solution.py:556
  113.3 0.0 collective-permute-start.7
  113.3 5.6 %all-to-all-done.4.tiles_ref = bf16[32,16,128]{2,1,0:T(8,128)(2,1)S(1)} async-done(((bf16[32,16,128]{2,1,0:T(8,128)(2,1)}), bf16[32,16,128]{2,1,0:T(8,128)(2,1)S(1)}, u32[]{:S(2)}, u32[]{:S(2)}) %all-to-all-start.4) | async-done | bytes 131104 | tf_op jit(solution)/shard_map/all_to_all | solution.py:546
  118.9 0.7 shard_map.138
  119.6 0.0 collective-permute-done.5
  119.6 0.0 collective-permute-done.6
  119.7 0.1 add_convert_fusion.refs_0_
  119.7 2.8 %collective-permute-start.10 = (bf16[256,256]{1,0:T(8,128)(2,1)S(1)}, bf16[256,256]{1,0:T(8,128)(2,1)S(1)}, u32[]{:S(2)}, u32[]{:S(2)}) collective-permute-start(bf16[256,256]{1,0:T(8,128)(2,1)S(1)} %add_convert_fusion.refs_0_), channel_id=1, source_target_pairs={{0,6},{1,7},{2,0},{3,1},{4,2},{5,3},{6,4},{7,5},{8,14},{9,15},{10,... | collective-permute-start | bytes 393224 | tf_op jit(solution)/shard_map/ppermute | solution.py:556
  122.6 0.0 collective-permute-start.9
  122.6 0.7 collective-permute-start.8
  123.2 9.2 %all-to-all-start.5 = ((bf16[32,16,128]{2,1,0:T(8,128)(2,1)}), bf16[32,16,128]{2,1,0:T(8,128)(2,1)S(1)}, u32[]{:S(2)}, u32[]{:S(2)}) async-start(bf16[32,16,128]{2,1,0:T(8,128)(2,1)} %shard_map.138), calls=%async_computation.5 | async-start | bytes 262144 | tf_op jit(solution)/shard_map/all_to_all | solution.py:546
  132.5 1.4 collective-permute-start.11
  133.9 0.0 collective-permute-done.10.refs_3_
  133.9 0.1 collective-permute-start.14
  134.0 0.4 collective-permute-start.13
  134.4 0.0 collective-permute-done.8.refs_1_
  134.4 0.1 collective-permute-start.12
  134.5 0.4 collective-permute-done.11.refs_4_
  134.9 6.8 %all-to-all-done.5.refs_0_ = bf16[32,16,128]{2,1,0:T(8,128)(2,1)S(1)} async-done(((bf16[32,16,128]{2,1,0:T(8,128)(2,1)}), bf16[32,16,128]{2,1,0:T(8,128)(2,1)S(1)}, u32[]{:S(2)}, u32[]{:S(2)}) %all-to-all-start.5) | async-done | bytes 131104 | tf_op jit(solution)/shard_map/all_to_all | solution.py:546
  141.6 0.0 collective-permute-done.14.refs_7_
  141.7 2.1 %collective-permute-start.17 = (bf16[32,16,128]{2,1,0:T(8,128)(2,1)S(1)}, bf16[32,16,128]{2,1,0:T(8,128)(2,1)S(1)}, u32[]{:S(2)}, u32[]{:S(2)}) collective-permute-start(bf16[32,16,128]{2,1,0:T(8,128)(2,1)S(1)} %all-to-all-done.5.refs_0_), channel_id=1, source_target_pairs={{0,6},{1,7},{2,0},{3,1},{4,2},{5,3},{6,4},{7,5},{8,14},{9,15},{10,... | collective-permute-start | bytes 393224 | tf_op jit(solution)/shard_map/ppermute | solution.py:556
  143.7 1.7 %collective-permute-start.16 = (bf16[32,16,128]{2,1,0:T(8,128)(2,1)S(1)}, bf16[32,16,128]{2,1,0:T(8,128)(2,1)S(1)}, u32[]{:S(2)}, u32[]{:S(2)}) collective-permute-start(bf16[32,16,128]{2,1,0:T(8,128)(2,1)S(1)} %all-to-all-done.5.refs_0_), channel_id=1, source_target_pairs={{0,4},{1,5},{2,6},{3,7},{4,0},{5,1},{6,2},{7,3},{8,12},{9,13},{10,... | collective-permute-start | bytes 393224 | tf_op jit(solution)/shard_map/ppermute | solution.py:556
  145.5 3.5 %collective-permute-start.18 = (bf16[32,16,128]{2,1,0:T(8,128)(2,1)S(1)}, bf16[32,16,128]{2,1,0:T(8,128)(2,1)S(1)}, u32[]{:S(2)}, u32[]{:S(2)}) collective-permute-start(bf16[32,16,128]{2,1,0:T(8,128)(2,1)S(1)} %all-to-all-done.5.refs_0_), channel_id=1, source_target_pairs={{0,1},{1,0},{2,3},{3,2},{4,5},{5,4},{6,7},{7,6},{8,9},{9,8},{10,11... | collective-permute-start | bytes 393224 | tf_op jit(solution)/shard_map/ppermute | solution.py:551
  148.9 0.0 collective-permute-done.17.refs_3_
  148.9 0.9 collective-permute-start.21
  149.8 0.0 collective-permute-done.16.refs_2_
  149.8 3.2 %collective-permute-start.20 = (bf16[32,16,128]{2,1,0:T(8,128)(2,1)S(1)}, bf16[32,16,128]{2,1,0:T(8,128)(2,1)S(1)}, u32[]{:S(2)}, u32[]{:S(2)}) collective-permute-start(bf16[32,16,128]{2,1,0:T(8,128)(2,1)S(1)} %collective-permute-done.16.refs_2_), channel_id=1, source_target_pairs={{0,1},{1,0},{2,3},{3,2},{4,5},{5,4},{6,7},{7,6},{8,9},{9,8},{10,11... | collective-permute-start | bytes 393224 | tf_op jit(solution)/shard_map/ppermute | solution.py:551
  153.0 2.1 %collective-permute-start.19 = (bf16[32,16,128]{2,1,0:T(8,128)(2,1)S(1)}, bf16[32,16,128]{2,1,0:T(8,128)(2,1)S(1)}, u32[]{:S(2)}, u32[]{:S(2)}) collective-permute-start(bf16[32,16,128]{2,1,0:T(8,128)(2,1)S(1)} %collective-permute-done.15.refs_1_), channel_id=1, source_target_pairs={{0,1},{1,0},{2,3},{3,2},{4,5},{5,4},{6,7},{7,6},{8,9},{9,8},{10,11... | collective-permute-start | bytes 393224 | tf_op jit(solution)/shard_map/ppermute | solution.py:551
  155.1 1.5 shard_map.142
  156.7 0.0 collective-permute-done.21.refs_7_
  156.7 0.0 collective-permute-done.20.refs_6_
  156.7 1.5 shard_map.141
  (13 shorter events, 0.0 us)
Async XLA Ops:
  28.2 16.9 %all-to-all-start.1 = ((bf16[32,32,256]{2,1,0:T(8,128)(2,1)}), bf16[32,32,256]{2,1,0:T(8,128)(2,1)S(1)}, u32[]{:S(2)}, u32[]{:S(2)}) async-start(bf16[32,32,256]{2,1,0:T(8,128)(2,1)} %bitcast.7), calls=%async_computation.1 | async-start | bytes 1048576 | tf_op jit(solution)/shard_map/all_to_all | solution.py:546
  45.1 0.8 copy-start.3
  50.8 19.7 %all-to-all-start.2 = ((bf16[8,144,256]{2,1,0:T(8,128)(2,1)}), bf16[8,144,256]{2,1,0:T(8,128)(2,1)S(1)}, u32[]{:S(2)}, u32[]{:S(2)}) async-start(bf16[8,144,256]{2,1,0:T(8,128)(2,1)} %get-tuple-element.42), calls=%async_computation.2 | async-start | bytes 1179648 | tf_op jit(solution)/shard_map/all_to_all | solution.py:546
  70.5 0.8 copy-start.2
  78.1 19.2 %copy-start.1 = (s32[32,1,128]{2,1,0:T(1,128)S(1)}, s32[32,1,128]{2,1,0:T(1,128)}, u32[]{:S(2)}) copy-start(s32[32,1,128]{2,1,0:T(1,128)} %all_to_all.30.wanted_ref) | copy-start | bytes 49156
  78.1 19.2 %all-to-all-start.3 = ((bf16[32,32,256]{2,1,0:T(8,128)(2,1)}), bf16[32,32,256]{2,1,0:T(8,128)(2,1)S(1)}, u32[]{:S(2)}, u32[]{:S(2)}) async-start(bf16[32,32,256]{2,1,0:T(8,128)(2,1)} %bitcast.8), calls=%async_computation.3 | async-start | bytes 1048576 | tf_op jit(solution)/shard_map/all_to_all | solution.py:546
  83.1 3.0 %collective-permute-start = (bf16[1024,256]{1,0:T(8,128)(2,1)}, bf16[1024,256]{1,0:T(8,128)(2,1)S(1)}, u32[]{:S(2)}, u32[]{:S(2)}) collective-permute-start(bf16[1024,256]{1,0:T(8,128)(2,1)} %get-tuple-element.47), channel_id=1, source_target_pairs={{0,1},{1,0},{2,3},{3,2},{4,5},{5,4},{6,7},{7,6},{8,9},{9,8},{10,11... | collective-permute-start | bytes 1572872 | tf_op jit(solution)/shard_map/ppermute | solution.py:551
  86.1 1.2 copy-start
  87.4 6.6 %collective-permute-start.1 = (bf16[256,256]{1,0:T(8,128)(2,1)S(1)}, bf16[256,256]{1,0:T(8,128)(2,1)S(1)}, u32[]{:S(2)}, u32[]{:S(2)}) collective-permute-start(bf16[256,256]{1,0:T(8,128)(2,1)S(1)} %get-tuple-element.49), channel_id=1, source_target_pairs={{0,2},{1,3},{2,4},{3,5},{4,6},{5,7},{6,0},{7,1},{8,10},{9,11},{10,... | collective-permute-start | bytes 393224 | tf_op jit(solution)/shard_map/ppermute | solution.py:556
  87.8 7.9 %collective-permute-start.2 = (bf16[256,256]{1,0:T(8,128)(2,1)S(1)}, bf16[256,256]{1,0:T(8,128)(2,1)S(1)}, u32[]{:S(2)}, u32[]{:S(2)}) collective-permute-start(bf16[256,256]{1,0:T(8,128)(2,1)S(1)} %get-tuple-element.50), channel_id=1, source_target_pairs={{0,4},{1,5},{2,6},{3,7},{4,0},{5,1},{6,2},{7,3},{8,12},{9,13},{10,... | collective-permute-start | bytes 393224 | tf_op jit(solution)/shard_map/ppermute | solution.py:556
  89.6 7.0 %collective-permute-start.3 = (bf16[256,256]{1,0:T(8,128)(2,1)S(1)}, bf16[256,256]{1,0:T(8,128)(2,1)S(1)}, u32[]{:S(2)}, u32[]{:S(2)}) collective-permute-start(bf16[256,256]{1,0:T(8,128)(2,1)S(1)} %get-tuple-element.51), channel_id=1, source_target_pairs={{0,6},{1,7},{2,0},{3,1},{4,2},{5,3},{6,4},{7,5},{8,14},{9,15},{10,... | collective-permute-start | bytes 393224 | tf_op jit(solution)/shard_map/ppermute | solution.py:556
  98.7 11.1 %collective-permute-start.4 = (bf16[1024,256]{1,0:T(8,128)(2,1)S(1)}, bf16[1024,256]{1,0:T(8,128)(2,1)S(1)}, u32[]{:S(2)}, u32[]{:S(2)}) collective-permute-start(bf16[1024,256]{1,0:T(8,128)(2,1)S(1)} %get-tuple-element.55), channel_id=1, source_target_pairs={{0,1},{1,0},{2,3},{3,2},{4,5},{5,4},{6,7},{7,6},{8,9},{9,8},{10,11... | collective-permute-start | bytes 1572872 | tf_op jit(solution)/shard_map/ppermute | solution.py:551
  102.6 16.3 %all-to-all-start.4 = ((bf16[32,16,128]{2,1,0:T(8,128)(2,1)}), bf16[32,16,128]{2,1,0:T(8,128)(2,1)S(1)}, u32[]{:S(2)}, u32[]{:S(2)}) async-start(bf16[32,16,128]{2,1,0:T(8,128)(2,1)} %shard_map.137), calls=%async_computation.4 | async-start | bytes 262144 | tf_op jit(solution)/shard_map/all_to_all | solution.py:546
  109.9 9.7 %collective-permute-start.5 = (bf16[256,256]{1,0:T(8,128)(2,1)S(1)}, bf16[256,256]{1,0:T(8,128)(2,1)S(1)}, u32[]{:S(2)}, u32[]{:S(2)}) collective-permute-start(bf16[256,256]{1,0:T(8,128)(2,1)S(1)} %get-tuple-element.57), channel_id=1, source_target_pairs={{0,2},{1,3},{2,4},{3,5},{4,6},{5,7},{6,0},{7,1},{8,10},{9,11},{10,... | collective-permute-start | bytes 393224 | tf_op jit(solution)/shard_map/ppermute | solution.py:556
  110.1 9.6 %collective-permute-start.6 = (bf16[256,256]{1,0:T(8,128)(2,1)S(1)}, bf16[256,256]{1,0:T(8,128)(2,1)S(1)}, u32[]{:S(2)}, u32[]{:S(2)}) collective-permute-start(bf16[256,256]{1,0:T(8,128)(2,1)S(1)} %get-tuple-element.58), channel_id=1, source_target_pairs={{0,4},{1,5},{2,6},{3,7},{4,0},{5,1},{6,2},{7,3},{8,12},{9,13},{10,... | collective-permute-start | bytes 393224 | tf_op jit(solution)/shard_map/ppermute | solution.py:556
  113.3 6.3 %collective-permute-start.7 = (bf16[256,256]{1,0:T(8,128)(2,1)S(1)}, bf16[256,256]{1,0:T(8,128)(2,1)S(1)}, u32[]{:S(2)}, u32[]{:S(2)}) collective-permute-start(bf16[256,256]{1,0:T(8,128)(2,1)S(1)} %get-tuple-element.59), channel_id=1, source_target_pairs={{0,6},{1,7},{2,0},{3,1},{4,2},{5,3},{6,4},{7,5},{8,14},{9,15},{10,... | collective-permute-start | bytes 393224 | tf_op jit(solution)/shard_map/ppermute | solution.py:556
  119.7 14.2 %collective-permute-start.10 = (bf16[256,256]{1,0:T(8,128)(2,1)S(1)}, bf16[256,256]{1,0:T(8,128)(2,1)S(1)}, u32[]{:S(2)}, u32[]{:S(2)}) collective-permute-start(bf16[256,256]{1,0:T(8,128)(2,1)S(1)} %add_convert_fusion.refs_0_), channel_id=1, source_target_pairs={{0,6},{1,7},{2,0},{3,1},{4,2},{5,3},{6,4},{7,5},{8,14},{9,15},{10,... | collective-permute-start | bytes 393224 | tf_op jit(solution)/shard_map/ppermute | solution.py:556
  122.6 11.4 %collective-permute-start.9 = (bf16[256,256]{1,0:T(8,128)(2,1)S(1)}, bf16[256,256]{1,0:T(8,128)(2,1)S(1)}, u32[]{:S(2)}, u32[]{:S(2)}) collective-permute-start(bf16[256,256]{1,0:T(8,128)(2,1)S(1)} %add_convert_fusion.refs_0_), channel_id=1, source_target_pairs={{0,4},{1,5},{2,6},{3,7},{4,0},{5,1},{6,2},{7,3},{8,12},{9,13},{10,... | collective-permute-start | bytes 393224 | tf_op jit(solution)/shard_map/ppermute | solution.py:556
  122.6 11.8 %collective-permute-start.8 = (bf16[256,256]{1,0:T(8,128)(2,1)S(1)}, bf16[256,256]{1,0:T(8,128)(2,1)S(1)}, u32[]{:S(2)}, u32[]{:S(2)}) collective-permute-start(bf16[256,256]{1,0:T(8,128)(2,1)S(1)} %add_convert_fusion.refs_0_), channel_id=1, source_target_pairs={{0,2},{1,3},{2,4},{3,5},{4,6},{5,7},{6,0},{7,1},{8,10},{9,11},{10,... | collective-permute-start | bytes 393224 | tf_op jit(solution)/shard_map/ppermute | solution.py:556
  123.2 18.4 %all-to-all-start.5 = ((bf16[32,16,128]{2,1,0:T(8,128)(2,1)}), bf16[32,16,128]{2,1,0:T(8,128)(2,1)S(1)}, u32[]{:S(2)}, u32[]{:S(2)}) async-start(bf16[32,16,128]{2,1,0:T(8,128)(2,1)} %shard_map.138), calls=%async_computation.5 | async-start | bytes 262144 | tf_op jit(solution)/shard_map/all_to_all | solution.py:546
  132.5 2.4 %collective-permute-start.11 = (bf16[256,256]{1,0:T(8,128)(2,1)S(1)}, bf16[256,256]{1,0:T(8,128)(2,1)S(1)}, u32[]{:S(2)}, u32[]{:S(2)}) collective-permute-start(bf16[256,256]{1,0:T(8,128)(2,1)S(1)} %add_convert_fusion.refs_0_), channel_id=1, source_target_pairs={{0,1},{1,0},{2,3},{3,2},{4,5},{5,4},{6,7},{7,6},{8,9},{9,8},{10,11... | collective-permute-start | bytes 393224 | tf_op jit(solution)/shard_map/ppermute | solution.py:551
  133.9 7.8 %collective-permute-start.14 = (bf16[256,256]{1,0:T(8,128)(2,1)S(1)}, bf16[256,256]{1,0:T(8,128)(2,1)S(1)}, u32[]{:S(2)}, u32[]{:S(2)}) collective-permute-start(bf16[256,256]{1,0:T(8,128)(2,1)S(1)} %collective-permute-done.10.refs_3_), channel_id=1, source_target_pairs={{0,1},{1,0},{2,3},{3,2},{4,5},{5,4},{6,7},{7,6},{8,9},{9,8},{10,11... | collective-permute-start | bytes 393224 | tf_op jit(solution)/shard_map/ppermute | solution.py:551
  134.0 7.6 %collective-permute-start.13 = (bf16[256,256]{1,0:T(8,128)(2,1)S(1)}, bf16[256,256]{1,0:T(8,128)(2,1)S(1)}, u32[]{:S(2)}, u32[]{:S(2)}) collective-permute-start(bf16[256,256]{1,0:T(8,128)(2,1)S(1)} %collective-permute-done.9.refs_2_), channel_id=1, source_target_pairs={{0,1},{1,0},{2,3},{3,2},{4,5},{5,4},{6,7},{7,6},{8,9},{9,8},{10,11... | collective-permute-start | bytes 393224 | tf_op jit(solution)/shard_map/ppermute | solution.py:551
  134.4 7.2 %collective-permute-start.12 = (bf16[256,256]{1,0:T(8,128)(2,1)S(1)}, bf16[256,256]{1,0:T(8,128)(2,1)S(1)}, u32[]{:S(2)}, u32[]{:S(2)}) collective-permute-start(bf16[256,256]{1,0:T(8,128)(2,1)S(1)} %collective-permute-done.8.refs_1_), channel_id=1, source_target_pairs={{0,1},{1,0},{2,3},{3,2},{4,5},{5,4},{6,7},{7,6},{8,9},{9,8},{10,11... | collective-permute-start | bytes 393224 | tf_op jit(solution)/shard_map/ppermute | solution.py:551
  141.7 7.3 %collective-permute-start.17 = (bf16[32,16,128]{2,1,0:T(8,128)(2,1)S(1)}, bf16[32,16,128]{2,1,0:T(8,128)(2,1)S(1)}, u32[]{:S(2)}, u32[]{:S(2)}) collective-permute-start(bf16[32,16,128]{2,1,0:T(8,128)(2,1)S(1)} %all-to-all-done.5.refs_0_), channel_id=1, source_target_pairs={{0,6},{1,7},{2,0},{3,1},{4,2},{5,3},{6,4},{7,5},{8,14},{9,15},{10,... | collective-permute-start | bytes 393224 | tf_op jit(solution)/shard_map/ppermute | solution.py:556
  143.7 6.1 %collective-permute-start.16 = (bf16[32,16,128]{2,1,0:T(8,128)(2,1)S(1)}, bf16[32,16,128]{2,1,0:T(8,128)(2,1)S(1)}, u32[]{:S(2)}, u32[]{:S(2)}) collective-permute-start(bf16[32,16,128]{2,1,0:T(8,128)(2,1)S(1)} %all-to-all-done.5.refs_0_), channel_id=1, source_target_pairs={{0,4},{1,5},{2,6},{3,7},{4,0},{5,1},{6,2},{7,3},{8,12},{9,13},{10,... | collective-permute-start | bytes 393224 | tf_op jit(solution)/shard_map/ppermute | solution.py:556
  145.5 7.5 %collective-permute-start.15 = (bf16[32,16,128]{2,1,0:T(8,128)(2,1)S(1)}, bf16[32,16,128]{2,1,0:T(8,128)(2,1)S(1)}, u32[]{:S(2)}, u32[]{:S(2)}) collective-permute-start(bf16[32,16,128]{2,1,0:T(8,128)(2,1)S(1)} %all-to-all-done.5.refs_0_), channel_id=1, source_target_pairs={{0,2},{1,3},{2,4},{3,5},{4,6},{5,7},{6,0},{7,1},{8,10},{9,11},{10,... | collective-permute-start | bytes 393224 | tf_op jit(solution)/shard_map/ppermute | solution.py:556
  145.5 11.2 %collective-permute-start.18 = (bf16[32,16,128]{2,1,0:T(8,128)(2,1)S(1)}, bf16[32,16,128]{2,1,0:T(8,128)(2,1)S(1)}, u32[]{:S(2)}, u32[]{:S(2)}) collective-permute-start(bf16[32,16,128]{2,1,0:T(8,128)(2,1)S(1)} %all-to-all-done.5.refs_0_), channel_id=1, source_target_pairs={{0,1},{1,0},{2,3},{3,2},{4,5},{5,4},{6,7},{7,6},{8,9},{9,8},{10,11... | collective-permute-start | bytes 393224 | tf_op jit(solution)/shard_map/ppermute | solution.py:551
  148.9 7.7 %collective-permute-start.21 = (bf16[32,16,128]{2,1,0:T(8,128)(2,1)S(1)}, bf16[32,16,128]{2,1,0:T(8,128)(2,1)S(1)}, u32[]{:S(2)}, u32[]{:S(2)}) collective-permute-start(bf16[32,16,128]{2,1,0:T(8,128)(2,1)S(1)} %collective-permute-done.17.refs_3_), channel_id=1, source_target_pairs={{0,1},{1,0},{2,3},{3,2},{4,5},{5,4},{6,7},{7,6},{8,9},{9,8},{10,11... | collective-permute-start | bytes 393224 | tf_op jit(solution)/shard_map/ppermute | solution.py:551
  149.8 6.9 %collective-permute-start.20 = (bf16[32,16,128]{2,1,0:T(8,128)(2,1)S(1)}, bf16[32,16,128]{2,1,0:T(8,128)(2,1)S(1)}, u32[]{:S(2)}, u32[]{:S(2)}) collective-permute-start(bf16[32,16,128]{2,1,0:T(8,128)(2,1)S(1)} %collective-permute-done.16.refs_2_), channel_id=1, source_target_pairs={{0,1},{1,0},{2,3},{3,2},{4,5},{5,4},{6,7},{7,6},{8,9},{9,8},{10,11... | collective-permute-start | bytes 393224 | tf_op jit(solution)/shard_map/ppermute | solution.py:551
  153.0 3.7 %collective-permute-start.19 = (bf16[32,16,128]{2,1,0:T(8,128)(2,1)S(1)}, bf16[32,16,128]{2,1,0:T(8,128)(2,1)S(1)}, u32[]{:S(2)}, u32[]{:S(2)}) collective-permute-start(bf16[32,16,128]{2,1,0:T(8,128)(2,1)S(1)} %collective-permute-done.15.refs_1_), channel_id=1, source_target_pairs={{0,1},{1,0},{2,3},{3,2},{4,5},{5,4},{6,7},{7,6},{8,9},{9,8},{10,11... | collective-permute-start | bytes 393224 | tf_op jit(solution)/shard_map/ppermute | solution.py:551

commit v4 on v3

--- a/solution.py
+++ b/solution.py
@@ -12,7 +12,6 @@
 bf16 = jnp.bfloat16
 i32 = jnp.int32
 FULL = 62
-MOST = 60
 EXACT = lax.Precision.HIGHEST
 VM = pl.BlockSpec(memory_space=pltpu.VMEM)
 SM = pl.BlockSpec(memory_space=pltpu.SMEM)
@@ -29,6 +28,14 @@
 
 def iota(shape, dim):
     return lax.broadcasted_iota(i32, shape, dim)
+
+
+def quotient(a, n):
+    return a >> (n.bit_length() - 1) if n & (n - 1) == 0 else a // n
+
+
+def remainder(a, n):
+    return a & (n - 1) if n & (n - 1) == 0 else a % n
 
 
 def where_bf16(mask, a):
@@ -85,16 +92,12 @@
     )(*args)
 
 
-def request_kernel(
-    len_ref, ids_hbm, out_ref, slot_ref, ids_ref, arrived, *, rows_own, cap
-):
-    copies = begin([(ids_hbm, ids_ref)], arrived)
+def request_kernel(len_ref, ids_ref, out_ref, slot_ref, *, rows_own, cap):
     users, block = ids_ref.shape
     shards, _, lanes = out_ref.shape
     shift = rows_own.bit_length() - 1
     earlier = where_bf16(iota((block, block), 0) < iota((block, block), 1), 1.0)
     place = iota((lanes, block), 0)
-    finish(copies)
     total = jnp.zeros((shards, lanes), f32)
     count = jnp.int32(0)
     slot_ref[...] = jnp.zeros_like(slot_ref)
@@ -116,31 +119,32 @@
 
 
 def answer_kernel(
-    wanted_ref, table_hbm, out_hbm, hot_ref, table_ref, out_ref, arrived, *, per
+    wanted_hbm, table_hbm, out_hbm, wanted_ref, table_ref, out_ref, arrived, *, per
 ):
-    copies = begin([(table_hbm, table_ref)], arrived)
     shards, _, lanes = wanted_ref.shape
-    slots = shards * per
+    copies = begin(((wanted_hbm, wanted_ref), (table_hbm, table_ref)), arrived)
+    parts = 4
+    group = shards // parts
+    slots = group * per
     rows = table_ref.shape[0]
+    repeat = where_bf16(quotient(iota((slots, group), 0), per) == iota((slots, group), 1), 1.0)
+    own = remainder(iota((slots, lanes), 0), per) == iota((slots, lanes), 1)
+    ones = jnp.ones((lanes, 128), bf16)
+    finish(copies[:1])
     wanted = jnp.where(iota((shards, lanes), 1) < per, wanted_ref[:, 0, :], 0)
-    high, low = halves(wanted)
-    repeat = where_bf16(iota((slots, shards), 0) // per == iota((slots, shards), 1), 1.0)
-    own = iota((slots, lanes), 0) % per == iota((slots, lanes), 1)
-    ones = jnp.ones((lanes, 128), bf16)
-    high = dot(where_bf16(own, dot(repeat, high.astype(bf16))), ones)
-    low = dot(where_bf16(own, dot(repeat, low.astype(bf16))), ones)
-    column = (16.0 * high + low).astype(i32) - 1
-    spot = iota((slots, 128), 1)
-    for j in range(rows // 128):
-        hot_ref[:, j * 128 : (j + 1) * 128] = where_bf16(column == spot + j * 128, 1.0)
-    finish(copies)
-    copies = []
-    part = slots // 4
-    for j in range(4):
-        at = slice(j * part, (j + 1) * part)
-        out_ref[at, :] = dot(hot_ref[at, :], table_ref[...]).astype(bf16)
-        copies += begin([(out_ref.at[at, :], out_hbm.at[at, :])], arrived, 1 + j)
-    finish(copies)
+    stores = []
+    for j in range(parts):
+        high, low = halves(wanted[j * group : (j + 1) * group, :])
+        high = dot(where_bf16(own, dot(repeat, high.astype(bf16))), ones)
+        low = dot(where_bf16(own, dot(repeat, low.astype(bf16))), ones)
+        column = (16.0 * high + low).astype(i32) - 1
+        hot = tiled_match(column, rows)
+        if j == 0:
+            finish(copies[1:])
+        at = slice(j * slots, (j + 1) * slots)
+        out_ref[at, :] = dot(hot, table_ref[...]).astype(bf16)
+        stores += begin([(out_ref.at[at, :], out_hbm.at[at, :])], arrived, 2 + j)
+    finish(stores)
 
 
 def quotient_kernel(
@@ -181,7 +185,7 @@
 
 def over_heads(columns, heads, width):
     n = columns.shape[0]
-    head_of = iota((n, width), 1) // (width // heads)
+    head_of = quotient(iota((n, width), 1), width // heads)
     wide = jnp.broadcast_to(columns[:, 0:1], (n, width))
     for h in range(1, heads):
         wide = jnp.where(head_of == h, jnp.broadcast_to(columns[:, h : h + 1], (n, width)), wide)
@@ -191,7 +195,7 @@
 def diagonal_heads(square, heads):
     width = square.shape[1]
     size = width // heads
-    head_of = iota((size, width), 1) // size
+    head_of = quotient(iota((size, width), 1), size)
     out = square[0:size, :]
     for h in range(1, heads):
         out = jnp.where(head_of == h, square[h * size : (h + 1) * size, :], out)
@@ -200,14 +204,14 @@
 
 def block_diagonal(state, heads):
     size, width = state.shape
-    head_of = iota((size, width), 1) // (width // heads)
+    head_of = quotient(iota((size, width), 1), width // heads)
     return jnp.concatenate([where_bf16(head_of == h, state) for h in range(heads)], axis=0)
 
 
 def project_kernel(
     at_ref,
     slot_hbm,
-    answered_ref,
+    answered_hbm,
     quot_hbm,
     wq_hbm,
     wk_hbm,
@@ -217,6 +221,7 @@
     rem_hbm,
     payload_hbm,
     slot_ref,
+    answered_ref,
     quot_ref,
     wq_ref,
     wk_ref,
@@ -239,6 +244,7 @@
     copies = begin(
         (
             (slot_hbm, slot_ref),
+            (answered_hbm, answered_ref),
             (quot_hbm, quot_ref),
             (wq_hbm, wq_ref),
             (wk_hbm, wk_ref),
@@ -250,16 +256,18 @@
     )
     finish(copies[:1])
     hot = [tiled_match(spread_column(slot_ref[u : u + 1, :]), slots) for u in range(users)]
-    finish(copies[1:])
-    copies = []
+    finish(copies[1:6])
+    waits, copies = copies[6:], []
     for u in range(users):
         at = slice(u * block, (u + 1) * block)
         rem_ref[at, :] = dot(hot[u], answered_ref[...]).astype(bf16)
-        copies += begin([(rem_ref.at[at, :], rem_hbm.at[at, :])], arrived, u)
+        copies += begin([(rem_ref.at[at, :], rem_hbm.at[at, :])], arrived, 8 + u)
         embedded = (quot_ref[at, :].astype(f32) * rem_ref[at, :].astype(f32)).astype(bf16)
         q = dot(embedded, wq_ref[...]).astype(bf16)
         k = dot(embedded, wk_ref[...]).astype(bf16)
         v = dot(embedded, wv_ref[...]).astype(bf16)
+        if u == 0:
+            finish(waits)
         wide = wide_ref[at, :]
         end = wide[block - 1 : block, :]
         ends.append(end)
@@ -282,7 +290,7 @@
     states_ref[1, users * size :, :] = tail
     which = [jnp.where(peer > me, 0, 1) for peer in range(peers)]
     pairs = [(states_ref.at[which[peer]], payload_hbm.at[peer]) for peer in range(peers)]
-    finish(copies + begin(pairs, arrived, users))
+    finish(copies + begin(pairs, arrived, 8 + users))
 
 
 def within_kernel(
@@ -302,7 +310,7 @@
     users, heads, block = decay_ref.shape
     width = quot_ref.shape[1]
     copies = []
-    head_of = iota((block, width), 1) // (width // heads)
+    head_of = quotient(iota((block, width), 1), width // heads)
     lower_tri = iota((block, block), 0) >= iota((block, block), 1)
     for u in range(users):
         at = slice(u * block, (u + 1) * block)
@@ -349,7 +357,7 @@
 
 def gradient_kernel(
     at_ref,
-    payload_ref,
+    payload_hbm,
     within_hbm,
     dmixed_hbm,
     wide_hbm,
@@ -365,6 +373,7 @@
     rem_send_hbm,
     keep_hbm,
     give_hbm,
+    payload_ref,
     within_ref,
     dmixed_ref,
     wide_ref,
@@ -389,6 +398,7 @@
     width = quot_ref.shape[1]
     copies = begin(
         (
+            (payload_hbm, payload_ref),
             (quot_hbm, quot_ref),
             (rem_hbm, rem_ref),
             (wq_hbm, wq_ref),
@@ -397,12 +407,16 @@
             (wide_hbm, wide_ref),
             (dmixed_hbm, dmixed_ref),
             (w_out_hbm, w_out_ref),
-            (within_hbm, within_ref),
             (slot_hbm, slot_ref),
             (ids_hbm, ids_ref),
         ),
         arrived,
     )
+    waits = []
+    for u in range(users):
+        at = slice(u * block, (u + 1) * block)
+        waits += begin([(within_hbm.at[:, at, :], within_ref.at[:, at, :])], arrived, 11 + u)
+    finish(copies[:1])
     peers = payload_ref.shape[0]
     size = width // heads
     slots = rem_send_ref.shape[0]
@@ -428,7 +442,7 @@
             linked = jnp.exp(ends[peer]) * leaving + part
             leaving = jnp.where(peer > me, linked, leaving)
         carried.append((block_diagonal(entering, heads), block_diagonal(leaving, heads)))
-    finish(copies)
+    finish(copies[1:])
     copies = []
     rem_terms, quot_terms = [], []
     for u in range(users):
@@ -440,11 +454,12 @@
         v = dot(embedded, wv_ref[...]).astype(bf16)
         dmixed = dmixed_ref[at, :]
         wide = wide_ref[at, :]
+        finish(waits[u : u + 1])
         growth = scale * jnp.exp(wide)
         falloff = scale * jnp.exp(wide[block - 1 : block, :] - wide)
         mixed = (within_ref[0, at, :] + growth * dot(q, entering)).astype(bf16)
         out_ref[u] = dot(mixed, w_out_ref[...]).astype(bf16)
-        copies += begin([(out_ref.at[u], out_hbm.at[u])], arrived, u)
+        copies += begin([(out_ref.at[u], out_hbm.at[u])], arrived, 11 + users + u)
         dq = (within_ref[1, at, :] + growth * dot(dmixed, entering, NT)).astype(bf16)
         dk = (within_ref[2, at, :] + falloff * dot(v, leaving, NT)).astype(bf16)
         dv = (within_ref[3, at, :] + falloff * dot(k, leaving)).astype(bf16)
@@ -456,14 +471,22 @@
     slot = jnp.concatenate([slot_ref[u : u + 1, :] for u in range(users)], axis=1)
     ids = jnp.concatenate([ids_ref[u : u + 1, :] for u in range(users)], axis=1)
     spot = iota((block, users * block), 0)
+    n = 11 + 2 * users
     for j in range(slots // block):
         hot = where_bf16(spot + j * block == slot, 1.0)
-        rem_send_ref[j * block : (j + 1) * block, :] = dot(hot, rem_terms).astype(bf16)
-    copies += begin([(rem_send_ref, rem_send_hbm)], arrived, users)
-    sum_half(ids, quot_terms, 1 - me % 2, give_ref)
-    copies += begin([(give_ref, give_hbm)], arrived, users + 1)
-    sum_half(ids, quot_terms, me % 2, keep_ref)
-    copies += begin([(keep_ref, keep_hbm)], arrived, users + 2)
+        at = slice(j * block, (j + 1) * block)
+        rem_send_ref[at, :] = dot(hot, rem_terms).astype(bf16)
+        copies += begin([(rem_send_ref.at[at, :], rem_send_hbm.at[at, :])], arrived, n + j)
+    n += slots // block
+    for ref, hbm, owner in ((give_ref, give_hbm, 1 - me % 2), (keep_ref, keep_hbm, me % 2)):
+        half = ref.shape[0]
+        near = ids - owner * half
+        for j in range(half // block):
+            hot = where_bf16(spot + j * block == near, 1.0)
+            at = slice(j * block, (j + 1) * block)
+            ref[at, :] = dot(hot, quot_terms).astype(bf16)
+            copies += begin([(ref.at[at, :], hbm.at[at, :])], arrived, n)
+            n += 1
     finish(copies)
 
 
@@ -472,8 +495,8 @@
     slots = shards * per
     wanted = jnp.where(iota((shards, lanes), 1) < per, wanted_ref[:, 0, :], 0)
     high, low = halves(wanted)
-    tile = where_bf16(iota((lanes, slots), 1) % per == iota((lanes, slots), 0), 1.0)
-    own = iota((shards, slots), 1) // per == iota((shards, slots), 0)
+    tile = where_bf16(remainder(iota((lanes, slots), 1), per) == iota((lanes, slots), 0), 1.0)
+    own = quotient(iota((shards, slots), 1), per) == iota((shards, slots), 0)
     high = jnp.sum(jnp.where(own, dot(high.astype(bf16), tile), 0.0), axis=0, keepdims=True)
     low = jnp.sum(jnp.where(own, dot(low.astype(bf16), tile), 0.0), axis=0, keepdims=True)
     row = (16.0 * high + low).astype(i32) - 1
@@ -486,7 +509,7 @@
     rows = out_refs[0].shape[0]
     for d, out_ref in enumerate(out_refs):
         base = pl.multiple_of(lax.rem(at_ref[0] // 2 + d, chips) * rows, rows)
-        both = keep_ref[pl.ds(base, rows), :] + got_ref[pl.ds(base, rows), :].astype(f32)
+        both = keep_ref[pl.ds(base, rows), :].astype(f32) + got_ref[pl.ds(base, rows), :].astype(f32)
         out_ref[...] = both.astype(bf16)
 
 
@@ -556,22 +579,19 @@
     return lax.ppermute(array, "hist", [(i, (i + 2 * steps) % peers) for i in range(peers)])
 
 
-def reduced(at, keep, give):
+def split(at, keep, give):
     chips = lax.axis_size("hist") // 2
-    rows = keep.shape[0] // chips
-    chunks = call(
-        split_kernel,
-        [((rows, keep.shape[1]), bf16)] * chips,
-        (at, keep, to_core(give)),
-        [SM, VM, VM],
-    )
-    return [chunks[0]] + [to_chip(chunks[d], d) for d in range(1, chips)]
-
-
-def everywhere(chunk):
+    outs = [((keep.shape[0] // chips, keep.shape[1]), bf16)] * chips
+    return call(split_kernel, outs, (at, keep, to_core(give)), [SM, VM, VM])
+
+
+def shared(chunks):
+    return [chunks[0]] + [to_chip(chunks[d], d) for d in range(1, len(chunks))]
+
+
+def along_chips(chunk):
     chips = lax.axis_size("hist") // 2
-    mine = [chunk] + [to_chip(chunk, d) for d in range(1, chips)]
-    return mine + [to_core(c) for c in mine]
+    return [chunk] + [to_chip(chunk, d) for d in range(1, chips)]
 
 
 def placed(at, wanted, chunks, rows, width, per, total):
@@ -615,8 +635,7 @@
         functools.partial(request_kernel, rows_own=rows_own, cap=cap),
         [((shards, 1, lanes), i32), ((8, block), i32)],
         (lengths, rem_ids),
-        [SM, HB],
-        [pltpu.VMEM((users, block), i32), dma(1)],
+        [SM, VM],
         limit=FULL,
     )
     wanted = exchange(requests, "user")
@@ -635,12 +654,12 @@
         functools.partial(answer_kernel, per=per),
         [((slots, width), bf16)],
         (wanted, rem_table),
-        [VM, HB],
+        [HB, HB],
         [
-            pltpu.VMEM((slots, rows_own), bf16),
+            pltpu.VMEM((shards, 1, lanes), i32),
             pltpu.VMEM((rows_own, width), bf16),
             pltpu.VMEM((slots, width), bf16),
-            dma(5),
+            dma(6),
         ],
         [HB],
         FULL,
@@ -652,13 +671,13 @@
         functools.partial(project_kernel, users=users, heads=heads),
         [((users * block, width), bf16), ((peers, users * size + 16, width), bf16)],
         (at, slot, answered, quot_emb, w_query, w_key, w_value, wide, dmixed),
-        [SM, HB, VM] + [HB] * 6,
-        [pltpu.VMEM((8, block), i32), events]
+        [SM] + [HB] * 8,
+        [pltpu.VMEM((8, block), i32), pltpu.VMEM((slots, width), bf16), events]
         + [square] * 3
         + [pltpu.VMEM((users * block, width), f32), events, events]
         + [pltpu.VMEM((2, users * size + 16, width), bf16), dma(8 + users + peers)],
         [HB, HB],
-        MOST,
+        FULL,
     )
     states = exchange(payload, "hist")
     parts = (4, users * block, width)
@@ -675,25 +694,25 @@
         [
             ((users, block, width), bf16),
             ((slots, width), bf16),
-            ((rows_all // 2, width), f32),
+            ((rows_all // 2, width), bf16),
             ((rows_all // 2, width), bf16),
         ],
         (at, states, within, dmixed, wide, rem_emb, quot_emb, slot, quot_ids)
         + (w_query, w_key, w_value, w_out),
-        [SM, VM] + [HB] * 11,
-        [pltpu.VMEM(parts, f32), events]
+        [SM] + [HB] * 12,
+        [pltpu.VMEM(payload.shape, bf16), pltpu.VMEM(parts, f32), events]
         + [pltpu.VMEM((users * block, width), f32), events, events]
         + [pltpu.VMEM((8, block), i32), pltpu.VMEM((users, block), i32)]
         + [square] * 4
         + [pltpu.VMEM((users, block, width), bf16), pltpu.VMEM((slots, width), bf16)]
-        + [pltpu.VMEM((rows_all // 2, width), f32), pltpu.VMEM((rows_all // 2, width), bf16)]
-        + [dma(12)],
+        + [pltpu.VMEM((rows_all // 2, width), bf16)] * 2
+        + [dma(11 + 2 * users + (slots + rows_all) // block)],
         [HB] * 4,
-        MOST,
+        FULL,
     )
     rem_back = exchange(rem_send.reshape(shards, per, width), "user").reshape(slots, width)
     tiles = (shards, rows_all // peers * width // shards // 128, 128)
-    (quot_tiles,) = call(total_kernel, [(tiles, bf16)], reduced(at, keep, give))
+    (quot_tiles,) = call(total_kernel, [(tiles, bf16)], shared(split(at, keep, give)))
     rem_back, quot_tiles = lax.optimization_barrier((rem_back, quot_tiles))
     quot_back = exchange(quot_tiles, "user")
     keep, give = call(
@@ -702,15 +721,19 @@
         (at, wanted, rem_back),
         [SM, VM, VM],
     )
-    rem_sum = sum(c.astype(f32) for c in reduced(at, keep, give)).astype(bf16)
+    chunks = split(at, keep, give)
     (quot_tiles,) = call(repeat_kernel, [(tiles, bf16)], (quot_back,))
-    quot_tiles, rem_sum = lax.optimization_barrier((quot_tiles, rem_sum))
+    quot_tiles, *_ = lax.optimization_barrier((quot_tiles, *chunks))
     quot_tiles = exchange(quot_tiles, "user")
-    rem_chunks = everywhere(rem_sum)
-    quot_tiles, *rem_chunks = lax.optimization_barrier((quot_tiles, *rem_chunks))
+    rem_sum = sum(c.astype(f32) for c in shared(chunks)).astype(bf16)
+    rem_mine = along_chips(rem_sum)
+    quot_tiles, *rem_mine = lax.optimization_barrier((quot_tiles, *rem_mine))
     total = float(users * shards * block * peers)
+    rem_chunks = rem_mine + [to_core(c) for c in rem_mine]
     rem_grad = placed(at, wanted, rem_chunks, rows_own, width, per, total)
-    quot_grad = placed(at, wanted, everywhere(quot_tiles), rows_all, width, per, total)
+    quot_mine = along_chips(quot_tiles)
+    quot_chunks = quot_mine + [to_core(c) for c in quot_mine]
+    quot_grad = placed(at, wanted, quot_chunks, rows_all, width, per, total)
     return (output, quot_grad, rem_grad)
 
 

time: 159 us -> 149 us (0.937)
  starting transfers between devices: 65.2 us -> 54.9 us
  waiting for transfers between devices: 34.5 us -> 38.7 us
  Pallas kernels: 34 us -> 30.5 us
    ppermute x12, waiting for transfers between devices: 6.32 us -> 11.7 us  [to_chip(): lax.ppermute(array, 'hist', [(i, (i + 2 * steps) % peers) for i in range(...]
    all_to_all x5, starting transfers between devices: 34.8 us -> 30.1 us  [exchange(): return lax.all_to_all(array, axis, split_axis=0, concat_axis=0, tiled=True)]
    pallas_call x13, Pallas kernels: 34 us -> 30.5 us  [call(): pl.pallas_call(kernel, out_shape=tuple((jax.ShapeDtypeStruct(s, d) for s,...]
    ppermute x10, starting transfers between devices: 16.8 us -> 13.4 us  [to_core(): return lax.ppermute(array, 'hist', [(i, i ^ 1) for i in range(peers)])]
    ppermute x12, starting transfers between devices: 13.6 us -> 11.4 us  [to_chip(): lax.ppermute(array, 'hist', [(i, (i + 2 * steps) % peers) for i in range(...]
  transfers between devices with their start and end apart: 27 -> 27, of which waited for: 9 -> 11; matrix products, arithmetic and copies ran while one was open for 0% -> 0% of each run, Pallas kernels for 8% -> 8%
where the time goes in v4:
time: 149 us; the launch traced here: 148 us
  starting transfers between devices  54.9 us (37%)
  waiting for transfers between devices  38.7 us (26%)
  Pallas kernels  30.5 us (20%)
  blocking collectives  20.5 us (14%)
  local copies, waits for them, and re-layouts  2.65 us (2%)
    pallas_call x13, Pallas kernels, call(): pl.pallas_call(kernel, out_shape=tuple((jax.ShapeDtypeStruct(s, d) for s,...  30.5 us
    all_to_all x5, starting transfers between devices, exchange(): return lax.all_to_all(array, axis, split_axis=0, concat_axis=0, tiled=True)  30.1 us
    all_to_all x5, waiting for transfers between devices, exchange(): return lax.all_to_all(array, axis, split_axis=0, concat_axis=0, tiled=True)  25.3 us
    all_to_all x1, blocking collectives, exchange(): return lax.all_to_all(array, axis, split_axis=0, concat_axis=0, tiled=True)  20.5 us
    ppermute x10, starting transfers between devices, to_core(): return lax.ppermute(array, 'hist', [(i, i ^ 1) for i in range(peers)])  13.4 us
    ppermute x12, waiting for transfers between devices, to_chip(): lax.ppermute(array, 'hist', [(i, (i + 2 * steps) % peers) for i in range(...  11.7 us
    ppermute x12, starting transfers between devices, to_chip(): lax.ppermute(array, 'hist', [(i, (i + 2 * steps) % peers) for i in range(...  11.4 us
  transfers between devices with their start and end apart: 27, of which 11 were waited for; matrix products, arithmetic and copies ran while one was open for 0% of the time, Pallas kernels for 8%

profile of v4, /device:TPU:1, one launch (start us, length us, event | category | flops | bytes accessed | tf_op | source)
XLA Modules:
  0.0 148.5 jit_solution(5470350032231019932)
XLA Ops:
  0.6 1.9 %shard_map.130 = (s32[32,1,128]{2,1,0:T(1,128)}, s32[8,256]{1,0:T(8,128)}) custom-call(s32[2]{0:T(128)} %len_ref.3, s32[2,256]{1,0:T(2,128)} %ids_ref.2), custom_call_target="tpu_custom_call" | custom-call | tf_op jit(solution)/shard_map/pallas_call | solution.py:85
  2.5 20.5 %all_to_all.30.wanted_hbm.wanted_ref = s32[32,1,128]{2,1,0:T(1,128)} all-to-all(s32[32,1,128]{2,1,0:T(1,128)} %get-tuple-element.33), channel_id=1, replica_groups=mesh['user'=32,'hist'=8] {'user'}, dimensions={0} | all-to-all | bytes 32768 | tf_op jit(solution)/shard_map/all_to_all | solution.py:569
  23.1 4.0 %shard_map.131 = bf16[1024,256]{1,0:T(8,128)(2,1)} custom-call(s32[32,1,128]{2,1,0:T(1,128)} %all_to_all.30.wanted_hbm.wanted_ref, bf16[2048,256]{1,0:T(8,128)(2,1)} %table_hbm.1), custom_call_target="tpu_custom_call" | custom-call | tf_op jit(solution)/shard_map/pallas_call | solution.py:85
  27.1 3.9 %all-to-all-start.1 = ((bf16[32,32,256]{2,1,0:T(8,128)(2,1)}), bf16[32,32,256]{2,1,0:T(8,128)(2,1)S(1)}, u32[]{:S(2)}, u32[]{:S(2)}) async-start(bf16[32,32,256]{2,1,0:T(8,128)(2,1)} %bitcast.7), calls=%async_computation.1 | async-start | bytes 1048576 | tf_op jit(solution)/shard_map/all_to_all | solution.py:569
  31.0 3.7 %shard_map.132 = (bf16[512,256]{1,0:T(8,128)(2,1)}, bf16[512,256]{1,0:T(8,128)(2,1)}, f32[512,256]{1,0:T(8,128)}) custom-call(s32[2]{0:T(128)} %len_ref.3, s32[1]{0:T(128)} %bitcast.at_ref, s32[2,256]{1,0:T(2,128)} %ids_hbm.1, bf16[2048,256]{1,0:T(8,128)(2,1)} %table_ref.1, bf16[2,256,256]{2,1,0:T(8,128)(2,1)} %cot_ref.1, f32[2,4,256]{2,1,0:T(4,128)} %decay_ref.3, ...), custom_call_target="tpu_custom_call" | custom-call | tf_op jit(solution)/shard_map/pallas_call | solution.py:85
  34.7 9.0 %all-to-all-done.1 = bf16[32,32,256]{2,1,0:T(8,128)(2,1)S(1)} async-done(((bf16[32,32,256]{2,1,0:T(8,128)(2,1)}), bf16[32,32,256]{2,1,0:T(8,128)(2,1)S(1)}, u32[]{:S(2)}, u32[]{:S(2)}) %all-to-all-start.1) | async-done | bytes 524320 | tf_op jit(solution)/shard_map/all_to_all | solution.py:569
  43.8 0.8 copy-done.3
  44.6 3.9 %shard_map.133 = (bf16[512,256]{1,0:T(8,128)(2,1)}, bf16[8,144,256]{2,1,0:T(8,128)(2,1)}) custom-call(s32[1]{0:T(128)} %bitcast.at_ref, s32[8,256]{1,0:T(8,128)} %get-tuple-element.32.slot_hbm, bf16[1024,256]{1,0:T(8,128)(2,1)} %bitcast.6, bf16[512,256]{1,0:T(8,128)(2,1)} %get-tuple-element.34.quot_hbm.quot_ref, bf16[256,256]{1,0:T(8,128)(2,1)} %wq_hbm.3, ...), custom_call_target="tpu_custom_call" | custom-call | tf_op jit(solution)/shard_map/pallas_call | solution.py:85
  48.4 9.5 %all-to-all-start.2 = ((bf16[8,144,256]{2,1,0:T(8,128)(2,1)}), bf16[8,144,256]{2,1,0:T(8,128)(2,1)S(1)}, u32[]{:S(2)}, u32[]{:S(2)}) async-start(bf16[8,144,256]{2,1,0:T(8,128)(2,1)} %get-tuple-element.37), calls=%async_computation.2 | async-start | bytes 1179648 | tf_op jit(solution)/shard_map/all_to_all | solution.py:569
  57.9 5.7 %shard_map.134.within_hbm = f32[4,512,256]{2,1,0:T(8,128)} custom-call(bf16[512,256]{1,0:T(8,128)(2,1)} %get-tuple-element.34.quot_hbm.quot_ref, bf16[512,256]{1,0:T(8,128)(2,1)} %get-tuple-element.38.rem_ref.rem_hbm, bf16[512,256]{1,0:T(8,128)(2,1)} %get-tuple-element.36.dmixed_hbm.dmixed_ref, f32[2,4,256]{2,1,0:T(4,128)} %decay_ref.3, ...), custom_call_target="tpu_custom_call" | custom-call | tf_op jit(solution)/shard_map/pallas_call | solution.py:85
  63.6 4.5 %all-to-all-done.2.payload_hbm = bf16[8,144,256]{2,1,0:T(8,128)(2,1)S(1)} async-done(((bf16[8,144,256]{2,1,0:T(8,128)(2,1)}), bf16[8,144,256]{2,1,0:T(8,128)(2,1)S(1)}, u32[]{:S(2)}, u32[]{:S(2)}) %all-to-all-start.2) | async-done | bytes 589856 | tf_op jit(solution)/shard_map/all_to_all | solution.py:569
  68.1 0.8 copy-done.2
  68.9 5.3 %shard_map.135 = (bf16[2,256,256]{2,1,0:T(8,128)(2,1)}, bf16[1024,256]{1,0:T(8,128)(2,1)}, bf16[1024,256]{1,0:T(8,128)(2,1)}, bf16[1024,256]{1,0:T(8,128)(2,1)}) custom-call(s32[1]{0:T(128)} %bitcast.at_ref, bf16[8,144,256]{2,1,0:T(8,128)(2,1)} %copy-done.2, f32[4,512,256]{2,1,0:T(8,128)} %shard_map.134.within_hbm, ...), custom_call_target="tpu_custom_call" | custom-call | tf_op jit(solution)/shard_map/pallas_call | solution.py:85
  74.2 5.2 %all-to-all-start.3 = ((bf16[32,32,256]{2,1,0:T(8,128)(2,1)}), bf16[32,32,256]{2,1,0:T(8,128)(2,1)S(1)}, u32[]{:S(2)}, u32[]{:S(2)}) async-start(bf16[32,32,256]{2,1,0:T(8,128)(2,1)} %bitcast.8), calls=%async_computation.3 | async-start | bytes 1048576 | tf_op jit(solution)/shard_map/all_to_all | solution.py:569
  79.5 1.2 collective-permute-start
  80.7 1.7 %collective-permute-done.got_ref = bf16[1024,256]{1,0:T(8,128)(2,1)S(1)} collective-permute-done((bf16[1024,256]{1,0:T(8,128)(2,1)}, bf16[1024,256]{1,0:T(8,128)(2,1)S(1)}, u32[]{:S(2)}, u32[]{:S(2)}) %collective-permute-start) | collective-permute-done | bytes 524320 | tf_op jit(solution)/shard_map/ppermute | solution.py:574
  82.4 1.0 copy-done
  83.5 0.1 shard_map.136
  83.6 0.4 collective-permute-start.1
  84.0 1.8 %collective-permute-start.2 = (bf16[256,256]{1,0:T(8,128)(2,1)S(1)}, bf16[256,256]{1,0:T(8,128)(2,1)S(1)}, u32[]{:S(2)}, u32[]{:S(2)}) collective-permute-start(bf16[256,256]{1,0:T(8,128)(2,1)S(1)} %get-tuple-element.45), channel_id=1, source_target_pairs={{0,4},{1,5},{2,6},{3,7},{4,0},{5,1},{6,2},{7,3},{8,12},{9,13},{10,... | collective-permute-start | bytes 393224 | tf_op jit(solution)/shard_map/ppermute | solution.py:579
  85.8 0.7 collective-permute-start.3
  86.5 3.7 %collective-permute-done.1.refs_1_ = bf16[256,256]{1,0:T(8,128)(2,1)S(1)} collective-permute-done((bf16[256,256]{1,0:T(8,128)(2,1)S(1)}, bf16[256,256]{1,0:T(8,128)(2,1)S(1)}, u32[]{:S(2)}, u32[]{:S(2)}) %collective-permute-start.1) | collective-permute-done | bytes 131104 | tf_op jit(solution)/shard_map/ppermute | solution.py:579
  90.2 1.6 %collective-permute-done.2.refs_2_ = bf16[256,256]{1,0:T(8,128)(2,1)S(1)} collective-permute-done((bf16[256,256]{1,0:T(8,128)(2,1)S(1)}, bf16[256,256]{1,0:T(8,128)(2,1)S(1)}, u32[]{:S(2)}, u32[]{:S(2)}) %collective-permute-start.2) | collective-permute-done | bytes 131104 | tf_op jit(solution)/shard_map/ppermute | solution.py:579
  91.9 0.9 collective-permute-done.3.refs_3_
  92.8 0.7 shard_map.137
  93.5 0.0 all-to-all-done.3
  93.5 1.4 shard_map.139
  94.9 4.1 %collective-permute-start.4 = (bf16[1024,256]{1,0:T(8,128)(2,1)S(1)}, bf16[1024,256]{1,0:T(8,128)(2,1)S(1)}, u32[]{:S(2)}, u32[]{:S(2)}) collective-permute-start(bf16[1024,256]{1,0:T(8,128)(2,1)S(1)} %get-tuple-element.50), channel_id=1, source_target_pairs={{0,1},{1,0},{2,3},{3,2},{4,5},{5,4},{6,7},{7,6},{8,9},{9,8},{10,11... | collective-permute-start | bytes 1572872 | tf_op jit(solution)/shard_map/ppermute | solution.py:574
  99.0 7.0 %all-to-all-start.4 = ((bf16[32,16,128]{2,1,0:T(8,128)(2,1)}), bf16[32,16,128]{2,1,0:T(8,128)(2,1)S(1)}, u32[]{:S(2)}, u32[]{:S(2)}) async-start(bf16[32,16,128]{2,1,0:T(8,128)(2,1)} %shard_map.137), calls=%async_computation.4 | async-start | bytes 262144 | tf_op jit(solution)/shard_map/all_to_all | solution.py:569
  106.0 0.0 collective-permute-done.4.got_ref
  106.0 0.1 shard_map.140
  106.1 0.1 collective-permute-start.5
  106.2 3.3 %collective-permute-start.6 = (bf16[256,256]{1,0:T(8,128)(2,1)S(1)}, bf16[256,256]{1,0:T(8,128)(2,1)S(1)}, u32[]{:S(2)}, u32[]{:S(2)}) collective-permute-start(bf16[256,256]{1,0:T(8,128)(2,1)S(1)} %get-tuple-element.53), channel_id=1, source_target_pairs={{0,4},{1,5},{2,6},{3,7},{4,0},{5,1},{6,2},{7,3},{8,12},{9,13},{10,... | collective-permute-start | bytes 393224 | tf_op jit(solution)/shard_map/ppermute | solution.py:579
  109.5 5.6 %all-to-all-done.4.tiles_ref = bf16[32,16,128]{2,1,0:T(8,128)(2,1)S(1)} async-done(((bf16[32,16,128]{2,1,0:T(8,128)(2,1)}), bf16[32,16,128]{2,1,0:T(8,128)(2,1)S(1)}, u32[]{:S(2)}, u32[]{:S(2)}) %all-to-all-start.4) | async-done | bytes 131104 | tf_op jit(solution)/shard_map/all_to_all | solution.py:569
  115.1 0.7 shard_map.138
  115.8 4.5 %all-to-all-start.5 = ((bf16[32,16,128]{2,1,0:T(8,128)(2,1)}), bf16[32,16,128]{2,1,0:T(8,128)(2,1)S(1)}, u32[]{:S(2)}, u32[]{:S(2)}) async-start(bf16[32,16,128]{2,1,0:T(8,128)(2,1)} %shard_map.138), calls=%async_computation.5 | async-start | bytes 262144 | tf_op jit(solution)/shard_map/all_to_all | solution.py:569
  120.4 0.0 collective-permute-done.6
  120.4 0.0 collective-permute-done.7
  120.4 0.1 add_convert_fusion.refs_0_
  120.5 2.2 %collective-permute-start.10 = (bf16[256,256]{1,0:T(8,128)(2,1)S(1)}, bf16[256,256]{1,0:T(8,128)(2,1)S(1)}, u32[]{:S(2)}, u32[]{:S(2)}) collective-permute-start(bf16[256,256]{1,0:T(8,128)(2,1)S(1)} %add_convert_fusion.refs_0_), channel_id=1, source_target_pairs={{0,6},{1,7},{2,0},{3,1},{4,2},{5,3},{6,4},{7,5},{8,14},{9,15},{10,... | collective-permute-start | bytes 393224 | tf_op jit(solution)/shard_map/ppermute | solution.py:579
  122.7 0.2 collective-permute-start.9
  122.9 0.5 collective-permute-start.8
  123.4 6.1 %all-to-all-done.5.refs_0_ = bf16[32,16,128]{2,1,0:T(8,128)(2,1)S(1)} async-done(((bf16[32,16,128]{2,1,0:T(8,128)(2,1)}), bf16[32,16,128]{2,1,0:T(8,128)(2,1)S(1)}, u32[]{:S(2)}, u32[]{:S(2)}) %all-to-all-start.5) | async-done | bytes 131104 | tf_op jit(solution)/shard_map/all_to_all | solution.py:569
  129.5 0.0 collective-permute-done.10.refs_3_
  129.5 0.0 collective-permute-done.9.refs_2_
  129.5 1.7 %collective-permute-done.8.refs_1_ = bf16[256,256]{1,0:T(8,128)(2,1)S(1)} collective-permute-done((bf16[256,256]{1,0:T(8,128)(2,1)S(1)}, bf16[256,256]{1,0:T(8,128)(2,1)S(1)}, u32[]{:S(2)}, u32[]{:S(2)}) %collective-permute-start.8) | collective-permute-done | bytes 131104 | tf_op jit(solution)/shard_map/ppermute | solution.py:579
  131.2 1.6 %collective-permute-start.18 = (bf16[256,256]{1,0:T(8,128)(2,1)S(1)}, bf16[256,256]{1,0:T(8,128)(2,1)S(1)}, u32[]{:S(2)}, u32[]{:S(2)}) collective-permute-start(bf16[256,256]{1,0:T(8,128)(2,1)S(1)} %add_convert_fusion.refs_0_), channel_id=1, source_target_pairs={{0,1},{1,0},{2,3},{3,2},{4,5},{5,4},{6,7},{7,6},{8,9},{9,8},{10,11... | collective-permute-start | bytes 393224 | tf_op jit(solution)/shard_map/ppermute | solution.py:574
  132.8 0.0 collective-permute-start.19
  132.8 0.5 collective-permute-start.20
  133.3 1.6 %collective-permute-start.13 = (bf16[32,16,128]{2,1,0:T(8,128)(2,1)S(1)}, bf16[32,16,128]{2,1,0:T(8,128)(2,1)S(1)}, u32[]{:S(2)}, u32[]{:S(2)}) collective-permute-start(bf16[32,16,128]{2,1,0:T(8,128)(2,1)S(1)} %all-to-all-done.5.refs_0_), channel_id=1, source_target_pairs={{0,6},{1,7},{2,0},{3,1},{4,2},{5,3},{6,4},{7,5},{8,14},{9,15},{10,... | collective-permute-start | bytes 393224 | tf_op jit(solution)/shard_map/ppermute | solution.py:579
  135.0 0.5 collective-permute-start.12
  135.5 0.1 collective-permute-start.11
  135.5 0.7 collective-permute-start.14
  136.2 0.0 collective-permute-done.20.refs_6_
  136.2 0.1 collective-permute-start.21
  136.3 2.1 %collective-permute-done.13.refs_3_ = bf16[32,16,128]{2,1,0:T(8,128)(2,1)S(1)} collective-permute-done((bf16[32,16,128]{2,1,0:T(8,128)(2,1)S(1)}, bf16[32,16,128]{2,1,0:T(8,128)(2,1)S(1)}, u32[]{:S(2)}, u32[]{:S(2)}) %collective-permute-start.13) | collective-permute-done | bytes 131104 | tf_op jit(solution)/shard_map/ppermute | solution.py:579
  138.5 3.1 %collective-permute-start.17 = (bf16[32,16,128]{2,1,0:T(8,128)(2,1)S(1)}, bf16[32,16,128]{2,1,0:T(8,128)(2,1)S(1)}, u32[]{:S(2)}, u32[]{:S(2)}) collective-permute-start(bf16[32,16,128]{2,1,0:T(8,128)(2,1)S(1)} %collective-permute-done.13.refs_3_), channel_id=1, source_target_pairs={{0,1},{1,0},{2,3},{3,2},{4,5},{5,4},{6,7},{7,6},{8,9},{9,8},{10,11... | collective-permute-start | bytes 393224 | tf_op jit(solution)/shard_map/ppermute | solution.py:574
  141.5 0.0 collective-permute-done.12.refs_2_
  141.5 1.7 %collective-permute-start.16 = (bf16[32,16,128]{2,1,0:T(8,128)(2,1)S(1)}, bf16[32,16,128]{2,1,0:T(8,128)(2,1)S(1)}, u32[]{:S(2)}, u32[]{:S(2)}) collective-permute-start(bf16[32,16,128]{2,1,0:T(8,128)(2,1)S(1)} %collective-permute-done.12.refs_2_), channel_id=1, source_target_pairs={{0,1},{1,0},{2,3},{3,2},{4,5},{5,4},{6,7},{7,6},{8,9},{9,8},{10,11... | collective-permute-start | bytes 393224 | tf_op jit(solution)/shard_map/ppermute | solution.py:574
  143.2 1.5 %collective-permute-done.11.refs_1_ = bf16[32,16,128]{2,1,0:T(8,128)(2,1)S(1)} collective-permute-done((bf16[32,16,128]{2,1,0:T(8,128)(2,1)S(1)}, bf16[32,16,128]{2,1,0:T(8,128)(2,1)S(1)}, u32[]{:S(2)}, u32[]{:S(2)}) %collective-permute-start.11) | collective-permute-done | bytes 131104 | tf_op jit(solution)/shard_map/ppermute | solution.py:579
  144.7 0.5 collective-permute-start.15
  145.2 1.5 %shard_map.142 = f32[2048,256]{1,0:T(8,128)} custom-call(s32[1]{0:T(128)} %bitcast.at_ref, s32[32,1,128]{2,1,0:T(1,128)S(1)} %copy-done.1, bf16[256,256]{1,0:T(8,128)(2,1)S(1)} %add_convert_fusion.refs_0_, bf16[256,256]{1,0:T(8,128)(2,1)S(1)} %collective-permute-done.8.refs_1_, bf16[256,256]{1,0:T(8,128)(2,1)S(1)} %collective-permute-done.9.refs_2_, ...), custom_call_target="tpu_custom_call" | custom-call | tf_op jit(solution)/shard_map/pallas_call | solution.py:85
  146.7 0.0 collective-permute-done.14.refs_4_
  146.8 1.5 %shard_map.141 = f32[2048,256]{1,0:T(8,128)} custom-call(s32[1]{0:T(128)} %bitcast.at_ref, s32[32,1,128]{2,1,0:T(1,128)S(1)} %copy-done.1, bf16[32,16,128]{2,1,0:T(8,128)(2,1)S(1)} %all-to-all-done.5.refs_0_, bf16[32,16,128]{2,1,0:T(8,128)(2,1)S(1)} %collective-permute-done.11.refs_1_, bf16[32,16,128]{2,1,0:T(8,128)(2,1)S(1)} %collective-permute-done.12.refs_2_, ...), custom_call_target="tpu_custom_call" | custom-call | tf_op jit(solution)/shard_map/pallas_call | solution.py:85
  (13 shorter events, 0.0 us)
Async XLA Ops:
  27.1 16.7 %all-to-all-start.1 = ((bf16[32,32,256]{2,1,0:T(8,128)(2,1)}), bf16[32,32,256]{2,1,0:T(8,128)(2,1)S(1)}, u32[]{:S(2)}, u32[]{:S(2)}) async-start(bf16[32,32,256]{2,1,0:T(8,128)(2,1)} %bitcast.7), calls=%async_computation.1 | async-start | bytes 1048576 | tf_op jit(solution)/shard_map/all_to_all | solution.py:569
  43.8 0.8 copy-start.3
  48.4 19.6 %all-to-all-start.2 = ((bf16[8,144,256]{2,1,0:T(8,128)(2,1)}), bf16[8,144,256]{2,1,0:T(8,128)(2,1)S(1)}, u32[]{:S(2)}, u32[]{:S(2)}) async-start(bf16[8,144,256]{2,1,0:T(8,128)(2,1)} %get-tuple-element.37), calls=%async_computation.2 | async-start | bytes 1179648 | tf_op jit(solution)/shard_map/all_to_all | solution.py:569
  68.1 0.8 copy-start.2
  74.2 19.3 %copy-start.1 = (s32[32,1,128]{2,1,0:T(1,128)S(1)}, s32[32,1,128]{2,1,0:T(1,128)}, u32[]{:S(2)}) copy-start(s32[32,1,128]{2,1,0:T(1,128)} %all_to_all.30.wanted_hbm.wanted_ref) | copy-start | bytes 49156
  74.2 19.3 %all-to-all-start.3 = ((bf16[32,32,256]{2,1,0:T(8,128)(2,1)}), bf16[32,32,256]{2,1,0:T(8,128)(2,1)S(1)}, u32[]{:S(2)}, u32[]{:S(2)}) async-start(bf16[32,32,256]{2,1,0:T(8,128)(2,1)} %bitcast.8), calls=%async_computation.3 | async-start | bytes 1048576 | tf_op jit(solution)/shard_map/all_to_all | solution.py:569
  79.5 3.0 %collective-permute-start = (bf16[1024,256]{1,0:T(8,128)(2,1)}, bf16[1024,256]{1,0:T(8,128)(2,1)S(1)}, u32[]{:S(2)}, u32[]{:S(2)}) collective-permute-start(bf16[1024,256]{1,0:T(8,128)(2,1)} %get-tuple-element.42), channel_id=1, source_target_pairs={{0,1},{1,0},{2,3},{3,2},{4,5},{5,4},{6,7},{7,6},{8,9},{9,8},{10,11... | collective-permute-start | bytes 1572872 | tf_op jit(solution)/shard_map/ppermute | solution.py:574
  82.4 1.0 copy-start
  83.6 6.6 %collective-permute-start.1 = (bf16[256,256]{1,0:T(8,128)(2,1)S(1)}, bf16[256,256]{1,0:T(8,128)(2,1)S(1)}, u32[]{:S(2)}, u32[]{:S(2)}) collective-permute-start(bf16[256,256]{1,0:T(8,128)(2,1)S(1)} %get-tuple-element.44), channel_id=1, source_target_pairs={{0,2},{1,3},{2,4},{3,5},{4,6},{5,7},{6,0},{7,1},{8,10},{9,11},{10,... | collective-permute-start | bytes 393224 | tf_op jit(solution)/shard_map/ppermute | solution.py:579
  84.0 7.9 %collective-permute-start.2 = (bf16[256,256]{1,0:T(8,128)(2,1)S(1)}, bf16[256,256]{1,0:T(8,128)(2,1)S(1)}, u32[]{:S(2)}, u32[]{:S(2)}) collective-permute-start(bf16[256,256]{1,0:T(8,128)(2,1)S(1)} %get-tuple-element.45), channel_id=1, source_target_pairs={{0,4},{1,5},{2,6},{3,7},{4,0},{5,1},{6,2},{7,3},{8,12},{9,13},{10,... | collective-permute-start | bytes 393224 | tf_op jit(solution)/shard_map/ppermute | solution.py:579
  85.8 7.0 %collective-permute-start.3 = (bf16[256,256]{1,0:T(8,128)(2,1)S(1)}, bf16[256,256]{1,0:T(8,128)(2,1)S(1)}, u32[]{:S(2)}, u32[]{:S(2)}) collective-permute-start(bf16[256,256]{1,0:T(8,128)(2,1)S(1)} %get-tuple-element.46), channel_id=1, source_target_pairs={{0,6},{1,7},{2,0},{3,1},{4,2},{5,3},{6,4},{7,5},{8,14},{9,15},{10,... | collective-permute-start | bytes 393224 | tf_op jit(solution)/shard_map/ppermute | solution.py:579
  94.9 11.1 %collective-permute-start.4 = (bf16[1024,256]{1,0:T(8,128)(2,1)S(1)}, bf16[1024,256]{1,0:T(8,128)(2,1)S(1)}, u32[]{:S(2)}, u32[]{:S(2)}) collective-permute-start(bf16[1024,256]{1,0:T(8,128)(2,1)S(1)} %get-tuple-element.50), channel_id=1, source_target_pairs={{0,1},{1,0},{2,3},{3,2},{4,5},{5,4},{6,7},{7,6},{8,9},{9,8},{10,11... | collective-permute-start | bytes 1572872 | tf_op jit(solution)/shard_map/ppermute | solution.py:574
  99.0 16.2 %all-to-all-start.4 = ((bf16[32,16,128]{2,1,0:T(8,128)(2,1)}), bf16[32,16,128]{2,1,0:T(8,128)(2,1)S(1)}, u32[]{:S(2)}, u32[]{:S(2)}) async-start(bf16[32,16,128]{2,1,0:T(8,128)(2,1)} %shard_map.137), calls=%async_computation.4 | async-start | bytes 262144 | tf_op jit(solution)/shard_map/all_to_all | solution.py:569
  106.1 14.3 %collective-permute-start.5 = (bf16[256,256]{1,0:T(8,128)(2,1)S(1)}, bf16[256,256]{1,0:T(8,128)(2,1)S(1)}, u32[]{:S(2)}, u32[]{:S(2)}) collective-permute-start(bf16[256,256]{1,0:T(8,128)(2,1)S(1)} %get-tuple-element.52), channel_id=1, source_target_pairs={{0,2},{1,3},{2,4},{3,5},{4,6},{5,7},{6,0},{7,1},{8,10},{9,11},{10,... | collective-permute-start | bytes 393224 | tf_op jit(solution)/shard_map/ppermute | solution.py:579
  106.2 14.1 %collective-permute-start.6 = (bf16[256,256]{1,0:T(8,128)(2,1)S(1)}, bf16[256,256]{1,0:T(8,128)(2,1)S(1)}, u32[]{:S(2)}, u32[]{:S(2)}) collective-permute-start(bf16[256,256]{1,0:T(8,128)(2,1)S(1)} %get-tuple-element.53), channel_id=1, source_target_pairs={{0,4},{1,5},{2,6},{3,7},{4,0},{5,1},{6,2},{7,3},{8,12},{9,13},{10,... | collective-permute-start | bytes 393224 | tf_op jit(solution)/shard_map/ppermute | solution.py:579
  109.5 10.9 %collective-permute-start.7 = (bf16[256,256]{1,0:T(8,128)(2,1)S(1)}, bf16[256,256]{1,0:T(8,128)(2,1)S(1)}, u32[]{:S(2)}, u32[]{:S(2)}) collective-permute-start(bf16[256,256]{1,0:T(8,128)(2,1)S(1)} %get-tuple-element.54), channel_id=1, source_target_pairs={{0,6},{1,7},{2,0},{3,1},{4,2},{5,3},{6,4},{7,5},{8,14},{9,15},{10,... | collective-permute-start | bytes 393224 | tf_op jit(solution)/shard_map/ppermute | solution.py:579
  115.8 13.7 %all-to-all-start.5 = ((bf16[32,16,128]{2,1,0:T(8,128)(2,1)}), bf16[32,16,128]{2,1,0:T(8,128)(2,1)S(1)}, u32[]{:S(2)}, u32[]{:S(2)}) async-start(bf16[32,16,128]{2,1,0:T(8,128)(2,1)} %shard_map.138), calls=%async_computation.5 | async-start | bytes 262144 | tf_op jit(solution)/shard_map/all_to_all | solution.py:569
  120.5 9.0 %collective-permute-start.10 = (bf16[256,256]{1,0:T(8,128)(2,1)S(1)}, bf16[256,256]{1,0:T(8,128)(2,1)S(1)}, u32[]{:S(2)}, u32[]{:S(2)}) collective-permute-start(bf16[256,256]{1,0:T(8,128)(2,1)S(1)} %add_convert_fusion.refs_0_), channel_id=1, source_target_pairs={{0,6},{1,7},{2,0},{3,1},{4,2},{5,3},{6,4},{7,5},{8,14},{9,15},{10,... | collective-permute-start | bytes 393224 | tf_op jit(solution)/shard_map/ppermute | solution.py:579
  122.7 6.8 %collective-permute-start.9 = (bf16[256,256]{1,0:T(8,128)(2,1)S(1)}, bf16[256,256]{1,0:T(8,128)(2,1)S(1)}, u32[]{:S(2)}, u32[]{:S(2)}) collective-permute-start(bf16[256,256]{1,0:T(8,128)(2,1)S(1)} %add_convert_fusion.refs_0_), channel_id=1, source_target_pairs={{0,4},{1,5},{2,6},{3,7},{4,0},{5,1},{6,2},{7,3},{8,12},{9,13},{10,... | collective-permute-start | bytes 393224 | tf_op jit(solution)/shard_map/ppermute | solution.py:579
  122.9 8.4 %collective-permute-start.8 = (bf16[256,256]{1,0:T(8,128)(2,1)S(1)}, bf16[256,256]{1,0:T(8,128)(2,1)S(1)}, u32[]{:S(2)}, u32[]{:S(2)}) collective-permute-start(bf16[256,256]{1,0:T(8,128)(2,1)S(1)} %add_convert_fusion.refs_0_), channel_id=1, source_target_pairs={{0,2},{1,3},{2,4},{3,5},{4,6},{5,7},{6,0},{7,1},{8,10},{9,11},{10,... | collective-permute-start | bytes 393224 | tf_op jit(solution)/shard_map/ppermute | solution.py:579
  131.2 4.2 %collective-permute-start.18 = (bf16[256,256]{1,0:T(8,128)(2,1)S(1)}, bf16[256,256]{1,0:T(8,128)(2,1)S(1)}, u32[]{:S(2)}, u32[]{:S(2)}) collective-permute-start(bf16[256,256]{1,0:T(8,128)(2,1)S(1)} %add_convert_fusion.refs_0_), channel_id=1, source_target_pairs={{0,1},{1,0},{2,3},{3,2},{4,5},{5,4},{6,7},{7,6},{8,9},{9,8},{10,11... | collective-permute-start | bytes 393224 | tf_op jit(solution)/shard_map/ppermute | solution.py:574
  132.8 2.7 %collective-permute-start.19 = (bf16[256,256]{1,0:T(8,128)(2,1)S(1)}, bf16[256,256]{1,0:T(8,128)(2,1)S(1)}, u32[]{:S(2)}, u32[]{:S(2)}) collective-permute-start(bf16[256,256]{1,0:T(8,128)(2,1)S(1)} %collective-permute-done.8.refs_1_), channel_id=1, source_target_pairs={{0,1},{1,0},{2,3},{3,2},{4,5},{5,4},{6,7},{7,6},{8,9},{9,8},{10,11... | collective-permute-start | bytes 393224 | tf_op jit(solution)/shard_map/ppermute | solution.py:574
  132.8 3.4 %collective-permute-start.20 = (bf16[256,256]{1,0:T(8,128)(2,1)S(1)}, bf16[256,256]{1,0:T(8,128)(2,1)S(1)}, u32[]{:S(2)}, u32[]{:S(2)}) collective-permute-start(bf16[256,256]{1,0:T(8,128)(2,1)S(1)} %collective-permute-done.9.refs_2_), channel_id=1, source_target_pairs={{0,1},{1,0},{2,3},{3,2},{4,5},{5,4},{6,7},{7,6},{8,9},{9,8},{10,11... | collective-permute-start | bytes 393224 | tf_op jit(solution)/shard_map/ppermute | solution.py:574
  133.3 5.1 %collective-permute-start.13 = (bf16[32,16,128]{2,1,0:T(8,128)(2,1)S(1)}, bf16[32,16,128]{2,1,0:T(8,128)(2,1)S(1)}, u32[]{:S(2)}, u32[]{:S(2)}) collective-permute-start(bf16[32,16,128]{2,1,0:T(8,128)(2,1)S(1)} %all-to-all-done.5.refs_0_), channel_id=1, source_target_pairs={{0,6},{1,7},{2,0},{3,1},{4,2},{5,3},{6,4},{7,5},{8,14},{9,15},{10,... | collective-permute-start | bytes 393224 | tf_op jit(solution)/shard_map/ppermute | solution.py:579
  135.0 6.6 %collective-permute-start.12 = (bf16[32,16,128]{2,1,0:T(8,128)(2,1)S(1)}, bf16[32,16,128]{2,1,0:T(8,128)(2,1)S(1)}, u32[]{:S(2)}, u32[]{:S(2)}) collective-permute-start(bf16[32,16,128]{2,1,0:T(8,128)(2,1)S(1)} %all-to-all-done.5.refs_0_), channel_id=1, source_target_pairs={{0,4},{1,5},{2,6},{3,7},{4,0},{5,1},{6,2},{7,3},{8,12},{9,13},{10,... | collective-permute-start | bytes 393224 | tf_op jit(solution)/shard_map/ppermute | solution.py:579
  135.5 9.2 %collective-permute-start.11 = (bf16[32,16,128]{2,1,0:T(8,128)(2,1)S(1)}, bf16[32,16,128]{2,1,0:T(8,128)(2,1)S(1)}, u32[]{:S(2)}, u32[]{:S(2)}) collective-permute-start(bf16[32,16,128]{2,1,0:T(8,128)(2,1)S(1)} %all-to-all-done.5.refs_0_), channel_id=1, source_target_pairs={{0,2},{1,3},{2,4},{3,5},{4,6},{5,7},{6,0},{7,1},{8,10},{9,11},{10,... | collective-permute-start | bytes 393224 | tf_op jit(solution)/shard_map/ppermute | solution.py:579
  135.5 11.2 %collective-permute-start.14 = (bf16[32,16,128]{2,1,0:T(8,128)(2,1)S(1)}, bf16[32,16,128]{2,1,0:T(8,128)(2,1)S(1)}, u32[]{:S(2)}, u32[]{:S(2)}) collective-permute-start(bf16[32,16,128]{2,1,0:T(8,128)(2,1)S(1)} %all-to-all-done.5.refs_0_), channel_id=1, source_target_pairs={{0,1},{1,0},{2,3},{3,2},{4,5},{5,4},{6,7},{7,6},{8,9},{9,8},{10,11... | collective-permute-start | bytes 393224 | tf_op jit(solution)/shard_map/ppermute | solution.py:574
  136.2 9.0 %collective-permute-start.21 = (bf16[256,256]{1,0:T(8,128)(2,1)S(1)}, bf16[256,256]{1,0:T(8,128)(2,1)S(1)}, u32[]{:S(2)}, u32[]{:S(2)}) collective-permute-start(bf16[256,256]{1,0:T(8,128)(2,1)S(1)} %collective-permute-done.10.refs_3_), channel_id=1, source_target_pairs={{0,1},{1,0},{2,3},{3,2},{4,5},{5,4},{6,7},{7,6},{8,9},{9,8},{10,11... | collective-permute-start | bytes 393224 | tf_op jit(solution)/shard_map/ppermute | solution.py:574
  138.5 8.3 %collective-permute-start.17 = (bf16[32,16,128]{2,1,0:T(8,128)(2,1)S(1)}, bf16[32,16,128]{2,1,0:T(8,128)(2,1)S(1)}, u32[]{:S(2)}, u32[]{:S(2)}) collective-permute-start(bf16[32,16,128]{2,1,0:T(8,128)(2,1)S(1)} %collective-permute-done.13.refs_3_), channel_id=1, source_target_pairs={{0,1},{1,0},{2,3},{3,2},{4,5},{5,4},{6,7},{7,6},{8,9},{9,8},{10,11... | collective-permute-start | bytes 393224 | tf_op jit(solution)/shard_map/ppermute | solution.py:574
  141.5 5.2 %collective-permute-start.16 = (bf16[32,16,128]{2,1,0:T(8,128)(2,1)S(1)}, bf16[32,16,128]{2,1,0:T(8,128)(2,1)S(1)}, u32[]{:S(2)}, u32[]{:S(2)}) collective-permute-start(bf16[32,16,128]{2,1,0:T(8,128)(2,1)S(1)} %collective-permute-done.12.refs_2_), channel_id=1, source_target_pairs={{0,1},{1,0},{2,3},{3,2},{4,5},{5,4},{6,7},{7,6},{8,9},{9,8},{10,11... | collective-permute-start | bytes 393224 | tf_op jit(solution)/shard_map/ppermute | solution.py:574
  144.7 2.1 %collective-permute-start.15 = (bf16[32,16,128]{2,1,0:T(8,128)(2,1)S(1)}, bf16[32,16,128]{2,1,0:T(8,128)(2,1)S(1)}, u32[]{:S(2)}, u32[]{:S(2)}) collective-permute-start(bf16[32,16,128]{2,1,0:T(8,128)(2,1)S(1)} %collective-permute-done.11.refs_1_), channel_id=1, source_target_pairs={{0,1},{1,0},{2,3},{3,2},{4,5},{5,4},{6,7},{7,6},{8,9},{9,8},{10,11... | collective-permute-start | bytes 393224 | tf_op jit(solution)/shard_map/ppermute | solution.py:574

commit v5 on v4

--- a/solution.py
+++ b/solution.py
@@ -12,6 +12,7 @@
 bf16 = jnp.bfloat16
 i32 = jnp.int32
 FULL = 62
+MOST = 24
 EXACT = lax.Precision.HIGHEST
 VM = pl.BlockSpec(memory_space=pltpu.VMEM)
 SM = pl.BlockSpec(memory_space=pltpu.SMEM)
@@ -82,17 +83,29 @@
 
 
 def call(kernel, outs, args, specs=None, scratch=(), out_specs=None, limit=16):
+    out_specs = out_specs if out_specs is not None else [VM] * len(outs)
+    shapes = [
+        pltpu.HBM(s, d) if spec is HB else jax.ShapeDtypeStruct(s, d)
+        for (s, d), spec in zip(outs, out_specs, strict=True)
+    ]
+    specs = specs if specs is not None else [VM] * len(args)
+    args = [
+        pltpu.with_memory_space_constraint(a, pltpu.HBM) if spec is HB else a
+        for a, spec in zip(args, specs, strict=True)
+    ]
     return pl.pallas_call(
         kernel,
-        out_shape=tuple(jax.ShapeDtypeStruct(s, d) for s, d in outs),
-        in_specs=specs if specs is not None else [VM] * len(args),
-        out_specs=tuple(out_specs if out_specs is not None else (VM for _ in outs)),
+        out_shape=tuple(shapes),
+        in_specs=specs,
+        out_specs=tuple(out_specs),
         scratch_shapes=list(scratch),
         compiler_params=pltpu.CompilerParams(vmem_limit_bytes=limit * 1024 * 1024),
     )(*args)
 
 
-def request_kernel(len_ref, ids_ref, out_ref, slot_ref, *, rows_own, cap):
+def request_kernel(
+    len_ref, ids_ref, out_ref, slot_hbm, slot_ref, arrived, *, rows_own, cap
+):
     users, block = ids_ref.shape
     shards, _, lanes = out_ref.shape
     shift = rows_own.bit_length() - 1
@@ -114,8 +127,10 @@
         total = total + dot(named_16, where_bf16(chosen, low), NT)
         slot_ref[u : u + 1, :] = (owner * users + u) * cap + rank
         count = count + len_ref[u]
+    copies = begin([(slot_ref, slot_hbm)], arrived)
     wanted = jnp.where(iota((shards, lanes), 1) == users * cap, count, total.astype(i32))
     out_ref[:, 0, :] = wanted
+    finish(copies)
 
 
 def answer_kernel(
@@ -155,9 +170,13 @@
     cot_ref,
     decay_ref,
     w_out_ref,
+    quot_hbm,
+    dmixed_hbm,
+    wide_hbm,
     quot_ref,
     dmixed_ref,
     wide_ref,
+    arrived,
 ):
     users, block = ids_ref.shape
     heads = decay_ref.shape[1]
@@ -171,6 +190,8 @@
         dmixed_ref[at, :] = dot(masked, w_out_ref[...], NT).astype(bf16)
         _, columns = decays(decay_ref[u], width)
         wide_ref[at, :] = over_heads(columns, heads, width)
+    pairs = ((quot_ref, quot_hbm), (dmixed_ref, dmixed_hbm), (wide_ref, wide_hbm))
+    finish(begin(pairs, arrived))
 
 
 def decays(log_decay, width):
@@ -211,7 +232,7 @@
 def project_kernel(
     at_ref,
     slot_hbm,
-    answered_hbm,
+    answered_ref,
     quot_hbm,
     wq_hbm,
     wk_hbm,
@@ -221,7 +242,6 @@
     rem_hbm,
     payload_hbm,
     slot_ref,
-    answered_ref,
     quot_ref,
     wq_ref,
     wk_ref,
@@ -244,7 +264,6 @@
     copies = begin(
         (
             (slot_hbm, slot_ref),
-            (answered_hbm, answered_ref),
             (quot_hbm, quot_ref),
             (wq_hbm, wq_ref),
             (wk_hbm, wk_ref),
@@ -256,8 +275,8 @@
     )
     finish(copies[:1])
     hot = [tiled_match(spread_column(slot_ref[u : u + 1, :]), slots) for u in range(users)]
-    finish(copies[1:6])
-    waits, copies = copies[6:], []
+    finish(copies[1:5])
+    waits, copies = copies[5:], []
     for u in range(users):
         at = slice(u * block, (u + 1) * block)
         rem_ref[at, :] = dot(hot[u], answered_ref[...]).astype(bf16)
@@ -357,7 +376,7 @@
 
 def gradient_kernel(
     at_ref,
-    payload_hbm,
+    payload_ref,
     within_hbm,
     dmixed_hbm,
     wide_hbm,
@@ -373,7 +392,6 @@
     rem_send_hbm,
     keep_hbm,
     give_hbm,
-    payload_ref,
     within_ref,
     dmixed_ref,
     wide_ref,
@@ -398,7 +416,6 @@
     width = quot_ref.shape[1]
     copies = begin(
         (
-            (payload_hbm, payload_ref),
             (quot_hbm, quot_ref),
             (rem_hbm, rem_ref),
             (wq_hbm, wq_ref),
@@ -416,7 +433,6 @@
     for u in range(users):
         at = slice(u * block, (u + 1) * block)
         waits += begin([(within_hbm.at[:, at, :], within_ref.at[:, at, :])], arrived, 11 + u)
-    finish(copies[:1])
     peers = payload_ref.shape[0]
     size = width // heads
     slots = rem_send_ref.shape[0]
@@ -442,7 +458,7 @@
             linked = jnp.exp(ends[peer]) * leaving + part
             leaving = jnp.where(peer > me, linked, leaving)
         carried.append((block_diagonal(entering, heads), block_diagonal(leaving, heads)))
-    finish(copies[1:])
+    finish(copies)
     copies = []
     rem_terms, quot_terms = [], []
     for u in range(users):
@@ -504,12 +520,20 @@
     sum_half(row, back_ref[...], at_ref[0] % 2, keep_ref)
 
 
-def split_kernel(at_ref, keep_ref, got_ref, *out_refs):
-    chips = len(out_refs)
+def split_kernel(at_ref, keep_ref, got_ref, *refs, chips):
+    out_refs = refs[:chips]
     rows = out_refs[0].shape[0]
+    bases = [
+        pl.multiple_of(lax.rem(at_ref[0] // 2 + d, chips) * rows, rows) for d in range(chips)
+    ]
+    copies = []
+    if len(refs) > chips:
+        near_ref, arrived = refs[chips:]
+        copies = begin([(keep_ref.at[pl.ds(b, rows), :], near_ref.at[d]) for d, b in enumerate(bases)], arrived)
     for d, out_ref in enumerate(out_refs):
-        base = pl.multiple_of(lax.rem(at_ref[0] // 2 + d, chips) * rows, rows)
-        both = keep_ref[pl.ds(base, rows), :].astype(f32) + got_ref[pl.ds(base, rows), :].astype(f32)
+        finish(copies[d : d + 1])
+        kept = near_ref[d] if copies else keep_ref[pl.ds(bases[d], rows), :]
+        both = kept.astype(f32) + got_ref[pl.ds(bases[d], rows), :].astype(f32)
         out_ref[...] = both.astype(bf16)
 
 
@@ -579,10 +603,13 @@
     return lax.ppermute(array, "hist", [(i, (i + 2 * steps) % peers) for i in range(peers)])
 
 
-def split(at, keep, give):
+def split(at, keep, give, spec=VM):
     chips = lax.axis_size("hist") // 2
-    outs = [((keep.shape[0] // chips, keep.shape[1]), bf16)] * chips
-    return call(split_kernel, outs, (at, keep, to_core(give)), [SM, VM, VM])
+    rows, width = keep.shape[0] // chips, keep.shape[1]
+    kernel = functools.partial(split_kernel, chips=chips)
+    scratch = [pltpu.VMEM((chips, rows, width), keep.dtype), dma(chips)] if spec is HB else []
+    args = (at, keep, to_core(give))
+    return call(kernel, [((rows, width), bf16)] * chips, args, [SM, spec, VM], scratch)
 
 
 def shared(chunks):
@@ -631,12 +658,16 @@
     at = lax.axis_index("hist").astype(i32).reshape(1)
     lanes = (per // 128 + 1) * 128
 
+    events = pltpu.VMEM((users * block, width), bf16)
+    square = pltpu.VMEM((width, width), bf16)
     requests, slot = call(
         functools.partial(request_kernel, rows_own=rows_own, cap=cap),
         [((shards, 1, lanes), i32), ((8, block), i32)],
         (lengths, rem_ids),
         [SM, VM],
-        limit=FULL,
+        [pltpu.VMEM((8, block), i32), dma(1)],
+        [VM, HB],
+        FULL,
     )
     wanted = exchange(requests, "user")
     quot_emb, dmixed, wide = call(
@@ -648,7 +679,9 @@
         ],
         (lengths, at, quot_ids, quot_table, cotangent, log_decay, w_out),
         [SM, SM] + [VM] * 5,
-        limit=FULL,
+        [events, events, pltpu.VMEM((users * block, width), f32), dma(3)],
+        [HB] * 3,
+        FULL,
     )
     (found,) = call(
         functools.partial(answer_kernel, per=per),
@@ -665,19 +698,17 @@
         FULL,
     )
     answered = exchange(found.reshape(shards, per, width), "user").reshape(slots, width)
-    events = pltpu.VMEM((users * block, width), bf16)
-    square = pltpu.VMEM((width, width), bf16)
     rem_emb, payload = call(
         functools.partial(project_kernel, users=users, heads=heads),
         [((users * block, width), bf16), ((peers, users * size + 16, width), bf16)],
         (at, slot, answered, quot_emb, w_query, w_key, w_value, wide, dmixed),
-        [SM] + [HB] * 8,
-        [pltpu.VMEM((8, block), i32), pltpu.VMEM((slots, width), bf16), events]
+        [SM, HB, VM] + [HB] * 6,
+        [pltpu.VMEM((8, block), i32), events]
         + [square] * 3
         + [pltpu.VMEM((users * block, width), f32), events, events]
         + [pltpu.VMEM((2, users * size + 16, width), bf16), dma(8 + users + peers)],
         [HB, HB],
-        FULL,
+        MOST,
     )
     states = exchange(payload, "hist")
     parts = (4, users * block, width)
@@ -699,8 +730,8 @@
         ],
         (at, states, within, dmixed, wide, rem_emb, quot_emb, slot, quot_ids)
         + (w_query, w_key, w_value, w_out),
-        [SM] + [HB] * 12,
-        [pltpu.VMEM(payload.shape, bf16), pltpu.VMEM(parts, f32), events]
+        [SM, VM] + [HB] * 11,
+        [pltpu.VMEM(parts, f32), events]
         + [pltpu.VMEM((users * block, width), f32), events, events]
         + [pltpu.VMEM((8, block), i32), pltpu.VMEM((users, block), i32)]
         + [square] * 4
@@ -708,11 +739,11 @@
         + [pltpu.VMEM((rows_all // 2, width), bf16)] * 2
         + [dma(11 + 2 * users + (slots + rows_all) // block)],
         [HB] * 4,
-        FULL,
+        MOST,
     )
     rem_back = exchange(rem_send.reshape(shards, per, width), "user").reshape(slots, width)
     tiles = (shards, rows_all // peers * width // shards // 128, 128)
-    (quot_tiles,) = call(total_kernel, [(tiles, bf16)], shared(split(at, keep, give)))
+    (quot_tiles,) = call(total_kernel, [(tiles, bf16)], shared(split(at, keep, give, HB)))
     rem_back, quot_tiles = lax.optimization_barrier((rem_back, quot_tiles))
     quot_back = exchange(quot_tiles, "user")
     keep, give = call(
@@ -727,7 +758,7 @@
     quot_tiles = exchange(quot_tiles, "user")
     rem_sum = sum(c.astype(f32) for c in shared(chunks)).astype(bf16)
     rem_mine = along_chips(rem_sum)
-    quot_tiles, *rem_mine = lax.optimization_barrier((quot_tiles, *rem_mine))
+    quot_tiles, _ = lax.optimization_barrier((quot_tiles, rem_sum))
     total = float(users * shards * block * peers)
     rem_chunks = rem_mine + [to_core(c) for c in rem_mine]
     rem_grad = placed(at, wanted, rem_chunks, rows_own, width, per, total)

time: 149 us -> 146 us (0.980)
  waiting for transfers between devices: 38.7 us -> 32.2 us
  starting transfers between devices: 54.9 us -> 59.2 us
  local copies, waits for them, and re-layouts: 2.65 us -> 0.01 us
    ppermute x12, waiting for transfers between devices: 11.7 us -> 6.33 us  [to_chip(): lax.ppermute(array, 'hist', [(i, (i + 2 * steps) % peers) for i in range(...]
    ppermute x10, starting transfers between devices: 13.4 us -> 17.5 us  [to_core(): return lax.ppermute(array, 'hist', [(i, i ^ 1) for i in range(peers)])]
    unnamed x8 -> x2, local copies, waits for them, and re-layouts: 2.65 us -> 0.01 us
  transfers between devices with their start and end apart: 27 -> 27, of which waited for: 11 -> 8; matrix products, arithmetic and copies ran while one was open for 0% -> 0% of each run, Pallas kernels for 8% -> 9%
where the time goes in v5:
time: 146 us; the launch traced here: 145 us
  starting transfers between devices  59.2 us (41%)
  waiting for transfers between devices  32.2 us (22%)
  Pallas kernels  31.8 us (22%)
  blocking collectives  20.7 us (14%)
    pallas_call x13, Pallas kernels, call(): pl.pallas_call(kernel, out_shape=tuple(shapes), in_specs=specs, out_specs...  31.8 us
    all_to_all x5, starting transfers between devices, exchange(): return lax.all_to_all(array, axis, split_axis=0, concat_axis=0, tiled=True)  29.9 us
    all_to_all x5, waiting for transfers between devices, exchange(): return lax.all_to_all(array, axis, split_axis=0, concat_axis=0, tiled=True)  24.1 us
    all_to_all x1, blocking collectives, exchange(): return lax.all_to_all(array, axis, split_axis=0, concat_axis=0, tiled=True)  20.7 us
    ppermute x10, starting transfers between devices, to_core(): return lax.ppermute(array, 'hist', [(i, i ^ 1) for i in range(peers)])  17.5 us
    ppermute x12, starting transfers between devices, to_chip(): lax.ppermute(array, 'hist', [(i, (i + 2 * steps) % peers) for i in range(...  11.7 us
    ppermute x12, waiting for transfers between devices, to_chip(): lax.ppermute(array, 'hist', [(i, (i + 2 * steps) % peers) for i in range(...  6.33 us
  transfers between devices with their start and end apart: 27, of which 8 were waited for; matrix products, arithmetic and copies ran while one was open for 0% of the time, Pallas kernels for 9%

profile of v5, /device:TPU:1, one launch (start us, length us, event | category | flops | bytes accessed | tf_op | source)
XLA Modules:
  0.0 145.0 jit_solution(16389840816054816729)
XLA Ops:
  0.6 2.3 %shard_map.130 = (s32[32,1,128]{2,1,0:T(1,128)}, s32[8,256]{1,0:T(8,128)}) custom-call(s32[2]{0:T(128)} %len_ref.3, s32[2,256]{1,0:T(2,128)} %ids_ref.2), custom_call_target="tpu_custom_call" | custom-call | tf_op jit(solution)/shard_map/pallas_call | solution.py:96
  2.9 20.7 %all_to_all.30.wanted_hbm.wanted_ref = s32[32,1,128]{2,1,0:T(1,128)} all-to-all(s32[32,1,128]{2,1,0:T(1,128)} %get-tuple-element.29), channel_id=1, replica_groups=mesh['user'=32,'hist'=8] {'user'}, dimensions={0} | all-to-all | bytes 32768 | tf_op jit(solution)/shard_map/all_to_all | solution.py:593
  23.6 4.0 %shard_map.131 = bf16[1024,256]{1,0:T(8,128)(2,1)} custom-call(s32[32,1,128]{2,1,0:T(1,128)} %all_to_all.30.wanted_hbm.wanted_ref, bf16[2048,256]{1,0:T(8,128)(2,1)} %table_hbm.1), custom_call_target="tpu_custom_call" | custom-call | tf_op jit(solution)/shard_map/pallas_call | solution.py:96
  27.7 3.9 %all-to-all-start.1 = ((bf16[32,32,256]{2,1,0:T(8,128)(2,1)}), bf16[32,32,256]{2,1,0:T(8,128)(2,1)S(1)}, u32[]{:S(2)}, u32[]{:S(2)}) async-start(bf16[32,32,256]{2,1,0:T(8,128)(2,1)} %bitcast.7), calls=%async_computation.1 | async-start | bytes 1048576 | tf_op jit(solution)/shard_map/all_to_all | solution.py:593
  31.6 3.8 %shard_map.132 = (bf16[512,256]{1,0:T(8,128)(2,1)}, bf16[512,256]{1,0:T(8,128)(2,1)}, f32[512,256]{1,0:T(8,128)}) custom-call(s32[2]{0:T(128)} %len_ref.3, s32[1]{0:T(128)} %bitcast.at_ref, s32[2,256]{1,0:T(2,128)} %ids_hbm.1, bf16[2048,256]{1,0:T(8,128)(2,1)} %table_ref.1, bf16[2,256,256]{2,1,0:T(8,128)(2,1)} %cot_ref.1, f32[2,4,256]{2,1,0:T(4,128)} %decay_ref.3, ...), custom_call_target="tpu_custom_call" | custom-call | tf_op jit(solution)/shard_map/pallas_call | solution.py:96
  35.4 9.1 %all-to-all-done.1 = bf16[32,32,256]{2,1,0:T(8,128)(2,1)S(1)} async-done(((bf16[32,32,256]{2,1,0:T(8,128)(2,1)}), bf16[32,32,256]{2,1,0:T(8,128)(2,1)S(1)}, u32[]{:S(2)}, u32[]{:S(2)}) %all-to-all-start.1) | async-done | bytes 524320 | tf_op jit(solution)/shard_map/all_to_all | solution.py:593
  44.6 3.7 %shard_map.133 = (bf16[512,256]{1,0:T(8,128)(2,1)}, bf16[8,144,256]{2,1,0:T(8,128)(2,1)}) custom-call(s32[1]{0:T(128)} %bitcast.at_ref, s32[8,256]{1,0:T(8,128)} %get-tuple-element.28.slot_hbm, bf16[1024,256]{1,0:T(8,128)(2,1)S(1)} %bitcast.5, bf16[512,256]{1,0:T(8,128)(2,1)} %get-tuple-element.30.quot_hbm.quot_ref, bf16[256,256]{1,0:T(8,128)(2,1)} %wq_hbm.3, ...), custom_call_target="tpu_custom_call" | custom-call | tf_op jit(solution)/shard_map/pallas_call | solution.py:96
  48.3 9.5 %all-to-all-start.2 = ((bf16[8,144,256]{2,1,0:T(8,128)(2,1)}), bf16[8,144,256]{2,1,0:T(8,128)(2,1)S(1)}, u32[]{:S(2)}, u32[]{:S(2)}) async-start(bf16[8,144,256]{2,1,0:T(8,128)(2,1)} %get-tuple-element.33), calls=%async_computation.2 | async-start | bytes 1179648 | tf_op jit(solution)/shard_map/all_to_all | solution.py:593
  57.8 5.7 %shard_map.134.within_hbm = f32[4,512,256]{2,1,0:T(8,128)} custom-call(bf16[512,256]{1,0:T(8,128)(2,1)} %get-tuple-element.30.quot_hbm.quot_ref, bf16[512,256]{1,0:T(8,128)(2,1)} %get-tuple-element.34.rem_ref.rem_hbm, bf16[512,256]{1,0:T(8,128)(2,1)} %get-tuple-element.32.dmixed_hbm.dmixed_ref, f32[2,4,256]{2,1,0:T(4,128)} %decay_ref.3, ...), custom_call_target="tpu_custom_call" | custom-call | tf_op jit(solution)/shard_map/pallas_call | solution.py:96
  63.5 4.5 %all-to-all-done.2.payload_ref = bf16[8,144,256]{2,1,0:T(8,128)(2,1)S(1)} async-done(((bf16[8,144,256]{2,1,0:T(8,128)(2,1)}), bf16[8,144,256]{2,1,0:T(8,128)(2,1)S(1)}, u32[]{:S(2)}, u32[]{:S(2)}) %all-to-all-start.2) | async-done | bytes 589856 | tf_op jit(solution)/shard_map/all_to_all | solution.py:593
  68.0 5.1 %shard_map.135 = (bf16[2,256,256]{2,1,0:T(8,128)(2,1)}, bf16[1024,256]{1,0:T(8,128)(2,1)}, bf16[1024,256]{1,0:T(8,128)(2,1)}, bf16[1024,256]{1,0:T(8,128)(2,1)}) custom-call(s32[1]{0:T(128)} %bitcast.at_ref, bf16[8,144,256]{2,1,0:T(8,128)(2,1)S(1)} %all-to-all-done.2.payload_ref, f32[4,512,256]{2,1,0:T(8,128)} %shard_map.134.within_hbm, ...), custom_call_target="tpu_custom_call" | custom-call | tf_op jit(solution)/shard_map/pallas_call | solution.py:96
  73.1 5.0 %all-to-all-start.3 = ((bf16[32,32,256]{2,1,0:T(8,128)(2,1)}), bf16[32,32,256]{2,1,0:T(8,128)(2,1)S(1)}, u32[]{:S(2)}, u32[]{:S(2)}) async-start(bf16[32,32,256]{2,1,0:T(8,128)(2,1)} %bitcast.8), calls=%async_computation.3 | async-start | bytes 1048576 | tf_op jit(solution)/shard_map/all_to_all | solution.py:593
  78.1 1.2 collective-permute-start
  79.4 1.7 %collective-permute-done.got_ref = bf16[1024,256]{1,0:T(8,128)(2,1)S(1)} collective-permute-done((bf16[1024,256]{1,0:T(8,128)(2,1)}, bf16[1024,256]{1,0:T(8,128)(2,1)S(1)}, u32[]{:S(2)}, u32[]{:S(2)}) %collective-permute-start) | collective-permute-done | bytes 524320 | tf_op jit(solution)/shard_map/ppermute | solution.py:598
  81.1 1.2 shard_map.136
  82.3 0.4 collective-permute-start.1
  82.6 1.8 %collective-permute-start.2 = (bf16[256,256]{1,0:T(8,128)(2,1)S(1)}, bf16[256,256]{1,0:T(8,128)(2,1)S(1)}, u32[]{:S(2)}, u32[]{:S(2)}) collective-permute-start(bf16[256,256]{1,0:T(8,128)(2,1)S(1)} %get-tuple-element.41), channel_id=1, source_target_pairs={{0,4},{1,5},{2,6},{3,7},{4,0},{5,1},{6,2},{7,3},{8,12},{9,13},{10,... | collective-permute-start | bytes 393224 | tf_op jit(solution)/shard_map/ppermute | solution.py:603
  84.4 0.7 collective-permute-start.3
  85.1 3.7 %collective-permute-done.1.refs_1_ = bf16[256,256]{1,0:T(8,128)(2,1)S(1)} collective-permute-done((bf16[256,256]{1,0:T(8,128)(2,1)S(1)}, bf16[256,256]{1,0:T(8,128)(2,1)S(1)}, u32[]{:S(2)}, u32[]{:S(2)}) %collective-permute-start.1) | collective-permute-done | bytes 131104 | tf_op jit(solution)/shard_map/ppermute | solution.py:603
  88.9 1.6 %collective-permute-done.2.refs_2_ = bf16[256,256]{1,0:T(8,128)(2,1)S(1)} collective-permute-done((bf16[256,256]{1,0:T(8,128)(2,1)S(1)}, bf16[256,256]{1,0:T(8,128)(2,1)S(1)}, u32[]{:S(2)}, u32[]{:S(2)}) %collective-permute-start.2) | collective-permute-done | bytes 131104 | tf_op jit(solution)/shard_map/ppermute | solution.py:603
  90.5 0.9 collective-permute-done.3.refs_3_
  91.4 0.7 shard_map.137
  92.2 0.0 all-to-all-done.3
  92.2 1.4 shard_map.139
  93.6 4.1 %collective-permute-start.4 = (bf16[1024,256]{1,0:T(8,128)(2,1)S(1)}, bf16[1024,256]{1,0:T(8,128)(2,1)S(1)}, u32[]{:S(2)}, u32[]{:S(2)}) collective-permute-start(bf16[1024,256]{1,0:T(8,128)(2,1)S(1)} %get-tuple-element.46), channel_id=1, source_target_pairs={{0,1},{1,0},{2,3},{3,2},{4,5},{5,4},{6,7},{7,6},{8,9},{9,8},{10,11... | collective-permute-start | bytes 1572872 | tf_op jit(solution)/shard_map/ppermute | solution.py:598
  97.7 7.0 %all-to-all-start.4 = ((bf16[32,16,128]{2,1,0:T(8,128)(2,1)}), bf16[32,16,128]{2,1,0:T(8,128)(2,1)S(1)}, u32[]{:S(2)}, u32[]{:S(2)}) async-start(bf16[32,16,128]{2,1,0:T(8,128)(2,1)} %shard_map.137), calls=%async_computation.4 | async-start | bytes 262144 | tf_op jit(solution)/shard_map/all_to_all | solution.py:593
  104.6 0.0 collective-permute-done.4.got_ref
  104.7 0.1 shard_map.140
  104.8 0.1 collective-permute-start.5
  104.9 3.3 %collective-permute-start.6 = (bf16[256,256]{1,0:T(8,128)(2,1)S(1)}, bf16[256,256]{1,0:T(8,128)(2,1)S(1)}, u32[]{:S(2)}, u32[]{:S(2)}) collective-permute-start(bf16[256,256]{1,0:T(8,128)(2,1)S(1)} %get-tuple-element.49), channel_id=1, source_target_pairs={{0,4},{1,5},{2,6},{3,7},{4,0},{5,1},{6,2},{7,3},{8,12},{9,13},{10,... | collective-permute-start | bytes 393224 | tf_op jit(solution)/shard_map/ppermute | solution.py:603
  108.2 0.0 collective-permute-start.7
  108.2 5.6 %all-to-all-done.4.tiles_ref = bf16[32,16,128]{2,1,0:T(8,128)(2,1)S(1)} async-done(((bf16[32,16,128]{2,1,0:T(8,128)(2,1)}), bf16[32,16,128]{2,1,0:T(8,128)(2,1)S(1)}, u32[]{:S(2)}, u32[]{:S(2)}) %all-to-all-start.4) | async-done | bytes 131104 | tf_op jit(solution)/shard_map/all_to_all | solution.py:593
  113.8 0.7 shard_map.138
  114.5 4.5 %all-to-all-start.5 = ((bf16[32,16,128]{2,1,0:T(8,128)(2,1)}), bf16[32,16,128]{2,1,0:T(8,128)(2,1)S(1)}, u32[]{:S(2)}, u32[]{:S(2)}) async-start(bf16[32,16,128]{2,1,0:T(8,128)(2,1)} %shard_map.138), calls=%async_computation.5 | async-start | bytes 262144 | tf_op jit(solution)/shard_map/all_to_all | solution.py:593
  119.0 0.0 collective-permute-done.5
  119.0 0.0 collective-permute-done.6
  119.0 0.0 collective-permute-done.7
  119.1 0.1 add_convert_fusion.refs_0_
  119.1 1.5 %collective-permute-start.18 = (bf16[256,256]{1,0:T(8,128)(2,1)S(1)}, bf16[256,256]{1,0:T(8,128)(2,1)S(1)}, u32[]{:S(2)}, u32[]{:S(2)}) collective-permute-start(bf16[256,256]{1,0:T(8,128)(2,1)S(1)} %add_convert_fusion.refs_0_), channel_id=1, source_target_pairs={{0,1},{1,0},{2,3},{3,2},{4,5},{5,4},{6,7},{7,6},{8,9},{9,8},{10,11... | collective-permute-start | bytes 393224 | tf_op jit(solution)/shard_map/ppermute | solution.py:598
  120.6 2.2 %collective-permute-start.17 = (bf16[256,256]{1,0:T(8,128)(2,1)S(1)}, bf16[256,256]{1,0:T(8,128)(2,1)S(1)}, u32[]{:S(2)}, u32[]{:S(2)}) collective-permute-start(bf16[256,256]{1,0:T(8,128)(2,1)S(1)} %add_convert_fusion.refs_0_), channel_id=1, source_target_pairs={{0,6},{1,7},{2,0},{3,1},{4,2},{5,3},{6,4},{7,5},{8,14},{9,15},{10,... | collective-permute-start | bytes 393224 | tf_op jit(solution)/shard_map/ppermute | solution.py:603
  122.8 0.5 collective-permute-start.16
  123.3 0.1 collective-permute-start.15
  123.4 4.8 %all-to-all-done.5.refs_0_ = bf16[32,16,128]{2,1,0:T(8,128)(2,1)S(1)} async-done(((bf16[32,16,128]{2,1,0:T(8,128)(2,1)}), bf16[32,16,128]{2,1,0:T(8,128)(2,1)S(1)}, u32[]{:S(2)}, u32[]{:S(2)}) %all-to-all-start.5) | async-done | bytes 131104 | tf_op jit(solution)/shard_map/all_to_all | solution.py:593
  128.2 2.2 %collective-permute-start.10 = (bf16[32,16,128]{2,1,0:T(8,128)(2,1)S(1)}, bf16[32,16,128]{2,1,0:T(8,128)(2,1)S(1)}, u32[]{:S(2)}, u32[]{:S(2)}) collective-permute-start(bf16[32,16,128]{2,1,0:T(8,128)(2,1)S(1)} %all-to-all-done.5.refs_0_), channel_id=1, source_target_pairs={{0,6},{1,7},{2,0},{3,1},{4,2},{5,3},{6,4},{7,5},{8,14},{9,15},{10,... | collective-permute-start | bytes 393224 | tf_op jit(solution)/shard_map/ppermute | solution.py:603
  130.3 0.0 collective-permute-done.18.refs_4_
  130.3 0.2 collective-permute-start.9
  130.6 0.0 collective-permute-done.17.refs_3_
  130.6 0.4 collective-permute-start.8
  130.9 3.2 %collective-permute-start.21 = (bf16[256,256]{1,0:T(8,128)(2,1)S(1)}, bf16[256,256]{1,0:T(8,128)(2,1)S(1)}, u32[]{:S(2)}, u32[]{:S(2)}) collective-permute-start(bf16[256,256]{1,0:T(8,128)(2,1)S(1)} %collective-permute-done.17.refs_3_), channel_id=1, source_target_pairs={{0,1},{1,0},{2,3},{3,2},{4,5},{5,4},{6,7},{7,6},{8,9},{9,8},{10,11... | collective-permute-start | bytes 393224 | tf_op jit(solution)/shard_map/ppermute | solution.py:598
  134.2 0.0 collective-permute-done.15.refs_1_
  134.2 0.1 collective-permute-start.20
  134.3 2.9 %collective-permute-start.11 = (bf16[32,16,128]{2,1,0:T(8,128)(2,1)S(1)}, bf16[32,16,128]{2,1,0:T(8,128)(2,1)S(1)}, u32[]{:S(2)}, u32[]{:S(2)}) collective-permute-start(bf16[32,16,128]{2,1,0:T(8,128)(2,1)S(1)} %all-to-all-done.5.refs_0_), channel_id=1, source_target_pairs={{0,1},{1,0},{2,3},{3,2},{4,5},{5,4},{6,7},{7,6},{8,9},{9,8},{10,11... | collective-permute-start | bytes 393224 | tf_op jit(solution)/shard_map/ppermute | solution.py:598
  137.2 0.0 collective-permute-done.9.refs_2_
  137.2 2.6 %collective-permute-start.19 = (bf16[256,256]{1,0:T(8,128)(2,1)S(1)}, bf16[256,256]{1,0:T(8,128)(2,1)S(1)}, u32[]{:S(2)}, u32[]{:S(2)}) collective-permute-start(bf16[256,256]{1,0:T(8,128)(2,1)S(1)} %collective-permute-done.15.refs_1_), channel_id=1, source_target_pairs={{0,1},{1,0},{2,3},{3,2},{4,5},{5,4},{6,7},{7,6},{8,9},{9,8},{10,11... | collective-permute-start | bytes 393224 | tf_op jit(solution)/shard_map/ppermute | solution.py:598
  139.9 0.0 collective-permute-done.8.refs_1_
  139.9 1.3 collective-permute-start.14
  141.2 0.0 collective-permute-done.21.refs_7_
  141.2 0.0 collective-permute-start.13
  141.2 0.5 collective-permute-start.12
  141.7 0.0 collective-permute-done.19.refs_5_
  141.7 1.5 %shard_map.142 = f32[2048,256]{1,0:T(8,128)} custom-call(s32[1]{0:T(128)} %bitcast.at_ref, s32[32,1,128]{2,1,0:T(1,128)S(1)} %copy-done, bf16[256,256]{1,0:T(8,128)(2,1)S(1)} %add_convert_fusion.refs_0_, bf16[256,256]{1,0:T(8,128)(2,1)S(1)} %collective-permute-done.15.refs_1_, bf16[256,256]{1,0:T(8,128)(2,1)S(1)} %collective-permute-done.16.refs_2_, ...), custom_call_target="tpu_custom_call" | custom-call | tf_op jit(solution)/shard_map/pallas_call | solution.py:96
  143.2 0.0 collective-permute-done.14.refs_7_
  143.2 0.0 collective-permute-done.13.refs_6_
  143.3 1.5 %shard_map.141 = f32[2048,256]{1,0:T(8,128)} custom-call(s32[1]{0:T(128)} %bitcast.at_ref, s32[32,1,128]{2,1,0:T(1,128)S(1)} %copy-done, bf16[32,16,128]{2,1,0:T(8,128)(2,1)S(1)} %all-to-all-done.5.refs_0_, bf16[32,16,128]{2,1,0:T(8,128)(2,1)S(1)} %collective-permute-done.8.refs_1_, bf16[32,16,128]{2,1,0:T(8,128)(2,1)S(1)} %collective-permute-done.9.refs_2_, ...), custom_call_target="tpu_custom_call" | custom-call | tf_op jit(solution)/shard_map/pallas_call | solution.py:96
  (7 shorter events, 0.0 us)
Async XLA Ops:
  27.7 16.9 %all-to-all-start.1 = ((bf16[32,32,256]{2,1,0:T(8,128)(2,1)}), bf16[32,32,256]{2,1,0:T(8,128)(2,1)S(1)}, u32[]{:S(2)}, u32[]{:S(2)}) async-start(bf16[32,32,256]{2,1,0:T(8,128)(2,1)} %bitcast.7), calls=%async_computation.1 | async-start | bytes 1048576 | tf_op jit(solution)/shard_map/all_to_all | solution.py:593
  48.3 19.7 %all-to-all-start.2 = ((bf16[8,144,256]{2,1,0:T(8,128)(2,1)}), bf16[8,144,256]{2,1,0:T(8,128)(2,1)S(1)}, u32[]{:S(2)}, u32[]{:S(2)}) async-start(bf16[8,144,256]{2,1,0:T(8,128)(2,1)} %get-tuple-element.33), calls=%async_computation.2 | async-start | bytes 1179648 | tf_op jit(solution)/shard_map/all_to_all | solution.py:593
  73.1 19.1 %copy-start = (s32[32,1,128]{2,1,0:T(1,128)S(1)}, s32[32,1,128]{2,1,0:T(1,128)}, u32[]{:S(2)}) copy-start(s32[32,1,128]{2,1,0:T(1,128)} %all_to_all.30.wanted_hbm.wanted_ref) | copy-start | bytes 49156
  73.1 19.0 %all-to-all-start.3 = ((bf16[32,32,256]{2,1,0:T(8,128)(2,1)}), bf16[32,32,256]{2,1,0:T(8,128)(2,1)S(1)}, u32[]{:S(2)}, u32[]{:S(2)}) async-start(bf16[32,32,256]{2,1,0:T(8,128)(2,1)} %bitcast.8), calls=%async_computation.3 | async-start | bytes 1048576 | tf_op jit(solution)/shard_map/all_to_all | solution.py:593
  78.1 3.0 %collective-permute-start = (bf16[1024,256]{1,0:T(8,128)(2,1)}, bf16[1024,256]{1,0:T(8,128)(2,1)S(1)}, u32[]{:S(2)}, u32[]{:S(2)}) collective-permute-start(bf16[1024,256]{1,0:T(8,128)(2,1)} %get-tuple-element.38), channel_id=1, source_target_pairs={{0,1},{1,0},{2,3},{3,2},{4,5},{5,4},{6,7},{7,6},{8,9},{9,8},{10,11... | collective-permute-start | bytes 1572872 | tf_op jit(solution)/shard_map/ppermute | solution.py:598
  82.3 6.6 %collective-permute-start.1 = (bf16[256,256]{1,0:T(8,128)(2,1)S(1)}, bf16[256,256]{1,0:T(8,128)(2,1)S(1)}, u32[]{:S(2)}, u32[]{:S(2)}) collective-permute-start(bf16[256,256]{1,0:T(8,128)(2,1)S(1)} %get-tuple-element.40), channel_id=1, source_target_pairs={{0,2},{1,3},{2,4},{3,5},{4,6},{5,7},{6,0},{7,1},{8,10},{9,11},{10,... | collective-permute-start | bytes 393224 | tf_op jit(solution)/shard_map/ppermute | solution.py:603
  82.6 7.9 %collective-permute-start.2 = (bf16[256,256]{1,0:T(8,128)(2,1)S(1)}, bf16[256,256]{1,0:T(8,128)(2,1)S(1)}, u32[]{:S(2)}, u32[]{:S(2)}) collective-permute-start(bf16[256,256]{1,0:T(8,128)(2,1)S(1)} %get-tuple-element.41), channel_id=1, source_target_pairs={{0,4},{1,5},{2,6},{3,7},{4,0},{5,1},{6,2},{7,3},{8,12},{9,13},{10,... | collective-permute-start | bytes 393224 | tf_op jit(solution)/shard_map/ppermute | solution.py:603
  84.4 7.0 %collective-permute-start.3 = (bf16[256,256]{1,0:T(8,128)(2,1)S(1)}, bf16[256,256]{1,0:T(8,128)(2,1)S(1)}, u32[]{:S(2)}, u32[]{:S(2)}) collective-permute-start(bf16[256,256]{1,0:T(8,128)(2,1)S(1)} %get-tuple-element.42), channel_id=1, source_target_pairs={{0,6},{1,7},{2,0},{3,1},{4,2},{5,3},{6,4},{7,5},{8,14},{9,15},{10,... | collective-permute-start | bytes 393224 | tf_op jit(solution)/shard_map/ppermute | solution.py:603
  93.6 11.1 %collective-permute-start.4 = (bf16[1024,256]{1,0:T(8,128)(2,1)S(1)}, bf16[1024,256]{1,0:T(8,128)(2,1)S(1)}, u32[]{:S(2)}, u32[]{:S(2)}) collective-permute-start(bf16[1024,256]{1,0:T(8,128)(2,1)S(1)} %get-tuple-element.46), channel_id=1, source_target_pairs={{0,1},{1,0},{2,3},{3,2},{4,5},{5,4},{6,7},{7,6},{8,9},{9,8},{10,11... | collective-permute-start | bytes 1572872 | tf_op jit(solution)/shard_map/ppermute | solution.py:598
  97.7 16.1 %all-to-all-start.4 = ((bf16[32,16,128]{2,1,0:T(8,128)(2,1)}), bf16[32,16,128]{2,1,0:T(8,128)(2,1)S(1)}, u32[]{:S(2)}, u32[]{:S(2)}) async-start(bf16[32,16,128]{2,1,0:T(8,128)(2,1)} %shard_map.137), calls=%async_computation.4 | async-start | bytes 262144 | tf_op jit(solution)/shard_map/all_to_all | solution.py:593
  104.8 14.3 %collective-permute-start.5 = (bf16[256,256]{1,0:T(8,128)(2,1)S(1)}, bf16[256,256]{1,0:T(8,128)(2,1)S(1)}, u32[]{:S(2)}, u32[]{:S(2)}) collective-permute-start(bf16[256,256]{1,0:T(8,128)(2,1)S(1)} %get-tuple-element.48), channel_id=1, source_target_pairs={{0,2},{1,3},{2,4},{3,5},{4,6},{5,7},{6,0},{7,1},{8,10},{9,11},{10,... | collective-permute-start | bytes 393224 | tf_op jit(solution)/shard_map/ppermute | solution.py:603
  104.9 14.1 %collective-permute-start.6 = (bf16[256,256]{1,0:T(8,128)(2,1)S(1)}, bf16[256,256]{1,0:T(8,128)(2,1)S(1)}, u32[]{:S(2)}, u32[]{:S(2)}) collective-permute-start(bf16[256,256]{1,0:T(8,128)(2,1)S(1)} %get-tuple-element.49), channel_id=1, source_target_pairs={{0,4},{1,5},{2,6},{3,7},{4,0},{5,1},{6,2},{7,3},{8,12},{9,13},{10,... | collective-permute-start | bytes 393224 | tf_op jit(solution)/shard_map/ppermute | solution.py:603
  108.2 10.9 %collective-permute-start.7 = (bf16[256,256]{1,0:T(8,128)(2,1)S(1)}, bf16[256,256]{1,0:T(8,128)(2,1)S(1)}, u32[]{:S(2)}, u32[]{:S(2)}) collective-permute-start(bf16[256,256]{1,0:T(8,128)(2,1)S(1)} %get-tuple-element.50), channel_id=1, source_target_pairs={{0,6},{1,7},{2,0},{3,1},{4,2},{5,3},{6,4},{7,5},{8,14},{9,15},{10,... | collective-permute-start | bytes 393224 | tf_op jit(solution)/shard_map/ppermute | solution.py:603
  114.5 13.7 %all-to-all-start.5 = ((bf16[32,16,128]{2,1,0:T(8,128)(2,1)}), bf16[32,16,128]{2,1,0:T(8,128)(2,1)S(1)}, u32[]{:S(2)}, u32[]{:S(2)}) async-start(bf16[32,16,128]{2,1,0:T(8,128)(2,1)} %shard_map.138), calls=%async_computation.5 | async-start | bytes 262144 | tf_op jit(solution)/shard_map/all_to_all | solution.py:593
  119.1 11.2 %collective-permute-start.18 = (bf16[256,256]{1,0:T(8,128)(2,1)S(1)}, bf16[256,256]{1,0:T(8,128)(2,1)S(1)}, u32[]{:S(2)}, u32[]{:S(2)}) collective-permute-start(bf16[256,256]{1,0:T(8,128)(2,1)S(1)} %add_convert_fusion.refs_0_), channel_id=1, source_target_pairs={{0,1},{1,0},{2,3},{3,2},{4,5},{5,4},{6,7},{7,6},{8,9},{9,8},{10,11... | collective-permute-start | bytes 393224 | tf_op jit(solution)/shard_map/ppermute | solution.py:598
  120.6 9.9 %collective-permute-start.17 = (bf16[256,256]{1,0:T(8,128)(2,1)S(1)}, bf16[256,256]{1,0:T(8,128)(2,1)S(1)}, u32[]{:S(2)}, u32[]{:S(2)}) collective-permute-start(bf16[256,256]{1,0:T(8,128)(2,1)S(1)} %add_convert_fusion.refs_0_), channel_id=1, source_target_pairs={{0,6},{1,7},{2,0},{3,1},{4,2},{5,3},{6,4},{7,5},{8,14},{9,15},{10,... | collective-permute-start | bytes 393224 | tf_op jit(solution)/shard_map/ppermute | solution.py:603
  122.8 8.1 %collective-permute-start.16 = (bf16[256,256]{1,0:T(8,128)(2,1)S(1)}, bf16[256,256]{1,0:T(8,128)(2,1)S(1)}, u32[]{:S(2)}, u32[]{:S(2)}) collective-permute-start(bf16[256,256]{1,0:T(8,128)(2,1)S(1)} %add_convert_fusion.refs_0_), channel_id=1, source_target_pairs={{0,4},{1,5},{2,6},{3,7},{4,0},{5,1},{6,2},{7,3},{8,12},{9,13},{10,... | collective-permute-start | bytes 393224 | tf_op jit(solution)/shard_map/ppermute | solution.py:603
  123.3 10.9 %collective-permute-start.15 = (bf16[256,256]{1,0:T(8,128)(2,1)S(1)}, bf16[256,256]{1,0:T(8,128)(2,1)S(1)}, u32[]{:S(2)}, u32[]{:S(2)}) collective-permute-start(bf16[256,256]{1,0:T(8,128)(2,1)S(1)} %add_convert_fusion.refs_0_), channel_id=1, source_target_pairs={{0,2},{1,3},{2,4},{3,5},{4,6},{5,7},{6,0},{7,1},{8,10},{9,11},{10,... | collective-permute-start | bytes 393224 | tf_op jit(solution)/shard_map/ppermute | solution.py:603
  128.2 6.1 %collective-permute-start.10 = (bf16[32,16,128]{2,1,0:T(8,128)(2,1)S(1)}, bf16[32,16,128]{2,1,0:T(8,128)(2,1)S(1)}, u32[]{:S(2)}, u32[]{:S(2)}) collective-permute-start(bf16[32,16,128]{2,1,0:T(8,128)(2,1)S(1)} %all-to-all-done.5.refs_0_), channel_id=1, source_target_pairs={{0,6},{1,7},{2,0},{3,1},{4,2},{5,3},{6,4},{7,5},{8,14},{9,15},{10,... | collective-permute-start | bytes 393224 | tf_op jit(solution)/shard_map/ppermute | solution.py:603
  130.3 6.9 %collective-permute-start.9 = (bf16[32,16,128]{2,1,0:T(8,128)(2,1)S(1)}, bf16[32,16,128]{2,1,0:T(8,128)(2,1)S(1)}, u32[]{:S(2)}, u32[]{:S(2)}) collective-permute-start(bf16[32,16,128]{2,1,0:T(8,128)(2,1)S(1)} %all-to-all-done.5.refs_0_), channel_id=1, source_target_pairs={{0,4},{1,5},{2,6},{3,7},{4,0},{5,1},{6,2},{7,3},{8,12},{9,13},{10,... | collective-permute-start | bytes 393224 | tf_op jit(solution)/shard_map/ppermute | solution.py:603
  130.6 9.3 %collective-permute-start.8 = (bf16[32,16,128]{2,1,0:T(8,128)(2,1)S(1)}, bf16[32,16,128]{2,1,0:T(8,128)(2,1)S(1)}, u32[]{:S(2)}, u32[]{:S(2)}) collective-permute-start(bf16[32,16,128]{2,1,0:T(8,128)(2,1)S(1)} %all-to-all-done.5.refs_0_), channel_id=1, source_target_pairs={{0,2},{1,3},{2,4},{3,5},{4,6},{5,7},{6,0},{7,1},{8,10},{9,11},{10,... | collective-permute-start | bytes 393224 | tf_op jit(solution)/shard_map/ppermute | solution.py:603
  130.9 10.2 %collective-permute-start.21 = (bf16[256,256]{1,0:T(8,128)(2,1)S(1)}, bf16[256,256]{1,0:T(8,128)(2,1)S(1)}, u32[]{:S(2)}, u32[]{:S(2)}) collective-permute-start(bf16[256,256]{1,0:T(8,128)(2,1)S(1)} %collective-permute-done.17.refs_3_), channel_id=1, source_target_pairs={{0,1},{1,0},{2,3},{3,2},{4,5},{5,4},{6,7},{7,6},{8,9},{9,8},{10,11... | collective-permute-start | bytes 393224 | tf_op jit(solution)/shard_map/ppermute | solution.py:598
  134.2 7.0 %collective-permute-start.20 = (bf16[256,256]{1,0:T(8,128)(2,1)S(1)}, bf16[256,256]{1,0:T(8,128)(2,1)S(1)}, u32[]{:S(2)}, u32[]{:S(2)}) collective-permute-start(bf16[256,256]{1,0:T(8,128)(2,1)S(1)} %collective-permute-done.16.refs_2_), channel_id=1, source_target_pairs={{0,1},{1,0},{2,3},{3,2},{4,5},{5,4},{6,7},{7,6},{8,9},{9,8},{10,11... | collective-permute-start | bytes 393224 | tf_op jit(solution)/shard_map/ppermute | solution.py:598
  134.3 8.9 %collective-permute-start.11 = (bf16[32,16,128]{2,1,0:T(8,128)(2,1)S(1)}, bf16[32,16,128]{2,1,0:T(8,128)(2,1)S(1)}, u32[]{:S(2)}, u32[]{:S(2)}) collective-permute-start(bf16[32,16,128]{2,1,0:T(8,128)(2,1)S(1)} %all-to-all-done.5.refs_0_), channel_id=1, source_target_pairs={{0,1},{1,0},{2,3},{3,2},{4,5},{5,4},{6,7},{7,6},{8,9},{9,8},{10,11... | collective-permute-start | bytes 393224 | tf_op jit(solution)/shard_map/ppermute | solution.py:598
  137.2 4.5 %collective-permute-start.19 = (bf16[256,256]{1,0:T(8,128)(2,1)S(1)}, bf16[256,256]{1,0:T(8,128)(2,1)S(1)}, u32[]{:S(2)}, u32[]{:S(2)}) collective-permute-start(bf16[256,256]{1,0:T(8,128)(2,1)S(1)} %collective-permute-done.15.refs_1_), channel_id=1, source_target_pairs={{0,1},{1,0},{2,3},{3,2},{4,5},{5,4},{6,7},{7,6},{8,9},{9,8},{10,11... | collective-permute-start | bytes 393224 | tf_op jit(solution)/shard_map/ppermute | solution.py:598
  139.9 3.4 %collective-permute-start.14 = (bf16[32,16,128]{2,1,0:T(8,128)(2,1)S(1)}, bf16[32,16,128]{2,1,0:T(8,128)(2,1)S(1)}, u32[]{:S(2)}, u32[]{:S(2)}) collective-permute-start(bf16[32,16,128]{2,1,0:T(8,128)(2,1)S(1)} %collective-permute-done.10.refs_3_), channel_id=1, source_target_pairs={{0,1},{1,0},{2,3},{3,2},{4,5},{5,4},{6,7},{7,6},{8,9},{9,8},{10,11... | collective-permute-start | bytes 393224 | tf_op jit(solution)/shard_map/ppermute | solution.py:598
  141.2 2.1 %collective-permute-start.13 = (bf16[32,16,128]{2,1,0:T(8,128)(2,1)S(1)}, bf16[32,16,128]{2,1,0:T(8,128)(2,1)S(1)}, u32[]{:S(2)}, u32[]{:S(2)}) collective-permute-start(bf16[32,16,128]{2,1,0:T(8,128)(2,1)S(1)} %collective-permute-done.9.refs_2_), channel_id=1, source_target_pairs={{0,1},{1,0},{2,3},{3,2},{4,5},{5,4},{6,7},{7,6},{8,9},{9,8},{10,11... | collective-permute-start | bytes 393224 | tf_op jit(solution)/shard_map/ppermute | solution.py:598
  141.2 2.1 %collective-permute-start.12 = (bf16[32,16,128]{2,1,0:T(8,128)(2,1)S(1)}, bf16[32,16,128]{2,1,0:T(8,128)(2,1)S(1)}, u32[]{:S(2)}, u32[]{:S(2)}) collective-permute-start(bf16[32,16,128]{2,1,0:T(8,128)(2,1)S(1)} %collective-permute-done.8.refs_1_), channel_id=1, source_target_pairs={{0,1},{1,0},{2,3},{3,2},{4,5},{5,4},{6,7},{7,6},{8,9},{9,8},{10,11... | collective-permute-start | bytes 393224 | tf_op jit(solution)/shard_map/ppermute | solution.py:598

commit v6 on v5

--- a/solution.py
+++ b/solution.py
@@ -57,10 +57,19 @@
 
 
 def tiled_match(column, width):
-    n = column.shape[0]
-    lanes = iota((n, 128), 1)
-    parts = [where_bf16(column == lanes + j * 128, 1.0) for j in range(width // 128)]
+    near = where_bf16(iota(column.shape, 1) == (column & 127), 1.0)
+    tile = (column >> 7).astype(f32).astype(bf16)
+    zero = jnp.zeros_like(near)
+    parts = [jnp.where(tile == jnp.asarray(j, bf16), near, zero) for j in range(width // 128)]
     return jnp.concatenate(parts, axis=1)
+
+
+def stacked_match(row, chunk, count):
+    row = jnp.broadcast_to(row, (chunk, row.shape[1]))
+    near = where_bf16(iota(row.shape, 0) == (row & (chunk - 1)), 1.0)
+    part = (row >> (chunk.bit_length() - 1)).astype(f32).astype(bf16)
+    zero = jnp.zeros_like(near)
+    return [jnp.where(part == jnp.asarray(j, bf16), near, zero) for j in range(count)]
 
 
 def begin(pairs, arrived, at=0):
@@ -82,7 +91,11 @@
     return pltpu.SemaphoreType.DMA((n,))
 
 
-def call(kernel, outs, args, specs=None, scratch=(), out_specs=None, limit=16):
+def in_hbm(array):
+    return pltpu.with_memory_space_constraint(array, pltpu.HBM)
+
+
+def call(kernel, outs, args, specs=None, scratch=(), out_specs=None, limit=16, aliases={}):
     out_specs = out_specs if out_specs is not None else [VM] * len(outs)
     shapes = [
         pltpu.HBM(s, d) if spec is HB else jax.ShapeDtypeStruct(s, d)
@@ -90,7 +103,7 @@
     ]
     specs = specs if specs is not None else [VM] * len(args)
     args = [
-        pltpu.with_memory_space_constraint(a, pltpu.HBM) if spec is HB else a
+        in_hbm(a) if spec is HB else a
         for a, spec in zip(args, specs, strict=True)
     ]
     return pl.pallas_call(
@@ -98,6 +111,7 @@
         out_shape=tuple(shapes),
         in_specs=specs,
         out_specs=tuple(out_specs),
+        input_output_aliases=aliases,
         scratch_shapes=list(scratch),
         compiler_params=pltpu.CompilerParams(vmem_limit_bytes=limit * 1024 * 1024),
     )(*args)
@@ -134,10 +148,10 @@
 
 
 def answer_kernel(
-    wanted_hbm, table_hbm, out_hbm, wanted_ref, table_ref, out_ref, arrived, *, per
+    wanted_ref, table_hbm, out_hbm, table_ref, out_ref, arrived, *, per
 ):
     shards, _, lanes = wanted_ref.shape
-    copies = begin(((wanted_hbm, wanted_ref), (table_hbm, table_ref)), arrived)
+    copies = begin([(table_hbm, table_ref)], arrived)
     parts = 4
     group = shards // parts
     slots = group * per
@@ -145,7 +159,6 @@
     repeat = where_bf16(quotient(iota((slots, group), 0), per) == iota((slots, group), 1), 1.0)
     own = remainder(iota((slots, lanes), 0), per) == iota((slots, lanes), 1)
     ones = jnp.ones((lanes, 128), bf16)
-    finish(copies[:1])
     wanted = jnp.where(iota((shards, lanes), 1) < per, wanted_ref[:, 0, :], 0)
     stores = []
     for j in range(parts):
@@ -155,10 +168,10 @@
         column = (16.0 * high + low).astype(i32) - 1
         hot = tiled_match(column, rows)
         if j == 0:
-            finish(copies[1:])
+            finish(copies)
         at = slice(j * slots, (j + 1) * slots)
         out_ref[at, :] = dot(hot, table_ref[...]).astype(bf16)
-        stores += begin([(out_ref.at[at, :], out_hbm.at[at, :])], arrived, 2 + j)
+        stores += begin([(out_ref.at[at, :], out_hbm.at[at, :])], arrived, 1 + j)
     finish(stores)
 
 
@@ -367,10 +380,7 @@
 def sum_half(ids, terms, owner, out_ref):
     half = out_ref.shape[0]
     chunk = min(256, half)
-    spot = iota((chunk, ids.shape[1]), 0)
-    near = ids - owner * half
-    for j in range(half // chunk):
-        hot = where_bf16(spot + j * chunk == near, 1.0)
+    for j, hot in enumerate(stacked_match(ids - owner * half, chunk, half // chunk)):
         out_ref[j * chunk : (j + 1) * chunk, :] = dot(hot, terms).astype(out_ref.dtype)
 
 
@@ -486,19 +496,15 @@
     quot_terms = jnp.concatenate(quot_terms, axis=0)
     slot = jnp.concatenate([slot_ref[u : u + 1, :] for u in range(users)], axis=1)
     ids = jnp.concatenate([ids_ref[u : u + 1, :] for u in range(users)], axis=1)
-    spot = iota((block, users * block), 0)
     n = 11 + 2 * users
-    for j in range(slots // block):
-        hot = where_bf16(spot + j * block == slot, 1.0)
+    for j, hot in enumerate(stacked_match(slot, block, slots // block)):
         at = slice(j * block, (j + 1) * block)
         rem_send_ref[at, :] = dot(hot, rem_terms).astype(bf16)
         copies += begin([(rem_send_ref.at[at, :], rem_send_hbm.at[at, :])], arrived, n + j)
     n += slots // block
     for ref, hbm, owner in ((give_ref, give_hbm, 1 - me % 2), (keep_ref, keep_hbm, me % 2)):
         half = ref.shape[0]
-        near = ids - owner * half
-        for j in range(half // block):
-            hot = where_bf16(spot + j * block == near, 1.0)
+        for j, hot in enumerate(stacked_match(ids - owner * half, block, half // block)):
             at = slice(j * block, (j + 1) * block)
             ref[at, :] = dot(hot, quot_terms).astype(bf16)
             copies += begin([(ref.at[at, :], hbm.at[at, :])], arrived, n)
@@ -559,33 +565,29 @@
         out_ref[i] = total
 
 
-def place_kernel(at_ref, wanted_ref, *refs, per, total):
+def place_kernel(at_ref, wanted_ref, *refs, chips, per, total, other):
     out_hbm, out_ref, arrived = refs[-3:]
-    chunks = refs[:-3]
+    chunks = refs[:chips]
     copies = []
-    chips = len(chunks) // 2
     _, rows, width = out_ref.shape
     shards, _, lanes = wanted_ref.shape
     counted = jnp.where(iota((shards, lanes), 1) == per, wanted_ref[:, 0, :], 0)
     ratio = total / jnp.sum(counted.astype(f32), axis=(0, 1), keepdims=True)
     chip, core = at_ref[0] // 2, at_ref[0] % 2
-    for other in range(2):
-        half = core + other - 2 * core * other
-        for d in range(chips):
-            spot = half * chips + lax.rem(chip + chips - d, chips)
-            base = pl.multiple_of(spot * rows, rows)
-            chunk = chunks[other * chips + d]
-            n = other * chips + d
-            if len(chunk.shape) == 2:
-                out_ref[n] = ratio * chunk[...].astype(f32)
-            else:
-                part = chunk.shape[1]
-                for i in range(shards):
-                    across = i % (width // 128) * 128
-                    down = i // (width // 128) * part
-                    tile = ratio * chunk[i].astype(f32)
-                    out_ref[n, down : down + part, across : across + 128] = tile
-            copies += begin([(out_ref.at[n], out_hbm.at[pl.ds(base, rows), :])], arrived, n)
+    half = core + other - 2 * core * other
+    for d, chunk in enumerate(chunks):
+        spot = half * chips + lax.rem(chip + chips - d, chips)
+        base = pl.multiple_of(spot * rows, rows)
+        if len(chunk.shape) == 2:
+            out_ref[d] = ratio * chunk[...].astype(f32)
+        else:
+            part = chunk.shape[1]
+            for i in range(shards):
+                across = i % (width // 128) * 128
+                down = i // (width // 128) * part
+                tile = ratio * chunk[i].astype(f32)
+                out_ref[d, down : down + part, across : across + 128] = tile
+        copies += begin([(out_ref.at[d], out_hbm.at[pl.ds(base, rows), :])], arrived, d)
     finish(copies)
 
 
@@ -621,13 +623,15 @@
     return [chunk] + [to_chip(chunk, d) for d in range(1, chips)]
 
 
-def placed(at, wanted, chunks, rows, width, per, total):
-    kernel = functools.partial(place_kernel, per=per, total=total)
-    specs = [SM] + [VM] * (1 + len(chunks))
-    n = len(chunks)
-    scratch = [pltpu.VMEM((n, rows // n, width), f32), dma(n)]
-    args = (at, wanted, *chunks)
-    (out,) = call(kernel, [((rows, width), f32)], args, specs, scratch, [HB])
+def place(at, wanted, chunks, rows, width, per, total, out=None):
+    chips = len(chunks)
+    scratch = [pltpu.VMEM((chips, rows // (2 * chips), width), f32), dma(chips)]
+    other = 0 if out is None else 1
+    kernel = functools.partial(place_kernel, chips=chips, per=per, total=total, other=other)
+    args, specs, aliases = (at, wanted, *chunks), [SM] + [VM] * (1 + chips), {}
+    if other:
+        args, specs, aliases = args + (out,), specs + [HB], {len(args): 0}
+    (out,) = call(kernel, [((rows, width), f32)], args, specs, scratch, [HB], aliases=aliases)
     return out
 
 
@@ -663,11 +667,11 @@
     requests, slot = call(
         functools.partial(request_kernel, rows_own=rows_own, cap=cap),
         [((shards, 1, lanes), i32), ((8, block), i32)],
-        (lengths, rem_ids),
+        (in_hbm(lengths), in_hbm(rem_ids)),
         [SM, VM],
         [pltpu.VMEM((8, block), i32), dma(1)],
         [VM, HB],
-        FULL,
+        MOST,
     )
     wanted = exchange(requests, "user")
     quot_emb, dmixed, wide = call(
@@ -687,15 +691,14 @@
         functools.partial(answer_kernel, per=per),
         [((slots, width), bf16)],
         (wanted, rem_table),
-        [HB, HB],
+        [VM, HB],
         [
-            pltpu.VMEM((shards, 1, lanes), i32),
             pltpu.VMEM((rows_own, width), bf16),
             pltpu.VMEM((slots, width), bf16),
-            dma(6),
+            dma(5),
         ],
         [HB],
-        FULL,
+        MOST,
     )
     answered = exchange(found.reshape(shards, per, width), "user").reshape(slots, width)
     rem_emb, payload = call(
@@ -760,11 +763,14 @@
     rem_mine = along_chips(rem_sum)
     quot_tiles, _ = lax.optimization_barrier((quot_tiles, rem_sum))
     total = float(users * shards * block * peers)
-    rem_chunks = rem_mine + [to_core(c) for c in rem_mine]
-    rem_grad = placed(at, wanted, rem_chunks, rows_own, width, per, total)
+    rem_grad = place(at, wanted, rem_mine, rows_own, width, per, total)
     quot_mine = along_chips(quot_tiles)
-    quot_chunks = quot_mine + [to_core(c) for c in quot_mine]
-    quot_grad = placed(at, wanted, quot_chunks, rows_all, width, per, total)
+    rem_theirs = [to_core(c) for c in rem_mine]
+    *quot_mine, rem_grad = lax.optimization_barrier((*quot_mine, rem_grad))
+    rem_grad = place(at, wanted, rem_theirs, rows_own, width, per, total, rem_grad)
+    quot_theirs = [to_core(c) for c in quot_mine]
+    quot_grad = place(at, wanted, quot_mine, rows_all, width, per, total)
+    quot_grad = place(at, wanted, quot_theirs, rows_all, width, per, total, quot_grad)
     return (output, quot_grad, rem_grad)
 
 

time: 146 us -> 145 us (level)
  starting transfers between devices: 59.2 us -> 56.8 us
    ppermute x10, starting transfers between devices: 17.5 us -> 15 us  [to_core(): return lax.ppermute(array, 'hist', [(i, i ^ 1) for i in range(peers)])]
    pallas_call x13 -> x15, Pallas kernels: 31.8 us -> 32.7 us  [call(): pl.pallas_call(kernel, out_shape=tuple(shapes), in_specs=specs, out_specs...]
  transfers between devices with their start and end apart: 27 -> 27, of which waited for: 8 -> 8; matrix products, arithmetic and copies ran while one was open for 0% -> 0% of each run, Pallas kernels for 9% -> 11%
where the time goes in v6:
time: 145 us; the launch traced here: 144 us
  starting transfers between devices  56.8 us (39%)
  waiting for transfers between devices  33.5 us (23%)
  Pallas kernels  32.7 us (23%)
  blocking collectives  20.5 us (14%)
    pallas_call x15, Pallas kernels, call(): pl.pallas_call(kernel, out_shape=tuple(shapes), in_specs=specs, out_specs...  32.7 us
    all_to_all x5, starting transfers between devices, exchange(): return lax.all_to_all(array, axis, split_axis=0, concat_axis=0, tiled=True)  29.9 us
    all_to_all x5, waiting for transfers between devices, exchange(): return lax.all_to_all(array, axis, split_axis=0, concat_axis=0, tiled=True)  25.4 us
    all_to_all x1, blocking collectives, exchange(): return lax.all_to_all(array, axis, split_axis=0, concat_axis=0, tiled=True)  20.5 us
    ppermute x10, starting transfers between devices, to_core(): return lax.ppermute(array, 'hist', [(i, i ^ 1) for i in range(peers)])  15 us
    ppermute x12, starting transfers between devices, to_chip(): lax.ppermute(array, 'hist', [(i, (i + 2 * steps) % peers) for i in range(...  11.9 us
    ppermute x12, waiting for transfers between devices, to_chip(): lax.ppermute(array, 'hist', [(i, (i + 2 * steps) % peers) for i in range(...  6.33 us
  transfers between devices with their start and end apart: 27, of which 8 were waited for; matrix products, arithmetic and copies ran while one was open for 0% of the time, Pallas kernels for 11%

profile of v6, /device:TPU:1, one launch (start us, length us, event | category | flops | bytes accessed | tf_op | source)
XLA Modules:
  0.0 144.5 jit_solution(5523612736657289939)
XLA Ops:
  0.6 1.7 %shard_map.130 = (s32[32,1,128]{2,1,0:T(1,128)S(1)}, s32[8,256]{1,0:T(8,128)}) custom-call(s32[2]{0:T(128)} %len_ref.3, s32[2,256]{1,0:T(2,128)} %ids_ref.2), custom_call_target="tpu_custom_call" | custom-call | tf_op jit(solution)/shard_map/pallas_call | solution.py:109
  2.3 20.5 %all_to_all.30.wanted_ref = s32[32,1,128]{2,1,0:T(1,128)S(1)} all-to-all(s32[32,1,128]{2,1,0:T(1,128)S(1)} %get-tuple-element.34), channel_id=1, replica_groups=mesh['user'=32,'hist'=8] {'user'}, dimensions={0} | all-to-all | bytes 32768 | tf_op jit(solution)/shard_map/all_to_all | solution.py:595
  22.8 3.9 %shard_map.131 = bf16[1024,256]{1,0:T(8,128)(2,1)} custom-call(s32[32,1,128]{2,1,0:T(1,128)S(1)} %all_to_all.30.wanted_ref, bf16[2048,256]{1,0:T(8,128)(2,1)} %table_hbm.1), custom_call_target="tpu_custom_call" | custom-call | tf_op jit(solution)/shard_map/pallas_call | solution.py:109
  26.7 3.9 %all-to-all-start.1 = ((bf16[32,32,256]{2,1,0:T(8,128)(2,1)}), bf16[32,32,256]{2,1,0:T(8,128)(2,1)S(1)}, u32[]{:S(2)}, u32[]{:S(2)}) async-start(bf16[32,32,256]{2,1,0:T(8,128)(2,1)} %bitcast.7), calls=%async_computation.1 | async-start | bytes 1048576 | tf_op jit(solution)/shard_map/all_to_all | solution.py:595
  30.6 3.9 %shard_map.132 = (bf16[512,256]{1,0:T(8,128)(2,1)}, bf16[512,256]{1,0:T(8,128)(2,1)}, f32[512,256]{1,0:T(8,128)}) custom-call(s32[2]{0:T(128)} %len_ref.3, s32[1]{0:T(128)} %bitcast.at_ref, s32[2,256]{1,0:T(2,128)} %ids_hbm.1, bf16[2048,256]{1,0:T(8,128)(2,1)} %table_ref.1, bf16[2,256,256]{2,1,0:T(8,128)(2,1)} %cot_ref.1, f32[2,4,256]{2,1,0:T(4,128)} %decay_ref.3, ...), custom_call_target="tpu_custom_call" | custom-call | tf_op jit(solution)/shard_map/pallas_call | solution.py:109
  34.5 9.1 %all-to-all-done.1 = bf16[32,32,256]{2,1,0:T(8,128)(2,1)S(1)} async-done(((bf16[32,32,256]{2,1,0:T(8,128)(2,1)}), bf16[32,32,256]{2,1,0:T(8,128)(2,1)S(1)}, u32[]{:S(2)}, u32[]{:S(2)}) %all-to-all-start.1) | async-done | bytes 524320 | tf_op jit(solution)/shard_map/all_to_all | solution.py:595
  43.6 3.7 %shard_map.133 = (bf16[512,256]{1,0:T(8,128)(2,1)}, bf16[8,144,256]{2,1,0:T(8,128)(2,1)}) custom-call(s32[1]{0:T(128)} %bitcast.at_ref, s32[8,256]{1,0:T(8,128)} %get-tuple-element.33.slot_hbm, bf16[1024,256]{1,0:T(8,128)(2,1)S(1)} %bitcast.5, bf16[512,256]{1,0:T(8,128)(2,1)} %get-tuple-element.35.quot_hbm.quot_ref, bf16[256,256]{1,0:T(8,128)(2,1)} %wq_hbm.3, ...), custom_call_target="tpu_custom_call" | custom-call | tf_op jit(solution)/shard_map/pallas_call | solution.py:109
  47.3 9.5 %all-to-all-start.2 = ((bf16[8,144,256]{2,1,0:T(8,128)(2,1)}), bf16[8,144,256]{2,1,0:T(8,128)(2,1)S(1)}, u32[]{:S(2)}, u32[]{:S(2)}) async-start(bf16[8,144,256]{2,1,0:T(8,128)(2,1)} %get-tuple-element.38), calls=%async_computation.2 | async-start | bytes 1179648 | tf_op jit(solution)/shard_map/all_to_all | solution.py:595
  56.8 5.7 %shard_map.134.within_hbm = f32[4,512,256]{2,1,0:T(8,128)} custom-call(bf16[512,256]{1,0:T(8,128)(2,1)} %get-tuple-element.35.quot_hbm.quot_ref, bf16[512,256]{1,0:T(8,128)(2,1)} %get-tuple-element.39.rem_ref.rem_hbm, bf16[512,256]{1,0:T(8,128)(2,1)} %get-tuple-element.37.dmixed_hbm.dmixed_ref, f32[2,4,256]{2,1,0:T(4,128)} %decay_ref.3, ...), custom_call_target="tpu_custom_call" | custom-call | tf_op jit(solution)/shard_map/pallas_call | solution.py:109
  62.5 4.5 %all-to-all-done.2.payload_ref = bf16[8,144,256]{2,1,0:T(8,128)(2,1)S(1)} async-done(((bf16[8,144,256]{2,1,0:T(8,128)(2,1)}), bf16[8,144,256]{2,1,0:T(8,128)(2,1)S(1)}, u32[]{:S(2)}, u32[]{:S(2)}) %all-to-all-start.2) | async-done | bytes 589856 | tf_op jit(solution)/shard_map/all_to_all | solution.py:595
  67.0 5.1 %shard_map.135 = (bf16[2,256,256]{2,1,0:T(8,128)(2,1)}, bf16[1024,256]{1,0:T(8,128)(2,1)}, bf16[1024,256]{1,0:T(8,128)(2,1)}, bf16[1024,256]{1,0:T(8,128)(2,1)}) custom-call(s32[1]{0:T(128)} %bitcast.at_ref, bf16[8,144,256]{2,1,0:T(8,128)(2,1)S(1)} %all-to-all-done.2.payload_ref, f32[4,512,256]{2,1,0:T(8,128)} %shard_map.134.within_hbm, ...), custom_call_target="tpu_custom_call" | custom-call | tf_op jit(solution)/shard_map/pallas_call | solution.py:109
  72.1 5.0 %all-to-all-start.3 = ((bf16[32,32,256]{2,1,0:T(8,128)(2,1)}), bf16[32,32,256]{2,1,0:T(8,128)(2,1)S(1)}, u32[]{:S(2)}, u32[]{:S(2)}) async-start(bf16[32,32,256]{2,1,0:T(8,128)(2,1)} %bitcast.8), calls=%async_computation.3 | async-start | bytes 1048576 | tf_op jit(solution)/shard_map/all_to_all | solution.py:595
  77.1 1.2 collective-permute-start
  78.4 1.7 %collective-permute-done.got_ref = bf16[1024,256]{1,0:T(8,128)(2,1)S(1)} collective-permute-done((bf16[1024,256]{1,0:T(8,128)(2,1)}, bf16[1024,256]{1,0:T(8,128)(2,1)S(1)}, u32[]{:S(2)}, u32[]{:S(2)}) %collective-permute-start) | collective-permute-done | bytes 524320 | tf_op jit(solution)/shard_map/ppermute | solution.py:600
  80.1 1.2 shard_map.136
  81.3 0.4 collective-permute-start.1
  81.6 1.8 %collective-permute-start.2 = (bf16[256,256]{1,0:T(8,128)(2,1)S(1)}, bf16[256,256]{1,0:T(8,128)(2,1)S(1)}, u32[]{:S(2)}, u32[]{:S(2)}) collective-permute-start(bf16[256,256]{1,0:T(8,128)(2,1)S(1)} %get-tuple-element.46), channel_id=1, source_target_pairs={{0,4},{1,5},{2,6},{3,7},{4,0},{5,1},{6,2},{7,3},{8,12},{9,13},{10,... | collective-permute-start | bytes 393224 | tf_op jit(solution)/shard_map/ppermute | solution.py:605
  83.4 0.7 collective-permute-start.3
  84.1 3.7 %collective-permute-done.1.refs_1_ = bf16[256,256]{1,0:T(8,128)(2,1)S(1)} collective-permute-done((bf16[256,256]{1,0:T(8,128)(2,1)S(1)}, bf16[256,256]{1,0:T(8,128)(2,1)S(1)}, u32[]{:S(2)}, u32[]{:S(2)}) %collective-permute-start.1) | collective-permute-done | bytes 131104 | tf_op jit(solution)/shard_map/ppermute | solution.py:605
  87.9 1.7 %collective-permute-done.2.refs_2_ = bf16[256,256]{1,0:T(8,128)(2,1)S(1)} collective-permute-done((bf16[256,256]{1,0:T(8,128)(2,1)S(1)}, bf16[256,256]{1,0:T(8,128)(2,1)S(1)}, u32[]{:S(2)}, u32[]{:S(2)}) %collective-permute-start.2) | collective-permute-done | bytes 131104 | tf_op jit(solution)/shard_map/ppermute | solution.py:605
  89.5 0.9 collective-permute-done.3.refs_3_
  90.4 0.7 shard_map.137
  91.2 0.0 all-to-all-done.3
  91.2 1.4 shard_map.139
  92.6 4.1 %collective-permute-start.4 = (bf16[1024,256]{1,0:T(8,128)(2,1)S(1)}, bf16[1024,256]{1,0:T(8,128)(2,1)S(1)}, u32[]{:S(2)}, u32[]{:S(2)}) collective-permute-start(bf16[1024,256]{1,0:T(8,128)(2,1)S(1)} %get-tuple-element.51), channel_id=1, source_target_pairs={{0,1},{1,0},{2,3},{3,2},{4,5},{5,4},{6,7},{7,6},{8,9},{9,8},{10,11... | collective-permute-start | bytes 1572872 | tf_op jit(solution)/shard_map/ppermute | solution.py:600
  96.7 7.0 %all-to-all-start.4 = ((bf16[32,16,128]{2,1,0:T(8,128)(2,1)}), bf16[32,16,128]{2,1,0:T(8,128)(2,1)S(1)}, u32[]{:S(2)}, u32[]{:S(2)}) async-start(bf16[32,16,128]{2,1,0:T(8,128)(2,1)} %shard_map.137), calls=%async_computation.4 | async-start | bytes 262144 | tf_op jit(solution)/shard_map/all_to_all | solution.py:595
  103.7 0.0 collective-permute-done.4.got_ref
  103.7 0.1 shard_map.140
  103.8 0.1 collective-permute-start.5
  103.9 3.3 %collective-permute-start.6 = (bf16[256,256]{1,0:T(8,128)(2,1)S(1)}, bf16[256,256]{1,0:T(8,128)(2,1)S(1)}, u32[]{:S(2)}, u32[]{:S(2)}) collective-permute-start(bf16[256,256]{1,0:T(8,128)(2,1)S(1)} %get-tuple-element.54), channel_id=1, source_target_pairs={{0,4},{1,5},{2,6},{3,7},{4,0},{5,1},{6,2},{7,3},{8,12},{9,13},{10,... | collective-permute-start | bytes 393224 | tf_op jit(solution)/shard_map/ppermute | solution.py:605
  107.2 0.0 collective-permute-start.7
  107.2 5.6 %all-to-all-done.4.tiles_ref = bf16[32,16,128]{2,1,0:T(8,128)(2,1)S(1)} async-done(((bf16[32,16,128]{2,1,0:T(8,128)(2,1)}), bf16[32,16,128]{2,1,0:T(8,128)(2,1)S(1)}, u32[]{:S(2)}, u32[]{:S(2)}) %all-to-all-start.4) | async-done | bytes 131104 | tf_op jit(solution)/shard_map/all_to_all | solution.py:595
  112.8 0.7 shard_map.138
  113.5 4.5 %all-to-all-start.5 = ((bf16[32,16,128]{2,1,0:T(8,128)(2,1)}), bf16[32,16,128]{2,1,0:T(8,128)(2,1)S(1)}, u32[]{:S(2)}, u32[]{:S(2)}) async-start(bf16[32,16,128]{2,1,0:T(8,128)(2,1)} %shard_map.138), calls=%async_computation.5 | async-start | bytes 262144 | tf_op jit(solution)/shard_map/all_to_all | solution.py:595
  118.1 0.0 collective-permute-done.6
  118.1 0.0 collective-permute-done.7
  118.1 0.1 add_convert_fusion.refs_0_
  118.2 2.2 %collective-permute-start.13 = (bf16[256,256]{1,0:T(8,128)(2,1)S(1)}, bf16[256,256]{1,0:T(8,128)(2,1)S(1)}, u32[]{:S(2)}, u32[]{:S(2)}) collective-permute-start(bf16[256,256]{1,0:T(8,128)(2,1)S(1)} %add_convert_fusion.refs_0_), channel_id=1, source_target_pairs={{0,6},{1,7},{2,0},{3,1},{4,2},{5,3},{6,4},{7,5},{8,14},{9,15},{10,... | collective-permute-start | bytes 393224 | tf_op jit(solution)/shard_map/ppermute | solution.py:605
  120.4 0.2 collective-permute-start.12
  120.6 0.5 collective-permute-start.11
  121.1 6.1 %all-to-all-done.5.refs_0_ = bf16[32,16,128]{2,1,0:T(8,128)(2,1)S(1)} async-done(((bf16[32,16,128]{2,1,0:T(8,128)(2,1)}), bf16[32,16,128]{2,1,0:T(8,128)(2,1)S(1)}, u32[]{:S(2)}, u32[]{:S(2)}) %all-to-all-start.5) | async-done | bytes 131104 | tf_op jit(solution)/shard_map/all_to_all | solution.py:595
  127.2 2.1 %collective-permute-start.10 = (bf16[32,16,128]{2,1,0:T(8,128)(2,1)S(1)}, bf16[32,16,128]{2,1,0:T(8,128)(2,1)S(1)}, u32[]{:S(2)}, u32[]{:S(2)}) collective-permute-start(bf16[32,16,128]{2,1,0:T(8,128)(2,1)S(1)} %all-to-all-done.5.refs_0_), channel_id=1, source_target_pairs={{0,6},{1,7},{2,0},{3,1},{4,2},{5,3},{6,4},{7,5},{8,14},{9,15},{10,... | collective-permute-start | bytes 393224 | tf_op jit(solution)/shard_map/ppermute | solution.py:605
  129.3 0.2 collective-permute-start.9
  129.6 0.0 collective-permute-done.13.refs_3_
  129.6 0.4 collective-permute-start.8
  129.9 3.5 %collective-permute-start.18 = (bf16[256,256]{1,0:T(8,128)(2,1)S(1)}, bf16[256,256]{1,0:T(8,128)(2,1)S(1)}, u32[]{:S(2)}, u32[]{:S(2)}) collective-permute-start(bf16[256,256]{1,0:T(8,128)(2,1)S(1)} %add_convert_fusion.refs_0_), channel_id=1, source_target_pairs={{0,1},{1,0},{2,3},{3,2},{4,5},{5,4},{6,7},{7,6},{8,9},{9,8},{10,11... | collective-permute-start | bytes 393224 | tf_op jit(solution)/shard_map/ppermute | solution.py:600
  133.4 0.0 collective-permute-done.11.refs_1_
  133.4 0.1 collective-permute-start.21
  133.5 2.7 %collective-permute-start.20 = (bf16[256,256]{1,0:T(8,128)(2,1)S(1)}, bf16[256,256]{1,0:T(8,128)(2,1)S(1)}, u32[]{:S(2)}, u32[]{:S(2)}) collective-permute-start(bf16[256,256]{1,0:T(8,128)(2,1)S(1)} %collective-permute-done.12.refs_2_), channel_id=1, source_target_pairs={{0,1},{1,0},{2,3},{3,2},{4,5},{5,4},{6,7},{7,6},{8,9},{9,8},{10,11... | collective-permute-start | bytes 393224 | tf_op jit(solution)/shard_map/ppermute | solution.py:600
  136.2 1.1 shard_map.141.refs_4_
  137.4 1.5 %collective-permute-start.19 = (bf16[256,256]{1,0:T(8,128)(2,1)S(1)}, bf16[256,256]{1,0:T(8,128)(2,1)S(1)}, u32[]{:S(2)}, u32[]{:S(2)}) collective-permute-start(bf16[256,256]{1,0:T(8,128)(2,1)S(1)} %collective-permute-done.11.refs_1_), channel_id=1, source_target_pairs={{0,1},{1,0},{2,3},{3,2},{4,5},{5,4},{6,7},{7,6},{8,9},{9,8},{10,11... | collective-permute-start | bytes 393224 | tf_op jit(solution)/shard_map/ppermute | solution.py:600
  138.9 0.0 collective-permute-done.8.refs_1_
  138.9 1.3 collective-permute-start.14
  140.2 0.0 collective-permute-done.18.refs_0_
  140.2 0.0 collective-permute-start.15
  140.2 0.0 collective-permute-done.21.refs_3_
  140.2 0.5 collective-permute-start.16
  140.7 0.0 collective-permute-done.20.refs_2_
  140.7 0.1 collective-permute-start.17
  140.8 1.1 shard_map.142.refs_4_
  141.9 0.0 collective-permute-done.19.refs_1_
  141.9 1.2 shard_map.144
  143.1 0.0 collective-permute-done.15.refs_1_
  143.1 1.2 shard_map.143
  (7 shorter events, 0.0 us)
Async XLA Ops:
  26.7 16.9 %all-to-all-start.1 = ((bf16[32,32,256]{2,1,0:T(8,128)(2,1)}), bf16[32,32,256]{2,1,0:T(8,128)(2,1)S(1)}, u32[]{:S(2)}, u32[]{:S(2)}) async-start(bf16[32,32,256]{2,1,0:T(8,128)(2,1)} %bitcast.7), calls=%async_computation.1 | async-start | bytes 1048576 | tf_op jit(solution)/shard_map/all_to_all | solution.py:595
  47.3 19.7 %all-to-all-start.2 = ((bf16[8,144,256]{2,1,0:T(8,128)(2,1)}), bf16[8,144,256]{2,1,0:T(8,128)(2,1)S(1)}, u32[]{:S(2)}, u32[]{:S(2)}) async-start(bf16[8,144,256]{2,1,0:T(8,128)(2,1)} %get-tuple-element.38), calls=%async_computation.2 | async-start | bytes 1179648 | tf_op jit(solution)/shard_map/all_to_all | solution.py:595
  72.1 19.1 %all-to-all-start.3 = ((bf16[32,32,256]{2,1,0:T(8,128)(2,1)}), bf16[32,32,256]{2,1,0:T(8,128)(2,1)S(1)}, u32[]{:S(2)}, u32[]{:S(2)}) async-start(bf16[32,32,256]{2,1,0:T(8,128)(2,1)} %bitcast.8), calls=%async_computation.3 | async-start | bytes 1048576 | tf_op jit(solution)/shard_map/all_to_all | solution.py:595
  77.1 3.0 %collective-permute-start = (bf16[1024,256]{1,0:T(8,128)(2,1)}, bf16[1024,256]{1,0:T(8,128)(2,1)S(1)}, u32[]{:S(2)}, u32[]{:S(2)}) collective-permute-start(bf16[1024,256]{1,0:T(8,128)(2,1)} %get-tuple-element.43), channel_id=1, source_target_pairs={{0,1},{1,0},{2,3},{3,2},{4,5},{5,4},{6,7},{7,6},{8,9},{9,8},{10,11... | collective-permute-start | bytes 1572872 | tf_op jit(solution)/shard_map/ppermute | solution.py:600
  81.3 6.6 %collective-permute-start.1 = (bf16[256,256]{1,0:T(8,128)(2,1)S(1)}, bf16[256,256]{1,0:T(8,128)(2,1)S(1)}, u32[]{:S(2)}, u32[]{:S(2)}) collective-permute-start(bf16[256,256]{1,0:T(8,128)(2,1)S(1)} %get-tuple-element.45), channel_id=1, source_target_pairs={{0,2},{1,3},{2,4},{3,5},{4,6},{5,7},{6,0},{7,1},{8,10},{9,11},{10,... | collective-permute-start | bytes 393224 | tf_op jit(solution)/shard_map/ppermute | solution.py:605
  81.6 7.9 %collective-permute-start.2 = (bf16[256,256]{1,0:T(8,128)(2,1)S(1)}, bf16[256,256]{1,0:T(8,128)(2,1)S(1)}, u32[]{:S(2)}, u32[]{:S(2)}) collective-permute-start(bf16[256,256]{1,0:T(8,128)(2,1)S(1)} %get-tuple-element.46), channel_id=1, source_target_pairs={{0,4},{1,5},{2,6},{3,7},{4,0},{5,1},{6,2},{7,3},{8,12},{9,13},{10,... | collective-permute-start | bytes 393224 | tf_op jit(solution)/shard_map/ppermute | solution.py:605
  83.4 7.0 %collective-permute-start.3 = (bf16[256,256]{1,0:T(8,128)(2,1)S(1)}, bf16[256,256]{1,0:T(8,128)(2,1)S(1)}, u32[]{:S(2)}, u32[]{:S(2)}) collective-permute-start(bf16[256,256]{1,0:T(8,128)(2,1)S(1)} %get-tuple-element.47), channel_id=1, source_target_pairs={{0,6},{1,7},{2,0},{3,1},{4,2},{5,3},{6,4},{7,5},{8,14},{9,15},{10,... | collective-permute-start | bytes 393224 | tf_op jit(solution)/shard_map/ppermute | solution.py:605
  92.6 11.1 %collective-permute-start.4 = (bf16[1024,256]{1,0:T(8,128)(2,1)S(1)}, bf16[1024,256]{1,0:T(8,128)(2,1)S(1)}, u32[]{:S(2)}, u32[]{:S(2)}) collective-permute-start(bf16[1024,256]{1,0:T(8,128)(2,1)S(1)} %get-tuple-element.51), channel_id=1, source_target_pairs={{0,1},{1,0},{2,3},{3,2},{4,5},{5,4},{6,7},{7,6},{8,9},{9,8},{10,11... | collective-permute-start | bytes 1572872 | tf_op jit(solution)/shard_map/ppermute | solution.py:600
  96.7 16.1 %all-to-all-start.4 = ((bf16[32,16,128]{2,1,0:T(8,128)(2,1)}), bf16[32,16,128]{2,1,0:T(8,128)(2,1)S(1)}, u32[]{:S(2)}, u32[]{:S(2)}) async-start(bf16[32,16,128]{2,1,0:T(8,128)(2,1)} %shard_map.137), calls=%async_computation.4 | async-start | bytes 262144 | tf_op jit(solution)/shard_map/all_to_all | solution.py:595
  103.8 14.3 %collective-permute-start.5 = (bf16[256,256]{1,0:T(8,128)(2,1)S(1)}, bf16[256,256]{1,0:T(8,128)(2,1)S(1)}, u32[]{:S(2)}, u32[]{:S(2)}) collective-permute-start(bf16[256,256]{1,0:T(8,128)(2,1)S(1)} %get-tuple-element.53), channel_id=1, source_target_pairs={{0,2},{1,3},{2,4},{3,5},{4,6},{5,7},{6,0},{7,1},{8,10},{9,11},{10,... | collective-permute-start | bytes 393224 | tf_op jit(solution)/shard_map/ppermute | solution.py:605
  103.9 14.1 %collective-permute-start.6 = (bf16[256,256]{1,0:T(8,128)(2,1)S(1)}, bf16[256,256]{1,0:T(8,128)(2,1)S(1)}, u32[]{:S(2)}, u32[]{:S(2)}) collective-permute-start(bf16[256,256]{1,0:T(8,128)(2,1)S(1)} %get-tuple-element.54), channel_id=1, source_target_pairs={{0,4},{1,5},{2,6},{3,7},{4,0},{5,1},{6,2},{7,3},{8,12},{9,13},{10,... | collective-permute-start | bytes 393224 | tf_op jit(solution)/shard_map/ppermute | solution.py:605
  107.2 10.9 %collective-permute-start.7 = (bf16[256,256]{1,0:T(8,128)(2,1)S(1)}, bf16[256,256]{1,0:T(8,128)(2,1)S(1)}, u32[]{:S(2)}, u32[]{:S(2)}) collective-permute-start(bf16[256,256]{1,0:T(8,128)(2,1)S(1)} %get-tuple-element.55), channel_id=1, source_target_pairs={{0,6},{1,7},{2,0},{3,1},{4,2},{5,3},{6,4},{7,5},{8,14},{9,15},{10,... | collective-permute-start | bytes 393224 | tf_op jit(solution)/shard_map/ppermute | solution.py:605
  113.5 13.7 %all-to-all-start.5 = ((bf16[32,16,128]{2,1,0:T(8,128)(2,1)}), bf16[32,16,128]{2,1,0:T(8,128)(2,1)S(1)}, u32[]{:S(2)}, u32[]{:S(2)}) async-start(bf16[32,16,128]{2,1,0:T(8,128)(2,1)} %shard_map.138), calls=%async_computation.5 | async-start | bytes 262144 | tf_op jit(solution)/shard_map/all_to_all | solution.py:595
  118.2 11.4 %collective-permute-start.13 = (bf16[256,256]{1,0:T(8,128)(2,1)S(1)}, bf16[256,256]{1,0:T(8,128)(2,1)S(1)}, u32[]{:S(2)}, u32[]{:S(2)}) collective-permute-start(bf16[256,256]{1,0:T(8,128)(2,1)S(1)} %add_convert_fusion.refs_0_), channel_id=1, source_target_pairs={{0,6},{1,7},{2,0},{3,1},{4,2},{5,3},{6,4},{7,5},{8,14},{9,15},{10,... | collective-permute-start | bytes 393224 | tf_op jit(solution)/shard_map/ppermute | solution.py:605
  120.4 9.6 %collective-permute-start.12 = (bf16[256,256]{1,0:T(8,128)(2,1)S(1)}, bf16[256,256]{1,0:T(8,128)(2,1)S(1)}, u32[]{:S(2)}, u32[]{:S(2)}) collective-permute-start(bf16[256,256]{1,0:T(8,128)(2,1)S(1)} %add_convert_fusion.refs_0_), channel_id=1, source_target_pairs={{0,4},{1,5},{2,6},{3,7},{4,0},{5,1},{6,2},{7,3},{8,12},{9,13},{10,... | collective-permute-start | bytes 393224 | tf_op jit(solution)/shard_map/ppermute | solution.py:605
  120.6 12.8 %collective-permute-start.11 = (bf16[256,256]{1,0:T(8,128)(2,1)S(1)}, bf16[256,256]{1,0:T(8,128)(2,1)S(1)}, u32[]{:S(2)}, u32[]{:S(2)}) collective-permute-start(bf16[256,256]{1,0:T(8,128)(2,1)S(1)} %add_convert_fusion.refs_0_), channel_id=1, source_target_pairs={{0,2},{1,3},{2,4},{3,5},{4,6},{5,7},{6,0},{7,1},{8,10},{9,11},{10,... | collective-permute-start | bytes 393224 | tf_op jit(solution)/shard_map/ppermute | solution.py:605
  127.2 6.3 %collective-permute-start.10 = (bf16[32,16,128]{2,1,0:T(8,128)(2,1)S(1)}, bf16[32,16,128]{2,1,0:T(8,128)(2,1)S(1)}, u32[]{:S(2)}, u32[]{:S(2)}) collective-permute-start(bf16[32,16,128]{2,1,0:T(8,128)(2,1)S(1)} %all-to-all-done.5.refs_0_), channel_id=1, source_target_pairs={{0,6},{1,7},{2,0},{3,1},{4,2},{5,3},{6,4},{7,5},{8,14},{9,15},{10,... | collective-permute-start | bytes 393224 | tf_op jit(solution)/shard_map/ppermute | solution.py:605
  129.3 8.0 %collective-permute-start.9 = (bf16[32,16,128]{2,1,0:T(8,128)(2,1)S(1)}, bf16[32,16,128]{2,1,0:T(8,128)(2,1)S(1)}, u32[]{:S(2)}, u32[]{:S(2)}) collective-permute-start(bf16[32,16,128]{2,1,0:T(8,128)(2,1)S(1)} %all-to-all-done.5.refs_0_), channel_id=1, source_target_pairs={{0,4},{1,5},{2,6},{3,7},{4,0},{5,1},{6,2},{7,3},{8,12},{9,13},{10,... | collective-permute-start | bytes 393224 | tf_op jit(solution)/shard_map/ppermute | solution.py:605
  129.6 9.3 %collective-permute-start.8 = (bf16[32,16,128]{2,1,0:T(8,128)(2,1)S(1)}, bf16[32,16,128]{2,1,0:T(8,128)(2,1)S(1)}, u32[]{:S(2)}, u32[]{:S(2)}) collective-permute-start(bf16[32,16,128]{2,1,0:T(8,128)(2,1)S(1)} %all-to-all-done.5.refs_0_), channel_id=1, source_target_pairs={{0,2},{1,3},{2,4},{3,5},{4,6},{5,7},{6,0},{7,1},{8,10},{9,11},{10,... | collective-permute-start | bytes 393224 | tf_op jit(solution)/shard_map/ppermute | solution.py:605
  129.9 10.2 %collective-permute-start.18 = (bf16[256,256]{1,0:T(8,128)(2,1)S(1)}, bf16[256,256]{1,0:T(8,128)(2,1)S(1)}, u32[]{:S(2)}, u32[]{:S(2)}) collective-permute-start(bf16[256,256]{1,0:T(8,128)(2,1)S(1)} %add_convert_fusion.refs_0_), channel_id=1, source_target_pairs={{0,1},{1,0},{2,3},{3,2},{4,5},{5,4},{6,7},{7,6},{8,9},{9,8},{10,11... | collective-permute-start | bytes 393224 | tf_op jit(solution)/shard_map/ppermute | solution.py:600
  133.4 6.8 %collective-permute-start.21 = (bf16[256,256]{1,0:T(8,128)(2,1)S(1)}, bf16[256,256]{1,0:T(8,128)(2,1)S(1)}, u32[]{:S(2)}, u32[]{:S(2)}) collective-permute-start(bf16[256,256]{1,0:T(8,128)(2,1)S(1)} %collective-permute-done.13.refs_3_), channel_id=1, source_target_pairs={{0,1},{1,0},{2,3},{3,2},{4,5},{5,4},{6,7},{7,6},{8,9},{9,8},{10,11... | collective-permute-start | bytes 393224 | tf_op jit(solution)/shard_map/ppermute | solution.py:600
  133.5 7.2 %collective-permute-start.20 = (bf16[256,256]{1,0:T(8,128)(2,1)S(1)}, bf16[256,256]{1,0:T(8,128)(2,1)S(1)}, u32[]{:S(2)}, u32[]{:S(2)}) collective-permute-start(bf16[256,256]{1,0:T(8,128)(2,1)S(1)} %collective-permute-done.12.refs_2_), channel_id=1, source_target_pairs={{0,1},{1,0},{2,3},{3,2},{4,5},{5,4},{6,7},{7,6},{8,9},{9,8},{10,11... | collective-permute-start | bytes 393224 | tf_op jit(solution)/shard_map/ppermute | solution.py:600
  137.4 4.6 %collective-permute-start.19 = (bf16[256,256]{1,0:T(8,128)(2,1)S(1)}, bf16[256,256]{1,0:T(8,128)(2,1)S(1)}, u32[]{:S(2)}, u32[]{:S(2)}) collective-permute-start(bf16[256,256]{1,0:T(8,128)(2,1)S(1)} %collective-permute-done.11.refs_1_), channel_id=1, source_target_pairs={{0,1},{1,0},{2,3},{3,2},{4,5},{5,4},{6,7},{7,6},{8,9},{9,8},{10,11... | collective-permute-start | bytes 393224 | tf_op jit(solution)/shard_map/ppermute | solution.py:600
  138.9 4.2 %collective-permute-start.14 = (bf16[32,16,128]{2,1,0:T(8,128)(2,1)S(1)}, bf16[32,16,128]{2,1,0:T(8,128)(2,1)S(1)}, u32[]{:S(2)}, u32[]{:S(2)}) collective-permute-start(bf16[32,16,128]{2,1,0:T(8,128)(2,1)S(1)} %all-to-all-done.5.refs_0_), channel_id=1, source_target_pairs={{0,1},{1,0},{2,3},{3,2},{4,5},{5,4},{6,7},{7,6},{8,9},{9,8},{10,11... | collective-permute-start | bytes 393224 | tf_op jit(solution)/shard_map/ppermute | solution.py:600
  140.2 3.0 %collective-permute-start.15 = (bf16[32,16,128]{2,1,0:T(8,128)(2,1)S(1)}, bf16[32,16,128]{2,1,0:T(8,128)(2,1)S(1)}, u32[]{:S(2)}, u32[]{:S(2)}) collective-permute-start(bf16[32,16,128]{2,1,0:T(8,128)(2,1)S(1)} %collective-permute-done.8.refs_1_), channel_id=1, source_target_pairs={{0,1},{1,0},{2,3},{3,2},{4,5},{5,4},{6,7},{7,6},{8,9},{9,8},{10,11... | collective-permute-start | bytes 393224 | tf_op jit(solution)/shard_map/ppermute | solution.py:600
  140.2 3.0 %collective-permute-start.16 = (bf16[32,16,128]{2,1,0:T(8,128)(2,1)S(1)}, bf16[32,16,128]{2,1,0:T(8,128)(2,1)S(1)}, u32[]{:S(2)}, u32[]{:S(2)}) collective-permute-start(bf16[32,16,128]{2,1,0:T(8,128)(2,1)S(1)} %collective-permute-done.9.refs_2_), channel_id=1, source_target_pairs={{0,1},{1,0},{2,3},{3,2},{4,5},{5,4},{6,7},{7,6},{8,9},{9,8},{10,11... | collective-permute-start | bytes 393224 | tf_op jit(solution)/shard_map/ppermute | solution.py:600
  140.7 2.5 %collective-permute-start.17 = (bf16[32,16,128]{2,1,0:T(8,128)(2,1)S(1)}, bf16[32,16,128]{2,1,0:T(8,128)(2,1)S(1)}, u32[]{:S(2)}, u32[]{:S(2)}) collective-permute-start(bf16[32,16,128]{2,1,0:T(8,128)(2,1)S(1)} %collective-permute-done.10.refs_3_), channel_id=1, source_target_pairs={{0,1},{1,0},{2,3},{3,2},{4,5},{5,4},{6,7},{7,6},{8,9},{9,8},{10,11... | collective-permute-start | bytes 393224 | tf_op jit(solution)/shard_map/ppermute | solution.py:600

commit v7 on v6

--- a/solution.py
+++ b/solution.py
@@ -17,6 +17,7 @@
 VM = pl.BlockSpec(memory_space=pltpu.VMEM)
 SM = pl.BlockSpec(memory_space=pltpu.SMEM)
 HB = pl.BlockSpec(memory_space=pltpu.HBM)
+IN_VM = pl.BlockSpec(memory_space=pltpu.VMEM)
 
 NN = (((1,), (0,)), ((), ()))
 NT = (((1,), (1,)), ((), ()))
@@ -91,6 +92,10 @@
     return pltpu.SemaphoreType.DMA((n,))
 
 
+def held(spec):
+    return pltpu.HBM if spec is HB else pltpu.VMEM if spec is IN_VM else None
+
+
 def in_hbm(array):
     return pltpu.with_memory_space_constraint(array, pltpu.HBM)
 
@@ -98,12 +103,12 @@
 def call(kernel, outs, args, specs=None, scratch=(), out_specs=None, limit=16, aliases={}):
     out_specs = out_specs if out_specs is not None else [VM] * len(outs)
     shapes = [
-        pltpu.HBM(s, d) if spec is HB else jax.ShapeDtypeStruct(s, d)
+        held(spec)(s, d) if held(spec) else jax.ShapeDtypeStruct(s, d)
         for (s, d), spec in zip(outs, out_specs, strict=True)
     ]
     specs = specs if specs is not None else [VM] * len(args)
     args = [
-        in_hbm(a) if spec is HB else a
+        pltpu.with_memory_space_constraint(a, held(spec)) if held(spec) else a
         for a, spec in zip(args, specs, strict=True)
     ]
     return pl.pallas_call(
@@ -118,8 +123,9 @@
 
 
 def request_kernel(
-    len_ref, ids_ref, out_ref, slot_hbm, slot_ref, arrived, *, rows_own, cap
+    len_ref, ids_ref, table_hbm, out_ref, slot_hbm, table_ref, slot_ref, arrived, *, rows_own, cap
 ):
+    tables = begin([(table_hbm, table_ref)], arrived, 1)
     users, block = ids_ref.shape
     shards, _, lanes = out_ref.shape
     shift = rows_own.bit_length() - 1
@@ -144,14 +150,13 @@
     copies = begin([(slot_ref, slot_hbm)], arrived)
     wanted = jnp.where(iota((shards, lanes), 1) == users * cap, count, total.astype(i32))
     out_ref[:, 0, :] = wanted
-    finish(copies)
+    finish(copies + tables)
 
 
 def answer_kernel(
-    wanted_ref, table_hbm, out_hbm, table_ref, out_ref, arrived, *, per
+    wanted_ref, table_ref, out_hbm, out_ref, arrived, *, per
 ):
     shards, _, lanes = wanted_ref.shape
-    copies = begin([(table_hbm, table_ref)], arrived)
     parts = 4
     group = shards // parts
     slots = group * per
@@ -167,11 +172,9 @@
         low = dot(where_bf16(own, dot(repeat, low.astype(bf16))), ones)
         column = (16.0 * high + low).astype(i32) - 1
         hot = tiled_match(column, rows)
-        if j == 0:
-            finish(copies)
         at = slice(j * slots, (j + 1) * slots)
         out_ref[at, :] = dot(hot, table_ref[...]).astype(bf16)
-        stores += begin([(out_ref.at[at, :], out_hbm.at[at, :])], arrived, 1 + j)
+        stores += begin([(out_ref.at[at, :], out_hbm.at[at, :])], arrived, j)
     finish(stores)
 
 
@@ -183,13 +186,9 @@
     cot_ref,
     decay_ref,
     w_out_ref,
-    quot_hbm,
-    dmixed_hbm,
-    wide_hbm,
     quot_ref,
     dmixed_ref,
     wide_ref,
-    arrived,
 ):
     users, block = ids_ref.shape
     heads = decay_ref.shape[1]
@@ -203,8 +202,6 @@
         dmixed_ref[at, :] = dot(masked, w_out_ref[...], NT).astype(bf16)
         _, columns = decays(decay_ref[u], width)
         wide_ref[at, :] = over_heads(columns, heads, width)
-    pairs = ((quot_ref, quot_hbm), (dmixed_ref, dmixed_hbm), (wide_ref, wide_hbm))
-    finish(begin(pairs, arrived))
 
 
 def decays(log_decay, width):
@@ -246,22 +243,18 @@
     at_ref,
     slot_hbm,
     answered_ref,
-    quot_hbm,
+    quot_ref,
     wq_hbm,
     wk_hbm,
     wv_hbm,
-    wide_hbm,
-    dmixed_hbm,
-    rem_hbm,
+    wide_ref,
+    dmixed_ref,
+    rem_ref,
     payload_hbm,
     slot_ref,
-    quot_ref,
     wq_ref,
     wk_ref,
     wv_ref,
-    wide_ref,
-    dmixed_ref,
-    rem_ref,
     states_ref,
     arrived,
     *,
@@ -277,29 +270,22 @@
     copies = begin(
         (
             (slot_hbm, slot_ref),
-            (quot_hbm, quot_ref),
             (wq_hbm, wq_ref),
             (wk_hbm, wk_ref),
             (wv_hbm, wv_ref),
-            (wide_hbm, wide_ref),
-            (dmixed_hbm, dmixed_ref),
         ),
         arrived,
     )
     finish(copies[:1])
     hot = [tiled_match(spread_column(slot_ref[u : u + 1, :]), slots) for u in range(users)]
-    finish(copies[1:5])
-    waits, copies = copies[5:], []
+    finish(copies[1:])
     for u in range(users):
         at = slice(u * block, (u + 1) * block)
         rem_ref[at, :] = dot(hot[u], answered_ref[...]).astype(bf16)
-        copies += begin([(rem_ref.at[at, :], rem_hbm.at[at, :])], arrived, 8 + u)
         embedded = (quot_ref[at, :].astype(f32) * rem_ref[at, :].astype(f32)).astype(bf16)
         q = dot(embedded, wq_ref[...]).astype(bf16)
         k = dot(embedded, wk_ref[...]).astype(bf16)
         v = dot(embedded, wv_ref[...]).astype(bf16)
-        if u == 0:
-            finish(waits)
         wide = wide_ref[at, :]
         end = wide[block - 1 : block, :]
         ends.append(end)
@@ -322,7 +308,7 @@
     states_ref[1, users * size :, :] = tail
     which = [jnp.where(peer > me, 0, 1) for peer in range(peers)]
     pairs = [(states_ref.at[which[peer]], payload_hbm.at[peer]) for peer in range(peers)]
-    finish(copies + begin(pairs, arrived, 8 + users))
+    finish(begin(pairs, arrived, 4))
 
 
 def within_kernel(
@@ -388,10 +374,10 @@
     at_ref,
     payload_ref,
     within_hbm,
-    dmixed_hbm,
-    wide_hbm,
-    rem_hbm,
-    quot_hbm,
+    dmixed_ref,
+    wide_ref,
+    rem_ref,
+    quot_ref,
     slot_hbm,
     ids_hbm,
     wq_hbm,
@@ -400,13 +386,9 @@
     w_out_hbm,
     out_hbm,
     rem_send_hbm,
-    keep_hbm,
-    give_hbm,
+    keep_ref,
+    give_ref,
     within_ref,
-    dmixed_ref,
-    wide_ref,
-    rem_ref,
-    quot_ref,
     slot_ref,
     ids_ref,
     wq_ref,
@@ -415,8 +397,6 @@
     w_out_ref,
     out_ref,
     rem_send_ref,
-    keep_ref,
-    give_ref,
     arrived,
     *,
     scale,
@@ -426,13 +406,9 @@
     width = quot_ref.shape[1]
     copies = begin(
         (
-            (quot_hbm, quot_ref),
-            (rem_hbm, rem_ref),
             (wq_hbm, wq_ref),
             (wk_hbm, wk_ref),
             (wv_hbm, wv_ref),
-            (wide_hbm, wide_ref),
-            (dmixed_hbm, dmixed_ref),
             (w_out_hbm, w_out_ref),
             (slot_hbm, slot_ref),
             (ids_hbm, ids_ref),
@@ -442,7 +418,7 @@
     waits = []
     for u in range(users):
         at = slice(u * block, (u + 1) * block)
-        waits += begin([(within_hbm.at[:, at, :], within_ref.at[:, at, :])], arrived, 11 + u)
+        waits += begin([(within_hbm.at[:, at, :], within_ref.at[:, at, :])], arrived, 6 + u)
     peers = payload_ref.shape[0]
     size = width // heads
     slots = rem_send_ref.shape[0]
@@ -485,7 +461,7 @@
         falloff = scale * jnp.exp(wide[block - 1 : block, :] - wide)
         mixed = (within_ref[0, at, :] + growth * dot(q, entering)).astype(bf16)
         out_ref[u] = dot(mixed, w_out_ref[...]).astype(bf16)
-        copies += begin([(out_ref.at[u], out_hbm.at[u])], arrived, 11 + users + u)
+        copies += begin([(out_ref.at[u], out_hbm.at[u])], arrived, 6 + users + u)
         dq = (within_ref[1, at, :] + growth * dot(dmixed, entering, NT)).astype(bf16)
         dk = (within_ref[2, at, :] + falloff * dot(v, leaving, NT)).astype(bf16)
         dv = (within_ref[3, at, :] + falloff * dot(k, leaving)).astype(bf16)
@@ -496,23 +472,17 @@
     quot_terms = jnp.concatenate(quot_terms, axis=0)
     slot = jnp.concatenate([slot_ref[u : u + 1, :] for u in range(users)], axis=1)
     ids = jnp.concatenate([ids_ref[u : u + 1, :] for u in range(users)], axis=1)
-    n = 11 + 2 * users
+    n = 6 + 2 * users
     for j, hot in enumerate(stacked_match(slot, block, slots // block)):
         at = slice(j * block, (j + 1) * block)
         rem_send_ref[at, :] = dot(hot, rem_terms).astype(bf16)
         copies += begin([(rem_send_ref.at[at, :], rem_send_hbm.at[at, :])], arrived, n + j)
-    n += slots // block
-    for ref, hbm, owner in ((give_ref, give_hbm, 1 - me % 2), (keep_ref, keep_hbm, me % 2)):
-        half = ref.shape[0]
-        for j, hot in enumerate(stacked_match(ids - owner * half, block, half // block)):
-            at = slice(j * block, (j + 1) * block)
-            ref[at, :] = dot(hot, quot_terms).astype(bf16)
-            copies += begin([(ref.at[at, :], hbm.at[at, :])], arrived, n)
-            n += 1
+    for ref, owner in ((give_ref, 1 - me % 2), (keep_ref, me % 2)):
+        sum_half(ids, quot_terms, owner, ref)
     finish(copies)
 
 
-def collect_kernel(at_ref, wanted_ref, back_ref, keep_ref, give_ref, *, per):
+def collect_kernel(at_ref, wanted_ref, back_ref, out_ref, *, per, other):
     shards, _, lanes = wanted_ref.shape
     slots = shards * per
     wanted = jnp.where(iota((shards, lanes), 1) < per, wanted_ref[:, 0, :], 0)
@@ -522,25 +492,19 @@
     high = jnp.sum(jnp.where(own, dot(high.astype(bf16), tile), 0.0), axis=0, keepdims=True)
     low = jnp.sum(jnp.where(own, dot(low.astype(bf16), tile), 0.0), axis=0, keepdims=True)
     row = (16.0 * high + low).astype(i32) - 1
-    sum_half(row, back_ref[...], 1 - at_ref[0] % 2, give_ref)
-    sum_half(row, back_ref[...], at_ref[0] % 2, keep_ref)
-
-
-def split_kernel(at_ref, keep_ref, got_ref, *refs, chips):
-    out_refs = refs[:chips]
+    core = at_ref[0] % 2
+    sum_half(row, back_ref[...], 1 - core if other else core, out_ref)
+
+
+def split_kernel(at_ref, keep_ref, got_ref, *out_refs):
+    chips = len(out_refs)
     rows = out_refs[0].shape[0]
     bases = [
         pl.multiple_of(lax.rem(at_ref[0] // 2 + d, chips) * rows, rows) for d in range(chips)
     ]
-    copies = []
-    if len(refs) > chips:
-        near_ref, arrived = refs[chips:]
-        copies = begin([(keep_ref.at[pl.ds(b, rows), :], near_ref.at[d]) for d, b in enumerate(bases)], arrived)
-    for d, out_ref in enumerate(out_refs):
-        finish(copies[d : d + 1])
-        kept = near_ref[d] if copies else keep_ref[pl.ds(bases[d], rows), :]
-        both = kept.astype(f32) + got_ref[pl.ds(bases[d], rows), :].astype(f32)
-        out_ref[...] = both.astype(bf16)
+    for base, out_ref in zip(bases, out_refs, strict=True):
+        at = pl.ds(base, rows)
+        out_ref[...] = (keep_ref[at, :].astype(f32) + got_ref[at, :].astype(f32)).astype(bf16)
 
 
 def cut(chunk, shards):
@@ -607,11 +571,8 @@
 
 def split(at, keep, give, spec=VM):
     chips = lax.axis_size("hist") // 2
-    rows, width = keep.shape[0] // chips, keep.shape[1]
-    kernel = functools.partial(split_kernel, chips=chips)
-    scratch = [pltpu.VMEM((chips, rows, width), keep.dtype), dma(chips)] if spec is HB else []
-    args = (at, keep, to_core(give))
-    return call(kernel, [((rows, width), bf16)] * chips, args, [SM, spec, VM], scratch)
+    outs = [((keep.shape[0] // chips, keep.shape[1]), bf16)] * chips
+    return call(split_kernel, outs, (at, keep, to_core(give)), [SM, spec, VM])
 
 
 def shared(chunks):
@@ -662,15 +623,14 @@
     at = lax.axis_index("hist").astype(i32).reshape(1)
     lanes = (per // 128 + 1) * 128
 
-    events = pltpu.VMEM((users * block, width), bf16)
     square = pltpu.VMEM((width, width), bf16)
-    requests, slot = call(
+    requests, slot, table = call(
         functools.partial(request_kernel, rows_own=rows_own, cap=cap),
-        [((shards, 1, lanes), i32), ((8, block), i32)],
-        (in_hbm(lengths), in_hbm(rem_ids)),
-        [SM, VM],
-        [pltpu.VMEM((8, block), i32), dma(1)],
-        [VM, HB],
+        [((shards, 1, lanes), i32), ((8, block), i32), (rem_table.shape, bf16)],
+        (in_hbm(lengths), in_hbm(rem_ids), rem_table),
+        [SM, VM, HB],
+        [pltpu.VMEM((8, block), i32), dma(2)],
+        [VM, HB, IN_VM],
         MOST,
     )
     wanted = exchange(requests, "user")
@@ -681,22 +641,19 @@
             ((users * block, width), bf16),
             ((users * block, width), f32),
         ],
-        (lengths, at, quot_ids, quot_table, cotangent, log_decay, w_out),
+        (lengths, at)
+        + tuple(in_hbm(a) for a in (quot_ids, quot_table, cotangent, log_decay, w_out)),
         [SM, SM] + [VM] * 5,
-        [events, events, pltpu.VMEM((users * block, width), f32), dma(3)],
-        [HB] * 3,
-        FULL,
+        (),
+        [IN_VM] * 3,
+        MOST,
     )
     (found,) = call(
         functools.partial(answer_kernel, per=per),
         [((slots, width), bf16)],
-        (wanted, rem_table),
-        [VM, HB],
-        [
-            pltpu.VMEM((rows_own, width), bf16),
-            pltpu.VMEM((slots, width), bf16),
-            dma(5),
-        ],
+        (wanted, table),
+        [VM, IN_VM],
+        [pltpu.VMEM((slots, width), bf16), dma(4)],
         [HB],
         MOST,
     )
@@ -705,12 +662,11 @@
         functools.partial(project_kernel, users=users, heads=heads),
         [((users * block, width), bf16), ((peers, users * size + 16, width), bf16)],
         (at, slot, answered, quot_emb, w_query, w_key, w_value, wide, dmixed),
-        [SM, HB, VM] + [HB] * 6,
-        [pltpu.VMEM((8, block), i32), events]
+        [SM, HB, VM, IN_VM, HB, HB, HB, IN_VM, IN_VM],
+        [pltpu.VMEM((8, block), i32)]
         + [square] * 3
-        + [pltpu.VMEM((users * block, width), f32), events, events]
-        + [pltpu.VMEM((2, users * size + 16, width), bf16), dma(8 + users + peers)],
-        [HB, HB],
+        + [pltpu.VMEM((2, users * size + 16, width), bf16), dma(4 + peers)],
+        [IN_VM, HB],
         MOST,
     )
     states = exchange(payload, "hist")
@@ -718,42 +674,45 @@
     (within,) = call(
         functools.partial(within_kernel, scale=scale),
         [(parts, f32)],
-        (quot_emb, rem_emb, dmixed, log_decay, w_query, w_key, w_value),
-        scratch=[pltpu.VMEM(parts, f32), dma(users)],
-        out_specs=[HB],
-        limit=FULL,
+        (quot_emb, rem_emb, dmixed)
+        + tuple(in_hbm(a) for a in (log_decay, w_query, w_key, w_value)),
+        [IN_VM] * 3 + [VM] * 4,
+        [pltpu.VMEM(parts, f32), dma(users)],
+        [HB],
+        MOST,
     )
     output, rem_send, keep, give = call(
         functools.partial(gradient_kernel, scale=scale, heads=heads),
         [
             ((users, block, width), bf16),
             ((slots, width), bf16),
-            ((rows_all // 2, width), bf16),
+            ((rows_all // 2, width), f32),
             ((rows_all // 2, width), bf16),
         ],
         (at, states, within, dmixed, wide, rem_emb, quot_emb, slot, quot_ids)
         + (w_query, w_key, w_value, w_out),
-        [SM, VM] + [HB] * 11,
-        [pltpu.VMEM(parts, f32), events]
-        + [pltpu.VMEM((users * block, width), f32), events, events]
+        [SM, VM, HB] + [IN_VM] * 4 + [HB] * 6,
+        [pltpu.VMEM(parts, f32)]
         + [pltpu.VMEM((8, block), i32), pltpu.VMEM((users, block), i32)]
         + [square] * 4
         + [pltpu.VMEM((users, block, width), bf16), pltpu.VMEM((slots, width), bf16)]
-        + [pltpu.VMEM((rows_all // 2, width), bf16)] * 2
-        + [dma(11 + 2 * users + (slots + rows_all) // block)],
-        [HB] * 4,
+        + [dma(6 + 2 * users + slots // block)],
+        [HB, HB, IN_VM, IN_VM],
         MOST,
     )
     rem_back = exchange(rem_send.reshape(shards, per, width), "user").reshape(slots, width)
     tiles = (shards, rows_all // peers * width // shards // 128, 128)
-    (quot_tiles,) = call(total_kernel, [(tiles, bf16)], shared(split(at, keep, give, HB)))
+    (quot_tiles,) = call(total_kernel, [(tiles, bf16)], shared(split(at, keep, give, IN_VM)))
     rem_back, quot_tiles = lax.optimization_barrier((rem_back, quot_tiles))
     quot_back = exchange(quot_tiles, "user")
-    keep, give = call(
-        functools.partial(collect_kernel, per=per),
-        [((rows_own // 2, width), f32), ((rows_own // 2, width), bf16)],
-        (at, wanted, rem_back),
-        [SM, VM, VM],
+    keep, give = (
+        call(
+            functools.partial(collect_kernel, per=per, other=other),
+            [((rows_own // 2, width), bf16 if other else f32)],
+            (at, wanted, rem_back),
+            [SM, VM, VM],
+        )[0]
+        for other in (False, True)
     )
     chunks = split(at, keep, give)
     (quot_tiles,) = call(repeat_kernel, [(tiles, bf16)], (quot_back,))

time: 145 us -> 142 us (0.979)
  Pallas kernels: 32.7 us -> 29.1 us
    pallas_call x15 -> x16, Pallas kernels: 32.7 us -> 29.1 us  [call(): pl.pallas_call(kernel, out_shape=tuple(shapes), in_specs=specs, out_specs...]
  transfers between devices with their start and end apart: 27 -> 27, of which waited for: 8 -> 9; matrix products, arithmetic and copies ran while one was open for 0% -> 0% of each run, Pallas kernels for 11% -> 10%
where the time goes in v7:
time: 142 us; the launch traced here: 141 us
  starting transfers between devices  56.3 us (40%)
  waiting for transfers between devices  34.2 us (24%)
  Pallas kernels  29.1 us (20%)
  blocking collectives  20.5 us (14%)
    pallas_call x16, Pallas kernels, call(): pl.pallas_call(kernel, out_shape=tuple(shapes), in_specs=specs, out_specs...  29.1 us
    all_to_all x5, starting transfers between devices, exchange(): return lax.all_to_all(array, axis, split_axis=0, concat_axis=0, tiled=True)  28.9 us
    all_to_all x5, waiting for transfers between devices, exchange(): return lax.all_to_all(array, axis, split_axis=0, concat_axis=0, tiled=True)  26.3 us
    all_to_all x1, blocking collectives, exchange(): return lax.all_to_all(array, axis, split_axis=0, concat_axis=0, tiled=True)  20.5 us
    ppermute x10, starting transfers between devices, to_core(): return lax.ppermute(array, 'hist', [(i, i ^ 1) for i in range(peers)])  14.6 us
    ppermute x12, starting transfers between devices, to_chip(): lax.ppermute(array, 'hist', [(i, (i + 2 * steps) % peers) for i in range(...  12.8 us
    ppermute x12, waiting for transfers between devices, to_chip(): lax.ppermute(array, 'hist', [(i, (i + 2 * steps) % peers) for i in range(...  6.33 us
  transfers between devices with their start and end apart: 27, of which 9 were waited for; matrix products, arithmetic and copies ran while one was open for 0% of the time, Pallas kernels for 10%

profile of v7, /device:TPU:1, one launch (start us, length us, event | category | flops | bytes accessed | tf_op | source)
XLA Modules:
  0.0 141.2 jit_solution(4358489958951955072)
XLA Ops:
  0.6 2.0 %shard_map.130 = (s32[32,1,128]{2,1,0:T(1,128)S(1)}, s32[8,256]{1,0:T(8,128)}, bf16[2048,256]{1,0:T(8,128)(2,1)S(1)}) custom-call(s32[2]{0:T(128)} %len_ref.3, s32[2,256]{1,0:T(2,128)} %ids_ref.2, bf16[2048,256]{1,0:T(8,128)(2,1)} %table_hbm.1), custom_call_target="tpu_custom_call" | custom-call | tf_op jit(solution)/shard_map/pallas_call | solution.py:114
  2.7 20.5 %all_to_all.30.wanted_ref = s32[32,1,128]{2,1,0:T(1,128)S(1)} all-to-all(s32[32,1,128]{2,1,0:T(1,128)S(1)} %get-tuple-element.33), channel_id=1, replica_groups=mesh['user'=32,'hist'=8] {'user'}, dimensions={0} | all-to-all | bytes 32768 | tf_op jit(solution)/shard_map/all_to_all | solution.py:559
  23.2 3.0 %shard_map.131 = bf16[1024,256]{1,0:T(8,128)(2,1)} custom-call(s32[32,1,128]{2,1,0:T(1,128)S(1)} %all_to_all.30.wanted_ref, bf16[2048,256]{1,0:T(8,128)(2,1)S(1)} %get-tuple-element.34.table_ref), custom_call_target="tpu_custom_call" | custom-call | tf_op jit(solution)/shard_map/pallas_call | solution.py:114
  26.1 3.9 %all-to-all-start.1 = ((bf16[32,32,256]{2,1,0:T(8,128)(2,1)}), bf16[32,32,256]{2,1,0:T(8,128)(2,1)S(1)}, u32[]{:S(2)}, u32[]{:S(2)}) async-start(bf16[32,32,256]{2,1,0:T(8,128)(2,1)} %bitcast.8), calls=%async_computation.1 | async-start | bytes 1048576 | tf_op jit(solution)/shard_map/all_to_all | solution.py:559
  30.1 2.9 %shard_map.132 = (bf16[512,256]{1,0:T(8,128)(2,1)S(1)}, bf16[512,256]{1,0:T(8,128)(2,1)S(1)}, f32[512,256]{1,0:T(8,128)S(1)}) custom-call(s32[2]{0:T(128)S(1)} %copy-done, s32[1]{0:T(128)} %bitcast.at_ref, s32[2,256]{1,0:T(2,128)} %ids_hbm.1, bf16[2048,256]{1,0:T(8,128)(2,1)} %table_ref.1, bf16[2,256,256]{2,1,0:T(8,128)(2,1)} %cot_ref.1, ...), custom_call_target="tpu_custom_call" | custom-call | tf_op jit(solution)/shard_map/pallas_call | solution.py:114
  33.0 10.0 %all-to-all-done.1 = bf16[32,32,256]{2,1,0:T(8,128)(2,1)S(1)} async-done(((bf16[32,32,256]{2,1,0:T(8,128)(2,1)}), bf16[32,32,256]{2,1,0:T(8,128)(2,1)S(1)}, u32[]{:S(2)}, u32[]{:S(2)}) %all-to-all-start.1) | async-done | bytes 524320 | tf_op jit(solution)/shard_map/all_to_all | solution.py:559
  43.0 3.5 %shard_map.133 = (bf16[512,256]{1,0:T(8,128)(2,1)S(1)}, bf16[8,144,256]{2,1,0:T(8,128)(2,1)}) custom-call(s32[1]{0:T(128)} %bitcast.at_ref, s32[8,256]{1,0:T(8,128)} %get-tuple-element.32.slot_hbm, bf16[1024,256]{1,0:T(8,128)(2,1)S(1)} %bitcast.7, bf16[512,256]{1,0:T(8,128)(2,1)S(1)} %get-tuple-element.35.quot_ref, bf16[256,256]{1,0:T(8,128)(2,1)} %wq_hbm.3, ...), custom_call_target="tpu_custom_call" | custom-call | tf_op jit(solution)/shard_map/pallas_call | solution.py:114
  46.6 9.5 %all-to-all-start.2 = ((bf16[8,144,256]{2,1,0:T(8,128)(2,1)}), bf16[8,144,256]{2,1,0:T(8,128)(2,1)S(1)}, u32[]{:S(2)}, u32[]{:S(2)}) async-start(bf16[8,144,256]{2,1,0:T(8,128)(2,1)} %get-tuple-element.38), calls=%async_computation.2 | async-start | bytes 1179648 | tf_op jit(solution)/shard_map/all_to_all | solution.py:559
  56.0 5.5 %shard_map.134.within_hbm = f32[4,512,256]{2,1,0:T(8,128)} custom-call(bf16[512,256]{1,0:T(8,128)(2,1)S(1)} %get-tuple-element.35.quot_ref, bf16[512,256]{1,0:T(8,128)(2,1)S(1)} %get-tuple-element.39.rem_ref, bf16[512,256]{1,0:T(8,128)(2,1)S(1)} %get-tuple-element.37.dmixed_ref, f32[2,4,256]{2,1,0:T(4,128)} %decay_ref.3, bf16[256,256]{1,0:T(8,128)(2,1)} %wq_hbm.3, ...), custom_call_target="tpu_custom_call" | custom-call | tf_op jit(solution)/shard_map/pallas_call | solution.py:114
  61.5 4.7 %all-to-all-done.2.payload_ref = bf16[8,144,256]{2,1,0:T(8,128)(2,1)S(1)} async-done(((bf16[8,144,256]{2,1,0:T(8,128)(2,1)}), bf16[8,144,256]{2,1,0:T(8,128)(2,1)S(1)}, u32[]{:S(2)}, u32[]{:S(2)}) %all-to-all-start.2) | async-done | bytes 589856 | tf_op jit(solution)/shard_map/all_to_all | solution.py:559
  66.2 4.2 %shard_map.135 = (bf16[2,256,256]{2,1,0:T(8,128)(2,1)}, bf16[1024,256]{1,0:T(8,128)(2,1)}, f32[1024,256]{1,0:T(8,128)S(1)}, bf16[1024,256]{1,0:T(8,128)(2,1)S(1)}) custom-call(s32[1]{0:T(128)} %bitcast.at_ref, bf16[8,144,256]{2,1,0:T(8,128)(2,1)S(1)} %all-to-all-done.2.payload_ref, f32[4,512,256]{2,1,0:T(8,128)} %shard_map.134.within_hbm, ...), custom_call_target="tpu_custom_call" | custom-call | tf_op jit(solution)/shard_map/pallas_call | solution.py:114
  70.4 5.0 %all-to-all-start.3 = ((bf16[32,32,256]{2,1,0:T(8,128)(2,1)}), bf16[32,32,256]{2,1,0:T(8,128)(2,1)S(1)}, u32[]{:S(2)}, u32[]{:S(2)}) async-start(bf16[32,32,256]{2,1,0:T(8,128)(2,1)} %bitcast.9), calls=%async_computation.3 | async-start | bytes 1048576 | tf_op jit(solution)/shard_map/all_to_all | solution.py:559
  75.5 1.4 %collective-permute-start = (bf16[1024,256]{1,0:T(8,128)(2,1)S(1)}, bf16[1024,256]{1,0:T(8,128)(2,1)S(1)}, u32[]{:S(2)}, u32[]{:S(2)}) collective-permute-start(bf16[1024,256]{1,0:T(8,128)(2,1)S(1)} %get-tuple-element.43), channel_id=1, source_target_pairs={{0,1},{1,0},{2,3},{3,2},{4,5},{5,4},{6,7},{7,6},{8,9},{9,8},{10,11... | collective-permute-start | bytes 1572872 | tf_op jit(solution)/shard_map/ppermute | solution.py:564
  76.9 1.5 %collective-permute-done.got_ref = bf16[1024,256]{1,0:T(8,128)(2,1)S(1)} collective-permute-done((bf16[1024,256]{1,0:T(8,128)(2,1)S(1)}, bf16[1024,256]{1,0:T(8,128)(2,1)S(1)}, u32[]{:S(2)}, u32[]{:S(2)}) %collective-permute-start) | collective-permute-done | bytes 524320 | tf_op jit(solution)/shard_map/ppermute | solution.py:564
  78.4 0.1 shard_map.136
  78.6 0.4 collective-permute-start.1
  78.9 1.8 %collective-permute-start.2 = (bf16[256,256]{1,0:T(8,128)(2,1)S(1)}, bf16[256,256]{1,0:T(8,128)(2,1)S(1)}, u32[]{:S(2)}, u32[]{:S(2)}) collective-permute-start(bf16[256,256]{1,0:T(8,128)(2,1)S(1)} %get-tuple-element.46), channel_id=1, source_target_pairs={{0,4},{1,5},{2,6},{3,7},{4,0},{5,1},{6,2},{7,3},{8,12},{9,13},{10,... | collective-permute-start | bytes 393224 | tf_op jit(solution)/shard_map/ppermute | solution.py:569
  80.7 0.7 collective-permute-start.3
  81.4 3.7 %collective-permute-done.1.refs_1_ = bf16[256,256]{1,0:T(8,128)(2,1)S(1)} collective-permute-done((bf16[256,256]{1,0:T(8,128)(2,1)S(1)}, bf16[256,256]{1,0:T(8,128)(2,1)S(1)}, u32[]{:S(2)}, u32[]{:S(2)}) %collective-permute-start.1) | collective-permute-done | bytes 131104 | tf_op jit(solution)/shard_map/ppermute | solution.py:569
  85.2 1.6 %collective-permute-done.2.refs_2_ = bf16[256,256]{1,0:T(8,128)(2,1)S(1)} collective-permute-done((bf16[256,256]{1,0:T(8,128)(2,1)S(1)}, bf16[256,256]{1,0:T(8,128)(2,1)S(1)}, u32[]{:S(2)}, u32[]{:S(2)}) %collective-permute-start.2) | collective-permute-done | bytes 131104 | tf_op jit(solution)/shard_map/ppermute | solution.py:569
  86.8 0.9 collective-permute-done.3.refs_3_
  87.7 0.7 shard_map.137
  88.4 1.1 all-to-all-done.3
  89.5 0.9 shard_map.140
  90.4 4.1 %collective-permute-start.4 = (bf16[1024,256]{1,0:T(8,128)(2,1)S(1)}, bf16[1024,256]{1,0:T(8,128)(2,1)S(1)}, u32[]{:S(2)}, u32[]{:S(2)}) collective-permute-start(bf16[1024,256]{1,0:T(8,128)(2,1)S(1)} %shard_map.140), channel_id=1, source_target_pairs={{0,1},{1,0},{2,3},{3,2},{4,5},{5,4},{6,7},{7,6},{8,9},{9,8},{10,11... | collective-permute-start | bytes 1572872 | tf_op jit(solution)/shard_map/ppermute | solution.py:564
  94.5 5.9 %all-to-all-start.4 = ((bf16[32,16,128]{2,1,0:T(8,128)(2,1)}), bf16[32,16,128]{2,1,0:T(8,128)(2,1)S(1)}, u32[]{:S(2)}, u32[]{:S(2)}) async-start(bf16[32,16,128]{2,1,0:T(8,128)(2,1)} %shard_map.137), calls=%async_computation.4 | async-start | bytes 262144 | tf_op jit(solution)/shard_map/all_to_all | solution.py:559
  100.4 0.9 shard_map.139.keep_ref
  101.3 0.0 collective-permute-done.4.got_ref
  101.3 0.1 shard_map.141
  101.4 0.1 collective-permute-start.5
  101.5 3.3 %collective-permute-start.6 = (bf16[256,256]{1,0:T(8,128)(2,1)S(1)}, bf16[256,256]{1,0:T(8,128)(2,1)S(1)}, u32[]{:S(2)}, u32[]{:S(2)}) collective-permute-start(bf16[256,256]{1,0:T(8,128)(2,1)S(1)} %get-tuple-element.52), channel_id=1, source_target_pairs={{0,4},{1,5},{2,6},{3,7},{4,0},{5,1},{6,2},{7,3},{8,12},{9,13},{10,... | collective-permute-start | bytes 393224 | tf_op jit(solution)/shard_map/ppermute | solution.py:569
  104.8 4.7 %all-to-all-done.4.tiles_ref = bf16[32,16,128]{2,1,0:T(8,128)(2,1)S(1)} async-done(((bf16[32,16,128]{2,1,0:T(8,128)(2,1)}), bf16[32,16,128]{2,1,0:T(8,128)(2,1)S(1)}, u32[]{:S(2)}, u32[]{:S(2)}) %all-to-all-start.4) | async-done | bytes 131104 | tf_op jit(solution)/shard_map/all_to_all | solution.py:559
  109.5 0.7 shard_map.138
  110.2 4.5 %all-to-all-start.5 = ((bf16[32,16,128]{2,1,0:T(8,128)(2,1)}), bf16[32,16,128]{2,1,0:T(8,128)(2,1)S(1)}, u32[]{:S(2)}, u32[]{:S(2)}) async-start(bf16[32,16,128]{2,1,0:T(8,128)(2,1)} %shard_map.138), calls=%async_computation.5 | async-start | bytes 262144 | tf_op jit(solution)/shard_map/all_to_all | solution.py:559
  114.8 0.0 collective-permute-done.5
  114.8 0.1 add_convert_fusion.refs_0_
  114.9 2.2 %collective-permute-start.13 = (bf16[256,256]{1,0:T(8,128)(2,1)S(1)}, bf16[256,256]{1,0:T(8,128)(2,1)S(1)}, u32[]{:S(2)}, u32[]{:S(2)}) collective-permute-start(bf16[256,256]{1,0:T(8,128)(2,1)S(1)} %add_convert_fusion.refs_0_), channel_id=1, source_target_pairs={{0,6},{1,7},{2,0},{3,1},{4,2},{5,3},{6,4},{7,5},{8,14},{9,15},{10,... | collective-permute-start | bytes 393224 | tf_op jit(solution)/shard_map/ppermute | solution.py:569
  117.1 1.1 collective-permute-start.12
  118.2 0.0 collective-permute-start.11
  118.2 5.8 %all-to-all-done.5.refs_0_ = bf16[32,16,128]{2,1,0:T(8,128)(2,1)S(1)} async-done(((bf16[32,16,128]{2,1,0:T(8,128)(2,1)}), bf16[32,16,128]{2,1,0:T(8,128)(2,1)S(1)}, u32[]{:S(2)}, u32[]{:S(2)}) %all-to-all-start.5) | async-done | bytes 131104 | tf_op jit(solution)/shard_map/all_to_all | solution.py:559
  123.9 2.2 %collective-permute-start.10 = (bf16[32,16,128]{2,1,0:T(8,128)(2,1)S(1)}, bf16[32,16,128]{2,1,0:T(8,128)(2,1)S(1)}, u32[]{:S(2)}, u32[]{:S(2)}) collective-permute-start(bf16[32,16,128]{2,1,0:T(8,128)(2,1)S(1)} %all-to-all-done.5.refs_0_), channel_id=1, source_target_pairs={{0,6},{1,7},{2,0},{3,1},{4,2},{5,3},{6,4},{7,5},{8,14},{9,15},{10,... | collective-permute-start | bytes 393224 | tf_op jit(solution)/shard_map/ppermute | solution.py:569
  126.1 1.1 collective-permute-start.9
  127.2 0.0 collective-permute-done.13.refs_3_
  127.2 0.0 collective-permute-start.8
  127.2 3.6 %collective-permute-start.18 = (bf16[256,256]{1,0:T(8,128)(2,1)S(1)}, bf16[256,256]{1,0:T(8,128)(2,1)S(1)}, u32[]{:S(2)}, u32[]{:S(2)}) collective-permute-start(bf16[256,256]{1,0:T(8,128)(2,1)S(1)} %add_convert_fusion.refs_0_), channel_id=1, source_target_pairs={{0,1},{1,0},{2,3},{3,2},{4,5},{5,4},{6,7},{7,6},{8,9},{9,8},{10,11... | collective-permute-start | bytes 393224 | tf_op jit(solution)/shard_map/ppermute | solution.py:564
  130.8 0.0 collective-permute-done.11.refs_1_
  130.8 0.3 collective-permute-start.21
  131.1 0.0 collective-permute-done.10.refs_3_
  131.1 1.8 %collective-permute-start.20 = (bf16[256,256]{1,0:T(8,128)(2,1)S(1)}, bf16[256,256]{1,0:T(8,128)(2,1)S(1)}, u32[]{:S(2)}, u32[]{:S(2)}) collective-permute-start(bf16[256,256]{1,0:T(8,128)(2,1)S(1)} %collective-permute-done.12.refs_2_), channel_id=1, source_target_pairs={{0,1},{1,0},{2,3},{3,2},{4,5},{5,4},{6,7},{7,6},{8,9},{9,8},{10,11... | collective-permute-start | bytes 393224 | tf_op jit(solution)/shard_map/ppermute | solution.py:564
  132.9 1.1 shard_map.142.refs_4_
  134.1 1.4 collective-permute-start.19
  135.5 1.4 collective-permute-start.14
  136.9 0.0 collective-permute-done.18.refs_0_
  136.9 0.0 collective-permute-start.15
  136.9 0.0 collective-permute-done.21.refs_3_
  136.9 0.5 collective-permute-start.16
  137.4 0.0 collective-permute-done.20.refs_2_
  137.4 0.1 collective-permute-start.17
  137.5 1.1 shard_map.143.refs_4_
  138.7 0.0 collective-permute-done.19.refs_1_
  138.7 1.2 shard_map.145
  139.8 0.0 collective-permute-done.15.refs_1_
  139.9 0.0 collective-permute-done.16.refs_2_
  139.9 1.2 shard_map.144
  (10 shorter events, 0.0 us)
Async XLA Ops:
  0.6 29.4 %copy-start = (s32[2]{0:T(128)S(1)}, s32[2]{0:T(128)}, u32[]{:S(2)}) copy-start(s32[2]{0:T(128)} %len_ref.3) | copy-start | bytes 28
  26.1 16.9 %all-to-all-start.1 = ((bf16[32,32,256]{2,1,0:T(8,128)(2,1)}), bf16[32,32,256]{2,1,0:T(8,128)(2,1)S(1)}, u32[]{:S(2)}, u32[]{:S(2)}) async-start(bf16[32,32,256]{2,1,0:T(8,128)(2,1)} %bitcast.8), calls=%async_computation.1 | async-start | bytes 1048576 | tf_op jit(solution)/shard_map/all_to_all | solution.py:559
  46.6 19.7 %all-to-all-start.2 = ((bf16[8,144,256]{2,1,0:T(8,128)(2,1)}), bf16[8,144,256]{2,1,0:T(8,128)(2,1)S(1)}, u32[]{:S(2)}, u32[]{:S(2)}) async-start(bf16[8,144,256]{2,1,0:T(8,128)(2,1)} %get-tuple-element.38), calls=%async_computation.2 | async-start | bytes 1179648 | tf_op jit(solution)/shard_map/all_to_all | solution.py:559
  70.4 19.1 %all-to-all-start.3 = ((bf16[32,32,256]{2,1,0:T(8,128)(2,1)}), bf16[32,32,256]{2,1,0:T(8,128)(2,1)S(1)}, u32[]{:S(2)}, u32[]{:S(2)}) async-start(bf16[32,32,256]{2,1,0:T(8,128)(2,1)} %bitcast.9), calls=%async_computation.3 | async-start | bytes 1048576 | tf_op jit(solution)/shard_map/all_to_all | solution.py:559
  75.5 3.0 %collective-permute-start = (bf16[1024,256]{1,0:T(8,128)(2,1)S(1)}, bf16[1024,256]{1,0:T(8,128)(2,1)S(1)}, u32[]{:S(2)}, u32[]{:S(2)}) collective-permute-start(bf16[1024,256]{1,0:T(8,128)(2,1)S(1)} %get-tuple-element.43), channel_id=1, source_target_pairs={{0,1},{1,0},{2,3},{3,2},{4,5},{5,4},{6,7},{7,6},{8,9},{9,8},{10,11... | collective-permute-start | bytes 1572872 | tf_op jit(solution)/shard_map/ppermute | solution.py:564
  78.6 6.6 %collective-permute-start.1 = (bf16[256,256]{1,0:T(8,128)(2,1)S(1)}, bf16[256,256]{1,0:T(8,128)(2,1)S(1)}, u32[]{:S(2)}, u32[]{:S(2)}) collective-permute-start(bf16[256,256]{1,0:T(8,128)(2,1)S(1)} %get-tuple-element.45), channel_id=1, source_target_pairs={{0,2},{1,3},{2,4},{3,5},{4,6},{5,7},{6,0},{7,1},{8,10},{9,11},{10,... | collective-permute-start | bytes 393224 | tf_op jit(solution)/shard_map/ppermute | solution.py:569
  78.9 7.9 %collective-permute-start.2 = (bf16[256,256]{1,0:T(8,128)(2,1)S(1)}, bf16[256,256]{1,0:T(8,128)(2,1)S(1)}, u32[]{:S(2)}, u32[]{:S(2)}) collective-permute-start(bf16[256,256]{1,0:T(8,128)(2,1)S(1)} %get-tuple-element.46), channel_id=1, source_target_pairs={{0,4},{1,5},{2,6},{3,7},{4,0},{5,1},{6,2},{7,3},{8,12},{9,13},{10,... | collective-permute-start | bytes 393224 | tf_op jit(solution)/shard_map/ppermute | solution.py:569
  80.7 7.0 %collective-permute-start.3 = (bf16[256,256]{1,0:T(8,128)(2,1)S(1)}, bf16[256,256]{1,0:T(8,128)(2,1)S(1)}, u32[]{:S(2)}, u32[]{:S(2)}) collective-permute-start(bf16[256,256]{1,0:T(8,128)(2,1)S(1)} %get-tuple-element.47), channel_id=1, source_target_pairs={{0,6},{1,7},{2,0},{3,1},{4,2},{5,3},{6,4},{7,5},{8,14},{9,15},{10,... | collective-permute-start | bytes 393224 | tf_op jit(solution)/shard_map/ppermute | solution.py:569
  90.4 10.9 %collective-permute-start.4 = (bf16[1024,256]{1,0:T(8,128)(2,1)S(1)}, bf16[1024,256]{1,0:T(8,128)(2,1)S(1)}, u32[]{:S(2)}, u32[]{:S(2)}) collective-permute-start(bf16[1024,256]{1,0:T(8,128)(2,1)S(1)} %shard_map.140), channel_id=1, source_target_pairs={{0,1},{1,0},{2,3},{3,2},{4,5},{5,4},{6,7},{7,6},{8,9},{9,8},{10,11... | collective-permute-start | bytes 1572872 | tf_op jit(solution)/shard_map/ppermute | solution.py:564
  94.5 15.1 %all-to-all-start.4 = ((bf16[32,16,128]{2,1,0:T(8,128)(2,1)}), bf16[32,16,128]{2,1,0:T(8,128)(2,1)S(1)}, u32[]{:S(2)}, u32[]{:S(2)}) async-start(bf16[32,16,128]{2,1,0:T(8,128)(2,1)} %shard_map.137), calls=%async_computation.4 | async-start | bytes 262144 | tf_op jit(solution)/shard_map/all_to_all | solution.py:559
  101.4 13.4 %collective-permute-start.5 = (bf16[256,256]{1,0:T(8,128)(2,1)S(1)}, bf16[256,256]{1,0:T(8,128)(2,1)S(1)}, u32[]{:S(2)}, u32[]{:S(2)}) collective-permute-start(bf16[256,256]{1,0:T(8,128)(2,1)S(1)} %get-tuple-element.51), channel_id=1, source_target_pairs={{0,2},{1,3},{2,4},{3,5},{4,6},{5,7},{6,0},{7,1},{8,10},{9,11},{10,... | collective-permute-start | bytes 393224 | tf_op jit(solution)/shard_map/ppermute | solution.py:569
  101.5 13.3 %collective-permute-start.6 = (bf16[256,256]{1,0:T(8,128)(2,1)S(1)}, bf16[256,256]{1,0:T(8,128)(2,1)S(1)}, u32[]{:S(2)}, u32[]{:S(2)}) collective-permute-start(bf16[256,256]{1,0:T(8,128)(2,1)S(1)} %get-tuple-element.52), channel_id=1, source_target_pairs={{0,4},{1,5},{2,6},{3,7},{4,0},{5,1},{6,2},{7,3},{8,12},{9,13},{10,... | collective-permute-start | bytes 393224 | tf_op jit(solution)/shard_map/ppermute | solution.py:569
  104.8 10.0 %collective-permute-start.7 = (bf16[256,256]{1,0:T(8,128)(2,1)S(1)}, bf16[256,256]{1,0:T(8,128)(2,1)S(1)}, u32[]{:S(2)}, u32[]{:S(2)}) collective-permute-start(bf16[256,256]{1,0:T(8,128)(2,1)S(1)} %get-tuple-element.53), channel_id=1, source_target_pairs={{0,6},{1,7},{2,0},{3,1},{4,2},{5,3},{6,4},{7,5},{8,14},{9,15},{10,... | collective-permute-start | bytes 393224 | tf_op jit(solution)/shard_map/ppermute | solution.py:569
  110.2 13.7 %all-to-all-start.5 = ((bf16[32,16,128]{2,1,0:T(8,128)(2,1)}), bf16[32,16,128]{2,1,0:T(8,128)(2,1)S(1)}, u32[]{:S(2)}, u32[]{:S(2)}) async-start(bf16[32,16,128]{2,1,0:T(8,128)(2,1)} %shard_map.138), calls=%async_computation.5 | async-start | bytes 262144 | tf_op jit(solution)/shard_map/all_to_all | solution.py:559
  114.9 12.3 %collective-permute-start.13 = (bf16[256,256]{1,0:T(8,128)(2,1)S(1)}, bf16[256,256]{1,0:T(8,128)(2,1)S(1)}, u32[]{:S(2)}, u32[]{:S(2)}) collective-permute-start(bf16[256,256]{1,0:T(8,128)(2,1)S(1)} %add_convert_fusion.refs_0_), channel_id=1, source_target_pairs={{0,6},{1,7},{2,0},{3,1},{4,2},{5,3},{6,4},{7,5},{8,14},{9,15},{10,... | collective-permute-start | bytes 393224 | tf_op jit(solution)/shard_map/ppermute | solution.py:569
  117.1 10.1 %collective-permute-start.12 = (bf16[256,256]{1,0:T(8,128)(2,1)S(1)}, bf16[256,256]{1,0:T(8,128)(2,1)S(1)}, u32[]{:S(2)}, u32[]{:S(2)}) collective-permute-start(bf16[256,256]{1,0:T(8,128)(2,1)S(1)} %add_convert_fusion.refs_0_), channel_id=1, source_target_pairs={{0,4},{1,5},{2,6},{3,7},{4,0},{5,1},{6,2},{7,3},{8,12},{9,13},{10,... | collective-permute-start | bytes 393224 | tf_op jit(solution)/shard_map/ppermute | solution.py:569
  118.2 12.6 %collective-permute-start.11 = (bf16[256,256]{1,0:T(8,128)(2,1)S(1)}, bf16[256,256]{1,0:T(8,128)(2,1)S(1)}, u32[]{:S(2)}, u32[]{:S(2)}) collective-permute-start(bf16[256,256]{1,0:T(8,128)(2,1)S(1)} %add_convert_fusion.refs_0_), channel_id=1, source_target_pairs={{0,2},{1,3},{2,4},{3,5},{4,6},{5,7},{6,0},{7,1},{8,10},{9,11},{10,... | collective-permute-start | bytes 393224 | tf_op jit(solution)/shard_map/ppermute | solution.py:569
  123.9 7.2 %collective-permute-start.10 = (bf16[32,16,128]{2,1,0:T(8,128)(2,1)S(1)}, bf16[32,16,128]{2,1,0:T(8,128)(2,1)S(1)}, u32[]{:S(2)}, u32[]{:S(2)}) collective-permute-start(bf16[32,16,128]{2,1,0:T(8,128)(2,1)S(1)} %all-to-all-done.5.refs_0_), channel_id=1, source_target_pairs={{0,6},{1,7},{2,0},{3,1},{4,2},{5,3},{6,4},{7,5},{8,14},{9,15},{10,... | collective-permute-start | bytes 393224 | tf_op jit(solution)/shard_map/ppermute | solution.py:569
  126.1 8.0 %collective-permute-start.9 = (bf16[32,16,128]{2,1,0:T(8,128)(2,1)S(1)}, bf16[32,16,128]{2,1,0:T(8,128)(2,1)S(1)}, u32[]{:S(2)}, u32[]{:S(2)}) collective-permute-start(bf16[32,16,128]{2,1,0:T(8,128)(2,1)S(1)} %all-to-all-done.5.refs_0_), channel_id=1, source_target_pairs={{0,4},{1,5},{2,6},{3,7},{4,0},{5,1},{6,2},{7,3},{8,12},{9,13},{10,... | collective-permute-start | bytes 393224 | tf_op jit(solution)/shard_map/ppermute | solution.py:569
  127.2 8.3 %collective-permute-start.8 = (bf16[32,16,128]{2,1,0:T(8,128)(2,1)S(1)}, bf16[32,16,128]{2,1,0:T(8,128)(2,1)S(1)}, u32[]{:S(2)}, u32[]{:S(2)}) collective-permute-start(bf16[32,16,128]{2,1,0:T(8,128)(2,1)S(1)} %all-to-all-done.5.refs_0_), channel_id=1, source_target_pairs={{0,2},{1,3},{2,4},{3,5},{4,6},{5,7},{6,0},{7,1},{8,10},{9,11},{10,... | collective-permute-start | bytes 393224 | tf_op jit(solution)/shard_map/ppermute | solution.py:569
  127.2 9.7 %collective-permute-start.18 = (bf16[256,256]{1,0:T(8,128)(2,1)S(1)}, bf16[256,256]{1,0:T(8,128)(2,1)S(1)}, u32[]{:S(2)}, u32[]{:S(2)}) collective-permute-start(bf16[256,256]{1,0:T(8,128)(2,1)S(1)} %add_convert_fusion.refs_0_), channel_id=1, source_target_pairs={{0,1},{1,0},{2,3},{3,2},{4,5},{5,4},{6,7},{7,6},{8,9},{9,8},{10,11... | collective-permute-start | bytes 393224 | tf_op jit(solution)/shard_map/ppermute | solution.py:564
  130.8 6.1 %collective-permute-start.21 = (bf16[256,256]{1,0:T(8,128)(2,1)S(1)}, bf16[256,256]{1,0:T(8,128)(2,1)S(1)}, u32[]{:S(2)}, u32[]{:S(2)}) collective-permute-start(bf16[256,256]{1,0:T(8,128)(2,1)S(1)} %collective-permute-done.13.refs_3_), channel_id=1, source_target_pairs={{0,1},{1,0},{2,3},{3,2},{4,5},{5,4},{6,7},{7,6},{8,9},{9,8},{10,11... | collective-permute-start | bytes 393224 | tf_op jit(solution)/shard_map/ppermute | solution.py:564
  131.1 6.3 %collective-permute-start.20 = (bf16[256,256]{1,0:T(8,128)(2,1)S(1)}, bf16[256,256]{1,0:T(8,128)(2,1)S(1)}, u32[]{:S(2)}, u32[]{:S(2)}) collective-permute-start(bf16[256,256]{1,0:T(8,128)(2,1)S(1)} %collective-permute-done.12.refs_2_), channel_id=1, source_target_pairs={{0,1},{1,0},{2,3},{3,2},{4,5},{5,4},{6,7},{7,6},{8,9},{9,8},{10,11... | collective-permute-start | bytes 393224 | tf_op jit(solution)/shard_map/ppermute | solution.py:564
  134.1 4.6 %collective-permute-start.19 = (bf16[256,256]{1,0:T(8,128)(2,1)S(1)}, bf16[256,256]{1,0:T(8,128)(2,1)S(1)}, u32[]{:S(2)}, u32[]{:S(2)}) collective-permute-start(bf16[256,256]{1,0:T(8,128)(2,1)S(1)} %collective-permute-done.11.refs_1_), channel_id=1, source_target_pairs={{0,1},{1,0},{2,3},{3,2},{4,5},{5,4},{6,7},{7,6},{8,9},{9,8},{10,11... | collective-permute-start | bytes 393224 | tf_op jit(solution)/shard_map/ppermute | solution.py:564
  135.5 4.3 %collective-permute-start.14 = (bf16[32,16,128]{2,1,0:T(8,128)(2,1)S(1)}, bf16[32,16,128]{2,1,0:T(8,128)(2,1)S(1)}, u32[]{:S(2)}, u32[]{:S(2)}) collective-permute-start(bf16[32,16,128]{2,1,0:T(8,128)(2,1)S(1)} %all-to-all-done.5.refs_0_), channel_id=1, source_target_pairs={{0,1},{1,0},{2,3},{3,2},{4,5},{5,4},{6,7},{7,6},{8,9},{9,8},{10,11... | collective-permute-start | bytes 393224 | tf_op jit(solution)/shard_map/ppermute | solution.py:564
  136.9 3.0 %collective-permute-start.15 = (bf16[32,16,128]{2,1,0:T(8,128)(2,1)S(1)}, bf16[32,16,128]{2,1,0:T(8,128)(2,1)S(1)}, u32[]{:S(2)}, u32[]{:S(2)}) collective-permute-start(bf16[32,16,128]{2,1,0:T(8,128)(2,1)S(1)} %collective-permute-done.8.refs_1_), channel_id=1, source_target_pairs={{0,1},{1,0},{2,3},{3,2},{4,5},{5,4},{6,7},{7,6},{8,9},{9,8},{10,11... | collective-permute-start | bytes 393224 | tf_op jit(solution)/shard_map/ppermute | solution.py:564
  136.9 3.0 %collective-permute-start.16 = (bf16[32,16,128]{2,1,0:T(8,128)(2,1)S(1)}, bf16[32,16,128]{2,1,0:T(8,128)(2,1)S(1)}, u32[]{:S(2)}, u32[]{:S(2)}) collective-permute-start(bf16[32,16,128]{2,1,0:T(8,128)(2,1)S(1)} %collective-permute-done.9.refs_2_), channel_id=1, source_target_pairs={{0,1},{1,0},{2,3},{3,2},{4,5},{5,4},{6,7},{7,6},{8,9},{9,8},{10,11... | collective-permute-start | bytes 393224 | tf_op jit(solution)/shard_map/ppermute | solution.py:564
  137.4 2.5 %collective-permute-start.17 = (bf16[32,16,128]{2,1,0:T(8,128)(2,1)S(1)}, bf16[32,16,128]{2,1,0:T(8,128)(2,1)S(1)}, u32[]{:S(2)}, u32[]{:S(2)}) collective-permute-start(bf16[32,16,128]{2,1,0:T(8,128)(2,1)S(1)} %collective-permute-done.10.refs_3_), channel_id=1, source_target_pairs={{0,1},{1,0},{2,3},{3,2},{4,5},{5,4},{6,7},{7,6},{8,9},{9,8},{10,11... | collective-permute-start | bytes 393224 | tf_op jit(solution)/shard_map/ppermute | solution.py:564

commit v8 on v7

--- a/solution.py
+++ b/solution.py
@@ -123,14 +123,15 @@
 
 
 def request_kernel(
-    len_ref, ids_ref, table_hbm, out_ref, slot_hbm, table_ref, slot_ref, arrived, *, rows_own, cap
+    len_ref, ids_hbm, table_hbm, out_ref, slot_ref, table_ref, ids_ref, arrived, *, rows_own, cap
 ):
-    tables = begin([(table_hbm, table_ref)], arrived, 1)
+    copies = begin(((ids_hbm, ids_ref), (table_hbm, table_ref)), arrived)
     users, block = ids_ref.shape
     shards, _, lanes = out_ref.shape
     shift = rows_own.bit_length() - 1
     earlier = where_bf16(iota((block, block), 0) < iota((block, block), 1), 1.0)
     place = iota((lanes, block), 0)
+    finish(copies[:1])
     total = jnp.zeros((shards, lanes), f32)
     count = jnp.int32(0)
     slot_ref[...] = jnp.zeros_like(slot_ref)
@@ -147,10 +148,9 @@
         total = total + dot(named_16, where_bf16(chosen, low), NT)
         slot_ref[u : u + 1, :] = (owner * users + u) * cap + rank
         count = count + len_ref[u]
-    copies = begin([(slot_ref, slot_hbm)], arrived)
     wanted = jnp.where(iota((shards, lanes), 1) == users * cap, count, total.astype(i32))
     out_ref[:, 0, :] = wanted
-    finish(copies + tables)
+    finish(copies[1:])
 
 
 def answer_kernel(
@@ -241,7 +241,7 @@
 
 def project_kernel(
     at_ref,
-    slot_hbm,
+    slot_ref,
     answered_ref,
     quot_ref,
     wq_hbm,
@@ -251,7 +251,6 @@
     dmixed_ref,
     rem_ref,
     payload_hbm,
-    slot_ref,
     wq_ref,
     wk_ref,
     wv_ref,
@@ -269,19 +268,19 @@
     ends = []
     copies = begin(
         (
-            (slot_hbm, slot_ref),
             (wq_hbm, wq_ref),
             (wk_hbm, wk_ref),
             (wv_hbm, wv_ref),
         ),
         arrived,
     )
-    finish(copies[:1])
     hot = [tiled_match(spread_column(slot_ref[u : u + 1, :]), slots) for u in range(users)]
-    finish(copies[1:])
     for u in range(users):
         at = slice(u * block, (u + 1) * block)
         rem_ref[at, :] = dot(hot[u], answered_ref[...]).astype(bf16)
+    finish(copies)
+    for u in range(users):
+        at = slice(u * block, (u + 1) * block)
         embedded = (quot_ref[at, :].astype(f32) * rem_ref[at, :].astype(f32)).astype(bf16)
         q = dot(embedded, wq_ref[...]).astype(bf16)
         k = dot(embedded, wk_ref[...]).astype(bf16)
@@ -308,7 +307,7 @@
     states_ref[1, users * size :, :] = tail
     which = [jnp.where(peer > me, 0, 1) for peer in range(peers)]
     pairs = [(states_ref.at[which[peer]], payload_hbm.at[peer]) for peer in range(peers)]
-    finish(begin(pairs, arrived, 4))
+    finish(begin(pairs, arrived, 3))
 
 
 def within_kernel(
@@ -319,8 +318,9 @@
     wq_ref,
     wk_ref,
     wv_ref,
-    out_hbm,
-    out_ref,
+    near_ref,
+    far_hbm,
+    far_ref,
     arrived,
     *,
     scale,
@@ -357,9 +357,10 @@
             dq = dq + dot(dweights, k_h)
             dk = dk + dot(dweights, q_h, TN)
             dv = dv + dot(weights, d_h, TN)
-        for i, part in enumerate((mixed, dq, dk, dv)):
-            out_ref[i, at, :] = part
-        copies += begin([(out_ref.at[:, at, :], out_hbm.at[:, at, :])], arrived, u)
+        near_ref[at, :] = mixed
+        for i, part in enumerate((dq, dk, dv)):
+            far_ref[i, at, :] = part
+        copies += begin([(far_ref.at[:, at, :], far_hbm.at[:, at, :])], arrived, u)
     finish(copies)
 
 
@@ -373,12 +374,13 @@
 def gradient_kernel(
     at_ref,
     payload_ref,
-    within_hbm,
+    near_ref,
+    far_hbm,
     dmixed_ref,
     wide_ref,
     rem_ref,
     quot_ref,
-    slot_hbm,
+    slot_ref,
     ids_hbm,
     wq_hbm,
     wk_hbm,
@@ -388,8 +390,7 @@
     rem_send_hbm,
     keep_ref,
     give_ref,
-    within_ref,
-    slot_ref,
+    far_ref,
     ids_ref,
     wq_ref,
     wk_ref,
@@ -410,7 +411,6 @@
             (wk_hbm, wk_ref),
             (wv_hbm, wv_ref),
             (w_out_hbm, w_out_ref),
-            (slot_hbm, slot_ref),
             (ids_hbm, ids_ref),
         ),
         arrived,
@@ -418,7 +418,7 @@
     waits = []
     for u in range(users):
         at = slice(u * block, (u + 1) * block)
-        waits += begin([(within_hbm.at[:, at, :], within_ref.at[:, at, :])], arrived, 6 + u)
+        waits += begin([(far_hbm.at[:, at, :], far_ref.at[:, at, :])], arrived, 5 + u)
     peers = payload_ref.shape[0]
     size = width // heads
     slots = rem_send_ref.shape[0]
@@ -456,15 +456,15 @@
         v = dot(embedded, wv_ref[...]).astype(bf16)
         dmixed = dmixed_ref[at, :]
         wide = wide_ref[at, :]
-        finish(waits[u : u + 1])
         growth = scale * jnp.exp(wide)
         falloff = scale * jnp.exp(wide[block - 1 : block, :] - wide)
-        mixed = (within_ref[0, at, :] + growth * dot(q, entering)).astype(bf16)
+        mixed = (near_ref[at, :] + growth * dot(q, entering)).astype(bf16)
         out_ref[u] = dot(mixed, w_out_ref[...]).astype(bf16)
-        copies += begin([(out_ref.at[u], out_hbm.at[u])], arrived, 6 + users + u)
-        dq = (within_ref[1, at, :] + growth * dot(dmixed, entering, NT)).astype(bf16)
-        dk = (within_ref[2, at, :] + falloff * dot(v, leaving, NT)).astype(bf16)
-        dv = (within_ref[3, at, :] + falloff * dot(k, leaving)).astype(bf16)
+        copies += begin([(out_ref.at[u], out_hbm.at[u])], arrived, 5 + users + u)
+        finish(waits[u : u + 1])
+        dq = (far_ref[0, at, :] + growth * dot(dmixed, entering, NT)).astype(bf16)
+        dk = (far_ref[1, at, :] + falloff * dot(v, leaving, NT)).astype(bf16)
+        dv = (far_ref[2, at, :] + falloff * dot(k, leaving)).astype(bf16)
         dembedded = dot(dq, wq_ref[...], NT) + dot(dk, wk_ref[...], NT) + dot(dv, wv_ref[...], NT)
         rem_terms.append((dembedded * quot_ref[at, :].astype(f32)).astype(bf16))
         quot_terms.append((dembedded * rem_ref[at, :].astype(f32)).astype(bf16))
@@ -472,7 +472,7 @@
     quot_terms = jnp.concatenate(quot_terms, axis=0)
     slot = jnp.concatenate([slot_ref[u : u + 1, :] for u in range(users)], axis=1)
     ids = jnp.concatenate([ids_ref[u : u + 1, :] for u in range(users)], axis=1)
-    n = 6 + 2 * users
+    n = 5 + 2 * users
     for j, hot in enumerate(stacked_match(slot, block, slots // block)):
         at = slice(j * block, (j + 1) * block)
         rem_send_ref[at, :] = dot(hot, rem_terms).astype(bf16)
@@ -529,29 +529,34 @@
         out_ref[i] = total
 
 
-def place_kernel(at_ref, wanted_ref, *refs, chips, per, total, other):
-    out_hbm, out_ref, arrived = refs[-3:]
-    chunks = refs[:chips]
+def place_kernel(at_ref, wanted_ref, *refs, jobs, chips, per, total):
+    outs = refs[-2 * len(jobs) - 1 : -len(jobs) - 1]
+    staged = refs[-len(jobs) - 1 : -1]
+    arrived = refs[-1]
     copies = []
-    _, rows, width = out_ref.shape
     shards, _, lanes = wanted_ref.shape
     counted = jnp.where(iota((shards, lanes), 1) == per, wanted_ref[:, 0, :], 0)
     ratio = total / jnp.sum(counted.astype(f32), axis=(0, 1), keepdims=True)
     chip, core = at_ref[0] // 2, at_ref[0] % 2
-    half = core + other - 2 * core * other
-    for d, chunk in enumerate(chunks):
-        spot = half * chips + lax.rem(chip + chips - d, chips)
-        base = pl.multiple_of(spot * rows, rows)
-        if len(chunk.shape) == 2:
-            out_ref[d] = ratio * chunk[...].astype(f32)
-        else:
-            part = chunk.shape[1]
-            for i in range(shards):
-                across = i % (width // 128) * 128
-                down = i // (width // 128) * part
-                tile = ratio * chunk[i].astype(f32)
-                out_ref[d, down : down + part, across : across + 128] = tile
-        copies += begin([(out_ref.at[d], out_hbm.at[pl.ds(base, rows), :])], arrived, d)
+    for n, other in enumerate(jobs):
+        out_hbm, out_ref = outs[n], staged[n]
+        _, rows, width = out_ref.shape
+        half = core + other - 2 * core * other
+        for d in range(chips):
+            chunk = refs[n * chips + d]
+            spot = half * chips + lax.rem(chip + chips - d, chips)
+            base = pl.multiple_of(spot * rows, rows)
+            if len(chunk.shape) == 2:
+                out_ref[d] = ratio * chunk[...].astype(f32)
+            else:
+                part = chunk.shape[1]
+                for i in range(shards):
+                    across = i % (width // 128) * 128
+                    down = i // (width // 128) * part
+                    tile = ratio * chunk[i].astype(f32)
+                    out_ref[d, down : down + part, across : across + 128] = tile
+            pair = (out_ref.at[d], out_hbm.at[pl.ds(base, rows), :])
+            copies += begin([pair], arrived, n * chips + d)
     finish(copies)
 
 
@@ -584,16 +589,23 @@
     return [chunk] + [to_chip(chunk, d) for d in range(1, chips)]
 
 
-def place(at, wanted, chunks, rows, width, per, total, out=None):
-    chips = len(chunks)
-    scratch = [pltpu.VMEM((chips, rows // (2 * chips), width), f32), dma(chips)]
-    other = 0 if out is None else 1
-    kernel = functools.partial(place_kernel, chips=chips, per=per, total=total, other=other)
-    args, specs, aliases = (at, wanted, *chunks), [SM] + [VM] * (1 + chips), {}
-    if other:
-        args, specs, aliases = args + (out,), specs + [HB], {len(args): 0}
-    (out,) = call(kernel, [((rows, width), f32)], args, specs, scratch, [HB], aliases=aliases)
-    return out
+def place(at, wanted, jobs, width, per, total):
+    chips = len(jobs[0][0])
+    args, specs, outs, scratch, others, aliases = (at, wanted), [SM, VM], [], [], [], {}
+    for chunks, rows, out in jobs:
+        args, specs = args + tuple(chunks), specs + [VM] * chips
+        outs.append(((rows, width), f32))
+        scratch.append(pltpu.VMEM((chips, rows // (2 * chips), width), f32))
+        others.append(0 if out is None else 1)
+    for n, (_, _, out) in enumerate(jobs):
+        if out is not None:
+            aliases[len(args)] = n
+            args, specs = args + (out,), specs + [HB]
+    kernel = functools.partial(
+        place_kernel, jobs=tuple(others), chips=chips, per=per, total=total
+    )
+    scratch.append(dma(chips * len(jobs)))
+    return call(kernel, outs, args, specs, scratch, [HB] * len(jobs), aliases=aliases)
 
 
 def body(
@@ -627,10 +639,10 @@
     requests, slot, table = call(
         functools.partial(request_kernel, rows_own=rows_own, cap=cap),
         [((shards, 1, lanes), i32), ((8, block), i32), (rem_table.shape, bf16)],
-        (in_hbm(lengths), in_hbm(rem_ids), rem_table),
-        [SM, VM, HB],
-        [pltpu.VMEM((8, block), i32), dma(2)],
-        [VM, HB, IN_VM],
+        (in_hbm(lengths), rem_ids, rem_table),
+        [SM, HB, HB],
+        [pltpu.VMEM((users, block), i32), dma(2)],
+        [VM, IN_VM, IN_VM],
         MOST,
     )
     wanted = exchange(requests, "user")
@@ -662,23 +674,21 @@
         functools.partial(project_kernel, users=users, heads=heads),
         [((users * block, width), bf16), ((peers, users * size + 16, width), bf16)],
         (at, slot, answered, quot_emb, w_query, w_key, w_value, wide, dmixed),
-        [SM, HB, VM, IN_VM, HB, HB, HB, IN_VM, IN_VM],
-        [pltpu.VMEM((8, block), i32)]
-        + [square] * 3
-        + [pltpu.VMEM((2, users * size + 16, width), bf16), dma(4 + peers)],
+        [SM, IN_VM, VM, IN_VM, HB, HB, HB, IN_VM, IN_VM],
+        [square] * 3 + [pltpu.VMEM((2, users * size + 16, width), bf16), dma(3 + peers)],
         [IN_VM, HB],
         MOST,
     )
     states = exchange(payload, "hist")
-    parts = (4, users * block, width)
-    (within,) = call(
+    parts = (3, users * block, width)
+    near, far = call(
         functools.partial(within_kernel, scale=scale),
-        [(parts, f32)],
+        [(parts[1:], f32), (parts, f32)],
         (quot_emb, rem_emb, dmixed)
         + tuple(in_hbm(a) for a in (log_decay, w_query, w_key, w_value)),
         [IN_VM] * 3 + [VM] * 4,
         [pltpu.VMEM(parts, f32), dma(users)],
-        [HB],
+        [IN_VM, HB],
         MOST,
     )
     output, rem_send, keep, give = call(
@@ -686,17 +696,16 @@
         [
             ((users, block, width), bf16),
             ((slots, width), bf16),
-            ((rows_all // 2, width), f32),
+            ((rows_all // 2, width), bf16),
             ((rows_all // 2, width), bf16),
         ],
-        (at, states, within, dmixed, wide, rem_emb, quot_emb, slot, quot_ids)
+        (at, states, near, far, dmixed, wide, rem_emb, quot_emb, slot, quot_ids)
         + (w_query, w_key, w_value, w_out),
-        [SM, VM, HB] + [IN_VM] * 4 + [HB] * 6,
-        [pltpu.VMEM(parts, f32)]
-        + [pltpu.VMEM((8, block), i32), pltpu.VMEM((users, block), i32)]
+        [SM, VM, IN_VM, HB] + [IN_VM] * 5 + [HB] * 5,
+        [pltpu.VMEM(parts, f32), pltpu.VMEM((users, block), i32)]
         + [square] * 4
         + [pltpu.VMEM((users, block, width), bf16), pltpu.VMEM((slots, width), bf16)]
-        + [dma(6 + 2 * users + slots // block)],
+        + [dma(5 + 2 * users + slots // block)],
         [HB, HB, IN_VM, IN_VM],
         MOST,
     )
@@ -722,14 +731,14 @@
     rem_mine = along_chips(rem_sum)
     quot_tiles, _ = lax.optimization_barrier((quot_tiles, rem_sum))
     total = float(users * shards * block * peers)
-    rem_grad = place(at, wanted, rem_mine, rows_own, width, per, total)
+    (rem_grad,) = place(at, wanted, [(rem_mine, rows_own, None)], width, per, total)
     quot_mine = along_chips(quot_tiles)
     rem_theirs = [to_core(c) for c in rem_mine]
     *quot_mine, rem_grad = lax.optimization_barrier((*quot_mine, rem_grad))
-    rem_grad = place(at, wanted, rem_theirs, rows_own, width, per, total, rem_grad)
     quot_theirs = [to_core(c) for c in quot_mine]
-    quot_grad = place(at, wanted, quot_mine, rows_all, width, per, total)
-    quot_grad = place(at, wanted, quot_theirs, rows_all, width, per, total, quot_grad)
+    jobs = [(quot_mine, rows_all, None), (rem_theirs, rows_own, rem_grad)]
+    quot_grad, rem_grad = place(at, wanted, jobs, width, per, total)
+    (quot_grad,) = place(at, wanted, [(quot_theirs, rows_all, quot_grad)], width, per, total)
     return (output, quot_grad, rem_grad)
 
 

time: 142 us -> 141 us (level)
    pallas_call x16 -> x15, Pallas kernels: 29.1 us -> 27.7 us  [call(): pl.pallas_call(kernel, out_shape=tuple(shapes), in_specs=specs, out_specs...]
where the time goes in v8:
time: 141 us; the launch traced here: 140 us
  starting transfers between devices  57.2 us (41%)
  waiting for transfers between devices  33.6 us (24%)
  Pallas kernels  27.7 us (20%)
  blocking collectives  20.5 us (15%)
    all_to_all x5, starting transfers between devices, exchange(): return lax.all_to_all(array, axis, split_axis=0, concat_axis=0, tiled=True)  28.9 us
    pallas_call x15, Pallas kernels, call(): pl.pallas_call(kernel, out_shape=tuple(shapes), in_specs=specs, out_specs...  27.7 us
    all_to_all x5, waiting for transfers between devices, exchange(): return lax.all_to_all(array, axis, split_axis=0, concat_axis=0, tiled=True)  25.7 us
    all_to_all x1, blocking collectives, exchange(): return lax.all_to_all(array, axis, split_axis=0, concat_axis=0, tiled=True)  20.5 us
    ppermute x10, starting transfers between devices, to_core(): return lax.ppermute(array, 'hist', [(i, i ^ 1) for i in range(peers)])  14.7 us
    ppermute x12, starting transfers between devices, to_chip(): lax.ppermute(array, 'hist', [(i, (i + 2 * steps) % peers) for i in range(...  13.6 us
    ppermute x12, waiting for transfers between devices, to_chip(): lax.ppermute(array, 'hist', [(i, (i + 2 * steps) % peers) for i in range(...  6.32 us
  transfers between devices with their start and end apart: 27, of which 9 were waited for; matrix products, arithmetic and copies ran while one was open for 0% of the time, Pallas kernels for 10%

profile of v8, /device:TPU:1, one launch (start us, length us, event | category | flops | bytes accessed | tf_op | source)
XLA Modules:
  0.0 140.0 jit_solution(14868594091041578400)
XLA Ops:
  0.6 2.1 %shard_map.130 = (s32[32,1,128]{2,1,0:T(1,128)S(1)}, s32[8,256]{1,0:T(8,128)S(1)}, bf16[2048,256]{1,0:T(8,128)(2,1)S(1)}) custom-call(s32[2]{0:T(128)} %len_ref.3, s32[2,256]{1,0:T(2,128)} %ids_hbm.2, bf16[2048,256]{1,0:T(8,128)(2,1)} %table_hbm.1), custom_call_target="tpu_custom_call" | custom-call | tf_op jit(solution)/shard_map/pallas_call | solution.py:114
  2.7 20.5 %all_to_all.30.wanted_ref = s32[32,1,128]{2,1,0:T(1,128)S(1)} all-to-all(s32[32,1,128]{2,1,0:T(1,128)S(1)} %get-tuple-element.37), channel_id=1, replica_groups=mesh['user'=32,'hist'=8] {'user'}, dimensions={0} | all-to-all | bytes 32768 | tf_op jit(solution)/shard_map/all_to_all | solution.py:564
  23.2 3.0 %shard_map.131 = bf16[1024,256]{1,0:T(8,128)(2,1)} custom-call(s32[32,1,128]{2,1,0:T(1,128)S(1)} %all_to_all.30.wanted_ref, bf16[2048,256]{1,0:T(8,128)(2,1)S(1)} %get-tuple-element.38.table_ref), custom_call_target="tpu_custom_call" | custom-call | tf_op jit(solution)/shard_map/pallas_call | solution.py:114
  26.2 3.9 %all-to-all-start.1 = ((bf16[32,32,256]{2,1,0:T(8,128)(2,1)}), bf16[32,32,256]{2,1,0:T(8,128)(2,1)S(1)}, u32[]{:S(2)}, u32[]{:S(2)}) async-start(bf16[32,32,256]{2,1,0:T(8,128)(2,1)} %bitcast.8), calls=%async_computation.1 | async-start | bytes 1048576 | tf_op jit(solution)/shard_map/all_to_all | solution.py:564
  30.1 2.9 %shard_map.132 = (bf16[512,256]{1,0:T(8,128)(2,1)S(1)}, bf16[512,256]{1,0:T(8,128)(2,1)S(1)}, f32[512,256]{1,0:T(8,128)S(1)}) custom-call(s32[2]{0:T(128)S(1)} %copy-done, s32[1]{0:T(128)} %bitcast.at_ref, s32[2,256]{1,0:T(2,128)} %ids_hbm.3, bf16[2048,256]{1,0:T(8,128)(2,1)} %table_ref.1, bf16[2,256,256]{2,1,0:T(8,128)(2,1)} %cot_ref.1, ...), custom_call_target="tpu_custom_call" | custom-call | tf_op jit(solution)/shard_map/pallas_call | solution.py:114
  33.0 10.0 %all-to-all-done.1 = bf16[32,32,256]{2,1,0:T(8,128)(2,1)S(1)} async-done(((bf16[32,32,256]{2,1,0:T(8,128)(2,1)}), bf16[32,32,256]{2,1,0:T(8,128)(2,1)S(1)}, u32[]{:S(2)}, u32[]{:S(2)}) %all-to-all-start.1) | async-done | bytes 524320 | tf_op jit(solution)/shard_map/all_to_all | solution.py:564
  43.0 3.0 %shard_map.133 = (bf16[512,256]{1,0:T(8,128)(2,1)S(1)}, bf16[8,144,256]{2,1,0:T(8,128)(2,1)}) custom-call(s32[1]{0:T(128)} %bitcast.at_ref, s32[8,256]{1,0:T(8,128)S(1)} %get-tuple-element.36.slot_ref, bf16[1024,256]{1,0:T(8,128)(2,1)S(1)} %bitcast.7, bf16[512,256]{1,0:T(8,128)(2,1)S(1)} %get-tuple-element.39.quot_ref, bf16[256,256]{1,0:T(8,128)(2,1)} %wq_hbm.3, ...), custom_call_target="tpu_custom_call" | custom-call | tf_op jit(solution)/shard_map/pallas_call | solution.py:114
  46.1 9.5 %all-to-all-start.2 = ((bf16[8,144,256]{2,1,0:T(8,128)(2,1)}), bf16[8,144,256]{2,1,0:T(8,128)(2,1)S(1)}, u32[]{:S(2)}, u32[]{:S(2)}) async-start(bf16[8,144,256]{2,1,0:T(8,128)(2,1)} %get-tuple-element.42), calls=%async_computation.2 | async-start | bytes 1179648 | tf_op jit(solution)/shard_map/all_to_all | solution.py:564
  55.5 5.4 %shard_map.134 = (f32[512,256]{1,0:T(8,128)S(1)}, f32[3,512,256]{2,1,0:T(8,128)}) custom-call(bf16[512,256]{1,0:T(8,128)(2,1)S(1)} %get-tuple-element.39.quot_ref, bf16[512,256]{1,0:T(8,128)(2,1)S(1)} %get-tuple-element.43.rem_ref, bf16[512,256]{1,0:T(8,128)(2,1)S(1)} %get-tuple-element.41.dmixed_ref, f32[2,4,256]{2,1,0:T(4,128)} %decay_ref.3, ...), custom_call_target="tpu_custom_call" | custom-call | tf_op jit(solution)/shard_map/pallas_call | solution.py:114
  60.9 4.8 %all-to-all-done.2.payload_ref = bf16[8,144,256]{2,1,0:T(8,128)(2,1)S(1)} async-done(((bf16[8,144,256]{2,1,0:T(8,128)(2,1)}), bf16[8,144,256]{2,1,0:T(8,128)(2,1)S(1)}, u32[]{:S(2)}, u32[]{:S(2)}) %all-to-all-start.2) | async-done | bytes 589856 | tf_op jit(solution)/shard_map/all_to_all | solution.py:564
  65.7 4.2 %shard_map.135 = (bf16[2,256,256]{2,1,0:T(8,128)(2,1)}, bf16[1024,256]{1,0:T(8,128)(2,1)}, bf16[1024,256]{1,0:T(8,128)(2,1)S(1)}, bf16[1024,256]{1,0:T(8,128)(2,1)S(1)}) custom-call(s32[1]{0:T(128)} %bitcast.at_ref, bf16[8,144,256]{2,1,0:T(8,128)(2,1)S(1)} %all-to-all-done.2.payload_ref, f32[512,256]{1,0:T(8,128)S(1)} %get-tuple-element.44.near_ref, ...), custom_call_target="tpu_custom_call" | custom-call | tf_op jit(solution)/shard_map/pallas_call | solution.py:114
  69.9 5.1 %all-to-all-start.3 = ((bf16[32,32,256]{2,1,0:T(8,128)(2,1)}), bf16[32,32,256]{2,1,0:T(8,128)(2,1)S(1)}, u32[]{:S(2)}, u32[]{:S(2)}) async-start(bf16[32,32,256]{2,1,0:T(8,128)(2,1)} %bitcast.9), calls=%async_computation.3 | async-start | bytes 1048576 | tf_op jit(solution)/shard_map/all_to_all | solution.py:564
  74.9 1.4 %collective-permute-start = (bf16[1024,256]{1,0:T(8,128)(2,1)S(1)}, bf16[1024,256]{1,0:T(8,128)(2,1)S(1)}, u32[]{:S(2)}, u32[]{:S(2)}) collective-permute-start(bf16[1024,256]{1,0:T(8,128)(2,1)S(1)} %get-tuple-element.49), channel_id=1, source_target_pairs={{0,1},{1,0},{2,3},{3,2},{4,5},{5,4},{6,7},{7,6},{8,9},{9,8},{10,11... | collective-permute-start | bytes 1572872 | tf_op jit(solution)/shard_map/ppermute | solution.py:569
  76.4 1.5 %collective-permute-done.got_ref = bf16[1024,256]{1,0:T(8,128)(2,1)S(1)} collective-permute-done((bf16[1024,256]{1,0:T(8,128)(2,1)S(1)}, bf16[1024,256]{1,0:T(8,128)(2,1)S(1)}, u32[]{:S(2)}, u32[]{:S(2)}) %collective-permute-start) | collective-permute-done | bytes 524320 | tf_op jit(solution)/shard_map/ppermute | solution.py:569
  77.9 0.1 shard_map.136
  78.0 0.4 collective-permute-start.1
  78.4 1.8 %collective-permute-start.2 = (bf16[256,256]{1,0:T(8,128)(2,1)S(1)}, bf16[256,256]{1,0:T(8,128)(2,1)S(1)}, u32[]{:S(2)}, u32[]{:S(2)}) collective-permute-start(bf16[256,256]{1,0:T(8,128)(2,1)S(1)} %get-tuple-element.52), channel_id=1, source_target_pairs={{0,4},{1,5},{2,6},{3,7},{4,0},{5,1},{6,2},{7,3},{8,12},{9,13},{10,... | collective-permute-start | bytes 393224 | tf_op jit(solution)/shard_map/ppermute | solution.py:574
  80.2 0.7 collective-permute-start.3
  80.9 3.7 %collective-permute-done.1.refs_1_ = bf16[256,256]{1,0:T(8,128)(2,1)S(1)} collective-permute-done((bf16[256,256]{1,0:T(8,128)(2,1)S(1)}, bf16[256,256]{1,0:T(8,128)(2,1)S(1)}, u32[]{:S(2)}, u32[]{:S(2)}) %collective-permute-start.1) | collective-permute-done | bytes 131104 | tf_op jit(solution)/shard_map/ppermute | solution.py:574
  84.6 1.6 %collective-permute-done.2.refs_2_ = bf16[256,256]{1,0:T(8,128)(2,1)S(1)} collective-permute-done((bf16[256,256]{1,0:T(8,128)(2,1)S(1)}, bf16[256,256]{1,0:T(8,128)(2,1)S(1)}, u32[]{:S(2)}, u32[]{:S(2)}) %collective-permute-start.2) | collective-permute-done | bytes 131104 | tf_op jit(solution)/shard_map/ppermute | solution.py:574
  86.3 0.9 collective-permute-done.3.refs_3_
  87.2 0.7 shard_map.137
  87.9 1.1 all-to-all-done.3
  89.0 0.9 shard_map.140
  89.8 4.1 %collective-permute-start.4 = (bf16[1024,256]{1,0:T(8,128)(2,1)S(1)}, bf16[1024,256]{1,0:T(8,128)(2,1)S(1)}, u32[]{:S(2)}, u32[]{:S(2)}) collective-permute-start(bf16[1024,256]{1,0:T(8,128)(2,1)S(1)} %shard_map.140), channel_id=1, source_target_pairs={{0,1},{1,0},{2,3},{3,2},{4,5},{5,4},{6,7},{7,6},{8,9},{9,8},{10,11... | collective-permute-start | bytes 1572872 | tf_op jit(solution)/shard_map/ppermute | solution.py:569
  93.9 5.9 %all-to-all-start.4 = ((bf16[32,16,128]{2,1,0:T(8,128)(2,1)}), bf16[32,16,128]{2,1,0:T(8,128)(2,1)S(1)}, u32[]{:S(2)}, u32[]{:S(2)}) async-start(bf16[32,16,128]{2,1,0:T(8,128)(2,1)} %shard_map.137), calls=%async_computation.4 | async-start | bytes 262144 | tf_op jit(solution)/shard_map/all_to_all | solution.py:564
  99.9 0.9 shard_map.139.keep_ref
  100.7 0.0 collective-permute-done.4.got_ref
  100.7 0.1 shard_map.141
  100.8 0.1 collective-permute-start.5
  101.0 3.3 %collective-permute-start.6 = (bf16[256,256]{1,0:T(8,128)(2,1)S(1)}, bf16[256,256]{1,0:T(8,128)(2,1)S(1)}, u32[]{:S(2)}, u32[]{:S(2)}) collective-permute-start(bf16[256,256]{1,0:T(8,128)(2,1)S(1)} %get-tuple-element.58), channel_id=1, source_target_pairs={{0,4},{1,5},{2,6},{3,7},{4,0},{5,1},{6,2},{7,3},{8,12},{9,13},{10,... | collective-permute-start | bytes 393224 | tf_op jit(solution)/shard_map/ppermute | solution.py:574
  104.3 0.0 collective-permute-start.7
  104.3 4.7 %all-to-all-done.4.tiles_ref = bf16[32,16,128]{2,1,0:T(8,128)(2,1)S(1)} async-done(((bf16[32,16,128]{2,1,0:T(8,128)(2,1)}), bf16[32,16,128]{2,1,0:T(8,128)(2,1)S(1)}, u32[]{:S(2)}, u32[]{:S(2)}) %all-to-all-start.4) | async-done | bytes 131104 | tf_op jit(solution)/shard_map/all_to_all | solution.py:564
  109.0 0.7 shard_map.138
  109.7 4.5 %all-to-all-start.5 = ((bf16[32,16,128]{2,1,0:T(8,128)(2,1)}), bf16[32,16,128]{2,1,0:T(8,128)(2,1)S(1)}, u32[]{:S(2)}, u32[]{:S(2)}) async-start(bf16[32,16,128]{2,1,0:T(8,128)(2,1)} %shard_map.138), calls=%async_computation.5 | async-start | bytes 262144 | tf_op jit(solution)/shard_map/all_to_all | solution.py:564
  114.2 0.0 collective-permute-done.5
  114.3 0.1 add_convert_fusion.refs_0_
  114.3 1.5 %collective-permute-start.11 = (bf16[256,256]{1,0:T(8,128)(2,1)S(1)}, bf16[256,256]{1,0:T(8,128)(2,1)S(1)}, u32[]{:S(2)}, u32[]{:S(2)}) collective-permute-start(bf16[256,256]{1,0:T(8,128)(2,1)S(1)} %add_convert_fusion.refs_0_), channel_id=1, source_target_pairs={{0,2},{1,3},{2,4},{3,5},{4,6},{5,7},{6,0},{7,1},{8,10},{9,11},{10,... | collective-permute-start | bytes 393224 | tf_op jit(solution)/shard_map/ppermute | solution.py:574
  115.9 1.9 %collective-permute-start.12 = (bf16[256,256]{1,0:T(8,128)(2,1)S(1)}, bf16[256,256]{1,0:T(8,128)(2,1)S(1)}, u32[]{:S(2)}, u32[]{:S(2)}) collective-permute-start(bf16[256,256]{1,0:T(8,128)(2,1)S(1)} %add_convert_fusion.refs_0_), channel_id=1, source_target_pairs={{0,4},{1,5},{2,6},{3,7},{4,0},{5,1},{6,2},{7,3},{8,12},{9,13},{10,... | collective-permute-start | bytes 393224 | tf_op jit(solution)/shard_map/ppermute | solution.py:574
  117.8 0.6 collective-permute-start.13
  118.4 5.0 %all-to-all-done.5.refs_0_ = bf16[32,16,128]{2,1,0:T(8,128)(2,1)S(1)} async-done(((bf16[32,16,128]{2,1,0:T(8,128)(2,1)}), bf16[32,16,128]{2,1,0:T(8,128)(2,1)S(1)}, u32[]{:S(2)}, u32[]{:S(2)}) %all-to-all-start.5) | async-done | bytes 131104 | tf_op jit(solution)/shard_map/all_to_all | solution.py:564
  123.4 2.2 %collective-permute-start.10 = (bf16[32,16,128]{2,1,0:T(8,128)(2,1)S(1)}, bf16[32,16,128]{2,1,0:T(8,128)(2,1)S(1)}, u32[]{:S(2)}, u32[]{:S(2)}) collective-permute-start(bf16[32,16,128]{2,1,0:T(8,128)(2,1)S(1)} %all-to-all-done.5.refs_0_), channel_id=1, source_target_pairs={{0,6},{1,7},{2,0},{3,1},{4,2},{5,3},{6,4},{7,5},{8,14},{9,15},{10,... | collective-permute-start | bytes 393224 | tf_op jit(solution)/shard_map/ppermute | solution.py:574
  125.6 0.0 collective-permute-start.8
  125.6 0.0 collective-permute-done.11.refs_1_
  125.6 1.2 collective-permute-start.9
  126.8 3.6 %collective-permute-start.18 = (bf16[256,256]{1,0:T(8,128)(2,1)S(1)}, bf16[256,256]{1,0:T(8,128)(2,1)S(1)}, u32[]{:S(2)}, u32[]{:S(2)}) collective-permute-start(bf16[256,256]{1,0:T(8,128)(2,1)S(1)} %add_convert_fusion.refs_0_), channel_id=1, source_target_pairs={{0,1},{1,0},{2,3},{3,2},{4,5},{5,4},{6,7},{7,6},{8,9},{9,8},{10,11... | collective-permute-start | bytes 393224 | tf_op jit(solution)/shard_map/ppermute | solution.py:569
  130.3 0.0 collective-permute-done.13.refs_3_
  130.4 0.3 collective-permute-start.19
  130.7 0.0 collective-permute-done.10.refs_3_
  130.7 1.7 %collective-permute-start.20 = (bf16[256,256]{1,0:T(8,128)(2,1)S(1)}, bf16[256,256]{1,0:T(8,128)(2,1)S(1)}, u32[]{:S(2)}, u32[]{:S(2)}) collective-permute-start(bf16[256,256]{1,0:T(8,128)(2,1)S(1)} %collective-permute-done.12.refs_2_), channel_id=1, source_target_pairs={{0,1},{1,0},{2,3},{3,2},{4,5},{5,4},{6,7},{7,6},{8,9},{9,8},{10,11... | collective-permute-start | bytes 393224 | tf_op jit(solution)/shard_map/ppermute | solution.py:569
  132.3 1.1 shard_map.142.refs_8_
  133.5 2.6 %collective-permute-start.21 = (bf16[256,256]{1,0:T(8,128)(2,1)S(1)}, bf16[256,256]{1,0:T(8,128)(2,1)S(1)}, u32[]{:S(2)}, u32[]{:S(2)}) collective-permute-start(bf16[256,256]{1,0:T(8,128)(2,1)S(1)} %collective-permute-done.13.refs_3_), channel_id=1, source_target_pairs={{0,1},{1,0},{2,3},{3,2},{4,5},{5,4},{6,7},{7,6},{8,9},{9,8},{10,11... | collective-permute-start | bytes 393224 | tf_op jit(solution)/shard_map/ppermute | solution.py:569
  136.1 0.0 collective-permute-done.9.refs_2_
  136.1 0.0 collective-permute-start.14
  136.1 0.5 collective-permute-start.15
  136.6 0.0 collective-permute-done.19.refs_5_
  136.6 0.1 collective-permute-start.16
  136.7 0.0 collective-permute-done.20.refs_6_
  136.7 0.4 collective-permute-start.17
  137.1 0.0 collective-permute-done.21.refs_7_
  137.1 1.5 %shard_map.143 = (f32[2048,256]{1,0:T(8,128)}, f32[2048,256]{1,0:T(8,128)}) custom-call(s32[1]{0:T(128)} %bitcast.at_ref, s32[32,1,128]{2,1,0:T(1,128)S(1)} %all_to_all.30.wanted_ref, bf16[32,16,128]{2,1,0:T(8,128)(2,1)S(1)} %all-to-all-done.5.refs_0_, bf16[32,16,128]{2,1,0:T(8,128)(2,1)S(1)} %collective-permute-done.8.refs_1_, ...), custom_call_target="tpu_custom_call", output_to_operand_aliasing={{1}: (10, {})} | custom-call | tf_op jit(solution)/shard_map/pallas_call | solution.py:114
  138.7 0.0 collective-permute-done.15.refs_1_
  138.7 0.0 collective-permute-done.16.refs_2_
  138.7 1.2 shard_map.144
  (9 shorter events, 0.0 us)
Async XLA Ops:
  0.6 29.4 %copy-start = (s32[2]{0:T(128)S(1)}, s32[2]{0:T(128)}, u32[]{:S(2)}) copy-start(s32[2]{0:T(128)} %len_ref.3) | copy-start | bytes 28
  26.2 16.9 %all-to-all-start.1 = ((bf16[32,32,256]{2,1,0:T(8,128)(2,1)}), bf16[32,32,256]{2,1,0:T(8,128)(2,1)S(1)}, u32[]{:S(2)}, u32[]{:S(2)}) async-start(bf16[32,32,256]{2,1,0:T(8,128)(2,1)} %bitcast.8), calls=%async_computation.1 | async-start | bytes 1048576 | tf_op jit(solution)/shard_map/all_to_all | solution.py:564
  46.1 19.6 %all-to-all-start.2 = ((bf16[8,144,256]{2,1,0:T(8,128)(2,1)}), bf16[8,144,256]{2,1,0:T(8,128)(2,1)S(1)}, u32[]{:S(2)}, u32[]{:S(2)}) async-start(bf16[8,144,256]{2,1,0:T(8,128)(2,1)} %get-tuple-element.42), calls=%async_computation.2 | async-start | bytes 1179648 | tf_op jit(solution)/shard_map/all_to_all | solution.py:564
  69.9 19.1 %all-to-all-start.3 = ((bf16[32,32,256]{2,1,0:T(8,128)(2,1)}), bf16[32,32,256]{2,1,0:T(8,128)(2,1)S(1)}, u32[]{:S(2)}, u32[]{:S(2)}) async-start(bf16[32,32,256]{2,1,0:T(8,128)(2,1)} %bitcast.9), calls=%async_computation.3 | async-start | bytes 1048576 | tf_op jit(solution)/shard_map/all_to_all | solution.py:564
  74.9 3.0 %collective-permute-start = (bf16[1024,256]{1,0:T(8,128)(2,1)S(1)}, bf16[1024,256]{1,0:T(8,128)(2,1)S(1)}, u32[]{:S(2)}, u32[]{:S(2)}) collective-permute-start(bf16[1024,256]{1,0:T(8,128)(2,1)S(1)} %get-tuple-element.49), channel_id=1, source_target_pairs={{0,1},{1,0},{2,3},{3,2},{4,5},{5,4},{6,7},{7,6},{8,9},{9,8},{10,11... | collective-permute-start | bytes 1572872 | tf_op jit(solution)/shard_map/ppermute | solution.py:569
  78.0 6.6 %collective-permute-start.1 = (bf16[256,256]{1,0:T(8,128)(2,1)S(1)}, bf16[256,256]{1,0:T(8,128)(2,1)S(1)}, u32[]{:S(2)}, u32[]{:S(2)}) collective-permute-start(bf16[256,256]{1,0:T(8,128)(2,1)S(1)} %get-tuple-element.51), channel_id=1, source_target_pairs={{0,2},{1,3},{2,4},{3,5},{4,6},{5,7},{6,0},{7,1},{8,10},{9,11},{10,... | collective-permute-start | bytes 393224 | tf_op jit(solution)/shard_map/ppermute | solution.py:574
  78.4 7.9 %collective-permute-start.2 = (bf16[256,256]{1,0:T(8,128)(2,1)S(1)}, bf16[256,256]{1,0:T(8,128)(2,1)S(1)}, u32[]{:S(2)}, u32[]{:S(2)}) collective-permute-start(bf16[256,256]{1,0:T(8,128)(2,1)S(1)} %get-tuple-element.52), channel_id=1, source_target_pairs={{0,4},{1,5},{2,6},{3,7},{4,0},{5,1},{6,2},{7,3},{8,12},{9,13},{10,... | collective-permute-start | bytes 393224 | tf_op jit(solution)/shard_map/ppermute | solution.py:574
  80.2 7.0 %collective-permute-start.3 = (bf16[256,256]{1,0:T(8,128)(2,1)S(1)}, bf16[256,256]{1,0:T(8,128)(2,1)S(1)}, u32[]{:S(2)}, u32[]{:S(2)}) collective-permute-start(bf16[256,256]{1,0:T(8,128)(2,1)S(1)} %get-tuple-element.53), channel_id=1, source_target_pairs={{0,6},{1,7},{2,0},{3,1},{4,2},{5,3},{6,4},{7,5},{8,14},{9,15},{10,... | collective-permute-start | bytes 393224 | tf_op jit(solution)/shard_map/ppermute | solution.py:574
  89.8 10.9 %collective-permute-start.4 = (bf16[1024,256]{1,0:T(8,128)(2,1)S(1)}, bf16[1024,256]{1,0:T(8,128)(2,1)S(1)}, u32[]{:S(2)}, u32[]{:S(2)}) collective-permute-start(bf16[1024,256]{1,0:T(8,128)(2,1)S(1)} %shard_map.140), channel_id=1, source_target_pairs={{0,1},{1,0},{2,3},{3,2},{4,5},{5,4},{6,7},{7,6},{8,9},{9,8},{10,11... | collective-permute-start | bytes 1572872 | tf_op jit(solution)/shard_map/ppermute | solution.py:569
  93.9 15.1 %all-to-all-start.4 = ((bf16[32,16,128]{2,1,0:T(8,128)(2,1)}), bf16[32,16,128]{2,1,0:T(8,128)(2,1)S(1)}, u32[]{:S(2)}, u32[]{:S(2)}) async-start(bf16[32,16,128]{2,1,0:T(8,128)(2,1)} %shard_map.137), calls=%async_computation.4 | async-start | bytes 262144 | tf_op jit(solution)/shard_map/all_to_all | solution.py:564
  100.8 13.4 %collective-permute-start.5 = (bf16[256,256]{1,0:T(8,128)(2,1)S(1)}, bf16[256,256]{1,0:T(8,128)(2,1)S(1)}, u32[]{:S(2)}, u32[]{:S(2)}) collective-permute-start(bf16[256,256]{1,0:T(8,128)(2,1)S(1)} %get-tuple-element.57), channel_id=1, source_target_pairs={{0,2},{1,3},{2,4},{3,5},{4,6},{5,7},{6,0},{7,1},{8,10},{9,11},{10,... | collective-permute-start | bytes 393224 | tf_op jit(solution)/shard_map/ppermute | solution.py:574
  101.0 13.3 %collective-permute-start.6 = (bf16[256,256]{1,0:T(8,128)(2,1)S(1)}, bf16[256,256]{1,0:T(8,128)(2,1)S(1)}, u32[]{:S(2)}, u32[]{:S(2)}) collective-permute-start(bf16[256,256]{1,0:T(8,128)(2,1)S(1)} %get-tuple-element.58), channel_id=1, source_target_pairs={{0,4},{1,5},{2,6},{3,7},{4,0},{5,1},{6,2},{7,3},{8,12},{9,13},{10,... | collective-permute-start | bytes 393224 | tf_op jit(solution)/shard_map/ppermute | solution.py:574
  104.3 10.0 %collective-permute-start.7 = (bf16[256,256]{1,0:T(8,128)(2,1)S(1)}, bf16[256,256]{1,0:T(8,128)(2,1)S(1)}, u32[]{:S(2)}, u32[]{:S(2)}) collective-permute-start(bf16[256,256]{1,0:T(8,128)(2,1)S(1)} %get-tuple-element.59), channel_id=1, source_target_pairs={{0,6},{1,7},{2,0},{3,1},{4,2},{5,3},{6,4},{7,5},{8,14},{9,15},{10,... | collective-permute-start | bytes 393224 | tf_op jit(solution)/shard_map/ppermute | solution.py:574
  109.7 13.7 %all-to-all-start.5 = ((bf16[32,16,128]{2,1,0:T(8,128)(2,1)}), bf16[32,16,128]{2,1,0:T(8,128)(2,1)S(1)}, u32[]{:S(2)}, u32[]{:S(2)}) async-start(bf16[32,16,128]{2,1,0:T(8,128)(2,1)} %shard_map.138), calls=%async_computation.5 | async-start | bytes 262144 | tf_op jit(solution)/shard_map/all_to_all | solution.py:564
  114.3 11.2 %collective-permute-start.11 = (bf16[256,256]{1,0:T(8,128)(2,1)S(1)}, bf16[256,256]{1,0:T(8,128)(2,1)S(1)}, u32[]{:S(2)}, u32[]{:S(2)}) collective-permute-start(bf16[256,256]{1,0:T(8,128)(2,1)S(1)} %add_convert_fusion.refs_0_), channel_id=1, source_target_pairs={{0,2},{1,3},{2,4},{3,5},{4,6},{5,7},{6,0},{7,1},{8,10},{9,11},{10,... | collective-permute-start | bytes 393224 | tf_op jit(solution)/shard_map/ppermute | solution.py:574
  115.9 10.9 %collective-permute-start.12 = (bf16[256,256]{1,0:T(8,128)(2,1)S(1)}, bf16[256,256]{1,0:T(8,128)(2,1)S(1)}, u32[]{:S(2)}, u32[]{:S(2)}) collective-permute-start(bf16[256,256]{1,0:T(8,128)(2,1)S(1)} %add_convert_fusion.refs_0_), channel_id=1, source_target_pairs={{0,4},{1,5},{2,6},{3,7},{4,0},{5,1},{6,2},{7,3},{8,12},{9,13},{10,... | collective-permute-start | bytes 393224 | tf_op jit(solution)/shard_map/ppermute | solution.py:574
  117.8 12.6 %collective-permute-start.13 = (bf16[256,256]{1,0:T(8,128)(2,1)S(1)}, bf16[256,256]{1,0:T(8,128)(2,1)S(1)}, u32[]{:S(2)}, u32[]{:S(2)}) collective-permute-start(bf16[256,256]{1,0:T(8,128)(2,1)S(1)} %add_convert_fusion.refs_0_), channel_id=1, source_target_pairs={{0,6},{1,7},{2,0},{3,1},{4,2},{5,3},{6,4},{7,5},{8,14},{9,15},{10,... | collective-permute-start | bytes 393224 | tf_op jit(solution)/shard_map/ppermute | solution.py:574
  123.4 7.3 %collective-permute-start.10 = (bf16[32,16,128]{2,1,0:T(8,128)(2,1)S(1)}, bf16[32,16,128]{2,1,0:T(8,128)(2,1)S(1)}, u32[]{:S(2)}, u32[]{:S(2)}) collective-permute-start(bf16[32,16,128]{2,1,0:T(8,128)(2,1)S(1)} %all-to-all-done.5.refs_0_), channel_id=1, source_target_pairs={{0,6},{1,7},{2,0},{3,1},{4,2},{5,3},{6,4},{7,5},{8,14},{9,15},{10,... | collective-permute-start | bytes 393224 | tf_op jit(solution)/shard_map/ppermute | solution.py:574
  125.6 7.9 %collective-permute-start.8 = (bf16[32,16,128]{2,1,0:T(8,128)(2,1)S(1)}, bf16[32,16,128]{2,1,0:T(8,128)(2,1)S(1)}, u32[]{:S(2)}, u32[]{:S(2)}) collective-permute-start(bf16[32,16,128]{2,1,0:T(8,128)(2,1)S(1)} %all-to-all-done.5.refs_0_), channel_id=1, source_target_pairs={{0,2},{1,3},{2,4},{3,5},{4,6},{5,7},{6,0},{7,1},{8,10},{9,11},{10,... | collective-permute-start | bytes 393224 | tf_op jit(solution)/shard_map/ppermute | solution.py:574
  125.6 10.5 %collective-permute-start.9 = (bf16[32,16,128]{2,1,0:T(8,128)(2,1)S(1)}, bf16[32,16,128]{2,1,0:T(8,128)(2,1)S(1)}, u32[]{:S(2)}, u32[]{:S(2)}) collective-permute-start(bf16[32,16,128]{2,1,0:T(8,128)(2,1)S(1)} %all-to-all-done.5.refs_0_), channel_id=1, source_target_pairs={{0,4},{1,5},{2,6},{3,7},{4,0},{5,1},{6,2},{7,3},{8,12},{9,13},{10,... | collective-permute-start | bytes 393224 | tf_op jit(solution)/shard_map/ppermute | solution.py:574
  126.8 9.3 %collective-permute-start.18 = (bf16[256,256]{1,0:T(8,128)(2,1)S(1)}, bf16[256,256]{1,0:T(8,128)(2,1)S(1)}, u32[]{:S(2)}, u32[]{:S(2)}) collective-permute-start(bf16[256,256]{1,0:T(8,128)(2,1)S(1)} %add_convert_fusion.refs_0_), channel_id=1, source_target_pairs={{0,1},{1,0},{2,3},{3,2},{4,5},{5,4},{6,7},{7,6},{8,9},{9,8},{10,11... | collective-permute-start | bytes 393224 | tf_op jit(solution)/shard_map/ppermute | solution.py:569
  130.4 6.3 %collective-permute-start.19 = (bf16[256,256]{1,0:T(8,128)(2,1)S(1)}, bf16[256,256]{1,0:T(8,128)(2,1)S(1)}, u32[]{:S(2)}, u32[]{:S(2)}) collective-permute-start(bf16[256,256]{1,0:T(8,128)(2,1)S(1)} %collective-permute-done.11.refs_1_), channel_id=1, source_target_pairs={{0,1},{1,0},{2,3},{3,2},{4,5},{5,4},{6,7},{7,6},{8,9},{9,8},{10,11... | collective-permute-start | bytes 393224 | tf_op jit(solution)/shard_map/ppermute | solution.py:569
  130.7 6.0 %collective-permute-start.20 = (bf16[256,256]{1,0:T(8,128)(2,1)S(1)}, bf16[256,256]{1,0:T(8,128)(2,1)S(1)}, u32[]{:S(2)}, u32[]{:S(2)}) collective-permute-start(bf16[256,256]{1,0:T(8,128)(2,1)S(1)} %collective-permute-done.12.refs_2_), channel_id=1, source_target_pairs={{0,1},{1,0},{2,3},{3,2},{4,5},{5,4},{6,7},{7,6},{8,9},{9,8},{10,11... | collective-permute-start | bytes 393224 | tf_op jit(solution)/shard_map/ppermute | solution.py:569
  133.5 3.6 %collective-permute-start.21 = (bf16[256,256]{1,0:T(8,128)(2,1)S(1)}, bf16[256,256]{1,0:T(8,128)(2,1)S(1)}, u32[]{:S(2)}, u32[]{:S(2)}) collective-permute-start(bf16[256,256]{1,0:T(8,128)(2,1)S(1)} %collective-permute-done.13.refs_3_), channel_id=1, source_target_pairs={{0,1},{1,0},{2,3},{3,2},{4,5},{5,4},{6,7},{7,6},{8,9},{9,8},{10,11... | collective-permute-start | bytes 393224 | tf_op jit(solution)/shard_map/ppermute | solution.py:569
  136.1 2.6 %collective-permute-start.14 = (bf16[32,16,128]{2,1,0:T(8,128)(2,1)S(1)}, bf16[32,16,128]{2,1,0:T(8,128)(2,1)S(1)}, u32[]{:S(2)}, u32[]{:S(2)}) collective-permute-start(bf16[32,16,128]{2,1,0:T(8,128)(2,1)S(1)} %all-to-all-done.5.refs_0_), channel_id=1, source_target_pairs={{0,1},{1,0},{2,3},{3,2},{4,5},{5,4},{6,7},{7,6},{8,9},{9,8},{10,11... | collective-permute-start | bytes 393224 | tf_op jit(solution)/shard_map/ppermute | solution.py:569
  136.1 2.6 %collective-permute-start.15 = (bf16[32,16,128]{2,1,0:T(8,128)(2,1)S(1)}, bf16[32,16,128]{2,1,0:T(8,128)(2,1)S(1)}, u32[]{:S(2)}, u32[]{:S(2)}) collective-permute-start(bf16[32,16,128]{2,1,0:T(8,128)(2,1)S(1)} %collective-permute-done.8.refs_1_), channel_id=1, source_target_pairs={{0,1},{1,0},{2,3},{3,2},{4,5},{5,4},{6,7},{7,6},{8,9},{9,8},{10,11... | collective-permute-start | bytes 393224 | tf_op jit(solution)/shard_map/ppermute | solution.py:569
  136.6 2.1 %collective-permute-start.16 = (bf16[32,16,128]{2,1,0:T(8,128)(2,1)S(1)}, bf16[32,16,128]{2,1,0:T(8,128)(2,1)S(1)}, u32[]{:S(2)}, u32[]{:S(2)}) collective-permute-start(bf16[32,16,128]{2,1,0:T(8,128)(2,1)S(1)} %collective-permute-done.9.refs_2_), channel_id=1, source_target_pairs={{0,1},{1,0},{2,3},{3,2},{4,5},{5,4},{6,7},{7,6},{8,9},{9,8},{10,11... | collective-permute-start | bytes 393224 | tf_op jit(solution)/shard_map/ppermute | solution.py:569
  136.7 2.0 %collective-permute-start.17 = (bf16[32,16,128]{2,1,0:T(8,128)(2,1)S(1)}, bf16[32,16,128]{2,1,0:T(8,128)(2,1)S(1)}, u32[]{:S(2)}, u32[]{:S(2)}) collective-permute-start(bf16[32,16,128]{2,1,0:T(8,128)(2,1)S(1)} %collective-permute-done.10.refs_3_), channel_id=1, source_target_pairs={{0,1},{1,0},{2,3},{3,2},{4,5},{5,4},{6,7},{7,6},{8,9},{9,8},{10,11... | collective-permute-start | bytes 393224 | tf_op jit(solution)/shard_map/ppermute | solution.py:569

commit v9 on v8

--- a/solution.py
+++ b/solution.py
@@ -123,9 +123,10 @@
 
 
 def request_kernel(
-    len_ref, ids_hbm, table_hbm, out_ref, slot_ref, table_ref, ids_ref, arrived, *, rows_own, cap
+    len_hbm, ids_hbm, table_hbm, out_ref, slot_ref, table_ref, len_ref, ids_ref, arrived,
+    *, rows_own, cap,
 ):
-    copies = begin(((ids_hbm, ids_ref), (table_hbm, table_ref)), arrived)
+    copies = begin(((ids_hbm, ids_ref), (len_hbm, len_ref), (table_hbm, table_ref)), arrived)
     users, block = ids_ref.shape
     shards, _, lanes = out_ref.shape
     shift = rows_own.bit_length() - 1
@@ -134,6 +135,7 @@
     finish(copies[:1])
     total = jnp.zeros((shards, lanes), f32)
     count = jnp.int32(0)
+    finish(copies[1:2])
     slot_ref[...] = jnp.zeros_like(slot_ref)
     for u in range(users):
         ids = ids_ref[u : u + 1, :]
@@ -150,7 +152,7 @@
         count = count + len_ref[u]
     wanted = jnp.where(iota((shards, lanes), 1) == users * cap, count, total.astype(i32))
     out_ref[:, 0, :] = wanted
-    finish(copies[1:])
+    finish(copies[2:])
 
 
 def answer_kernel(
@@ -639,9 +641,9 @@
     requests, slot, table = call(
         functools.partial(request_kernel, rows_own=rows_own, cap=cap),
         [((shards, 1, lanes), i32), ((8, block), i32), (rem_table.shape, bf16)],
-        (in_hbm(lengths), rem_ids, rem_table),
-        [SM, HB, HB],
-        [pltpu.VMEM((users, block), i32), dma(2)],
+        (lengths, rem_ids, rem_table),
+        [HB, HB, HB],
+        [pltpu.SMEM((users,), i32), pltpu.VMEM((users, block), i32), dma(3)],
         [VM, IN_VM, IN_VM],
         MOST,
     )

time: 141 us -> 140 us (level)
  no operation moved by 1% of the time
where the time goes in v9:
time: 140 us; the launch traced here: 139 us
  starting transfers between devices  57.2 us (41%)
  waiting for transfers between devices  33.6 us (24%)
  Pallas kernels  27 us (19%)
  blocking collectives  20.5 us (15%)
    all_to_all x5, starting transfers between devices, exchange(): return lax.all_to_all(array, axis, split_axis=0, concat_axis=0, tiled=True)  28.9 us
    pallas_call x15, Pallas kernels, call(): pl.pallas_call(kernel, out_shape=tuple(shapes), in_specs=specs, out_specs...  27 us
    all_to_all x5, waiting for transfers between devices, exchange(): return lax.all_to_all(array, axis, split_axis=0, concat_axis=0, tiled=True)  25.7 us
    all_to_all x1, blocking collectives, exchange(): return lax.all_to_all(array, axis, split_axis=0, concat_axis=0, tiled=True)  20.5 us
    ppermute x10, starting transfers between devices, to_core(): return lax.ppermute(array, 'hist', [(i, i ^ 1) for i in range(peers)])  14.7 us
    ppermute x12, starting transfers between devices, to_chip(): lax.ppermute(array, 'hist', [(i, (i + 2 * steps) % peers) for i in range(...  13.6 us
    ppermute x12, waiting for transfers between devices, to_chip(): lax.ppermute(array, 'hist', [(i, (i + 2 * steps) % peers) for i in range(...  6.32 us
  transfers between devices with their start and end apart: 27, of which 9 were waited for; matrix products, arithmetic and copies ran while one was open for 0% of the time, Pallas kernels for 10%

profile of v9, /device:TPU:1, one launch (start us, length us, event | category | flops | bytes accessed | tf_op | source)
XLA Modules:
  0.0 139.4 jit_solution(930863136452892658)
XLA Ops:
  0.6 1.4 shard_map.130
  2.0 20.5 %all_to_all.30.wanted_ref = s32[32,1,128]{2,1,0:T(1,128)S(1)} all-to-all(s32[32,1,128]{2,1,0:T(1,128)S(1)} %get-tuple-element.37), channel_id=1, replica_groups=mesh['user'=32,'hist'=8] {'user'}, dimensions={0} | all-to-all | bytes 32768 | tf_op jit(solution)/shard_map/all_to_all | solution.py:566
  22.5 3.0 %shard_map.131 = bf16[1024,256]{1,0:T(8,128)(2,1)} custom-call(s32[32,1,128]{2,1,0:T(1,128)S(1)} %all_to_all.30.wanted_ref, bf16[2048,256]{1,0:T(8,128)(2,1)S(1)} %get-tuple-element.38.table_ref), custom_call_target="tpu_custom_call" | custom-call | tf_op jit(solution)/shard_map/pallas_call | solution.py:114
  25.5 3.9 %all-to-all-start.1 = ((bf16[32,32,256]{2,1,0:T(8,128)(2,1)}), bf16[32,32,256]{2,1,0:T(8,128)(2,1)S(1)}, u32[]{:S(2)}, u32[]{:S(2)}) async-start(bf16[32,32,256]{2,1,0:T(8,128)(2,1)} %bitcast.8), calls=%async_computation.1 | async-start | bytes 1048576 | tf_op jit(solution)/shard_map/all_to_all | solution.py:566
  29.4 2.9 %shard_map.132 = (bf16[512,256]{1,0:T(8,128)(2,1)S(1)}, bf16[512,256]{1,0:T(8,128)(2,1)S(1)}, f32[512,256]{1,0:T(8,128)S(1)}) custom-call(s32[2]{0:T(128)S(1)} %copy-done, s32[1]{0:T(128)} %bitcast.at_ref, s32[2,256]{1,0:T(2,128)} %ids_hbm.3, bf16[2048,256]{1,0:T(8,128)(2,1)} %table_ref.1, bf16[2,256,256]{2,1,0:T(8,128)(2,1)} %cot_ref.1, ...), custom_call_target="tpu_custom_call" | custom-call | tf_op jit(solution)/shard_map/pallas_call | solution.py:114
  32.3 10.0 %all-to-all-done.1 = bf16[32,32,256]{2,1,0:T(8,128)(2,1)S(1)} async-done(((bf16[32,32,256]{2,1,0:T(8,128)(2,1)}), bf16[32,32,256]{2,1,0:T(8,128)(2,1)S(1)}, u32[]{:S(2)}, u32[]{:S(2)}) %all-to-all-start.1) | async-done | bytes 524320 | tf_op jit(solution)/shard_map/all_to_all | solution.py:566
  42.4 3.0 %shard_map.133 = (bf16[512,256]{1,0:T(8,128)(2,1)S(1)}, bf16[8,144,256]{2,1,0:T(8,128)(2,1)}) custom-call(s32[1]{0:T(128)} %bitcast.at_ref, s32[8,256]{1,0:T(8,128)S(1)} %get-tuple-element.36.slot_ref, bf16[1024,256]{1,0:T(8,128)(2,1)S(1)} %bitcast.7, bf16[512,256]{1,0:T(8,128)(2,1)S(1)} %get-tuple-element.39.quot_ref, bf16[256,256]{1,0:T(8,128)(2,1)} %wq_hbm.3, ...), custom_call_target="tpu_custom_call" | custom-call | tf_op jit(solution)/shard_map/pallas_call | solution.py:114
  45.4 9.5 %all-to-all-start.2 = ((bf16[8,144,256]{2,1,0:T(8,128)(2,1)}), bf16[8,144,256]{2,1,0:T(8,128)(2,1)S(1)}, u32[]{:S(2)}, u32[]{:S(2)}) async-start(bf16[8,144,256]{2,1,0:T(8,128)(2,1)} %get-tuple-element.42), calls=%async_computation.2 | async-start | bytes 1179648 | tf_op jit(solution)/shard_map/all_to_all | solution.py:566
  54.9 5.4 %shard_map.134 = (f32[512,256]{1,0:T(8,128)S(1)}, f32[3,512,256]{2,1,0:T(8,128)}) custom-call(bf16[512,256]{1,0:T(8,128)(2,1)S(1)} %get-tuple-element.39.quot_ref, bf16[512,256]{1,0:T(8,128)(2,1)S(1)} %get-tuple-element.43.rem_ref, bf16[512,256]{1,0:T(8,128)(2,1)S(1)} %get-tuple-element.41.dmixed_ref, f32[2,4,256]{2,1,0:T(4,128)} %decay_ref.3, ...), custom_call_target="tpu_custom_call" | custom-call | tf_op jit(solution)/shard_map/pallas_call | solution.py:114
  60.3 4.8 %all-to-all-done.2.payload_ref = bf16[8,144,256]{2,1,0:T(8,128)(2,1)S(1)} async-done(((bf16[8,144,256]{2,1,0:T(8,128)(2,1)}), bf16[8,144,256]{2,1,0:T(8,128)(2,1)S(1)}, u32[]{:S(2)}, u32[]{:S(2)}) %all-to-all-start.2) | async-done | bytes 589856 | tf_op jit(solution)/shard_map/all_to_all | solution.py:566
  65.1 4.2 %shard_map.135 = (bf16[2,256,256]{2,1,0:T(8,128)(2,1)}, bf16[1024,256]{1,0:T(8,128)(2,1)}, bf16[1024,256]{1,0:T(8,128)(2,1)S(1)}, bf16[1024,256]{1,0:T(8,128)(2,1)S(1)}) custom-call(s32[1]{0:T(128)} %bitcast.at_ref, bf16[8,144,256]{2,1,0:T(8,128)(2,1)S(1)} %all-to-all-done.2.payload_ref, f32[512,256]{1,0:T(8,128)S(1)} %get-tuple-element.44.near_ref, ...), custom_call_target="tpu_custom_call" | custom-call | tf_op jit(solution)/shard_map/pallas_call | solution.py:114
  69.2 5.1 %all-to-all-start.3 = ((bf16[32,32,256]{2,1,0:T(8,128)(2,1)}), bf16[32,32,256]{2,1,0:T(8,128)(2,1)S(1)}, u32[]{:S(2)}, u32[]{:S(2)}) async-start(bf16[32,32,256]{2,1,0:T(8,128)(2,1)} %bitcast.9), calls=%async_computation.3 | async-start | bytes 1048576 | tf_op jit(solution)/shard_map/all_to_all | solution.py:566
  74.3 1.4 %collective-permute-start = (bf16[1024,256]{1,0:T(8,128)(2,1)S(1)}, bf16[1024,256]{1,0:T(8,128)(2,1)S(1)}, u32[]{:S(2)}, u32[]{:S(2)}) collective-permute-start(bf16[1024,256]{1,0:T(8,128)(2,1)S(1)} %get-tuple-element.49), channel_id=1, source_target_pairs={{0,1},{1,0},{2,3},{3,2},{4,5},{5,4},{6,7},{7,6},{8,9},{9,8},{10,11... | collective-permute-start | bytes 1572872 | tf_op jit(solution)/shard_map/ppermute | solution.py:571
  75.7 1.5 %collective-permute-done.got_ref = bf16[1024,256]{1,0:T(8,128)(2,1)S(1)} collective-permute-done((bf16[1024,256]{1,0:T(8,128)(2,1)S(1)}, bf16[1024,256]{1,0:T(8,128)(2,1)S(1)}, u32[]{:S(2)}, u32[]{:S(2)}) %collective-permute-start) | collective-permute-done | bytes 524320 | tf_op jit(solution)/shard_map/ppermute | solution.py:571
  77.2 0.1 shard_map.136
  77.4 0.4 collective-permute-start.1
  77.7 1.8 %collective-permute-start.2 = (bf16[256,256]{1,0:T(8,128)(2,1)S(1)}, bf16[256,256]{1,0:T(8,128)(2,1)S(1)}, u32[]{:S(2)}, u32[]{:S(2)}) collective-permute-start(bf16[256,256]{1,0:T(8,128)(2,1)S(1)} %get-tuple-element.52), channel_id=1, source_target_pairs={{0,4},{1,5},{2,6},{3,7},{4,0},{5,1},{6,2},{7,3},{8,12},{9,13},{10,... | collective-permute-start | bytes 393224 | tf_op jit(solution)/shard_map/ppermute | solution.py:576
  79.5 0.7 collective-permute-start.3
  80.2 3.7 %collective-permute-done.1.refs_1_ = bf16[256,256]{1,0:T(8,128)(2,1)S(1)} collective-permute-done((bf16[256,256]{1,0:T(8,128)(2,1)S(1)}, bf16[256,256]{1,0:T(8,128)(2,1)S(1)}, u32[]{:S(2)}, u32[]{:S(2)}) %collective-permute-start.1) | collective-permute-done | bytes 131104 | tf_op jit(solution)/shard_map/ppermute | solution.py:576
  84.0 1.6 %collective-permute-done.2.refs_2_ = bf16[256,256]{1,0:T(8,128)(2,1)S(1)} collective-permute-done((bf16[256,256]{1,0:T(8,128)(2,1)S(1)}, bf16[256,256]{1,0:T(8,128)(2,1)S(1)}, u32[]{:S(2)}, u32[]{:S(2)}) %collective-permute-start.2) | collective-permute-done | bytes 131104 | tf_op jit(solution)/shard_map/ppermute | solution.py:576
  85.6 0.9 collective-permute-done.3.refs_3_
  86.5 0.7 shard_map.137
  87.2 1.1 all-to-all-done.3
  88.3 0.9 shard_map.140
  89.2 4.1 %collective-permute-start.4 = (bf16[1024,256]{1,0:T(8,128)(2,1)S(1)}, bf16[1024,256]{1,0:T(8,128)(2,1)S(1)}, u32[]{:S(2)}, u32[]{:S(2)}) collective-permute-start(bf16[1024,256]{1,0:T(8,128)(2,1)S(1)} %shard_map.140), channel_id=1, source_target_pairs={{0,1},{1,0},{2,3},{3,2},{4,5},{5,4},{6,7},{7,6},{8,9},{9,8},{10,11... | collective-permute-start | bytes 1572872 | tf_op jit(solution)/shard_map/ppermute | solution.py:571
  93.3 5.9 %all-to-all-start.4 = ((bf16[32,16,128]{2,1,0:T(8,128)(2,1)}), bf16[32,16,128]{2,1,0:T(8,128)(2,1)S(1)}, u32[]{:S(2)}, u32[]{:S(2)}) async-start(bf16[32,16,128]{2,1,0:T(8,128)(2,1)} %shard_map.137), calls=%async_computation.4 | async-start | bytes 262144 | tf_op jit(solution)/shard_map/all_to_all | solution.py:566
  99.2 0.9 shard_map.139.keep_ref
  100.1 0.0 collective-permute-done.4.got_ref
  100.1 0.1 shard_map.141
  100.2 0.1 collective-permute-start.5
  100.3 3.3 %collective-permute-start.6 = (bf16[256,256]{1,0:T(8,128)(2,1)S(1)}, bf16[256,256]{1,0:T(8,128)(2,1)S(1)}, u32[]{:S(2)}, u32[]{:S(2)}) collective-permute-start(bf16[256,256]{1,0:T(8,128)(2,1)S(1)} %get-tuple-element.58), channel_id=1, source_target_pairs={{0,4},{1,5},{2,6},{3,7},{4,0},{5,1},{6,2},{7,3},{8,12},{9,13},{10,... | collective-permute-start | bytes 393224 | tf_op jit(solution)/shard_map/ppermute | solution.py:576
  103.6 0.0 collective-permute-start.7
  103.6 4.7 %all-to-all-done.4.tiles_ref = bf16[32,16,128]{2,1,0:T(8,128)(2,1)S(1)} async-done(((bf16[32,16,128]{2,1,0:T(8,128)(2,1)}), bf16[32,16,128]{2,1,0:T(8,128)(2,1)S(1)}, u32[]{:S(2)}, u32[]{:S(2)}) %all-to-all-start.4) | async-done | bytes 131104 | tf_op jit(solution)/shard_map/all_to_all | solution.py:566
  108.3 0.7 shard_map.138
  109.0 4.5 %all-to-all-start.5 = ((bf16[32,16,128]{2,1,0:T(8,128)(2,1)}), bf16[32,16,128]{2,1,0:T(8,128)(2,1)S(1)}, u32[]{:S(2)}, u32[]{:S(2)}) async-start(bf16[32,16,128]{2,1,0:T(8,128)(2,1)} %shard_map.138), calls=%async_computation.5 | async-start | bytes 262144 | tf_op jit(solution)/shard_map/all_to_all | solution.py:566
  113.6 0.0 collective-permute-done.5
  113.6 0.0 collective-permute-done.6
  113.6 0.1 add_convert_fusion.refs_0_
  113.7 1.5 %collective-permute-start.11 = (bf16[256,256]{1,0:T(8,128)(2,1)S(1)}, bf16[256,256]{1,0:T(8,128)(2,1)S(1)}, u32[]{:S(2)}, u32[]{:S(2)}) collective-permute-start(bf16[256,256]{1,0:T(8,128)(2,1)S(1)} %add_convert_fusion.refs_0_), channel_id=1, source_target_pairs={{0,2},{1,3},{2,4},{3,5},{4,6},{5,7},{6,0},{7,1},{8,10},{9,11},{10,... | collective-permute-start | bytes 393224 | tf_op jit(solution)/shard_map/ppermute | solution.py:576
  115.2 1.9 %collective-permute-start.12 = (bf16[256,256]{1,0:T(8,128)(2,1)S(1)}, bf16[256,256]{1,0:T(8,128)(2,1)S(1)}, u32[]{:S(2)}, u32[]{:S(2)}) collective-permute-start(bf16[256,256]{1,0:T(8,128)(2,1)S(1)} %add_convert_fusion.refs_0_), channel_id=1, source_target_pairs={{0,4},{1,5},{2,6},{3,7},{4,0},{5,1},{6,2},{7,3},{8,12},{9,13},{10,... | collective-permute-start | bytes 393224 | tf_op jit(solution)/shard_map/ppermute | solution.py:576
  117.1 0.6 collective-permute-start.13
  117.7 5.0 %all-to-all-done.5.refs_0_ = bf16[32,16,128]{2,1,0:T(8,128)(2,1)S(1)} async-done(((bf16[32,16,128]{2,1,0:T(8,128)(2,1)}), bf16[32,16,128]{2,1,0:T(8,128)(2,1)S(1)}, u32[]{:S(2)}, u32[]{:S(2)}) %all-to-all-start.5) | async-done | bytes 131104 | tf_op jit(solution)/shard_map/all_to_all | solution.py:566
  122.7 2.2 %collective-permute-start.10 = (bf16[32,16,128]{2,1,0:T(8,128)(2,1)S(1)}, bf16[32,16,128]{2,1,0:T(8,128)(2,1)S(1)}, u32[]{:S(2)}, u32[]{:S(2)}) collective-permute-start(bf16[32,16,128]{2,1,0:T(8,128)(2,1)S(1)} %all-to-all-done.5.refs_0_), channel_id=1, source_target_pairs={{0,6},{1,7},{2,0},{3,1},{4,2},{5,3},{6,4},{7,5},{8,14},{9,15},{10,... | collective-permute-start | bytes 393224 | tf_op jit(solution)/shard_map/ppermute | solution.py:576
  124.9 0.0 collective-permute-start.8
  124.9 0.0 collective-permute-done.11.refs_1_
  124.9 1.2 collective-permute-start.9
  126.1 0.0 collective-permute-done.12.refs_2_
  126.1 3.6 %collective-permute-start.18 = (bf16[256,256]{1,0:T(8,128)(2,1)S(1)}, bf16[256,256]{1,0:T(8,128)(2,1)S(1)}, u32[]{:S(2)}, u32[]{:S(2)}) collective-permute-start(bf16[256,256]{1,0:T(8,128)(2,1)S(1)} %add_convert_fusion.refs_0_), channel_id=1, source_target_pairs={{0,1},{1,0},{2,3},{3,2},{4,5},{5,4},{6,7},{7,6},{8,9},{9,8},{10,11... | collective-permute-start | bytes 393224 | tf_op jit(solution)/shard_map/ppermute | solution.py:571
  129.7 0.3 collective-permute-start.19
  130.0 0.0 collective-permute-done.10.refs_3_
  130.0 1.7 %collective-permute-start.20 = (bf16[256,256]{1,0:T(8,128)(2,1)S(1)}, bf16[256,256]{1,0:T(8,128)(2,1)S(1)}, u32[]{:S(2)}, u32[]{:S(2)}) collective-permute-start(bf16[256,256]{1,0:T(8,128)(2,1)S(1)} %collective-permute-done.12.refs_2_), channel_id=1, source_target_pairs={{0,1},{1,0},{2,3},{3,2},{4,5},{5,4},{6,7},{7,6},{8,9},{9,8},{10,11... | collective-permute-start | bytes 393224 | tf_op jit(solution)/shard_map/ppermute | solution.py:571
  131.7 1.1 shard_map.142.refs_8_
  132.8 2.6 %collective-permute-start.21 = (bf16[256,256]{1,0:T(8,128)(2,1)S(1)}, bf16[256,256]{1,0:T(8,128)(2,1)S(1)}, u32[]{:S(2)}, u32[]{:S(2)}) collective-permute-start(bf16[256,256]{1,0:T(8,128)(2,1)S(1)} %collective-permute-done.13.refs_3_), channel_id=1, source_target_pairs={{0,1},{1,0},{2,3},{3,2},{4,5},{5,4},{6,7},{7,6},{8,9},{9,8},{10,11... | collective-permute-start | bytes 393224 | tf_op jit(solution)/shard_map/ppermute | solution.py:571
  135.4 0.0 collective-permute-start.14
  135.4 0.5 collective-permute-start.15
  135.9 0.0 collective-permute-done.19.refs_5_
  135.9 0.1 collective-permute-start.16
  136.0 0.0 collective-permute-done.20.refs_6_
  136.0 0.4 collective-permute-start.17
  136.5 0.0 collective-permute-done.21.refs_7_
  136.5 1.5 %shard_map.143 = (f32[2048,256]{1,0:T(8,128)}, f32[2048,256]{1,0:T(8,128)}) custom-call(s32[1]{0:T(128)} %bitcast.at_ref, s32[32,1,128]{2,1,0:T(1,128)S(1)} %all_to_all.30.wanted_ref, bf16[32,16,128]{2,1,0:T(8,128)(2,1)S(1)} %all-to-all-done.5.refs_0_, bf16[32,16,128]{2,1,0:T(8,128)(2,1)S(1)} %collective-permute-done.8.refs_1_, ...), custom_call_target="tpu_custom_call", output_to_operand_aliasing={{1}: (10, {})} | custom-call | tf_op jit(solution)/shard_map/pallas_call | solution.py:114
  138.0 0.0 collective-permute-done.15.refs_1_
  138.0 0.0 collective-permute-done.16.refs_2_
  138.0 1.2 shard_map.144
  (9 shorter events, 0.0 us)
Async XLA Ops:
  0.6 28.8 %copy-start = (s32[2]{0:T(128)S(1)}, s32[2]{0:T(128)}, u32[]{:S(2)}) copy-start(s32[2]{0:T(128)} %len_ref.1) | copy-start | bytes 28
  25.5 16.9 %all-to-all-start.1 = ((bf16[32,32,256]{2,1,0:T(8,128)(2,1)}), bf16[32,32,256]{2,1,0:T(8,128)(2,1)S(1)}, u32[]{:S(2)}, u32[]{:S(2)}) async-start(bf16[32,32,256]{2,1,0:T(8,128)(2,1)} %bitcast.8), calls=%async_computation.1 | async-start | bytes 1048576 | tf_op jit(solution)/shard_map/all_to_all | solution.py:566
  45.4 19.7 %all-to-all-start.2 = ((bf16[8,144,256]{2,1,0:T(8,128)(2,1)}), bf16[8,144,256]{2,1,0:T(8,128)(2,1)S(1)}, u32[]{:S(2)}, u32[]{:S(2)}) async-start(bf16[8,144,256]{2,1,0:T(8,128)(2,1)} %get-tuple-element.42), calls=%async_computation.2 | async-start | bytes 1179648 | tf_op jit(solution)/shard_map/all_to_all | solution.py:566
  69.2 19.1 %all-to-all-start.3 = ((bf16[32,32,256]{2,1,0:T(8,128)(2,1)}), bf16[32,32,256]{2,1,0:T(8,128)(2,1)S(1)}, u32[]{:S(2)}, u32[]{:S(2)}) async-start(bf16[32,32,256]{2,1,0:T(8,128)(2,1)} %bitcast.9), calls=%async_computation.3 | async-start | bytes 1048576 | tf_op jit(solution)/shard_map/all_to_all | solution.py:566
  74.3 3.0 %collective-permute-start = (bf16[1024,256]{1,0:T(8,128)(2,1)S(1)}, bf16[1024,256]{1,0:T(8,128)(2,1)S(1)}, u32[]{:S(2)}, u32[]{:S(2)}) collective-permute-start(bf16[1024,256]{1,0:T(8,128)(2,1)S(1)} %get-tuple-element.49), channel_id=1, source_target_pairs={{0,1},{1,0},{2,3},{3,2},{4,5},{5,4},{6,7},{7,6},{8,9},{9,8},{10,11... | collective-permute-start | bytes 1572872 | tf_op jit(solution)/shard_map/ppermute | solution.py:571
  77.4 6.6 %collective-permute-start.1 = (bf16[256,256]{1,0:T(8,128)(2,1)S(1)}, bf16[256,256]{1,0:T(8,128)(2,1)S(1)}, u32[]{:S(2)}, u32[]{:S(2)}) collective-permute-start(bf16[256,256]{1,0:T(8,128)(2,1)S(1)} %get-tuple-element.51), channel_id=1, source_target_pairs={{0,2},{1,3},{2,4},{3,5},{4,6},{5,7},{6,0},{7,1},{8,10},{9,11},{10,... | collective-permute-start | bytes 393224 | tf_op jit(solution)/shard_map/ppermute | solution.py:576
  77.7 7.9 %collective-permute-start.2 = (bf16[256,256]{1,0:T(8,128)(2,1)S(1)}, bf16[256,256]{1,0:T(8,128)(2,1)S(1)}, u32[]{:S(2)}, u32[]{:S(2)}) collective-permute-start(bf16[256,256]{1,0:T(8,128)(2,1)S(1)} %get-tuple-element.52), channel_id=1, source_target_pairs={{0,4},{1,5},{2,6},{3,7},{4,0},{5,1},{6,2},{7,3},{8,12},{9,13},{10,... | collective-permute-start | bytes 393224 | tf_op jit(solution)/shard_map/ppermute | solution.py:576
  79.5 7.0 %collective-permute-start.3 = (bf16[256,256]{1,0:T(8,128)(2,1)S(1)}, bf16[256,256]{1,0:T(8,128)(2,1)S(1)}, u32[]{:S(2)}, u32[]{:S(2)}) collective-permute-start(bf16[256,256]{1,0:T(8,128)(2,1)S(1)} %get-tuple-element.53), channel_id=1, source_target_pairs={{0,6},{1,7},{2,0},{3,1},{4,2},{5,3},{6,4},{7,5},{8,14},{9,15},{10,... | collective-permute-start | bytes 393224 | tf_op jit(solution)/shard_map/ppermute | solution.py:576
  89.2 10.9 %collective-permute-start.4 = (bf16[1024,256]{1,0:T(8,128)(2,1)S(1)}, bf16[1024,256]{1,0:T(8,128)(2,1)S(1)}, u32[]{:S(2)}, u32[]{:S(2)}) collective-permute-start(bf16[1024,256]{1,0:T(8,128)(2,1)S(1)} %shard_map.140), channel_id=1, source_target_pairs={{0,1},{1,0},{2,3},{3,2},{4,5},{5,4},{6,7},{7,6},{8,9},{9,8},{10,11... | collective-permute-start | bytes 1572872 | tf_op jit(solution)/shard_map/ppermute | solution.py:571
  93.3 15.1 %all-to-all-start.4 = ((bf16[32,16,128]{2,1,0:T(8,128)(2,1)}), bf16[32,16,128]{2,1,0:T(8,128)(2,1)S(1)}, u32[]{:S(2)}, u32[]{:S(2)}) async-start(bf16[32,16,128]{2,1,0:T(8,128)(2,1)} %shard_map.137), calls=%async_computation.4 | async-start | bytes 262144 | tf_op jit(solution)/shard_map/all_to_all | solution.py:566
  100.2 13.4 %collective-permute-start.5 = (bf16[256,256]{1,0:T(8,128)(2,1)S(1)}, bf16[256,256]{1,0:T(8,128)(2,1)S(1)}, u32[]{:S(2)}, u32[]{:S(2)}) collective-permute-start(bf16[256,256]{1,0:T(8,128)(2,1)S(1)} %get-tuple-element.57), channel_id=1, source_target_pairs={{0,2},{1,3},{2,4},{3,5},{4,6},{5,7},{6,0},{7,1},{8,10},{9,11},{10,... | collective-permute-start | bytes 393224 | tf_op jit(solution)/shard_map/ppermute | solution.py:576
  100.3 13.3 %collective-permute-start.6 = (bf16[256,256]{1,0:T(8,128)(2,1)S(1)}, bf16[256,256]{1,0:T(8,128)(2,1)S(1)}, u32[]{:S(2)}, u32[]{:S(2)}) collective-permute-start(bf16[256,256]{1,0:T(8,128)(2,1)S(1)} %get-tuple-element.58), channel_id=1, source_target_pairs={{0,4},{1,5},{2,6},{3,7},{4,0},{5,1},{6,2},{7,3},{8,12},{9,13},{10,... | collective-permute-start | bytes 393224 | tf_op jit(solution)/shard_map/ppermute | solution.py:576
  103.6 10.0 %collective-permute-start.7 = (bf16[256,256]{1,0:T(8,128)(2,1)S(1)}, bf16[256,256]{1,0:T(8,128)(2,1)S(1)}, u32[]{:S(2)}, u32[]{:S(2)}) collective-permute-start(bf16[256,256]{1,0:T(8,128)(2,1)S(1)} %get-tuple-element.59), channel_id=1, source_target_pairs={{0,6},{1,7},{2,0},{3,1},{4,2},{5,3},{6,4},{7,5},{8,14},{9,15},{10,... | collective-permute-start | bytes 393224 | tf_op jit(solution)/shard_map/ppermute | solution.py:576
  109.0 13.7 %all-to-all-start.5 = ((bf16[32,16,128]{2,1,0:T(8,128)(2,1)}), bf16[32,16,128]{2,1,0:T(8,128)(2,1)S(1)}, u32[]{:S(2)}, u32[]{:S(2)}) async-start(bf16[32,16,128]{2,1,0:T(8,128)(2,1)} %shard_map.138), calls=%async_computation.5 | async-start | bytes 262144 | tf_op jit(solution)/shard_map/all_to_all | solution.py:566
  113.7 11.2 %collective-permute-start.11 = (bf16[256,256]{1,0:T(8,128)(2,1)S(1)}, bf16[256,256]{1,0:T(8,128)(2,1)S(1)}, u32[]{:S(2)}, u32[]{:S(2)}) collective-permute-start(bf16[256,256]{1,0:T(8,128)(2,1)S(1)} %add_convert_fusion.refs_0_), channel_id=1, source_target_pairs={{0,2},{1,3},{2,4},{3,5},{4,6},{5,7},{6,0},{7,1},{8,10},{9,11},{10,... | collective-permute-start | bytes 393224 | tf_op jit(solution)/shard_map/ppermute | solution.py:576
  115.2 10.9 %collective-permute-start.12 = (bf16[256,256]{1,0:T(8,128)(2,1)S(1)}, bf16[256,256]{1,0:T(8,128)(2,1)S(1)}, u32[]{:S(2)}, u32[]{:S(2)}) collective-permute-start(bf16[256,256]{1,0:T(8,128)(2,1)S(1)} %add_convert_fusion.refs_0_), channel_id=1, source_target_pairs={{0,4},{1,5},{2,6},{3,7},{4,0},{5,1},{6,2},{7,3},{8,12},{9,13},{10,... | collective-permute-start | bytes 393224 | tf_op jit(solution)/shard_map/ppermute | solution.py:576
  117.1 12.6 %collective-permute-start.13 = (bf16[256,256]{1,0:T(8,128)(2,1)S(1)}, bf16[256,256]{1,0:T(8,128)(2,1)S(1)}, u32[]{:S(2)}, u32[]{:S(2)}) collective-permute-start(bf16[256,256]{1,0:T(8,128)(2,1)S(1)} %add_convert_fusion.refs_0_), channel_id=1, source_target_pairs={{0,6},{1,7},{2,0},{3,1},{4,2},{5,3},{6,4},{7,5},{8,14},{9,15},{10,... | collective-permute-start | bytes 393224 | tf_op jit(solution)/shard_map/ppermute | solution.py:576
  122.7 7.3 %collective-permute-start.10 = (bf16[32,16,128]{2,1,0:T(8,128)(2,1)S(1)}, bf16[32,16,128]{2,1,0:T(8,128)(2,1)S(1)}, u32[]{:S(2)}, u32[]{:S(2)}) collective-permute-start(bf16[32,16,128]{2,1,0:T(8,128)(2,1)S(1)} %all-to-all-done.5.refs_0_), channel_id=1, source_target_pairs={{0,6},{1,7},{2,0},{3,1},{4,2},{5,3},{6,4},{7,5},{8,14},{9,15},{10,... | collective-permute-start | bytes 393224 | tf_op jit(solution)/shard_map/ppermute | solution.py:576
  124.9 7.9 %collective-permute-start.8 = (bf16[32,16,128]{2,1,0:T(8,128)(2,1)S(1)}, bf16[32,16,128]{2,1,0:T(8,128)(2,1)S(1)}, u32[]{:S(2)}, u32[]{:S(2)}) collective-permute-start(bf16[32,16,128]{2,1,0:T(8,128)(2,1)S(1)} %all-to-all-done.5.refs_0_), channel_id=1, source_target_pairs={{0,2},{1,3},{2,4},{3,5},{4,6},{5,7},{6,0},{7,1},{8,10},{9,11},{10,... | collective-permute-start | bytes 393224 | tf_op jit(solution)/shard_map/ppermute | solution.py:576
  124.9 10.5 %collective-permute-start.9 = (bf16[32,16,128]{2,1,0:T(8,128)(2,1)S(1)}, bf16[32,16,128]{2,1,0:T(8,128)(2,1)S(1)}, u32[]{:S(2)}, u32[]{:S(2)}) collective-permute-start(bf16[32,16,128]{2,1,0:T(8,128)(2,1)S(1)} %all-to-all-done.5.refs_0_), channel_id=1, source_target_pairs={{0,4},{1,5},{2,6},{3,7},{4,0},{5,1},{6,2},{7,3},{8,12},{9,13},{10,... | collective-permute-start | bytes 393224 | tf_op jit(solution)/shard_map/ppermute | solution.py:576
  126.1 9.3 %collective-permute-start.18 = (bf16[256,256]{1,0:T(8,128)(2,1)S(1)}, bf16[256,256]{1,0:T(8,128)(2,1)S(1)}, u32[]{:S(2)}, u32[]{:S(2)}) collective-permute-start(bf16[256,256]{1,0:T(8,128)(2,1)S(1)} %add_convert_fusion.refs_0_), channel_id=1, source_target_pairs={{0,1},{1,0},{2,3},{3,2},{4,5},{5,4},{6,7},{7,6},{8,9},{9,8},{10,11... | collective-permute-start | bytes 393224 | tf_op jit(solution)/shard_map/ppermute | solution.py:571
  129.7 6.3 %collective-permute-start.19 = (bf16[256,256]{1,0:T(8,128)(2,1)S(1)}, bf16[256,256]{1,0:T(8,128)(2,1)S(1)}, u32[]{:S(2)}, u32[]{:S(2)}) collective-permute-start(bf16[256,256]{1,0:T(8,128)(2,1)S(1)} %collective-permute-done.11.refs_1_), channel_id=1, source_target_pairs={{0,1},{1,0},{2,3},{3,2},{4,5},{5,4},{6,7},{7,6},{8,9},{9,8},{10,11... | collective-permute-start | bytes 393224 | tf_op jit(solution)/shard_map/ppermute | solution.py:571
  130.0 6.0 %collective-permute-start.20 = (bf16[256,256]{1,0:T(8,128)(2,1)S(1)}, bf16[256,256]{1,0:T(8,128)(2,1)S(1)}, u32[]{:S(2)}, u32[]{:S(2)}) collective-permute-start(bf16[256,256]{1,0:T(8,128)(2,1)S(1)} %collective-permute-done.12.refs_2_), channel_id=1, source_target_pairs={{0,1},{1,0},{2,3},{3,2},{4,5},{5,4},{6,7},{7,6},{8,9},{9,8},{10,11... | collective-permute-start | bytes 393224 | tf_op jit(solution)/shard_map/ppermute | solution.py:571
  132.8 3.6 %collective-permute-start.21 = (bf16[256,256]{1,0:T(8,128)(2,1)S(1)}, bf16[256,256]{1,0:T(8,128)(2,1)S(1)}, u32[]{:S(2)}, u32[]{:S(2)}) collective-permute-start(bf16[256,256]{1,0:T(8,128)(2,1)S(1)} %collective-permute-done.13.refs_3_), channel_id=1, source_target_pairs={{0,1},{1,0},{2,3},{3,2},{4,5},{5,4},{6,7},{7,6},{8,9},{9,8},{10,11... | collective-permute-start | bytes 393224 | tf_op jit(solution)/shard_map/ppermute | solution.py:571
  135.4 2.6 %collective-permute-start.14 = (bf16[32,16,128]{2,1,0:T(8,128)(2,1)S(1)}, bf16[32,16,128]{2,1,0:T(8,128)(2,1)S(1)}, u32[]{:S(2)}, u32[]{:S(2)}) collective-permute-start(bf16[32,16,128]{2,1,0:T(8,128)(2,1)S(1)} %all-to-all-done.5.refs_0_), channel_id=1, source_target_pairs={{0,1},{1,0},{2,3},{3,2},{4,5},{5,4},{6,7},{7,6},{8,9},{9,8},{10,11... | collective-permute-start | bytes 393224 | tf_op jit(solution)/shard_map/ppermute | solution.py:571
  135.4 2.6 %collective-permute-start.15 = (bf16[32,16,128]{2,1,0:T(8,128)(2,1)S(1)}, bf16[32,16,128]{2,1,0:T(8,128)(2,1)S(1)}, u32[]{:S(2)}, u32[]{:S(2)}) collective-permute-start(bf16[32,16,128]{2,1,0:T(8,128)(2,1)S(1)} %collective-permute-done.8.refs_1_), channel_id=1, source_target_pairs={{0,1},{1,0},{2,3},{3,2},{4,5},{5,4},{6,7},{7,6},{8,9},{9,8},{10,11... | collective-permute-start | bytes 393224 | tf_op jit(solution)/shard_map/ppermute | solution.py:571
  135.9 2.1 %collective-permute-start.16 = (bf16[32,16,128]{2,1,0:T(8,128)(2,1)S(1)}, bf16[32,16,128]{2,1,0:T(8,128)(2,1)S(1)}, u32[]{:S(2)}, u32[]{:S(2)}) collective-permute-start(bf16[32,16,128]{2,1,0:T(8,128)(2,1)S(1)} %collective-permute-done.9.refs_2_), channel_id=1, source_target_pairs={{0,1},{1,0},{2,3},{3,2},{4,5},{5,4},{6,7},{7,6},{8,9},{9,8},{10,11... | collective-permute-start | bytes 393224 | tf_op jit(solution)/shard_map/ppermute | solution.py:571
  136.0 2.0 %collective-permute-start.17 = (bf16[32,16,128]{2,1,0:T(8,128)(2,1)S(1)}, bf16[32,16,128]{2,1,0:T(8,128)(2,1)S(1)}, u32[]{:S(2)}, u32[]{:S(2)}) collective-permute-start(bf16[32,16,128]{2,1,0:T(8,128)(2,1)S(1)} %collective-permute-done.10.refs_3_), channel_id=1, source_target_pairs={{0,1},{1,0},{2,3},{3,2},{4,5},{5,4},{6,7},{7,6},{8,9},{9,8},{10,11... | collective-permute-start | bytes 393224 | tf_op jit(solution)/shard_map/ppermute | solution.py:571

commit v10 on v9

--- a/solution.py
+++ b/solution.py
@@ -446,25 +446,27 @@
             linked = jnp.exp(ends[peer]) * leaving + part
             leaving = jnp.where(peer > me, linked, leaving)
         carried.append((block_diagonal(entering, heads), block_diagonal(leaving, heads)))
-    finish(copies)
-    copies = []
+    late, copies = copies, []
     rem_terms, quot_terms = [], []
     for u in range(users):
         at = slice(u * block, (u + 1) * block)
         entering, leaving = carried[u]
+        dmixed = dmixed_ref[at, :]
+        wide = wide_ref[at, :]
+        growth = scale * jnp.exp(wide)
+        falloff = scale * jnp.exp(wide[block - 1 : block, :] - wide)
+        dq_carried = growth * dot(dmixed, entering, NT)
+        if u == 0:
+            finish(late)
         embedded = (quot_ref[at, :].astype(f32) * rem_ref[at, :].astype(f32)).astype(bf16)
         q = dot(embedded, wq_ref[...]).astype(bf16)
         k = dot(embedded, wk_ref[...]).astype(bf16)
         v = dot(embedded, wv_ref[...]).astype(bf16)
-        dmixed = dmixed_ref[at, :]
-        wide = wide_ref[at, :]
-        growth = scale * jnp.exp(wide)
-        falloff = scale * jnp.exp(wide[block - 1 : block, :] - wide)
         mixed = (near_ref[at, :] + growth * dot(q, entering)).astype(bf16)
         out_ref[u] = dot(mixed, w_out_ref[...]).astype(bf16)
         copies += begin([(out_ref.at[u], out_hbm.at[u])], arrived, 5 + users + u)
         finish(waits[u : u + 1])
-        dq = (far_ref[0, at, :] + growth * dot(dmixed, entering, NT)).astype(bf16)
+        dq = (far_ref[0, at, :] + dq_carried).astype(bf16)
         dk = (far_ref[1, at, :] + falloff * dot(v, leaving, NT)).astype(bf16)
         dv = (far_ref[2, at, :] + falloff * dot(k, leaving)).astype(bf16)
         dembedded = dot(dq, wq_ref[...], NT) + dot(dk, wk_ref[...], NT) + dot(dv, wv_ref[...], NT)

time: 140 us -> 140 us (level)
  no operation moved by 1% of the time
where the time goes in v10:
time: 140 us; the launch traced here: 139 us
  starting transfers between devices  57.2 us (41%)
  waiting for transfers between devices  33.6 us (24%)
  Pallas kernels  27 us (19%)
  blocking collectives  20.5 us (15%)
    all_to_all x5, starting transfers between devices, exchange(): return lax.all_to_all(array, axis, split_axis=0, concat_axis=0, tiled=True)  28.9 us
    pallas_call x15, Pallas kernels, call(): pl.pallas_call(kernel, out_shape=tuple(shapes), in_specs=specs, out_specs...  27 us
    all_to_all x5, waiting for transfers between devices, exchange(): return lax.all_to_all(array, axis, split_axis=0, concat_axis=0, tiled=True)  25.7 us
    all_to_all x1, blocking collectives, exchange(): return lax.all_to_all(array, axis, split_axis=0, concat_axis=0, tiled=True)  20.5 us
    ppermute x10, starting transfers between devices, to_core(): return lax.ppermute(array, 'hist', [(i, i ^ 1) for i in range(peers)])  14.7 us
    ppermute x12, starting transfers between devices, to_chip(): lax.ppermute(array, 'hist', [(i, (i + 2 * steps) % peers) for i in range(...  13.6 us
    ppermute x12, waiting for transfers between devices, to_chip(): lax.ppermute(array, 'hist', [(i, (i + 2 * steps) % peers) for i in range(...  6.31 us
  transfers between devices with their start and end apart: 27, of which 9 were waited for; matrix products, arithmetic and copies ran while one was open for 0% of the time, Pallas kernels for 10%

profile of v10, /device:TPU:1, one launch (start us, length us, event | category | flops | bytes accessed | tf_op | source)
XLA Modules:
  0.0 139.3 jit_solution(11969697484545051096)
XLA Ops:
  0.6 1.4 shard_map.130
  2.0 20.5 %all_to_all.30.wanted_ref = s32[32,1,128]{2,1,0:T(1,128)S(1)} all-to-all(s32[32,1,128]{2,1,0:T(1,128)S(1)} %get-tuple-element.37), channel_id=1, replica_groups=mesh['user'=32,'hist'=8] {'user'}, dimensions={0} | all-to-all | bytes 32768 | tf_op jit(solution)/shard_map/all_to_all | solution.py:568
  22.5 3.0 %shard_map.131 = bf16[1024,256]{1,0:T(8,128)(2,1)} custom-call(s32[32,1,128]{2,1,0:T(1,128)S(1)} %all_to_all.30.wanted_ref, bf16[2048,256]{1,0:T(8,128)(2,1)S(1)} %get-tuple-element.38.table_ref), custom_call_target="tpu_custom_call" | custom-call | tf_op jit(solution)/shard_map/pallas_call | solution.py:114
  25.5 3.9 %all-to-all-start.1 = ((bf16[32,32,256]{2,1,0:T(8,128)(2,1)}), bf16[32,32,256]{2,1,0:T(8,128)(2,1)S(1)}, u32[]{:S(2)}, u32[]{:S(2)}) async-start(bf16[32,32,256]{2,1,0:T(8,128)(2,1)} %bitcast.8), calls=%async_computation.1 | async-start | bytes 1048576 | tf_op jit(solution)/shard_map/all_to_all | solution.py:568
  29.4 2.9 %shard_map.132 = (bf16[512,256]{1,0:T(8,128)(2,1)S(1)}, bf16[512,256]{1,0:T(8,128)(2,1)S(1)}, f32[512,256]{1,0:T(8,128)S(1)}) custom-call(s32[2]{0:T(128)S(1)} %copy-done, s32[1]{0:T(128)} %bitcast.at_ref, s32[2,256]{1,0:T(2,128)} %ids_hbm.3, bf16[2048,256]{1,0:T(8,128)(2,1)} %table_ref.1, bf16[2,256,256]{2,1,0:T(8,128)(2,1)} %cot_ref.1, ...), custom_call_target="tpu_custom_call" | custom-call | tf_op jit(solution)/shard_map/pallas_call | solution.py:114
  32.3 10.0 %all-to-all-done.1 = bf16[32,32,256]{2,1,0:T(8,128)(2,1)S(1)} async-done(((bf16[32,32,256]{2,1,0:T(8,128)(2,1)}), bf16[32,32,256]{2,1,0:T(8,128)(2,1)S(1)}, u32[]{:S(2)}, u32[]{:S(2)}) %all-to-all-start.1) | async-done | bytes 524320 | tf_op jit(solution)/shard_map/all_to_all | solution.py:568
  42.4 3.0 %shard_map.133 = (bf16[512,256]{1,0:T(8,128)(2,1)S(1)}, bf16[8,144,256]{2,1,0:T(8,128)(2,1)}) custom-call(s32[1]{0:T(128)} %bitcast.at_ref, s32[8,256]{1,0:T(8,128)S(1)} %get-tuple-element.36.slot_ref, bf16[1024,256]{1,0:T(8,128)(2,1)S(1)} %bitcast.7, bf16[512,256]{1,0:T(8,128)(2,1)S(1)} %get-tuple-element.39.quot_ref, bf16[256,256]{1,0:T(8,128)(2,1)} %wq_hbm.3, ...), custom_call_target="tpu_custom_call" | custom-call | tf_op jit(solution)/shard_map/pallas_call | solution.py:114
  45.4 9.5 %all-to-all-start.2 = ((bf16[8,144,256]{2,1,0:T(8,128)(2,1)}), bf16[8,144,256]{2,1,0:T(8,128)(2,1)S(1)}, u32[]{:S(2)}, u32[]{:S(2)}) async-start(bf16[8,144,256]{2,1,0:T(8,128)(2,1)} %get-tuple-element.42), calls=%async_computation.2 | async-start | bytes 1179648 | tf_op jit(solution)/shard_map/all_to_all | solution.py:568
  54.9 5.4 %shard_map.134 = (f32[512,256]{1,0:T(8,128)S(1)}, f32[3,512,256]{2,1,0:T(8,128)}) custom-call(bf16[512,256]{1,0:T(8,128)(2,1)S(1)} %get-tuple-element.39.quot_ref, bf16[512,256]{1,0:T(8,128)(2,1)S(1)} %get-tuple-element.43.rem_ref, bf16[512,256]{1,0:T(8,128)(2,1)S(1)} %get-tuple-element.41.dmixed_ref, f32[2,4,256]{2,1,0:T(4,128)} %decay_ref.3, ...), custom_call_target="tpu_custom_call" | custom-call | tf_op jit(solution)/shard_map/pallas_call | solution.py:114
  60.3 4.8 %all-to-all-done.2.payload_ref = bf16[8,144,256]{2,1,0:T(8,128)(2,1)S(1)} async-done(((bf16[8,144,256]{2,1,0:T(8,128)(2,1)}), bf16[8,144,256]{2,1,0:T(8,128)(2,1)S(1)}, u32[]{:S(2)}, u32[]{:S(2)}) %all-to-all-start.2) | async-done | bytes 589856 | tf_op jit(solution)/shard_map/all_to_all | solution.py:568
  65.1 4.1 %shard_map.135 = (bf16[2,256,256]{2,1,0:T(8,128)(2,1)}, bf16[1024,256]{1,0:T(8,128)(2,1)}, bf16[1024,256]{1,0:T(8,128)(2,1)S(1)}, bf16[1024,256]{1,0:T(8,128)(2,1)S(1)}) custom-call(s32[1]{0:T(128)} %bitcast.at_ref, bf16[8,144,256]{2,1,0:T(8,128)(2,1)S(1)} %all-to-all-done.2.payload_ref, f32[512,256]{1,0:T(8,128)S(1)} %get-tuple-element.44.near_ref, ...), custom_call_target="tpu_custom_call" | custom-call | tf_op jit(solution)/shard_map/pallas_call | solution.py:114
  69.2 5.0 %all-to-all-start.3 = ((bf16[32,32,256]{2,1,0:T(8,128)(2,1)}), bf16[32,32,256]{2,1,0:T(8,128)(2,1)S(1)}, u32[]{:S(2)}, u32[]{:S(2)}) async-start(bf16[32,32,256]{2,1,0:T(8,128)(2,1)} %bitcast.9), calls=%async_computation.3 | async-start | bytes 1048576 | tf_op jit(solution)/shard_map/all_to_all | solution.py:568
  74.2 1.4 %collective-permute-start = (bf16[1024,256]{1,0:T(8,128)(2,1)S(1)}, bf16[1024,256]{1,0:T(8,128)(2,1)S(1)}, u32[]{:S(2)}, u32[]{:S(2)}) collective-permute-start(bf16[1024,256]{1,0:T(8,128)(2,1)S(1)} %get-tuple-element.49), channel_id=1, source_target_pairs={{0,1},{1,0},{2,3},{3,2},{4,5},{5,4},{6,7},{7,6},{8,9},{9,8},{10,11... | collective-permute-start | bytes 1572872 | tf_op jit(solution)/shard_map/ppermute | solution.py:573
  75.7 1.5 %collective-permute-done.got_ref = bf16[1024,256]{1,0:T(8,128)(2,1)S(1)} collective-permute-done((bf16[1024,256]{1,0:T(8,128)(2,1)S(1)}, bf16[1024,256]{1,0:T(8,128)(2,1)S(1)}, u32[]{:S(2)}, u32[]{:S(2)}) %collective-permute-start) | collective-permute-done | bytes 524320 | tf_op jit(solution)/shard_map/ppermute | solution.py:573
  77.2 0.1 shard_map.136
  77.3 0.4 collective-permute-start.1
  77.7 1.8 %collective-permute-start.2 = (bf16[256,256]{1,0:T(8,128)(2,1)S(1)}, bf16[256,256]{1,0:T(8,128)(2,1)S(1)}, u32[]{:S(2)}, u32[]{:S(2)}) collective-permute-start(bf16[256,256]{1,0:T(8,128)(2,1)S(1)} %get-tuple-element.52), channel_id=1, source_target_pairs={{0,4},{1,5},{2,6},{3,7},{4,0},{5,1},{6,2},{7,3},{8,12},{9,13},{10,... | collective-permute-start | bytes 393224 | tf_op jit(solution)/shard_map/ppermute | solution.py:578
  79.5 0.7 collective-permute-start.3
  80.2 3.7 %collective-permute-done.1.refs_1_ = bf16[256,256]{1,0:T(8,128)(2,1)S(1)} collective-permute-done((bf16[256,256]{1,0:T(8,128)(2,1)S(1)}, bf16[256,256]{1,0:T(8,128)(2,1)S(1)}, u32[]{:S(2)}, u32[]{:S(2)}) %collective-permute-start.1) | collective-permute-done | bytes 131104 | tf_op jit(solution)/shard_map/ppermute | solution.py:578
  83.9 1.6 %collective-permute-done.2.refs_2_ = bf16[256,256]{1,0:T(8,128)(2,1)S(1)} collective-permute-done((bf16[256,256]{1,0:T(8,128)(2,1)S(1)}, bf16[256,256]{1,0:T(8,128)(2,1)S(1)}, u32[]{:S(2)}, u32[]{:S(2)}) %collective-permute-start.2) | collective-permute-done | bytes 131104 | tf_op jit(solution)/shard_map/ppermute | solution.py:578
  85.6 0.9 collective-permute-done.3.refs_3_
  86.5 0.7 shard_map.137
  87.2 1.1 all-to-all-done.3
  88.3 0.9 shard_map.140
  89.1 4.1 %collective-permute-start.4 = (bf16[1024,256]{1,0:T(8,128)(2,1)S(1)}, bf16[1024,256]{1,0:T(8,128)(2,1)S(1)}, u32[]{:S(2)}, u32[]{:S(2)}) collective-permute-start(bf16[1024,256]{1,0:T(8,128)(2,1)S(1)} %shard_map.140), channel_id=1, source_target_pairs={{0,1},{1,0},{2,3},{3,2},{4,5},{5,4},{6,7},{7,6},{8,9},{9,8},{10,11... | collective-permute-start | bytes 1572872 | tf_op jit(solution)/shard_map/ppermute | solution.py:573
  93.2 5.9 %all-to-all-start.4 = ((bf16[32,16,128]{2,1,0:T(8,128)(2,1)}), bf16[32,16,128]{2,1,0:T(8,128)(2,1)S(1)}, u32[]{:S(2)}, u32[]{:S(2)}) async-start(bf16[32,16,128]{2,1,0:T(8,128)(2,1)} %shard_map.137), calls=%async_computation.4 | async-start | bytes 262144 | tf_op jit(solution)/shard_map/all_to_all | solution.py:568
  99.2 0.9 shard_map.139.keep_ref
  100.0 0.0 collective-permute-done.4.got_ref
  100.0 0.1 shard_map.141
  100.2 0.1 collective-permute-start.5
  100.3 3.3 %collective-permute-start.6 = (bf16[256,256]{1,0:T(8,128)(2,1)S(1)}, bf16[256,256]{1,0:T(8,128)(2,1)S(1)}, u32[]{:S(2)}, u32[]{:S(2)}) collective-permute-start(bf16[256,256]{1,0:T(8,128)(2,1)S(1)} %get-tuple-element.58), channel_id=1, source_target_pairs={{0,4},{1,5},{2,6},{3,7},{4,0},{5,1},{6,2},{7,3},{8,12},{9,13},{10,... | collective-permute-start | bytes 393224 | tf_op jit(solution)/shard_map/ppermute | solution.py:578
  103.6 0.0 collective-permute-start.7
  103.6 4.7 %all-to-all-done.4.tiles_ref = bf16[32,16,128]{2,1,0:T(8,128)(2,1)S(1)} async-done(((bf16[32,16,128]{2,1,0:T(8,128)(2,1)}), bf16[32,16,128]{2,1,0:T(8,128)(2,1)S(1)}, u32[]{:S(2)}, u32[]{:S(2)}) %all-to-all-start.4) | async-done | bytes 131104 | tf_op jit(solution)/shard_map/all_to_all | solution.py:568
  108.3 0.7 shard_map.138
  109.0 4.5 %all-to-all-start.5 = ((bf16[32,16,128]{2,1,0:T(8,128)(2,1)}), bf16[32,16,128]{2,1,0:T(8,128)(2,1)S(1)}, u32[]{:S(2)}, u32[]{:S(2)}) async-start(bf16[32,16,128]{2,1,0:T(8,128)(2,1)} %shard_map.138), calls=%async_computation.5 | async-start | bytes 262144 | tf_op jit(solution)/shard_map/all_to_all | solution.py:568
  113.5 0.0 collective-permute-done.5
  113.5 0.0 collective-permute-done.6
  113.6 0.0 collective-permute-done.7
  113.6 0.1 add_convert_fusion.refs_0_
  113.6 1.5 %collective-permute-start.11 = (bf16[256,256]{1,0:T(8,128)(2,1)S(1)}, bf16[256,256]{1,0:T(8,128)(2,1)S(1)}, u32[]{:S(2)}, u32[]{:S(2)}) collective-permute-start(bf16[256,256]{1,0:T(8,128)(2,1)S(1)} %add_convert_fusion.refs_0_), channel_id=1, source_target_pairs={{0,2},{1,3},{2,4},{3,5},{4,6},{5,7},{6,0},{7,1},{8,10},{9,11},{10,... | collective-permute-start | bytes 393224 | tf_op jit(solution)/shard_map/ppermute | solution.py:578
  115.2 1.9 %collective-permute-start.12 = (bf16[256,256]{1,0:T(8,128)(2,1)S(1)}, bf16[256,256]{1,0:T(8,128)(2,1)S(1)}, u32[]{:S(2)}, u32[]{:S(2)}) collective-permute-start(bf16[256,256]{1,0:T(8,128)(2,1)S(1)} %add_convert_fusion.refs_0_), channel_id=1, source_target_pairs={{0,4},{1,5},{2,6},{3,7},{4,0},{5,1},{6,2},{7,3},{8,12},{9,13},{10,... | collective-permute-start | bytes 393224 | tf_op jit(solution)/shard_map/ppermute | solution.py:578
  117.1 0.6 collective-permute-start.13
  117.7 5.0 %all-to-all-done.5.refs_0_ = bf16[32,16,128]{2,1,0:T(8,128)(2,1)S(1)} async-done(((bf16[32,16,128]{2,1,0:T(8,128)(2,1)}), bf16[32,16,128]{2,1,0:T(8,128)(2,1)S(1)}, u32[]{:S(2)}, u32[]{:S(2)}) %all-to-all-start.5) | async-done | bytes 131104 | tf_op jit(solution)/shard_map/all_to_all | solution.py:568
  122.7 2.2 %collective-permute-start.10 = (bf16[32,16,128]{2,1,0:T(8,128)(2,1)S(1)}, bf16[32,16,128]{2,1,0:T(8,128)(2,1)S(1)}, u32[]{:S(2)}, u32[]{:S(2)}) collective-permute-start(bf16[32,16,128]{2,1,0:T(8,128)(2,1)S(1)} %all-to-all-done.5.refs_0_), channel_id=1, source_target_pairs={{0,6},{1,7},{2,0},{3,1},{4,2},{5,3},{6,4},{7,5},{8,14},{9,15},{10,... | collective-permute-start | bytes 393224 | tf_op jit(solution)/shard_map/ppermute | solution.py:578
  124.9 0.0 collective-permute-start.8
  124.9 0.0 collective-permute-done.11.refs_1_
  124.9 1.2 collective-permute-start.9
  126.0 0.0 collective-permute-done.12.refs_2_
  126.0 3.6 %collective-permute-start.18 = (bf16[256,256]{1,0:T(8,128)(2,1)S(1)}, bf16[256,256]{1,0:T(8,128)(2,1)S(1)}, u32[]{:S(2)}, u32[]{:S(2)}) collective-permute-start(bf16[256,256]{1,0:T(8,128)(2,1)S(1)} %add_convert_fusion.refs_0_), channel_id=1, source_target_pairs={{0,1},{1,0},{2,3},{3,2},{4,5},{5,4},{6,7},{7,6},{8,9},{9,8},{10,11... | collective-permute-start | bytes 393224 | tf_op jit(solution)/shard_map/ppermute | solution.py:573
  129.6 0.0 collective-permute-done.13.refs_3_
  129.6 0.3 collective-permute-start.19
  130.0 0.0 collective-permute-done.10.refs_3_
  130.0 1.7 %collective-permute-start.20 = (bf16[256,256]{1,0:T(8,128)(2,1)S(1)}, bf16[256,256]{1,0:T(8,128)(2,1)S(1)}, u32[]{:S(2)}, u32[]{:S(2)}) collective-permute-start(bf16[256,256]{1,0:T(8,128)(2,1)S(1)} %collective-permute-done.12.refs_2_), channel_id=1, source_target_pairs={{0,1},{1,0},{2,3},{3,2},{4,5},{5,4},{6,7},{7,6},{8,9},{9,8},{10,11... | collective-permute-start | bytes 393224 | tf_op jit(solution)/shard_map/ppermute | solution.py:573
  131.6 1.1 shard_map.142.refs_8_
  132.8 0.0 collective-permute-done.8.refs_1_
  132.8 2.6 %collective-permute-start.21 = (bf16[256,256]{1,0:T(8,128)(2,1)S(1)}, bf16[256,256]{1,0:T(8,128)(2,1)S(1)}, u32[]{:S(2)}, u32[]{:S(2)}) collective-permute-start(bf16[256,256]{1,0:T(8,128)(2,1)S(1)} %collective-permute-done.13.refs_3_), channel_id=1, source_target_pairs={{0,1},{1,0},{2,3},{3,2},{4,5},{5,4},{6,7},{7,6},{8,9},{9,8},{10,11... | collective-permute-start | bytes 393224 | tf_op jit(solution)/shard_map/ppermute | solution.py:573
  135.4 0.0 collective-permute-start.14
  135.4 0.5 collective-permute-start.15
  135.9 0.1 collective-permute-start.16
  136.0 0.0 collective-permute-done.20.refs_6_
  136.0 0.4 collective-permute-start.17
  136.4 1.5 %shard_map.143 = (f32[2048,256]{1,0:T(8,128)}, f32[2048,256]{1,0:T(8,128)}) custom-call(s32[1]{0:T(128)} %bitcast.at_ref, s32[32,1,128]{2,1,0:T(1,128)S(1)} %all_to_all.30.wanted_ref, bf16[32,16,128]{2,1,0:T(8,128)(2,1)S(1)} %all-to-all-done.5.refs_0_, bf16[32,16,128]{2,1,0:T(8,128)(2,1)S(1)} %collective-permute-done.8.refs_1_, ...), custom_call_target="tpu_custom_call", output_to_operand_aliasing={{1}: (10, {})} | custom-call | tf_op jit(solution)/shard_map/pallas_call | solution.py:114
  138.0 0.0 collective-permute-done.16.refs_2_
  138.0 1.2 shard_map.144
  (9 shorter events, 0.0 us)
Async XLA Ops:
  0.6 28.8 %copy-start = (s32[2]{0:T(128)S(1)}, s32[2]{0:T(128)}, u32[]{:S(2)}) copy-start(s32[2]{0:T(128)} %len_ref.1) | copy-start | bytes 28
  25.5 16.9 %all-to-all-start.1 = ((bf16[32,32,256]{2,1,0:T(8,128)(2,1)}), bf16[32,32,256]{2,1,0:T(8,128)(2,1)S(1)}, u32[]{:S(2)}, u32[]{:S(2)}) async-start(bf16[32,32,256]{2,1,0:T(8,128)(2,1)} %bitcast.8), calls=%async_computation.1 | async-start | bytes 1048576 | tf_op jit(solution)/shard_map/all_to_all | solution.py:568
  45.4 19.7 %all-to-all-start.2 = ((bf16[8,144,256]{2,1,0:T(8,128)(2,1)}), bf16[8,144,256]{2,1,0:T(8,128)(2,1)S(1)}, u32[]{:S(2)}, u32[]{:S(2)}) async-start(bf16[8,144,256]{2,1,0:T(8,128)(2,1)} %get-tuple-element.42), calls=%async_computation.2 | async-start | bytes 1179648 | tf_op jit(solution)/shard_map/all_to_all | solution.py:568
  69.2 19.1 %all-to-all-start.3 = ((bf16[32,32,256]{2,1,0:T(8,128)(2,1)}), bf16[32,32,256]{2,1,0:T(8,128)(2,1)S(1)}, u32[]{:S(2)}, u32[]{:S(2)}) async-start(bf16[32,32,256]{2,1,0:T(8,128)(2,1)} %bitcast.9), calls=%async_computation.3 | async-start | bytes 1048576 | tf_op jit(solution)/shard_map/all_to_all | solution.py:568
  74.2 3.0 %collective-permute-start = (bf16[1024,256]{1,0:T(8,128)(2,1)S(1)}, bf16[1024,256]{1,0:T(8,128)(2,1)S(1)}, u32[]{:S(2)}, u32[]{:S(2)}) collective-permute-start(bf16[1024,256]{1,0:T(8,128)(2,1)S(1)} %get-tuple-element.49), channel_id=1, source_target_pairs={{0,1},{1,0},{2,3},{3,2},{4,5},{5,4},{6,7},{7,6},{8,9},{9,8},{10,11... | collective-permute-start | bytes 1572872 | tf_op jit(solution)/shard_map/ppermute | solution.py:573
  77.3 6.6 %collective-permute-start.1 = (bf16[256,256]{1,0:T(8,128)(2,1)S(1)}, bf16[256,256]{1,0:T(8,128)(2,1)S(1)}, u32[]{:S(2)}, u32[]{:S(2)}) collective-permute-start(bf16[256,256]{1,0:T(8,128)(2,1)S(1)} %get-tuple-element.51), channel_id=1, source_target_pairs={{0,2},{1,3},{2,4},{3,5},{4,6},{5,7},{6,0},{7,1},{8,10},{9,11},{10,... | collective-permute-start | bytes 393224 | tf_op jit(solution)/shard_map/ppermute | solution.py:578
  77.7 7.9 %collective-permute-start.2 = (bf16[256,256]{1,0:T(8,128)(2,1)S(1)}, bf16[256,256]{1,0:T(8,128)(2,1)S(1)}, u32[]{:S(2)}, u32[]{:S(2)}) collective-permute-start(bf16[256,256]{1,0:T(8,128)(2,1)S(1)} %get-tuple-element.52), channel_id=1, source_target_pairs={{0,4},{1,5},{2,6},{3,7},{4,0},{5,1},{6,2},{7,3},{8,12},{9,13},{10,... | collective-permute-start | bytes 393224 | tf_op jit(solution)/shard_map/ppermute | solution.py:578
  79.5 7.0 %collective-permute-start.3 = (bf16[256,256]{1,0:T(8,128)(2,1)S(1)}, bf16[256,256]{1,0:T(8,128)(2,1)S(1)}, u32[]{:S(2)}, u32[]{:S(2)}) collective-permute-start(bf16[256,256]{1,0:T(8,128)(2,1)S(1)} %get-tuple-element.53), channel_id=1, source_target_pairs={{0,6},{1,7},{2,0},{3,1},{4,2},{5,3},{6,4},{7,5},{8,14},{9,15},{10,... | collective-permute-start | bytes 393224 | tf_op jit(solution)/shard_map/ppermute | solution.py:578
  89.1 10.9 %collective-permute-start.4 = (bf16[1024,256]{1,0:T(8,128)(2,1)S(1)}, bf16[1024,256]{1,0:T(8,128)(2,1)S(1)}, u32[]{:S(2)}, u32[]{:S(2)}) collective-permute-start(bf16[1024,256]{1,0:T(8,128)(2,1)S(1)} %shard_map.140), channel_id=1, source_target_pairs={{0,1},{1,0},{2,3},{3,2},{4,5},{5,4},{6,7},{7,6},{8,9},{9,8},{10,11... | collective-permute-start | bytes 1572872 | tf_op jit(solution)/shard_map/ppermute | solution.py:573
  93.2 15.1 %all-to-all-start.4 = ((bf16[32,16,128]{2,1,0:T(8,128)(2,1)}), bf16[32,16,128]{2,1,0:T(8,128)(2,1)S(1)}, u32[]{:S(2)}, u32[]{:S(2)}) async-start(bf16[32,16,128]{2,1,0:T(8,128)(2,1)} %shard_map.137), calls=%async_computation.4 | async-start | bytes 262144 | tf_op jit(solution)/shard_map/all_to_all | solution.py:568
  100.2 13.4 %collective-permute-start.5 = (bf16[256,256]{1,0:T(8,128)(2,1)S(1)}, bf16[256,256]{1,0:T(8,128)(2,1)S(1)}, u32[]{:S(2)}, u32[]{:S(2)}) collective-permute-start(bf16[256,256]{1,0:T(8,128)(2,1)S(1)} %get-tuple-element.57), channel_id=1, source_target_pairs={{0,2},{1,3},{2,4},{3,5},{4,6},{5,7},{6,0},{7,1},{8,10},{9,11},{10,... | collective-permute-start | bytes 393224 | tf_op jit(solution)/shard_map/ppermute | solution.py:578
  100.3 13.3 %collective-permute-start.6 = (bf16[256,256]{1,0:T(8,128)(2,1)S(1)}, bf16[256,256]{1,0:T(8,128)(2,1)S(1)}, u32[]{:S(2)}, u32[]{:S(2)}) collective-permute-start(bf16[256,256]{1,0:T(8,128)(2,1)S(1)} %get-tuple-element.58), channel_id=1, source_target_pairs={{0,4},{1,5},{2,6},{3,7},{4,0},{5,1},{6,2},{7,3},{8,12},{9,13},{10,... | collective-permute-start | bytes 393224 | tf_op jit(solution)/shard_map/ppermute | solution.py:578
  103.6 10.0 %collective-permute-start.7 = (bf16[256,256]{1,0:T(8,128)(2,1)S(1)}, bf16[256,256]{1,0:T(8,128)(2,1)S(1)}, u32[]{:S(2)}, u32[]{:S(2)}) collective-permute-start(bf16[256,256]{1,0:T(8,128)(2,1)S(1)} %get-tuple-element.59), channel_id=1, source_target_pairs={{0,6},{1,7},{2,0},{3,1},{4,2},{5,3},{6,4},{7,5},{8,14},{9,15},{10,... | collective-permute-start | bytes 393224 | tf_op jit(solution)/shard_map/ppermute | solution.py:578
  109.0 13.7 %all-to-all-start.5 = ((bf16[32,16,128]{2,1,0:T(8,128)(2,1)}), bf16[32,16,128]{2,1,0:T(8,128)(2,1)S(1)}, u32[]{:S(2)}, u32[]{:S(2)}) async-start(bf16[32,16,128]{2,1,0:T(8,128)(2,1)} %shard_map.138), calls=%async_computation.5 | async-start | bytes 262144 | tf_op jit(solution)/shard_map/all_to_all | solution.py:568
  113.6 11.2 %collective-permute-start.11 = (bf16[256,256]{1,0:T(8,128)(2,1)S(1)}, bf16[256,256]{1,0:T(8,128)(2,1)S(1)}, u32[]{:S(2)}, u32[]{:S(2)}) collective-permute-start(bf16[256,256]{1,0:T(8,128)(2,1)S(1)} %add_convert_fusion.refs_0_), channel_id=1, source_target_pairs={{0,2},{1,3},{2,4},{3,5},{4,6},{5,7},{6,0},{7,1},{8,10},{9,11},{10,... | collective-permute-start | bytes 393224 | tf_op jit(solution)/shard_map/ppermute | solution.py:578
  115.2 10.9 %collective-permute-start.12 = (bf16[256,256]{1,0:T(8,128)(2,1)S(1)}, bf16[256,256]{1,0:T(8,128)(2,1)S(1)}, u32[]{:S(2)}, u32[]{:S(2)}) collective-permute-start(bf16[256,256]{1,0:T(8,128)(2,1)S(1)} %add_convert_fusion.refs_0_), channel_id=1, source_target_pairs={{0,4},{1,5},{2,6},{3,7},{4,0},{5,1},{6,2},{7,3},{8,12},{9,13},{10,... | collective-permute-start | bytes 393224 | tf_op jit(solution)/shard_map/ppermute | solution.py:578
  117.1 12.6 %collective-permute-start.13 = (bf16[256,256]{1,0:T(8,128)(2,1)S(1)}, bf16[256,256]{1,0:T(8,128)(2,1)S(1)}, u32[]{:S(2)}, u32[]{:S(2)}) collective-permute-start(bf16[256,256]{1,0:T(8,128)(2,1)S(1)} %add_convert_fusion.refs_0_), channel_id=1, source_target_pairs={{0,6},{1,7},{2,0},{3,1},{4,2},{5,3},{6,4},{7,5},{8,14},{9,15},{10,... | collective-permute-start | bytes 393224 | tf_op jit(solution)/shard_map/ppermute | solution.py:578
  122.7 7.3 %collective-permute-start.10 = (bf16[32,16,128]{2,1,0:T(8,128)(2,1)S(1)}, bf16[32,16,128]{2,1,0:T(8,128)(2,1)S(1)}, u32[]{:S(2)}, u32[]{:S(2)}) collective-permute-start(bf16[32,16,128]{2,1,0:T(8,128)(2,1)S(1)} %all-to-all-done.5.refs_0_), channel_id=1, source_target_pairs={{0,6},{1,7},{2,0},{3,1},{4,2},{5,3},{6,4},{7,5},{8,14},{9,15},{10,... | collective-permute-start | bytes 393224 | tf_op jit(solution)/shard_map/ppermute | solution.py:578
  124.9 7.9 %collective-permute-start.8 = (bf16[32,16,128]{2,1,0:T(8,128)(2,1)S(1)}, bf16[32,16,128]{2,1,0:T(8,128)(2,1)S(1)}, u32[]{:S(2)}, u32[]{:S(2)}) collective-permute-start(bf16[32,16,128]{2,1,0:T(8,128)(2,1)S(1)} %all-to-all-done.5.refs_0_), channel_id=1, source_target_pairs={{0,2},{1,3},{2,4},{3,5},{4,6},{5,7},{6,0},{7,1},{8,10},{9,11},{10,... | collective-permute-start | bytes 393224 | tf_op jit(solution)/shard_map/ppermute | solution.py:578
  124.9 10.5 %collective-permute-start.9 = (bf16[32,16,128]{2,1,0:T(8,128)(2,1)S(1)}, bf16[32,16,128]{2,1,0:T(8,128)(2,1)S(1)}, u32[]{:S(2)}, u32[]{:S(2)}) collective-permute-start(bf16[32,16,128]{2,1,0:T(8,128)(2,1)S(1)} %all-to-all-done.5.refs_0_), channel_id=1, source_target_pairs={{0,4},{1,5},{2,6},{3,7},{4,0},{5,1},{6,2},{7,3},{8,12},{9,13},{10,... | collective-permute-start | bytes 393224 | tf_op jit(solution)/shard_map/ppermute | solution.py:578
  126.0 9.3 %collective-permute-start.18 = (bf16[256,256]{1,0:T(8,128)(2,1)S(1)}, bf16[256,256]{1,0:T(8,128)(2,1)S(1)}, u32[]{:S(2)}, u32[]{:S(2)}) collective-permute-start(bf16[256,256]{1,0:T(8,128)(2,1)S(1)} %add_convert_fusion.refs_0_), channel_id=1, source_target_pairs={{0,1},{1,0},{2,3},{3,2},{4,5},{5,4},{6,7},{7,6},{8,9},{9,8},{10,11... | collective-permute-start | bytes 393224 | tf_op jit(solution)/shard_map/ppermute | solution.py:573
  129.6 6.3 %collective-permute-start.19 = (bf16[256,256]{1,0:T(8,128)(2,1)S(1)}, bf16[256,256]{1,0:T(8,128)(2,1)S(1)}, u32[]{:S(2)}, u32[]{:S(2)}) collective-permute-start(bf16[256,256]{1,0:T(8,128)(2,1)S(1)} %collective-permute-done.11.refs_1_), channel_id=1, source_target_pairs={{0,1},{1,0},{2,3},{3,2},{4,5},{5,4},{6,7},{7,6},{8,9},{9,8},{10,11... | collective-permute-start | bytes 393224 | tf_op jit(solution)/shard_map/ppermute | solution.py:573
  130.0 6.0 %collective-permute-start.20 = (bf16[256,256]{1,0:T(8,128)(2,1)S(1)}, bf16[256,256]{1,0:T(8,128)(2,1)S(1)}, u32[]{:S(2)}, u32[]{:S(2)}) collective-permute-start(bf16[256,256]{1,0:T(8,128)(2,1)S(1)} %collective-permute-done.12.refs_2_), channel_id=1, source_target_pairs={{0,1},{1,0},{2,3},{3,2},{4,5},{5,4},{6,7},{7,6},{8,9},{9,8},{10,11... | collective-permute-start | bytes 393224 | tf_op jit(solution)/shard_map/ppermute | solution.py:573
  132.8 3.6 %collective-permute-start.21 = (bf16[256,256]{1,0:T(8,128)(2,1)S(1)}, bf16[256,256]{1,0:T(8,128)(2,1)S(1)}, u32[]{:S(2)}, u32[]{:S(2)}) collective-permute-start(bf16[256,256]{1,0:T(8,128)(2,1)S(1)} %collective-permute-done.13.refs_3_), channel_id=1, source_target_pairs={{0,1},{1,0},{2,3},{3,2},{4,5},{5,4},{6,7},{7,6},{8,9},{9,8},{10,11... | collective-permute-start | bytes 393224 | tf_op jit(solution)/shard_map/ppermute | solution.py:573
  135.4 2.6 %collective-permute-start.14 = (bf16[32,16,128]{2,1,0:T(8,128)(2,1)S(1)}, bf16[32,16,128]{2,1,0:T(8,128)(2,1)S(1)}, u32[]{:S(2)}, u32[]{:S(2)}) collective-permute-start(bf16[32,16,128]{2,1,0:T(8,128)(2,1)S(1)} %all-to-all-done.5.refs_0_), channel_id=1, source_target_pairs={{0,1},{1,0},{2,3},{3,2},{4,5},{5,4},{6,7},{7,6},{8,9},{9,8},{10,11... | collective-permute-start | bytes 393224 | tf_op jit(solution)/shard_map/ppermute | solution.py:573
  135.4 2.6 %collective-permute-start.15 = (bf16[32,16,128]{2,1,0:T(8,128)(2,1)S(1)}, bf16[32,16,128]{2,1,0:T(8,128)(2,1)S(1)}, u32[]{:S(2)}, u32[]{:S(2)}) collective-permute-start(bf16[32,16,128]{2,1,0:T(8,128)(2,1)S(1)} %collective-permute-done.8.refs_1_), channel_id=1, source_target_pairs={{0,1},{1,0},{2,3},{3,2},{4,5},{5,4},{6,7},{7,6},{8,9},{9,8},{10,11... | collective-permute-start | bytes 393224 | tf_op jit(solution)/shard_map/ppermute | solution.py:573
  135.9 2.1 %collective-permute-start.16 = (bf16[32,16,128]{2,1,0:T(8,128)(2,1)S(1)}, bf16[32,16,128]{2,1,0:T(8,128)(2,1)S(1)}, u32[]{:S(2)}, u32[]{:S(2)}) collective-permute-start(bf16[32,16,128]{2,1,0:T(8,128)(2,1)S(1)} %collective-permute-done.9.refs_2_), channel_id=1, source_target_pairs={{0,1},{1,0},{2,3},{3,2},{4,5},{5,4},{6,7},{7,6},{8,9},{9,8},{10,11... | collective-permute-start | bytes 393224 | tf_op jit(solution)/shard_map/ppermute | solution.py:573
  136.0 2.0 %collective-permute-start.17 = (bf16[32,16,128]{2,1,0:T(8,128)(2,1)S(1)}, bf16[32,16,128]{2,1,0:T(8,128)(2,1)S(1)}, u32[]{:S(2)}, u32[]{:S(2)}) collective-permute-start(bf16[32,16,128]{2,1,0:T(8,128)(2,1)S(1)} %collective-permute-done.10.refs_3_), channel_id=1, source_target_pairs={{0,1},{1,0},{2,3},{3,2},{4,5},{5,4},{6,7},{7,6},{8,9},{9,8},{10,11... | collective-permute-start | bytes 393224 | tf_op jit(solution)/shard_map/ppermute | solution.py:573
